TPU v7x, 128 devices: a whole 4x4x4 slice. The times are simulated.
128 devices in a mesh: row: 16 (over x, y_hi, core), col: 8 (over y_lo, z).
Axes of the slice: x: 4, y: 4 (y_hi: 2, y_lo: 2; y = y_hi * 2 + y_lo), z: 4, core: 2. Of those that a mesh axis runs over, the one named last changes fastest.
Arguments:
- iterate: bfloat16 [4096, 12288], P('row', 'col'), may hold values from -0.0546875 to 0.0546875
Outputs:
- update: bfloat16 [4096, 12288], P('row', 'col')
All inputs are finite; a program needn't handle non-finite values.
Results may differ from a plain program's by a relative error of at most 0.03.
Values may be sent and summed in bfloat16 or wider, within the bound.
No kernel may reach another device: no remote copies, remote signals or barrier semaphores. Data moves between devices by JAX's collectives and lax.ppermute only.
A program may use at most 64 MiB of HBM per device.

v0:
```python
import math

import jax
import jax.numpy as jnp
from jax import lax
from jax.sharding import PartitionSpec as P

linear_coef = 3.4445
cubic_coef = -4.775
quintic_coef = 2.0315


def contract_last(left, right):
    return lax.dot_general(
        left, right, (((1,), (1,)), ((), ())), preferred_element_type=jnp.float32
    )


def on_device(iterate):
    rows_dev = iterate.shape[0]
    total_cols = iterate.shape[1] * lax.axis_size("col")
    total_rows = rows_dev * lax.axis_size("row")
    tile_cols = total_rows // lax.axis_size("col")
    gathered = lax.all_gather(iterate, "row", axis=0, tiled=True)
    partial_gram = contract_last(iterate, gathered)
    gram_tile = lax.psum_scatter(partial_gram, "col", scatter_dimension=1, tiled=True).astype(
        jnp.bfloat16
    )
    square = contract_last(gram_tile, lax.all_gather(gram_tile, "row", axis=0, tiled=True))
    offset = lax.axis_index("col") * tile_cols
    linear_part = lax.dynamic_update_slice(
        jnp.zeros_like(square), cubic_coef * gram_tile.astype(jnp.float32), (0, offset)
    )
    mixing = lax.psum(quintic_coef * square + linear_part, "col").astype(jnp.bfloat16)
    applied = jnp.dot(mixing, gathered, preferred_element_type=jnp.float32)
    update = linear_coef * iterate.astype(jnp.float32) + applied
    return (math.sqrt(total_cols) * update).astype(jnp.bfloat16)


def solution(mesh):
    return jax.shard_map(
        on_device,
        mesh=mesh,
        in_specs=(P("row", "col"),),
        out_specs=P("row", "col"),
        check_vma=False,
    )
```

profile of v0, /device:TPU:0, one launch (start us, length us, event | category | flops | bytes accessed | tf_op | source)
XLA Modules:
  0.0 335.6 jit_solution(5559986813975325096)
XLA Ops:
  6.5 0.0 all-gather.3.cloned.1.call-start
  6.5 0.7 all-gather.3.cloned.1.call-update
  7.3 0.0 reduce-scatter.2.cloned.1.call-start
  7.3 95.8 %all-gather.3.cloned.1.call-done = bf16[4096,1536]{1,0:T(8,128)(2,1)} async-done(((bf16[256,1536]{1,0:T(8,128)(2,1)}), bf16[4096,1536]{1,0:T(8,128)(2,1)}) %all-gather.3.cloned.1.call-update) | async-done | bytes 12582928 | tf_op jit(solution)/shard_map/all_gather | solution.py:24
  103.1 10.2 %fusion.3 = f32[256,4096]{1,0:T(8,128)} fusion(bf16[256,1536]{1,0:T(8,128)(2,1)} %param.1, bf16[4096,1536]{1,0:T(8,128)(2,1)} %all-gather.3.cloned.1.call-done), kind=kOutput, calls=%fused_computation.6 | convolution fusion | flops 3221225472 | bytes 17563648 | tf_op jit(solution)/shard_map/dot_general | solution.py:14
  113.3 0.0 reduce-scatter.2.cloned.1.call-update
  113.4 0.0 all-gather.5.cloned.1.call-start
  113.4 51.2 %reduce-scatter.2.cloned.1.call-done = f32[256,512]{1,0:T(8,128)} async-done(((f32[256,4096]{1,0:T(8,128)}), f32[256,512]{1,0:T(8,128)}) %reduce-scatter.2.cloned.1.call-update) | async-done | bytes 524304 | tf_op jit(solution)/shard_map/reduce_scatter | solution.py:26
  164.6 1.8 convert_element_type.16
  166.4 0.0 all-gather.5.cloned.1.call-update
  166.4 0.0 copy-start
  166.4 55.2 %all-gather.5.cloned.1.call-done = bf16[4096,512]{1,0:T(8,128)(2,1)} async-done(((bf16[256,512]{1,0:T(8,128)(2,1)}), bf16[4096,512]{1,0:T(8,128)(2,1)}) %all-gather.5.cloned.1.call-update) | async-done | bytes 4194320 | tf_op jit(solution)/shard_map/all_gather | solution.py:29
  221.7 5.5 %convolution_multiply_fusion = f32[256,4096]{1,0:T(8,128)} fusion(bf16[256,512]{1,0:T(8,128)(2,1)} %convert_element_type.16, bf16[4096,512]{1,0:T(8,128)(2,1)} %all-gather.5.cloned.1.call-done), kind=kOutput, calls=%fused_computation | convolution fusion | flops 1074790400 | bytes 8650752 | tf_op jit(solution)/shard_map/dot_general | solution.py:14
  227.2 0.0 copy-done
  227.2 0.0 copy-start.1
  227.2 2.0 add_dynamic-update-slice_fusion
  229.2 90.9 %all-reduce.1 = bf16[256,4096]{1,0:T(8,128)(2,1)S(1)} all-reduce(f32[256,4096]{1,0:T(8,128)} %add_dynamic-update-slice_fusion), channel_id=1, replica_groups=mesh['row'=16,'col'=8] {'col'}, use_global_device_ids=true, to_apply=%region_1.0 | all-reduce | flops 1048576 | bytes 6291456 | tf_op jit(solution)/shard_map/psum | solution.py:34
  320.1 0.0 copy-done.1
  320.2 8.9 %fusion.1 = bf16[256,1536]{1,0:T(8,128)(2,1)} fusion(bf16[4096,1536]{1,0:T(8,128)(2,1)} %all-gather.3.cloned.1.call-done, bf16[256,4096]{1,0:T(8,128)(2,1)S(1)} %all-reduce.1, bf16[256,1536]{1,0:T(8,128)(2,1)S(1)} %copy-done.1), kind=kOutput, calls=%fused_computation.3 | convolution fusion | flops 3223191552 | bytes 16252928 | tf_op jit(solution)/shard_map/dot_general | solution.py:35
Async XLA Ops:
  6.5 96.6 %all-gather.3.cloned.1.call-start = ((), (), s32[]{:S(2)}) async-start(), calls=%async_computation.1 | async-start | bytes 13369344 | tf_op jit(solution)/shard_map/all_gather | solution.py:24
  7.3 157.4 %reduce-scatter.2.cloned.1.call-start = ((), (), s32[]{:S(2)}) async-start(), calls=%async_computation.2 | async-start | bytes 4718592 | tf_op jit(solution)/shard_map/reduce_scatter | solution.py:26
  113.4 108.3 %all-gather.5.cloned.1.call-start = ((), (), s32[]{:S(2)}) async-start(), calls=%async_computation.3 | async-start | bytes 4456448 | tf_op jit(solution)/shard_map/all_gather | solution.py:29
  166.4 60.8 %copy-start = (f32[256,512]{1,0:T(8,128)S(1)}, f32[256,512]{1,0:T(8,128)}, u32[]{:S(2)}) copy-start(f32[256,512]{1,0:T(8,128)} %reduce-scatter.2.cloned.1.call-done) | copy-start | bytes 1572868
  227.2 92.9 %copy-start.1 = (bf16[256,1536]{1,0:T(8,128)(2,1)S(1)}, bf16[256,1536]{1,0:T(8,128)(2,1)}, u32[]{:S(2)}) copy-start(bf16[256,1536]{1,0:T(8,128)(2,1)} %param.1) | copy-start | bytes 2359300
Sparse Core Ops, SparseCore 0:
  9.7 93.3 all-gather.2
  113.5 51.0 reduce-scatter.1
  167.0 54.6 all-gather.4
where the time goes:
time: 336 us
  waiting for transfers between devices  203 us (60%)
  blocking collectives  90.9 us (27%)
  matrix products  24.6 us (7%)
  between operations  13.1 us (4%)
  other arithmetic  3.81 us (1%)
    all_gather x1, waiting for transfers between devices, on_device(): gathered = lax.all_gather(iterate, 'row', axis=0, tiled=True)  95.8 us
    psum x1, blocking collectives, on_device(): lax.psum(quintic_coef * square + linear_part, 'col').astype(jnp.bfloat16)  90.9 us
    all_gather x1, waiting for transfers between devices, on_device(): lax.all_gather(gram_tile, 'row', axis=0, tiled=True)  55.2 us
    reduce_scatter x1, waiting for transfers between devices, on_device(): lax.psum_scatter(partial_gram, 'col', scatter_dimension=1, tiled=True)  51.2 us
    dot_general x2, matrix products, contract_last(): lax.dot_general(left, right, (((1,), (1,)), ((), ())), preferred_element_...  15.7 us
    dot_general x1, matrix products, on_device(): applied = jnp.dot(mixing, gathered, preferred_element_type=jnp.float32)  8.87 us
  transfers between devices with their start and end apart: 3, of which 3 were waited for; matrix products, arithmetic and copies ran while one was open for 0% of the time, Pallas kernels for 0%

commit v1 on v0

v1 whole, which is shorter than its diff:
```python
import functools
import math

import jax
import jax.numpy as jnp
from jax import lax
from jax.experimental import pallas as pl
from jax.experimental.pallas import tpu as pltpu
from jax.sharding import PartitionSpec as P

linear_coef = 3.4445
cubic_coef = -4.775
quintic_coef = 2.0315

NX, NY, NC, NZ = 4, 2, 2, 4
BLOCK = 256
TILE = 2 * BLOCK
SLOTS = [(0, 0), (0, 1), (0, 3), (0, 2), (1, 0), (1, 1), (1, 3), (1, 2)]
MIB = 1 << 20


def pairs(move):
    out = []
    for x in range(NX):
        for yh in range(NY):
            for core in range(NC):
                for yl in range(NY):
                    for z in range(NZ):
                        source = ((x * 2 + yh) * 2 + core) * 8 + yl * 4 + z
                        a, b, c, d, e = move(x, yh, core, yl, z)
                        a, e = a % NX, e % NZ
                        out.append((source, ((a * 2 + b) * 2 + c) * 8 + d * 4 + e))
    return out


def way(core):
    return 1 - 2 * core


MOVES = {
    "core": lambda x, yh, c, yl, z: (x, yh, 1 - c, yl, z),
    "yh": lambda x, yh, c, yl, z: (x, 1 - yh, c, yl, z),
    "yl": lambda x, yh, c, yl, z: (x, yh, c, 1 - yl, z),
    "x_fore": lambda x, yh, c, yl, z: (x + way(c), yh, c, yl, z),
    "x_back": lambda x, yh, c, yl, z: (x - way(c), yh, c, yl, z),
    "z_fore": lambda x, yh, c, yl, z: (x, yh, c, yl, z + way(c)),
    "z_back": lambda x, yh, c, yl, z: (x, yh, c, yl, z - way(c)),
}
for _dy, _dz in SLOTS[1:]:
    MOVES[(_dy, _dz)] = lambda x, yh, c, yl, z, _dy=_dy, _dz=_dz: (x, yh, c, (yl + _dy) % 2, z + _dz)


def send(value, move):
    return lax.ppermute(value, ("row", "col"), pairs(MOVES[move]))


def place(delta, core):
    delta = lax.rem(delta + 8, 4)
    side = jnp.where(delta == 3 - 2 * core, 1, 2)
    return jnp.where(delta == 0, 0, jnp.where(delta == 2, 3, side))


def ahead(position, core):
    return (0, 2 * core - 1, 1 - 2 * core, 2)[position]


def nt(left, right):
    return lax.dot_general(left, right, (((1,), (1,)), ((), ())), preferred_element_type=jnp.float32)


def nn(left, right):
    return lax.dot_general(left, right, (((1,), (0,)), ((), ())), preferred_element_type=jnp.float32)


def gram_near_kernel(own, other, fore, fore_other, back, back_other, across, out, acc):
    step = pl.program_id(0)

    @pl.when(step == 0)
    def _():
        acc[...] = jnp.zeros_like(acc)

    for r, rows in enumerate((own, across)):
        for q, cols in enumerate((own, other, fore, fore_other, back, back_other)):
            acc[r, q // 2, :, (q % 2) * BLOCK : (q % 2 + 1) * BLOCK] += nt(rows[...], cols[...])

    @pl.when(step == pl.num_programs(0) - 1)
    def _():
        out[...] = acc[...].astype(out.dtype)


def gram_far_kernel(where, own, across, far, far_other, near, *rest):
    outs, (acc, tiles) = rest[:8], rest[8:]
    step = pl.program_id(0)

    @pl.when(step == 0)
    def _():
        acc[...] = jnp.zeros_like(acc)

    for r, rows in enumerate((own, across)):
        for q, cols in enumerate((far, far_other)):
            acc[r, :, q * BLOCK : (q + 1) * BLOCK] += nt(rows[...], cols[...])

    @pl.when(step == pl.num_programs(0) - 1)
    def _():
        x, yh, core, yl, z = (where[i] for i in range(5))
        for r in range(2):
            tiles[r, 0:3] = near[r]
            tiles[r, 3] = acc[r].astype(tiles.dtype)
        for out, (dy, dz) in zip(outs, SLOTS):
            row = lax.rem(yl + dy + yh, 2)
            out[...] = tiles[row, place(z + dz - x, core)]


def square_kernel(where, *rest):
    left, right, (mine, theirs), (held,) = rest[:8], rest[8:16], rest[16:18], rest[18:]
    x, yh, core, yl, z = (where[i] for i in range(5))
    for dy in range(2):
        for position in range(4):
            held[dy, position] = right[dy * 4 + position][...]
    total = jnp.zeros((TILE, TILE), jnp.float32)
    for dy in range(2):
        for position in range(4):
            row = lax.rem(yh + dy + yl, 2)
            col = place(z + ahead(position, core) - x, core)
            total += nn(left[dy * 4 + position][...], held[row, col])
    mine[...] = total[:BLOCK]
    theirs[:, :BLOCK] = total[BLOCK:, BLOCK:].astype(theirs.dtype)
    theirs[:, BLOCK:] = total[BLOCK:, :BLOCK].astype(theirs.dtype)


def apply_kernel(other_rows, where, *rest):
    mixing, blocks, rest = rest[:8], rest[8:16], rest[16:]
    out, held = rest[-2:]
    x, yh, core, yl, z = (where[i] for i in range(5))

    @pl.when(pl.program_id(0) == 0)
    def _():
        which = lax.rem(yh + yl + int(other_rows), 2)
        for dy in range(2):

            @pl.when(which == dy)
            def _():
                for position in range(4):
                    col = place(z + ahead(position, core) - x, core)
                    held[col] = mixing[dy * 4 + position][...]

    total = jnp.zeros(out.shape, jnp.float32)
    for position in range(4):
        for half in range(2):
            total += nn(
                held[position, :, half * BLOCK : (half + 1) * BLOCK], blocks[position * 2 + half][...]
            )
    if not other_rows:
        total = total + linear_coef * rest[0][...].astype(jnp.float32)
    out[...] = total.astype(out.dtype)


def params(mib):
    return pltpu.CompilerParams(vmem_limit_bytes=mib * MIB)


def smem():
    return pl.BlockSpec(memory_space=pltpu.SMEM)


def whole():
    return pl.BlockSpec(memory_space=pltpu.VMEM)


def cost(flops, moved):
    return pl.CostEstimate(flops=flops, bytes_accessed=moved, transcendentals=0)


def gram_tiles(where, own, other, fore, fore_other, back, back_other, far, far_other, across):
    depth = own.shape[1]
    chunk = 512
    steps = depth // chunk
    block = lambda: pl.BlockSpec((BLOCK, chunk), lambda k: (0, k))
    full = lambda shape: pl.BlockSpec(shape, lambda k: (0,) * len(shape))
    near = pl.pallas_call(
        gram_near_kernel,
        grid=(steps,),
        in_specs=[block() for _ in range(7)],
        out_specs=full((2, 3, BLOCK, TILE)),
        out_shape=jax.ShapeDtypeStruct((2, 3, BLOCK, TILE), jnp.bfloat16),
        scratch_shapes=[pltpu.VMEM((2, 3, BLOCK, TILE), jnp.float32)],
        compiler_params=params(32),
        cost_estimate=cost(2 * 6 * BLOCK * TILE * depth, 7 * BLOCK * depth * 2 + 6 * BLOCK * TILE * 2),
        name="gram_near",
    )(own, other, fore, fore_other, back, back_other, across)
    return pl.pallas_call(
        gram_far_kernel,
        grid=(steps,),
        in_specs=[smem()] + [block() for _ in range(4)] + [full((2, 3, BLOCK, TILE))],
        out_specs=[full((BLOCK, TILE)) for _ in range(8)],
        out_shape=[jax.ShapeDtypeStruct((BLOCK, TILE), jnp.bfloat16) for _ in range(8)],
        scratch_shapes=[
            pltpu.VMEM((2, BLOCK, TILE), jnp.float32),
            pltpu.VMEM((2, 4, BLOCK, TILE), jnp.bfloat16),
        ],
        compiler_params=params(32),
        cost_estimate=cost(2 * 2 * BLOCK * TILE * depth, 4 * BLOCK * depth * 2 + 14 * BLOCK * TILE * 2),
        name="gram_far",
    )(where, own, across, far, far_other, near)


def square_part(where, left, right):
    return pl.pallas_call(
        square_kernel,
        in_specs=[smem()] + [whole() for _ in range(16)],
        out_specs=[whole(), whole()],
        out_shape=[
            jax.ShapeDtypeStruct((BLOCK, TILE), jnp.float32),
            jax.ShapeDtypeStruct((BLOCK, TILE), jnp.bfloat16),
        ],
        scratch_shapes=[pltpu.VMEM((2, 4, BLOCK, TILE), jnp.bfloat16)],
        compiler_params=params(32),
        cost_estimate=cost(2 * 8 * TILE * TILE * BLOCK, 16 * BLOCK * TILE * 2),
        name="square_part",
    )(where, *left, *right)


def apply_part(other_rows, where, mixing, blocks, own):
    depth = own.shape[1]
    chunk = 512
    column = lambda: pl.BlockSpec((BLOCK, chunk), lambda k: (0, k))
    full = lambda shape: pl.BlockSpec(shape, lambda k: (0,) * len(shape))
    extra = [] if other_rows else [own]
    return pl.pallas_call(
        functools.partial(apply_kernel, other_rows),
        grid=(depth // chunk,),
        in_specs=[smem()] + [full((BLOCK, TILE)) for _ in range(8)] + [column() for _ in range(8 + len(extra))],
        out_specs=column(),
        out_shape=jax.ShapeDtypeStruct((BLOCK, depth), jnp.bfloat16 if other_rows else jnp.float32),
        scratch_shapes=[pltpu.VMEM((4, BLOCK, TILE), jnp.bfloat16)],
        compiler_params=params(32),
        cost_estimate=cost(2 * 8 * BLOCK * BLOCK * depth, 9 * BLOCK * depth * 2 + 8 * BLOCK * TILE * 2),
        name="apply_other" if other_rows else "apply_own",
    )(where, *mixing, *blocks, *extra)


def on_device(iterate):
    total_cols = iterate.shape[1] * lax.axis_size("col")
    row, col = lax.axis_index("row"), lax.axis_index("col")
    where = jnp.stack([row // 4, row // 2 % 2, row % 2, col // 4, col % 4]).astype(jnp.int32)

    fore = send(iterate, "x_fore")
    back = send(iterate, "x_back")
    across = send(iterate, "yh")
    other = send(iterate, "core")
    far = send(fore, "x_fore")
    fore_other, back_other = send(back, "core"), send(fore, "core")
    far_other = send(far, "core")

    tiles = gram_tiles(
        where, iterate, other, fore, fore_other, back, back_other, far, far_other, across
    )
    total = tiles[0].astype(jnp.float32)
    for tile, slot in zip(tiles[1:], SLOTS[1:]):
        total = total + send(tile, slot).astype(jnp.float32)
    gram = total.astype(jnp.bfloat16)

    row_part = jnp.concatenate([gram[:, :BLOCK], send(gram[:, BLOCK:], "core")], axis=0)
    left = gather_ring(row_part, "z", "yh")
    right = gather_ring(gram, "x", "yl")
    mine, theirs = square_part(where, left, right)
    square = mine + send(theirs, "core").astype(jnp.float32)
    mixing = (cubic_coef * gram.astype(jnp.float32) + quintic_coef * square).astype(jnp.bfloat16)

    pieces = gather_even(mixing, "z", "yl")
    blocks = [iterate, other, fore, fore_other, back, back_other, far, far_other]
    applied_other = apply_part(True, where, pieces, blocks, iterate)
    applied = apply_part(False, where, pieces, blocks, iterate)
    update = applied + send(applied_other, "yh").astype(jnp.float32)
    return (math.sqrt(total_cols) * update).astype(jnp.bfloat16)


def gather_ring(value, ring, pair):
    there = send(value, pair)
    fore, back = send(value, ring + "_fore"), send(value, ring + "_back")
    there_fore, there_back = send(there, ring + "_fore"), send(there, ring + "_back")
    far = send(jnp.concatenate([fore, there_fore], axis=0), ring + "_fore")
    count = value.shape[0]
    return [value, fore, back, far[:count], there, there_fore, there_back, far[count:]]


def gather_even(value, ring, pair):
    fore, back = send(value, ring + "_fore"), send(value, ring + "_back")
    there = send(value, pair)
    far = send(fore, ring + "_fore")
    there_fore = send(there, ring + "_fore")
    there_back = send(back, pair)
    there_far = send(there_fore, ring + "_fore")
    return [value, fore, back, far, there, there_fore, there_back, there_far]


def solution(mesh):
    return jax.shard_map(
        on_device,
        mesh=mesh,
        in_specs=(P("row", "col"),),
        out_specs=P("row", "col"),
        check_vma=False,
    )
```

time: 336 us -> 174 us (0.52)
  waiting for transfers between devices: 203 us -> 103 us
  blocking collectives: 90.9 us -> 0 us
  starting transfers between devices: 0.08 us -> 49.5 us
  matrix products: 24.6 us -> 0 us
  Pallas kernels: 0 us -> 18 us
  between operations: 13.1 us -> 0.19 us
    all_gather x2 -> x0, waiting for transfers between devices: 151 us -> none  [the longest x1 95.8 us: on_device(): gathered = lax.all_gather(iterate, 'row', axis=0, tiled=True)]
    ppermute x0 -> x37, waiting for transfers between devices: none -> 103 us  [send(): return lax.ppermute(value, ('row', 'col'), pairs(MOVES[move]))]
    psum x1 -> x0, blocking collectives: 90.9 us -> none  [on_device(): lax.psum(quintic_coef * square + linear_part, 'col').astype(jnp.bfloat16)]
    reduce_scatter x1 -> x0, waiting for transfers between devices: 51.2 us -> none  [on_device(): lax.psum_scatter(partial_gram, 'col', scatter_dimension=1, tiled=True)]
    ppermute x0 -> x37, starting transfers between devices: none -> 49.5 us  [send(): return lax.ppermute(value, ('row', 'col'), pairs(MOVES[move]))]
    dot_general x3 -> x0, matrix products: 24.6 us -> none  [the longest x2 15.7 us: contract_last(): lax.dot_general(left, right, (((1,), (1,)), ((), ())), preferred_element_...]
    pallas_call x0 -> x5, Pallas kernels: none -> 18 us  [the longest x2 7.82 us: apply_part(): pl.pallas_call(functools.partial(apply_kernel, other_rows), grid=(depth /...]
  transfers between devices with their start and end apart: 3 -> 37, of which waited for: 3 -> 19; matrix products, arithmetic and copies ran while one was open for 0% -> 0% of each run, Pallas kernels for 0% -> 5%
where the time goes in v1:
time: 174 us
  waiting for transfers between devices  103 us (59%)
  starting transfers between devices  49.5 us (28%)
  Pallas kernels  18 us (10%)
    ppermute x37, waiting for transfers between devices, send(): return lax.ppermute(value, ('row', 'col'), pairs(MOVES[move]))  103 us
    ppermute x37, starting transfers between devices, send(): return lax.ppermute(value, ('row', 'col'), pairs(MOVES[move]))  49.5 us
    pallas_call x2, Pallas kernels, apply_part(): pl.pallas_call(functools.partial(apply_kernel, other_rows), grid=(depth /...  7.82 us
    pallas_call x1, Pallas kernels, gram_tiles(): pl.pallas_call(gram_near_kernel, grid=(steps,), in_specs=[block() for _ i...  4.91 us
  transfers between devices with their start and end apart: 37, of which 19 were waited for; matrix products, arithmetic and copies ran while one was open for 0% of the time, Pallas kernels for 5%

profile of v1, /device:TPU:0, one launch (start us, length us, event | category | flops | bytes accessed | tf_op | source)
XLA Modules:
  0.0 174.0 jit_solution(16968701533296780961)
XLA Ops:
  3.2 17.1 %collective-permute-done.1.fore.rest_10_ = bf16[256,1536]{1,0:T(8,128)(2,1)S(1)} collective-permute-done((bf16[256,1536]{1,0:T(8,128)(2,1)}, bf16[256,1536]{1,0:T(8,128)(2,1)S(1)}, u32[]{:S(2)}, u32[]{:S(2)}) %collective-permute-start.1) | collective-permute-done | bytes 786464 | tf_op jit(solution)/shard_map/ppermute | solution.py:54
  20.4 1.7 collective-permute-start.2
  22.0 3.2 %collective-permute-start = (bf16[256,1536]{1,0:T(8,128)(2,1)}, bf16[256,1536]{1,0:T(8,128)(2,1)}, u32[]{:S(2)}, u32[]{:S(2)}) collective-permute-start(bf16[256,1536]{1,0:T(8,128)(2,1)} %rest_8_.3), channel_id=1, source_target_pairs={{0,16},{1,17},{2,18},{3,19},{4,20},{5,21},{6,22},{7,23},{8,24},{9,... | collective-permute-start | bytes 2359304 | tf_op jit(solution)/shard_map/ppermute | solution.py:54
  25.7 7.8 %collective-permute-done.2.far.rest_14_ = bf16[256,1536]{1,0:T(8,128)(2,1)S(1)} collective-permute-done((bf16[256,1536]{1,0:T(8,128)(2,1)S(1)}, bf16[256,1536]{1,0:T(8,128)(2,1)S(1)}, u32[]{:S(2)}, u32[]{:S(2)}) %collective-permute-start.2) | collective-permute-done | bytes 786464 | tf_op jit(solution)/shard_map/ppermute | solution.py:54
  33.6 10.2 %collective-permute-done.across = bf16[256,1536]{1,0:T(8,128)(2,1)} collective-permute-done((bf16[256,1536]{1,0:T(8,128)(2,1)}, bf16[256,1536]{1,0:T(8,128)(2,1)}, u32[]{:S(2)}, u32[]{:S(2)}) %collective-permute-start) | collective-permute-done | bytes 786464 | tf_op jit(solution)/shard_map/ppermute | solution.py:54
  45.0 4.9 %gram_near.1.near = bf16[2,3,256,512]{3,2,1,0:T(8,128)(2,1)S(1)} custom-call(bf16[256,1536]{1,0:T(8,128)(2,1)S(1)} %copy-done, bf16[256,1536]{1,0:T(8,128)(2,1)} %collective-permute-done.4.other.rest_9_, bf16[256,1536]{1,0:T(8,128)(2,1)S(1)} %collective-permute-done.1.fore.rest_10_, bf16[256,1536]{1,0:T(8,128)(2,1)} %collective-permute-done.6.fore_other.rest_11_, ...), custom_call_target="tpu_custom_call" | custom-call | flops 2415919104 | bytes 7077888 | tf_op jit(solution)/shard_map/gram_near/pallas_call | solution.py:180
  49.9 3.3 %gram_far.1 = (bf16[256,512]{1,0:T(8,128)(2,1)S(1)}, bf16[256,512]{1,0:T(8,128)(2,1)S(1)}, bf16[256,512]{1,0:T(8,128)(2,1)S(1)}, bf16[256,512]{1,0:T(8,128)(2,1)...) custom-call(s32[5]{0:T(128)S(1)} %stack.23.where, ...), custom_call_target="tpu_custom_call" | custom-call | flops 805306368 | bytes 6815744 | tf_op jit(solution)/shard_map/gram_far/pallas_call | solution.py:191
  53.2 2.0 %collective-permute-start.8 = (bf16[256,512]{1,0:T(8,128)(2,1)S(1)}, bf16[256,512]{1,0:T(8,128)(2,1)S(1)}, u32[]{:S(2)}, u32[]{:S(2)}) collective-permute-start(bf16[256,512]{1,0:T(8,128)(2,1)S(1)} %get-tuple-element.16), channel_id=1, source_target_pairs={{0,1},{1,2},{2,3},{3,0},{4,5},{5,6},{6,7},{7,4},{8,9},{9,10},{10,1... | collective-permute-start | bytes 786440 | tf_op jit(solution)/shard_map/ppermute | solution.py:54
  55.2 2.2 %collective-permute-start.9 = (bf16[256,512]{1,0:T(8,128)(2,1)S(1)}, bf16[256,512]{1,0:T(8,128)(2,1)S(1)}, u32[]{:S(2)}, u32[]{:S(2)}) collective-permute-start(bf16[256,512]{1,0:T(8,128)(2,1)S(1)} %get-tuple-element.17), channel_id=1, source_target_pairs={{0,3},{1,0},{2,1},{3,2},{4,7},{5,4},{6,5},{7,6},{8,11},{9,8},{10,9... | collective-permute-start | bytes 786440 | tf_op jit(solution)/shard_map/ppermute | solution.py:54
  57.4 1.8 %collective-permute-start.10 = (bf16[256,512]{1,0:T(8,128)(2,1)S(1)}, bf16[256,512]{1,0:T(8,128)(2,1)S(1)}, u32[]{:S(2)}, u32[]{:S(2)}) collective-permute-start(bf16[256,512]{1,0:T(8,128)(2,1)S(1)} %get-tuple-element.18), channel_id=1, source_target_pairs={{0,2},{1,3},{2,0},{3,1},{4,6},{5,7},{6,4},{7,5},{8,10},{9,11},{10,... | collective-permute-start | bytes 786440 | tf_op jit(solution)/shard_map/ppermute | solution.py:54
  61.7 1.9 %collective-permute-done.8 = bf16[256,512]{1,0:T(8,128)(2,1)S(1)} collective-permute-done((bf16[256,512]{1,0:T(8,128)(2,1)S(1)}, bf16[256,512]{1,0:T(8,128)(2,1)S(1)}, u32[]{:S(2)}, u32[]{:S(2)}) %collective-permute-start.8) | collective-permute-done | bytes 262176 | tf_op jit(solution)/shard_map/ppermute | solution.py:54
  63.6 4.0 %collective-permute-start.13 = (bf16[256,512]{1,0:T(8,128)(2,1)S(1)}, bf16[256,512]{1,0:T(8,128)(2,1)S(1)}, u32[]{:S(2)}, u32[]{:S(2)}) collective-permute-start(bf16[256,512]{1,0:T(8,128)(2,1)S(1)} %get-tuple-element.21), channel_id=1, source_target_pairs={{0,7},{1,4},{2,5},{3,6},{4,3},{5,0},{6,1},{7,2},{8,15},{9,12},{10,... | collective-permute-start | bytes 786440 | tf_op jit(solution)/shard_map/ppermute | solution.py:54
  68.5 8.2 %collective-permute-start.14 = (bf16[256,512]{1,0:T(8,128)(2,1)S(1)}, bf16[256,512]{1,0:T(8,128)(2,1)S(1)}, u32[]{:S(2)}, u32[]{:S(2)}) collective-permute-start(bf16[256,512]{1,0:T(8,128)(2,1)S(1)} %get-tuple-element.22), channel_id=1, source_target_pairs={{0,6},{1,7},{2,4},{3,5},{4,2},{5,3},{6,0},{7,1},{8,14},{9,15},{10,... | collective-permute-start | bytes 786440 | tf_op jit(solution)/shard_map/ppermute | solution.py:54
  76.7 4.4 %collective-permute-done.13 = bf16[256,512]{1,0:T(8,128)(2,1)S(1)} collective-permute-done((bf16[256,512]{1,0:T(8,128)(2,1)S(1)}, bf16[256,512]{1,0:T(8,128)(2,1)S(1)}, u32[]{:S(2)}, u32[]{:S(2)}) %collective-permute-start.13) | collective-permute-done | bytes 262176 | tf_op jit(solution)/shard_map/ppermute | solution.py:54
  81.2 3.5 %collective-permute-done.14 = bf16[256,512]{1,0:T(8,128)(2,1)S(1)} collective-permute-done((bf16[256,512]{1,0:T(8,128)(2,1)S(1)}, bf16[256,512]{1,0:T(8,128)(2,1)S(1)}, u32[]{:S(2)}, u32[]{:S(2)}) %collective-permute-start.14) | collective-permute-done | bytes 262176 | tf_op jit(solution)/shard_map/ppermute | solution.py:54
  85.0 1.7 collective-permute-start.24
  86.7 3.0 %collective-permute-start.18 = (bf16[512,256]{1,0:T(8,128)(2,1)S(1)}, bf16[512,256]{1,0:T(8,128)(2,1)S(1)}, u32[]{:S(2)}, u32[]{:S(2)}) collective-permute-start(bf16[512,256]{1,0:T(8,128)(2,1)S(1)} %pad_maximum_fusion.2.rest_0_), channel_id=1, source_target_pairs={{0,16},{1,17},{2,18},{3,19},{4,20},{5,21},{6,22},{7,23},{8,24},{9,... | collective-permute-start | bytes 786440 | tf_op jit(solution)/shard_map/ppermute | solution.py:54
  90.5 3.7 %collective-permute-done.24.rest_12_ = bf16[256,512]{1,0:T(8,128)(2,1)S(1)} collective-permute-done((bf16[256,512]{1,0:T(8,128)(2,1)S(1)}, bf16[256,512]{1,0:T(8,128)(2,1)S(1)}, u32[]{:S(2)}, u32[]{:S(2)}) %collective-permute-start.24) | collective-permute-done | bytes 262176 | tf_op jit(solution)/shard_map/ppermute | solution.py:54
  95.5 6.3 %collective-permute-done.18.rest_4_ = bf16[512,256]{1,0:T(8,128)(2,1)S(1)} collective-permute-done((bf16[512,256]{1,0:T(8,128)(2,1)S(1)}, bf16[512,256]{1,0:T(8,128)(2,1)S(1)}, u32[]{:S(2)}, u32[]{:S(2)}) %collective-permute-start.18) | collective-permute-done | bytes 262176 | tf_op jit(solution)/shard_map/ppermute | solution.py:54
  103.2 6.2 %collective-permute-done.19.rest_5_ = bf16[512,256]{1,0:T(8,128)(2,1)S(1)} collective-permute-done((bf16[512,256]{1,0:T(8,128)(2,1)S(1)}, bf16[512,256]{1,0:T(8,128)(2,1)S(1)}, u32[]{:S(2)}, u32[]{:S(2)}) %collective-permute-start.19) | collective-permute-done | bytes 262176 | tf_op jit(solution)/shard_map/ppermute | solution.py:54
  109.5 1.8 %collective-permute-start.23 = (bf16[256,512]{1,0:T(8,128)(2,1)S(1)}, bf16[256,512]{1,0:T(8,128)(2,1)S(1)}, u32[]{:S(2)}, u32[]{:S(2)}) collective-permute-start(bf16[256,512]{1,0:T(8,128)(2,1)S(1)} %add_convert_fusion.1.rest_8_), channel_id=1, source_target_pairs={{0,96},{1,97},{2,98},{3,99},{4,100},{5,101},{6,102},{7,103},{8,40}... | collective-permute-start | bytes 786440 | tf_op jit(solution)/shard_map/ppermute | solution.py:54
  111.4 3.2 %collective-permute-start.17 = (bf16[512,256]{1,0:T(8,128)(2,1)S(1)}, bf16[512,256]{1,0:T(8,128)(2,1)S(1)}, u32[]{:S(2)}, u32[]{:S(2)}) collective-permute-start(bf16[512,256]{1,0:T(8,128)(2,1)S(1)} %pad_maximum_fusion.2.rest_0_), channel_id=1, source_target_pairs={{0,3},{1,0},{2,1},{3,2},{4,7},{5,4},{6,5},{7,6},{8,9},{9,10},{10,1... | collective-permute-start | bytes 786440 | tf_op jit(solution)/shard_map/ppermute | solution.py:54
  116.9 8.4 %collective-permute-done.20 = bf16[1024,256]{1,0:T(8,128)(2,1)S(1)} collective-permute-done((bf16[1024,256]{1,0:T(8,128)(2,1)S(1)}, bf16[1024,256]{1,0:T(8,128)(2,1)S(1)}, u32[]{:S(2)}, u32[]{:S(2)}) %collective-permute-start.20) | collective-permute-done | bytes 524320 | tf_op jit(solution)/shard_map/ppermute | solution.py:54
  125.4 1.9 %square_part.1 = (f32[256,512]{1,0:T(8,128)S(1)}, bf16[256,512]{1,0:T(8,128)(2,1)S(1)}) custom-call(s32[5]{0:T(128)S(1)} %stack.23.where, bf16[512,256]{1,0:T(8,128)(2,1)S(1)} %pad_maximum_fusion.2.rest_0_, bf16[512,256]{1,0:T(8,128)(2,1)S(1)} %collective-permute-done.16.rest_1_, bf16[512,256]{1,0:T(8,128)(2,1)S(1)} %collective-permute-done.17.rest_2_, ...), custom_call_target="tpu_custom_call" | custom-call | flops 1073741824 | bytes 4194304 | tf_op jit(solution)/shard_map/square_part/pallas_call | solution.py:208
  129.3 2.0 %collective-permute-start.29 = (bf16[256,512]{1,0:T(8,128)(2,1)S(1)}, bf16[256,512]{1,0:T(8,128)(2,1)S(1)}, u32[]{:S(2)}, u32[]{:S(2)}) collective-permute-start(bf16[256,512]{1,0:T(8,128)(2,1)S(1)} %add_convert_fusion.rest_0_), channel_id=1, source_target_pairs={{0,1},{1,2},{2,3},{3,0},{4,5},{5,6},{6,7},{7,4},{8,11},{9,8},{10,9... | collective-permute-start | bytes 786440 | tf_op jit(solution)/shard_map/ppermute | solution.py:54
  131.3 6.2 %collective-permute-done.32.rest_4_ = bf16[256,512]{1,0:T(8,128)(2,1)S(1)} collective-permute-done((bf16[256,512]{1,0:T(8,128)(2,1)S(1)}, bf16[256,512]{1,0:T(8,128)(2,1)S(1)}, u32[]{:S(2)}, u32[]{:S(2)}) %collective-permute-start.32) | collective-permute-done | bytes 262176 | tf_op jit(solution)/shard_map/ppermute | solution.py:54
  139.2 5.8 %collective-permute-done.33.rest_5_ = bf16[256,512]{1,0:T(8,128)(2,1)S(1)} collective-permute-done((bf16[256,512]{1,0:T(8,128)(2,1)S(1)}, bf16[256,512]{1,0:T(8,128)(2,1)S(1)}, u32[]{:S(2)}, u32[]{:S(2)}) %collective-permute-start.33) | collective-permute-done | bytes 262176 | tf_op jit(solution)/shard_map/ppermute | solution.py:54
  146.2 1.7 collective-permute-done.31.rest_3_
  147.9 4.8 %collective-permute-done.35.rest_7_ = bf16[256,512]{1,0:T(8,128)(2,1)S(1)} collective-permute-done((bf16[256,512]{1,0:T(8,128)(2,1)S(1)}, bf16[256,512]{1,0:T(8,128)(2,1)S(1)}, u32[]{:S(2)}, u32[]{:S(2)}) %collective-permute-start.35) | collective-permute-done | bytes 262176 | tf_op jit(solution)/shard_map/ppermute | solution.py:54
  152.7 3.9 %apply_other.1 = bf16[256,1536]{1,0:T(8,128)(2,1)S(1)} custom-call(s32[5]{0:T(128)S(1)} %stack.23.where, bf16[256,512]{1,0:T(8,128)(2,1)S(1)} %add_convert_fusion.rest_0_, bf16[256,512]{1,0:T(8,128)(2,1)S(1)} %collective-permute-done.29.rest_1_, bf16[256,512]{1,0:T(8,128)(2,1)S(1)} %collective-permute-done.30.rest_2_, ...), custom_call_target="tpu_custom_call" | custom-call | flops 1610612736 | bytes 9175040 | tf_op jit(solution)/shard_map/apply_other/pallas_call | solution.py:229
  157.3 3.9 %apply_own.1 = f32[256,1536]{1,0:T(8,128)S(1)} custom-call(s32[5]{0:T(128)S(1)} %stack.23.where, bf16[256,512]{1,0:T(8,128)(2,1)S(1)} %add_convert_fusion.rest_0_, bf16[256,512]{1,0:T(8,128)(2,1)S(1)} %collective-permute-done.29.rest_1_, bf16[256,512]{1,0:T(8,128)(2,1)S(1)} %collective-permute-done.30.rest_2_, ...), custom_call_target="tpu_custom_call" | custom-call | flops 1610612736 | bytes 9175040 | tf_op jit(solution)/shard_map/apply_own/pallas_call | solution.py:229
  161.2 11.6 %collective-permute-done.36 = bf16[256,1536]{1,0:T(8,128)(2,1)S(1)} collective-permute-done((bf16[256,1536]{1,0:T(8,128)(2,1)S(1)}, bf16[256,1536]{1,0:T(8,128)(2,1)S(1)}, u32[]{:S(2)}, u32[]{:S(2)}) %collective-permute-start.36) | collective-permute-done | bytes 786464 | tf_op jit(solution)/shard_map/ppermute | solution.py:54
  (61 shorter events, 21.4 us)
Async XLA Ops:
  0.0 20.4 %collective-permute-start.1 = (bf16[256,1536]{1,0:T(8,128)(2,1)}, bf16[256,1536]{1,0:T(8,128)(2,1)S(1)}, u32[]{:S(2)}, u32[]{:S(2)}) collective-permute-start(bf16[256,1536]{1,0:T(8,128)(2,1)} %rest_8_.3), channel_id=1, source_target_pairs={{0,32},{1,33},{2,34},{3,35},{4,36},{5,37},{6,38},{7,39},{8,104},{9... | collective-permute-start | bytes 2359304 | tf_op jit(solution)/shard_map/ppermute | solution.py:54
  1.6 23.7 %collective-permute-start.5 = (bf16[256,1536]{1,0:T(8,128)(2,1)}, bf16[256,1536]{1,0:T(8,128)(2,1)S(1)}, u32[]{:S(2)}, u32[]{:S(2)}) collective-permute-start(bf16[256,1536]{1,0:T(8,128)(2,1)} %rest_8_.3), channel_id=1, source_target_pairs={{0,96},{1,97},{2,98},{3,99},{4,100},{5,101},{6,102},{7,103},{8,40}... | collective-permute-start | bytes 2359304 | tf_op jit(solution)/shard_map/ppermute | solution.py:54
  20.4 13.2 %collective-permute-start.2 = (bf16[256,1536]{1,0:T(8,128)(2,1)S(1)}, bf16[256,1536]{1,0:T(8,128)(2,1)S(1)}, u32[]{:S(2)}, u32[]{:S(2)}) collective-permute-start(bf16[256,1536]{1,0:T(8,128)(2,1)S(1)} %collective-permute-done.1.fore.rest_10_), channel_id=1, source_target_pairs={{0,32},{1,33},{2,34},{3,35},{4,36},{5,37},{6,38},{7,39},{8,104},{9... | collective-permute-start | bytes 2359304 | tf_op jit(solution)/shard_map/ppermute | solution.py:54
  22.0 11.6 %collective-permute-start.4 = (bf16[256,1536]{1,0:T(8,128)(2,1)}, bf16[256,1536]{1,0:T(8,128)(2,1)}, u32[]{:S(2)}, u32[]{:S(2)}) collective-permute-start(bf16[256,1536]{1,0:T(8,128)(2,1)} %rest_8_.3), channel_id=1, source_target_pairs={{0,8},{1,9},{2,10},{3,11},{4,12},{5,13},{6,14},{7,15},{8,0},{9,1},... | collective-permute-start | bytes 2359304 | tf_op jit(solution)/shard_map/ppermute | solution.py:54
  22.0 21.8 %collective-permute-start = (bf16[256,1536]{1,0:T(8,128)(2,1)}, bf16[256,1536]{1,0:T(8,128)(2,1)}, u32[]{:S(2)}, u32[]{:S(2)}) collective-permute-start(bf16[256,1536]{1,0:T(8,128)(2,1)} %rest_8_.3), channel_id=1, source_target_pairs={{0,16},{1,17},{2,18},{3,19},{4,20},{5,21},{6,22},{7,23},{8,24},{9,... | collective-permute-start | bytes 2359304 | tf_op jit(solution)/shard_map/ppermute | solution.py:54
  25.2 18.6 %collective-permute-start.6 = (bf16[256,1536]{1,0:T(8,128)(2,1)S(1)}, bf16[256,1536]{1,0:T(8,128)(2,1)}, u32[]{:S(2)}, u32[]{:S(2)}) collective-permute-start(bf16[256,1536]{1,0:T(8,128)(2,1)S(1)} %collective-permute-done.5.back.rest_12_), channel_id=1, source_target_pairs={{0,8},{1,9},{2,10},{3,11},{4,12},{5,13},{6,14},{7,15},{8,0},{9,1},... | collective-permute-start | bytes 2359304 | tf_op jit(solution)/shard_map/ppermute | solution.py:54
  25.5 18.4 %collective-permute-start.7 = (bf16[256,1536]{1,0:T(8,128)(2,1)S(1)}, bf16[256,1536]{1,0:T(8,128)(2,1)}, u32[]{:S(2)}, u32[]{:S(2)}) collective-permute-start(bf16[256,1536]{1,0:T(8,128)(2,1)S(1)} %collective-permute-done.1.fore.rest_10_), channel_id=1, source_target_pairs={{0,8},{1,9},{2,10},{3,11},{4,12},{5,13},{6,14},{7,15},{8,0},{9,1},... | collective-permute-start | bytes 2359304 | tf_op jit(solution)/shard_map/ppermute | solution.py:54
  33.6 16.3 %collective-permute-start.3 = (bf16[256,1536]{1,0:T(8,128)(2,1)S(1)}, bf16[256,1536]{1,0:T(8,128)(2,1)S(1)}, u32[]{:S(2)}, u32[]{:S(2)}) collective-permute-start(bf16[256,1536]{1,0:T(8,128)(2,1)S(1)} %collective-permute-done.2.far.rest_14_), channel_id=1, source_target_pairs={{0,8},{1,9},{2,10},{3,11},{4,12},{5,13},{6,14},{7,15},{8,0},{9,1},... | collective-permute-start | bytes 2359304 | tf_op jit(solution)/shard_map/ppermute | solution.py:54
  53.2 10.4 %collective-permute-start.8 = (bf16[256,512]{1,0:T(8,128)(2,1)S(1)}, bf16[256,512]{1,0:T(8,128)(2,1)S(1)}, u32[]{:S(2)}, u32[]{:S(2)}) collective-permute-start(bf16[256,512]{1,0:T(8,128)(2,1)S(1)} %get-tuple-element.16), channel_id=1, source_target_pairs={{0,1},{1,2},{2,3},{3,0},{4,5},{5,6},{6,7},{7,4},{8,9},{9,10},{10,1... | collective-permute-start | bytes 786440 | tf_op jit(solution)/shard_map/ppermute | solution.py:54
  55.2 13.3 %collective-permute-start.9 = (bf16[256,512]{1,0:T(8,128)(2,1)S(1)}, bf16[256,512]{1,0:T(8,128)(2,1)S(1)}, u32[]{:S(2)}, u32[]{:S(2)}) collective-permute-start(bf16[256,512]{1,0:T(8,128)(2,1)S(1)} %get-tuple-element.17), channel_id=1, source_target_pairs={{0,3},{1,0},{2,1},{3,2},{4,7},{5,4},{6,5},{7,6},{8,11},{9,8},{10,9... | collective-permute-start | bytes 786440 | tf_op jit(solution)/shard_map/ppermute | solution.py:54
  57.4 19.3 %collective-permute-start.10 = (bf16[256,512]{1,0:T(8,128)(2,1)S(1)}, bf16[256,512]{1,0:T(8,128)(2,1)S(1)}, u32[]{:S(2)}, u32[]{:S(2)}) collective-permute-start(bf16[256,512]{1,0:T(8,128)(2,1)S(1)} %get-tuple-element.18), channel_id=1, source_target_pairs={{0,2},{1,3},{2,0},{3,1},{4,6},{5,7},{6,4},{7,5},{8,10},{9,11},{10,... | collective-permute-start | bytes 786440 | tf_op jit(solution)/shard_map/ppermute | solution.py:54
  59.2 17.5 %collective-permute-start.11 = (bf16[256,512]{1,0:T(8,128)(2,1)S(1)}, bf16[256,512]{1,0:T(8,128)(2,1)S(1)}, u32[]{:S(2)}, u32[]{:S(2)}) collective-permute-start(bf16[256,512]{1,0:T(8,128)(2,1)S(1)} %get-tuple-element.19), channel_id=1, source_target_pairs={{0,4},{1,5},{2,6},{3,7},{4,0},{5,1},{6,2},{7,3},{8,12},{9,13},{10,... | collective-permute-start | bytes 786440 | tf_op jit(solution)/shard_map/ppermute | solution.py:54
  60.8 16.0 %collective-permute-start.12 = (bf16[256,512]{1,0:T(8,128)(2,1)S(1)}, bf16[256,512]{1,0:T(8,128)(2,1)S(1)}, u32[]{:S(2)}, u32[]{:S(2)}) collective-permute-start(bf16[256,512]{1,0:T(8,128)(2,1)S(1)} %get-tuple-element.20), channel_id=1, source_target_pairs={{0,5},{1,6},{2,7},{3,4},{4,1},{5,2},{6,3},{7,0},{8,13},{9,14},{10,... | collective-permute-start | bytes 786440 | tf_op jit(solution)/shard_map/ppermute | solution.py:54
  63.6 17.6 %collective-permute-start.13 = (bf16[256,512]{1,0:T(8,128)(2,1)S(1)}, bf16[256,512]{1,0:T(8,128)(2,1)S(1)}, u32[]{:S(2)}, u32[]{:S(2)}) collective-permute-start(bf16[256,512]{1,0:T(8,128)(2,1)S(1)} %get-tuple-element.21), channel_id=1, source_target_pairs={{0,7},{1,4},{2,5},{3,6},{4,3},{5,0},{6,1},{7,2},{8,15},{9,12},{10,... | collective-permute-start | bytes 786440 | tf_op jit(solution)/shard_map/ppermute | solution.py:54
  68.5 16.1 %collective-permute-start.14 = (bf16[256,512]{1,0:T(8,128)(2,1)S(1)}, bf16[256,512]{1,0:T(8,128)(2,1)S(1)}, u32[]{:S(2)}, u32[]{:S(2)}) collective-permute-start(bf16[256,512]{1,0:T(8,128)(2,1)S(1)} %get-tuple-element.22), channel_id=1, source_target_pairs={{0,6},{1,7},{2,4},{3,5},{4,2},{5,3},{6,0},{7,1},{8,14},{9,15},{10,... | collective-permute-start | bytes 786440 | tf_op jit(solution)/shard_map/ppermute | solution.py:54
  85.0 9.2 %collective-permute-start.24 = (bf16[256,512]{1,0:T(8,128)(2,1)S(1)}, bf16[256,512]{1,0:T(8,128)(2,1)S(1)}, u32[]{:S(2)}, u32[]{:S(2)}) collective-permute-start(bf16[256,512]{1,0:T(8,128)(2,1)S(1)} %add_convert_fusion.1.rest_8_), channel_id=1, source_target_pairs={{0,4},{1,5},{2,6},{3,7},{4,0},{5,1},{6,2},{7,3},{8,12},{9,13},{10,... | collective-permute-start | bytes 786440 | tf_op jit(solution)/shard_map/ppermute | solution.py:54
  86.7 15.1 %collective-permute-start.18 = (bf16[512,256]{1,0:T(8,128)(2,1)S(1)}, bf16[512,256]{1,0:T(8,128)(2,1)S(1)}, u32[]{:S(2)}, u32[]{:S(2)}) collective-permute-start(bf16[512,256]{1,0:T(8,128)(2,1)S(1)} %pad_maximum_fusion.2.rest_0_), channel_id=1, source_target_pairs={{0,16},{1,17},{2,18},{3,19},{4,20},{5,21},{6,22},{7,23},{8,24},{9,... | collective-permute-start | bytes 786440 | tf_op jit(solution)/shard_map/ppermute | solution.py:54
  89.7 12.7 %collective-permute-start.22 = (bf16[256,512]{1,0:T(8,128)(2,1)S(1)}, bf16[256,512]{1,0:T(8,128)(2,1)S(1)}, u32[]{:S(2)}, u32[]{:S(2)}) collective-permute-start(bf16[256,512]{1,0:T(8,128)(2,1)S(1)} %add_convert_fusion.1.rest_8_), channel_id=1, source_target_pairs={{0,32},{1,33},{2,34},{3,35},{4,36},{5,37},{6,38},{7,39},{8,104},{9... | collective-permute-start | bytes 786440 | tf_op jit(solution)/shard_map/ppermute | solution.py:54
  94.2 8.1 %collective-permute-start.25 = (bf16[256,512]{1,0:T(8,128)(2,1)S(1)}, bf16[256,512]{1,0:T(8,128)(2,1)S(1)}, u32[]{:S(2)}, u32[]{:S(2)}) collective-permute-start(bf16[256,512]{1,0:T(8,128)(2,1)S(1)} %collective-permute-done.24.rest_12_), channel_id=1, source_target_pairs={{0,32},{1,33},{2,34},{3,35},{4,36},{5,37},{6,38},{7,39},{8,104},{9... | collective-permute-start | bytes 786440 | tf_op jit(solution)/shard_map/ppermute | solution.py:54
  95.0 8.2 %collective-permute-start.16 = (bf16[512,256]{1,0:T(8,128)(2,1)S(1)}, bf16[512,256]{1,0:T(8,128)(2,1)S(1)}, u32[]{:S(2)}, u32[]{:S(2)}) collective-permute-start(bf16[512,256]{1,0:T(8,128)(2,1)S(1)} %pad_maximum_fusion.2.rest_0_), channel_id=1, source_target_pairs={{0,1},{1,2},{2,3},{3,0},{4,5},{5,6},{6,7},{7,4},{8,11},{9,8},{10,9... | collective-permute-start | bytes 786440 | tf_op jit(solution)/shard_map/ppermute | solution.py:54
  102.4 13.2 %collective-permute-start.26 = (bf16[512,512]{1,0:T(8,128)(2,1)S(1)}, bf16[512,512]{1,0:T(8,128)(2,1)S(1)}, u32[]{:S(2)}, u32[]{:S(2)}) collective-permute-start(bf16[512,512]{1,0:T(8,128)(2,1)S(1)} %pad_maximum_fusion.1), channel_id=1, source_target_pairs={{0,32},{1,33},{2,34},{3,35},{4,36},{5,37},{6,38},{7,39},{8,104},{9... | collective-permute-start | bytes 1572872 | tf_op jit(solution)/shard_map/ppermute | solution.py:54
  109.5 15.8 %collective-permute-start.20 = (bf16[1024,256]{1,0:T(8,128)(2,1)S(1)}, bf16[1024,256]{1,0:T(8,128)(2,1)S(1)}, u32[]{:S(2)}, u32[]{:S(2)}) collective-permute-start(bf16[1024,256]{1,0:T(8,128)(2,1)S(1)} %pad_maximum_fusion), channel_id=1, source_target_pairs={{0,1},{1,2},{2,3},{3,0},{4,5},{5,6},{6,7},{7,4},{8,11},{9,8},{10,9... | collective-permute-start | bytes 1572872 | tf_op jit(solution)/shard_map/ppermute | solution.py:54
  109.5 15.8 %collective-permute-start.23 = (bf16[256,512]{1,0:T(8,128)(2,1)S(1)}, bf16[256,512]{1,0:T(8,128)(2,1)S(1)}, u32[]{:S(2)}, u32[]{:S(2)}) collective-permute-start(bf16[256,512]{1,0:T(8,128)(2,1)S(1)} %add_convert_fusion.1.rest_8_), channel_id=1, source_target_pairs={{0,96},{1,97},{2,98},{3,99},{4,100},{5,101},{6,102},{7,103},{8,40}... | collective-permute-start | bytes 786440 | tf_op jit(solution)/shard_map/ppermute | solution.py:54
  111.4 14.0 %collective-permute-start.17 = (bf16[512,256]{1,0:T(8,128)(2,1)S(1)}, bf16[512,256]{1,0:T(8,128)(2,1)S(1)}, u32[]{:S(2)}, u32[]{:S(2)}) collective-permute-start(bf16[512,256]{1,0:T(8,128)(2,1)S(1)} %pad_maximum_fusion.2.rest_0_), channel_id=1, source_target_pairs={{0,3},{1,0},{2,1},{3,2},{4,7},{5,4},{6,5},{7,6},{8,9},{9,10},{10,1... | collective-permute-start | bytes 786440 | tf_op jit(solution)/shard_map/ppermute | solution.py:54
  114.5 10.9 %collective-permute-start.27 = (bf16[256,512]{1,0:T(8,128)(2,1)S(1)}, bf16[256,512]{1,0:T(8,128)(2,1)S(1)}, u32[]{:S(2)}, u32[]{:S(2)}) collective-permute-start(bf16[256,512]{1,0:T(8,128)(2,1)S(1)} %collective-permute-done.24.rest_12_), channel_id=1, source_target_pairs={{0,96},{1,97},{2,98},{3,99},{4,100},{5,101},{6,102},{7,103},{8,40}... | collective-permute-start | bytes 786440 | tf_op jit(solution)/shard_map/ppermute | solution.py:54
  115.6 9.7 %collective-permute-start.21 = (bf16[512,256]{1,0:T(8,128)(2,1)S(1)}, bf16[512,256]{1,0:T(8,128)(2,1)S(1)}, u32[]{:S(2)}, u32[]{:S(2)}) collective-permute-start(bf16[512,256]{1,0:T(8,128)(2,1)S(1)} %collective-permute-done.18.rest_4_), channel_id=1, source_target_pairs={{0,3},{1,0},{2,1},{3,2},{4,7},{5,4},{6,5},{7,6},{8,9},{9,10},{10,1... | collective-permute-start | bytes 786440 | tf_op jit(solution)/shard_map/ppermute | solution.py:54
  129.1 8.4 %collective-permute-start.32 = (bf16[256,512]{1,0:T(8,128)(2,1)S(1)}, bf16[256,512]{1,0:T(8,128)(2,1)S(1)}, u32[]{:S(2)}, u32[]{:S(2)}) collective-permute-start(bf16[256,512]{1,0:T(8,128)(2,1)S(1)} %add_convert_fusion.rest_0_), channel_id=1, source_target_pairs={{0,4},{1,5},{2,6},{3,7},{4,0},{5,1},{6,2},{7,3},{8,12},{9,13},{10,... | collective-permute-start | bytes 786440 | tf_op jit(solution)/shard_map/ppermute | solution.py:54
  129.3 8.4 %collective-permute-start.30 = (bf16[256,512]{1,0:T(8,128)(2,1)S(1)}, bf16[256,512]{1,0:T(8,128)(2,1)S(1)}, u32[]{:S(2)}, u32[]{:S(2)}) collective-permute-start(bf16[256,512]{1,0:T(8,128)(2,1)S(1)} %add_convert_fusion.rest_0_), channel_id=1, source_target_pairs={{0,3},{1,0},{2,1},{3,2},{4,7},{5,4},{6,5},{7,6},{8,9},{9,10},{10,1... | collective-permute-start | bytes 786440 | tf_op jit(solution)/shard_map/ppermute | solution.py:54
  129.3 10.0 %collective-permute-start.29 = (bf16[256,512]{1,0:T(8,128)(2,1)S(1)}, bf16[256,512]{1,0:T(8,128)(2,1)S(1)}, u32[]{:S(2)}, u32[]{:S(2)}) collective-permute-start(bf16[256,512]{1,0:T(8,128)(2,1)S(1)} %add_convert_fusion.rest_0_), channel_id=1, source_target_pairs={{0,1},{1,2},{2,3},{3,0},{4,5},{5,6},{6,7},{7,4},{8,11},{9,8},{10,9... | collective-permute-start | bytes 786440 | tf_op jit(solution)/shard_map/ppermute | solution.py:54
  137.7 8.5 %collective-permute-start.34 = (bf16[256,512]{1,0:T(8,128)(2,1)S(1)}, bf16[256,512]{1,0:T(8,128)(2,1)S(1)}, u32[]{:S(2)}, u32[]{:S(2)}) collective-permute-start(bf16[256,512]{1,0:T(8,128)(2,1)S(1)} %collective-permute-done.30.rest_2_), channel_id=1, source_target_pairs={{0,4},{1,5},{2,6},{3,7},{4,0},{5,1},{6,2},{7,3},{8,12},{9,13},{10,... | collective-permute-start | bytes 786440 | tf_op jit(solution)/shard_map/ppermute | solution.py:54
  139.2 8.6 %collective-permute-start.31 = (bf16[256,512]{1,0:T(8,128)(2,1)S(1)}, bf16[256,512]{1,0:T(8,128)(2,1)S(1)}, u32[]{:S(2)}, u32[]{:S(2)}) collective-permute-start(bf16[256,512]{1,0:T(8,128)(2,1)S(1)} %collective-permute-done.29.rest_1_), channel_id=1, source_target_pairs={{0,1},{1,2},{2,3},{3,0},{4,5},{5,6},{6,7},{7,4},{8,11},{9,8},{10,9... | collective-permute-start | bytes 786440 | tf_op jit(solution)/shard_map/ppermute | solution.py:54
  156.6 16.3 %collective-permute-start.36 = (bf16[256,1536]{1,0:T(8,128)(2,1)S(1)}, bf16[256,1536]{1,0:T(8,128)(2,1)S(1)}, u32[]{:S(2)}, u32[]{:S(2)}) collective-permute-start(bf16[256,1536]{1,0:T(8,128)(2,1)S(1)} %apply_other.1), channel_id=1, source_target_pairs={{0,16},{1,17},{2,18},{3,19},{4,20},{5,21},{6,22},{7,23},{8,24},{9,... | collective-permute-start | bytes 2359304 | tf_op jit(solution)/shard_map/ppermute | solution.py:54
  (7 other events, 32.2 us)

commit v2 on v1

v2 whole, which is shorter than its diff:
```python
import functools
import math

import jax
import jax.numpy as jnp
from jax import lax
from jax.experimental import pallas as pl
from jax.experimental.pallas import tpu as pltpu
from jax.sharding import PartitionSpec as P

linear_coef = 3.4445
cubic_coef = -4.775
quintic_coef = 2.0315

NX, NY, NC, NZ = 4, 2, 2, 4
BLOCK = 256
TILE = 2 * BLOCK
MIB = 1 << 20


def pairs(move):
    out = []
    for x in range(NX):
        for yh in range(NY):
            for core in range(NC):
                for yl in range(NY):
                    for z in range(NZ):
                        source = ((x * 2 + yh) * 2 + core) * 8 + yl * 4 + z
                        a, b, c, d, e = move(x, yh, core, yl, z)
                        a, e = a % NX, e % NZ
                        out.append((source, ((a * 2 + b) * 2 + c) * 8 + d * 4 + e))
    return out


def way(core):
    return 1 - 2 * core


MOVES = {
    "core": lambda x, yh, c, yl, z: (x, yh, 1 - c, yl, z),
    "yh": lambda x, yh, c, yl, z: (x, 1 - yh, c, yl, z),
    "yl": lambda x, yh, c, yl, z: (x, yh, c, 1 - yl, z),
    "x_fore": lambda x, yh, c, yl, z: (x + way(c), yh, c, yl, z),
    "x_back": lambda x, yh, c, yl, z: (x - way(c), yh, c, yl, z),
    "z_fore": lambda x, yh, c, yl, z: (x, yh, c, yl, z + way(c)),
    "z_back": lambda x, yh, c, yl, z: (x, yh, c, yl, z - way(c)),
}


def send(value, move):
    return lax.ppermute(value, ("row", "col"), pairs(MOVES[move]))


def place(delta, core):
    delta = lax.rem(delta + 8, 4)
    side = jnp.where(delta == 3 - 2 * core, 1, 2)
    return jnp.where(delta == 0, 0, jnp.where(delta == 2, 3, side))


def ahead(position, core):
    return (0, 2 * core - 1, 1 - 2 * core, 2)[position]


def nt(left, right):
    return lax.dot_general(left, right, (((1,), (1,)), ((), ())), preferred_element_type=jnp.float32)


def nn(left, right):
    return lax.dot_general(left, right, (((1,), (0,)), ((), ())), preferred_element_type=jnp.float32)


def gram_near_kernel(own, other, fore, fore_other, back, back_other, across, out):
    for r, rows in enumerate((own, across)):
        for q, cols in enumerate((own, other, fore, fore_other, back, back_other)):
            part = nt(rows[...], cols[...])
            out[r, q // 2, :, (q % 2) * BLOCK : (q % 2 + 1) * BLOCK] = part.astype(out.dtype)


def gram_far_kernel(where, own, across, far, far_other, near, *rest):
    outs, tiles = rest[:8], rest[8]
    x, yh, core, yl, z = (where[i] for i in range(5))
    for r, rows in enumerate((own, across)):
        for q, cols in enumerate((far, far_other)):
            tiles[r, :, q * BLOCK : (q + 1) * BLOCK] = nt(rows[...], cols[...]).astype(tiles.dtype)
    for index, out in enumerate(outs):
        dy, position = index // 4, index % 4
        row = lax.rem(yl + dy + yh, 2)
        col = place(z + ahead(position, core) - x, core)

        @pl.when(col == 3)
        def _():
            out[...] = tiles[row]

        @pl.when(col != 3)
        def _():
            out[...] = near[row, jnp.minimum(col, 2)]


def square_kernel(where, *rest):
    left, right, (mine, theirs), (held,) = rest[:8], rest[8:16], rest[16:18], rest[18:]
    x, yh, core, yl, z = (where[i] for i in range(5))
    for dy in range(2):
        for position in range(4):
            held[dy, position] = right[dy * 4 + position][...]
    total = jnp.zeros((TILE, TILE), jnp.float32)
    for dy in range(2):
        for position in range(4):
            row = lax.rem(yh + dy + yl, 2)
            col = place(z + ahead(position, core) - x, core)
            total += nn(left[dy * 4 + position][...], held[row, col])
    mine[...] = total[:BLOCK]
    theirs[:, :BLOCK] = total[BLOCK:, BLOCK:].astype(theirs.dtype)
    theirs[:, BLOCK:] = total[BLOCK:, :BLOCK].astype(theirs.dtype)


def apply_kernel(other_rows, where, *rest):
    mixing, blocks, rest = rest[:8], rest[8:16], rest[16:]
    out, held = rest[-2:]
    x, yh, core, yl, z = (where[i] for i in range(5))
    which = lax.rem(yh + yl + int(other_rows), 2)
    for dy in range(2):

        @pl.when(which == dy)
        def _():
            for position in range(4):
                col = place(z + ahead(position, core) - x, core)
                held[col] = mixing[dy * 4 + position][...]

    for start in range(0, out.shape[1], TILE):
        columns = slice(start, start + TILE)
        total = jnp.zeros((BLOCK, TILE), jnp.float32)
        for position in range(4):
            for half in range(2):
                total += nn(
                    held[position, :, half * BLOCK : (half + 1) * BLOCK],
                    blocks[position * 2 + half][:, columns],
                )
        if not other_rows:
            total = total + linear_coef * blocks[0][:, columns].astype(jnp.float32)
        out[:, columns] = total.astype(out.dtype)


def params(mib):
    return pltpu.CompilerParams(vmem_limit_bytes=mib * MIB)


def smem():
    return pl.BlockSpec(memory_space=pltpu.SMEM)


def whole():
    return pl.BlockSpec(memory_space=pltpu.VMEM)


def cost(flops, moved):
    return pl.CostEstimate(flops=flops, bytes_accessed=moved, transcendentals=0)


def gram_near(own, other, fore, fore_other, back, back_other, across):
    depth = own.shape[1]
    return pl.pallas_call(
        gram_near_kernel,
        in_specs=[whole() for _ in range(7)],
        out_specs=whole(),
        out_shape=jax.ShapeDtypeStruct((2, 3, BLOCK, TILE), jnp.bfloat16),
        compiler_params=params(24),
        cost_estimate=cost(2 * 6 * BLOCK * TILE * depth, 7 * BLOCK * depth * 2 + 6 * BLOCK * TILE * 2),
        name="gram_near",
    )(own, other, fore, fore_other, back, back_other, across)


def gram_far(where, own, across, far, far_other, near):
    depth = own.shape[1]
    return pl.pallas_call(
        gram_far_kernel,
        in_specs=[smem()] + [whole() for _ in range(5)],
        out_specs=[whole() for _ in range(8)],
        out_shape=[jax.ShapeDtypeStruct((BLOCK, TILE), jnp.bfloat16) for _ in range(8)],
        scratch_shapes=[pltpu.VMEM((2, BLOCK, TILE), jnp.bfloat16)],
        compiler_params=params(24),
        cost_estimate=cost(2 * 2 * BLOCK * TILE * depth, 4 * BLOCK * depth * 2 + 14 * BLOCK * TILE * 2),
        name="gram_far",
    )(where, own, across, far, far_other, near)


def square_part(where, left, right):
    return pl.pallas_call(
        square_kernel,
        in_specs=[smem()] + [whole() for _ in range(16)],
        out_specs=[whole(), whole()],
        out_shape=[
            jax.ShapeDtypeStruct((BLOCK, TILE), jnp.float32),
            jax.ShapeDtypeStruct((BLOCK, TILE), jnp.bfloat16),
        ],
        scratch_shapes=[pltpu.VMEM((2, 4, BLOCK, TILE), jnp.bfloat16)],
        compiler_params=params(24),
        cost_estimate=cost(2 * 8 * TILE * TILE * BLOCK, 16 * BLOCK * TILE * 2),
        name="square_part",
    )(where, *left, *right)


def apply_part(other_rows, where, mixing, blocks):
    depth = blocks[0].shape[1]
    return pl.pallas_call(
        functools.partial(apply_kernel, other_rows),
        in_specs=[smem()] + [whole() for _ in range(16)],
        out_specs=whole(),
        out_shape=jax.ShapeDtypeStruct((BLOCK, depth), jnp.bfloat16 if other_rows else jnp.float32),
        scratch_shapes=[pltpu.VMEM((4, BLOCK, TILE), jnp.bfloat16)],
        compiler_params=params(24),
        cost_estimate=cost(2 * 8 * BLOCK * BLOCK * depth, 9 * BLOCK * depth * 2 + 8 * BLOCK * TILE * 2),
        name="apply_other" if other_rows else "apply_own",
    )(where, *mixing, *blocks)


def add(left, right):
    return (left.astype(jnp.float32) + right.astype(jnp.float32)).astype(jnp.bfloat16)


def gather_rings(sides):
    first = [
        [send(value, pair), send(value, ring + "_fore"), send(value, ring + "_back")]
        for value, ring, pair in sides
    ]
    first = lax.optimization_barrier(first)
    second = [
        [
            send(jnp.concatenate([there, fore], axis=0), ring + "_fore"),
            send(there, ring + "_back"),
        ]
        for (there, fore, back), (value, ring, pair) in zip(first, sides)
    ]
    second = lax.optimization_barrier(second)
    out = []
    for (there, fore, back), (both, there_back), (value, ring, pair) in zip(first, second, sides):
        count = value.shape[0]
        there_fore, far = both[:count], both[count:]
        there_far = send(there_fore, ring + "_fore")
        out.append([value, fore, back, far, there, there_fore, there_back, there_far])
    return out


def gather_even(value, ring, pair):
    there, fore, back = lax.optimization_barrier(
        [send(value, pair), send(value, ring + "_fore"), send(value, ring + "_back")]
    )
    there_fore = send(there, ring + "_fore")
    far = send(fore, ring + "_fore")
    there_back = send(back, pair)
    there_far = send(there_fore, ring + "_fore")
    return [value, fore, back, far, there, there_fore, there_back, there_far]


def sum_over_col(tiles):
    chain = add(tiles[5], send(tiles[7], "z_back"))
    back = add(tiles[1], send(tiles[3], "z_back"))
    fore = add(tiles[2], send(tiles[6], "yl"))
    there = add(tiles[4], send(chain, "z_back"))
    total = tiles[0].astype(jnp.float32)
    total = total + send(back, "z_back").astype(jnp.float32)
    total = total + send(fore, "z_fore").astype(jnp.float32)
    total = total + send(there, "yl").astype(jnp.float32)
    return total.astype(jnp.bfloat16)


def on_device(iterate):
    total_cols = iterate.shape[1] * lax.axis_size("col")
    row, col = lax.axis_index("row"), lax.axis_index("col")
    where = jnp.stack([row >> 2, (row >> 1) & 1, row & 1, col >> 2, col & 3]).astype(jnp.int32)

    fore, back, across, other = lax.optimization_barrier(
        [send(iterate, move) for move in ("x_fore", "x_back", "yh", "core")]
    )
    far = send(fore, "x_fore")
    fore_other, back_other = send(back, "core"), send(fore, "core")
    near = gram_near(iterate, other, fore, fore_other, back, back_other, across)
    far_other = send(far, "core")
    gram = sum_over_col(gram_far(where, iterate, across, far, far_other, near))

    row_part = jnp.concatenate([gram[:, :BLOCK], send(gram[:, BLOCK:], "core")], axis=0)
    left, right = gather_rings([(row_part, "z", "yh"), (gram, "x", "yl")])
    mine, theirs = square_part(where, left, right)
    square = mine + send(theirs, "core").astype(jnp.float32)
    mixing = (cubic_coef * gram.astype(jnp.float32) + quintic_coef * square).astype(jnp.bfloat16)

    pieces = gather_even(mixing, "z", "yl")
    blocks = [iterate, other, fore, fore_other, back, back_other, far, far_other]
    applied_other = apply_part(True, where, pieces, blocks)
    applied = apply_part(False, where, pieces, blocks)
    update = applied + send(applied_other, "yh").astype(jnp.float32)
    return (math.sqrt(total_cols) * update).astype(jnp.bfloat16)


def solution(mesh):
    return jax.shard_map(
        on_device,
        mesh=mesh,
        in_specs=(P("row", "col"),),
        out_specs=P("row", "col"),
        check_vma=False,
    )
```

time: 174 us -> 162 us (0.931)
  waiting for transfers between devices: 103 us -> 94.2 us
  starting transfers between devices: 49.5 us -> 46 us
  Pallas kernels: 18 us -> 15 us
  local copies, waits for them, and re-layouts: 1.31 us -> 3.32 us
    ppermute x37, waiting for transfers between devices: 103 us -> 94.2 us  [send(): return lax.ppermute(value, ('row', 'col'), pairs(MOVES[move]))]
    ppermute x37, starting transfers between devices: 49.5 us -> 46 us  [send(): return lax.ppermute(value, ('row', 'col'), pairs(MOVES[move]))]
    pallas_call x4, Pallas kernels: 16 us -> 13.1 us  [the longest x2 7 us: apply_part(): pl.pallas_call(functools.partial(apply_kernel, other_rows), in_specs=[sme...]
    unnamed x4 -> x8, local copies, waits for them, and re-layouts: 1.14 us -> 3.14 us
  transfers between devices with their start and end apart: 37 -> 37, of which waited for: 19 -> 30; matrix products, arithmetic and copies ran while one was open for 0% -> 0% of each run, Pallas kernels for 5% -> 5%
where the time goes in v2:
time: 162 us; the launch traced here: 160 us
  waiting for transfers between devices  94.2 us (58%)
  starting transfers between devices  46 us (28%)
  Pallas kernels  15 us (9%)
  local copies, waits for them, and re-layouts  3.32 us (2%)
  other arithmetic  1.7 us (1%)
    ppermute x37, waiting for transfers between devices, send(): return lax.ppermute(value, ('row', 'col'), pairs(MOVES[move]))  94.2 us
    ppermute x37, starting transfers between devices, send(): return lax.ppermute(value, ('row', 'col'), pairs(MOVES[move]))  46 us
    pallas_call x2, Pallas kernels, apply_part(): pl.pallas_call(functools.partial(apply_kernel, other_rows), in_specs=[sme...  7 us
    pallas_call x1, Pallas kernels, gram_near(): pl.pallas_call(gram_near_kernel, in_specs=[whole() for _ in range(7)], ou...  4.31 us
  transfers between devices with their start and end apart: 37, of which 30 were waited for; matrix products, arithmetic and copies ran while one was open for 0% of the time, Pallas kernels for 5%

profile of v2, /device:TPU:0, one launch (start us, length us, event | category | flops | bytes accessed | tf_op | source)
XLA Modules:
  0.0 160.3 jit_solution(1545285993169371681)
XLA Ops:
  0.0 3.3 %collective-permute-start.2 = (bf16[256,1536]{1,0:T(8,128)(2,1)}, bf16[256,1536]{1,0:T(8,128)(2,1)S(1)}, u32[]{:S(2)}, u32[]{:S(2)}) collective-permute-start(bf16[256,1536]{1,0:T(8,128)(2,1)} %rest_8_.3), channel_id=1, source_target_pairs={{0,16},{1,17},{2,18},{3,19},{4,20},{5,21},{6,22},{7,23},{8,24},{9,... | collective-permute-start | bytes 2359304 | tf_op jit(solution)/shard_map/ppermute | solution.py:51
  3.3 2.8 %collective-permute-start.1 = (bf16[256,1536]{1,0:T(8,128)(2,1)}, bf16[256,1536]{1,0:T(8,128)(2,1)S(1)}, u32[]{:S(2)}, u32[]{:S(2)}) collective-permute-start(bf16[256,1536]{1,0:T(8,128)(2,1)} %rest_8_.3), channel_id=1, source_target_pairs={{0,96},{1,97},{2,98},{3,99},{4,100},{5,101},{6,102},{7,103},{8,40}... | collective-permute-start | bytes 2359304 | tf_op jit(solution)/shard_map/ppermute | solution.py:51
  6.0 15.7 %collective-permute-done.2.across = bf16[256,1536]{1,0:T(8,128)(2,1)S(1)} collective-permute-done((bf16[256,1536]{1,0:T(8,128)(2,1)}, bf16[256,1536]{1,0:T(8,128)(2,1)S(1)}, u32[]{:S(2)}, u32[]{:S(2)}) %collective-permute-start.2) | collective-permute-done | bytes 786464 | tf_op jit(solution)/shard_map/ppermute | solution.py:51
  26.7 11.2 %collective-permute-done.4.far.rest_14_ = bf16[256,1536]{1,0:T(8,128)(2,1)S(1)} collective-permute-done((bf16[256,1536]{1,0:T(8,128)(2,1)}, bf16[256,1536]{1,0:T(8,128)(2,1)S(1)}, u32[]{:S(2)}, u32[]{:S(2)}) %collective-permute-start.4) | collective-permute-done | bytes 786464 | tf_op jit(solution)/shard_map/ppermute | solution.py:51
  40.3 4.3 %gram_near.1.near = bf16[2,3,256,512]{3,2,1,0:T(8,128)(2,1)S(1)} custom-call(bf16[256,1536]{1,0:T(8,128)(2,1)S(1)} %copy-done, bf16[256,1536]{1,0:T(8,128)(2,1)S(1)} %collective-permute-done.3.other.rest_9_, bf16[256,1536]{1,0:T(8,128)(2,1)} %collective-permute-done.fore.rest_10_, bf16[256,1536]{1,0:T(8,128)(2,1)} %collective-permute-done.6.fore_other.rest_11_, ...), custom_call_target="tpu_custom_call" | custom-call | flops 2415919104 | bytes 7077888 | tf_op jit(solution)/shard_map/gram_near/pallas_call | solution.py:161
  44.6 1.8 %gram_far.1 = (bf16[256,512]{1,0:T(8,128)(2,1)S(1)}, bf16[256,512]{1,0:T(8,128)(2,1)S(1)}, bf16[256,512]{1,0:T(8,128)(2,1)S(1)}, bf16[256,512]{1,0:T(8,128)(2,1)...) custom-call(s32[5]{0:T(128)S(1)} %stack.23.where, ...), custom_call_target="tpu_custom_call" | custom-call | flops 805306368 | bytes 6815744 | tf_op jit(solution)/shard_map/gram_far/pallas_call | solution.py:174
  46.4 4.1 %collective-permute-start.12 = (bf16[256,512]{1,0:T(8,128)(2,1)S(1)}, bf16[256,512]{1,0:T(8,128)(2,1)S(1)}, u32[]{:S(2)}, u32[]{:S(2)}) collective-permute-start(bf16[256,512]{1,0:T(8,128)(2,1)S(1)} %get-tuple-element.43), channel_id=1, source_target_pairs={{0,3},{1,0},{2,1},{3,2},{4,7},{5,4},{6,5},{7,6},{8,9},{9,10},{10,1... | collective-permute-start | bytes 786440 | tf_op jit(solution)/shard_map/ppermute | solution.py:51
  51.6 2.8 %collective-permute-done.12 = bf16[256,512]{1,0:T(8,128)(2,1)S(1)} collective-permute-done((bf16[256,512]{1,0:T(8,128)(2,1)S(1)}, bf16[256,512]{1,0:T(8,128)(2,1)S(1)}, u32[]{:S(2)}, u32[]{:S(2)}) %collective-permute-start.12) | collective-permute-done | bytes 262176 | tf_op jit(solution)/shard_map/ppermute | solution.py:51
  54.4 3.8 %collective-permute-start.13 = (bf16[256,512]{1,0:T(8,128)(2,1)S(1)}, bf16[256,512]{1,0:T(8,128)(2,1)S(1)}, u32[]{:S(2)}, u32[]{:S(2)}) collective-permute-start(bf16[256,512]{1,0:T(8,128)(2,1)S(1)} %add_convert_fusion.3), channel_id=1, source_target_pairs={{0,3},{1,0},{2,1},{3,2},{4,7},{5,4},{6,5},{7,6},{8,9},{9,10},{10,1... | collective-permute-start | bytes 786440 | tf_op jit(solution)/shard_map/ppermute | solution.py:51
  58.3 2.7 %collective-permute-start.9 = (bf16[256,512]{1,0:T(8,128)(2,1)S(1)}, bf16[256,512]{1,0:T(8,128)(2,1)S(1)}, u32[]{:S(2)}, u32[]{:S(2)}) collective-permute-start(bf16[256,512]{1,0:T(8,128)(2,1)S(1)} %add_convert_fusion.5), channel_id=1, source_target_pairs={{0,3},{1,0},{2,1},{3,2},{4,7},{5,4},{6,5},{7,6},{8,9},{9,10},{10,1... | collective-permute-start | bytes 786440 | tf_op jit(solution)/shard_map/ppermute | solution.py:51
  61.2 2.3 %collective-permute-done.13 = bf16[256,512]{1,0:T(8,128)(2,1)S(1)} collective-permute-done((bf16[256,512]{1,0:T(8,128)(2,1)S(1)}, bf16[256,512]{1,0:T(8,128)(2,1)S(1)}, u32[]{:S(2)}, u32[]{:S(2)}) %collective-permute-start.13) | collective-permute-done | bytes 262176 | tf_op jit(solution)/shard_map/ppermute | solution.py:51
  64.3 3.4 %collective-permute-done.9 = bf16[256,512]{1,0:T(8,128)(2,1)S(1)} collective-permute-done((bf16[256,512]{1,0:T(8,128)(2,1)S(1)}, bf16[256,512]{1,0:T(8,128)(2,1)S(1)}, u32[]{:S(2)}, u32[]{:S(2)}) %collective-permute-start.9) | collective-permute-done | bytes 262176 | tf_op jit(solution)/shard_map/ppermute | solution.py:51
  70.2 1.7 %collective-permute-start.21 = (bf16[256,512]{1,0:T(8,128)(2,1)S(1)}, bf16[256,512]{1,0:T(8,128)(2,1)S(1)}, u32[]{:S(2)}, u32[]{:S(2)}) collective-permute-start(bf16[256,512]{1,0:T(8,128)(2,1)S(1)} %add_convert_fusion.1.rest_8_), channel_id=1, source_target_pairs={{0,96},{1,97},{2,98},{3,99},{4,100},{5,101},{6,102},{7,103},{8,40}... | collective-permute-start | bytes 786440 | tf_op jit(solution)/shard_map/ppermute | solution.py:51
  73.4 3.8 %collective-permute-start.18 = (bf16[512,256]{1,0:T(8,128)(2,1)S(1)}, bf16[512,256]{1,0:T(8,128)(2,1)S(1)}, u32[]{:S(2)}, u32[]{:S(2)}) collective-permute-start(bf16[512,256]{1,0:T(8,128)(2,1)S(1)} %pad_maximum_fusion.2.rest_0_), channel_id=1, source_target_pairs={{0,3},{1,0},{2,1},{3,2},{4,7},{5,4},{6,5},{7,6},{8,9},{9,10},{10,1... | collective-permute-start | bytes 786440 | tf_op jit(solution)/shard_map/ppermute | solution.py:51
  79.7 1.9 %collective-permute-done.19.rest_12_ = bf16[256,512]{1,0:T(8,128)(2,1)S(1)} collective-permute-done((bf16[256,512]{1,0:T(8,128)(2,1)S(1)}, bf16[256,512]{1,0:T(8,128)(2,1)S(1)}, u32[]{:S(2)}, u32[]{:S(2)}) %collective-permute-start.19) | collective-permute-done | bytes 262176 | tf_op jit(solution)/shard_map/ppermute | solution.py:51
  84.7 2.7 %collective-permute-done.16.rest_4_ = bf16[512,256]{1,0:T(8,128)(2,1)S(1)} collective-permute-done((bf16[512,256]{1,0:T(8,128)(2,1)S(1)}, bf16[512,256]{1,0:T(8,128)(2,1)S(1)}, u32[]{:S(2)}, u32[]{:S(2)}) %collective-permute-start.16) | collective-permute-done | bytes 262176 | tf_op jit(solution)/shard_map/ppermute | solution.py:51
  88.4 3.8 %collective-permute-start.23 = (bf16[512,256]{1,0:T(8,128)(2,1)S(1)}, bf16[512,256]{1,0:T(8,128)(2,1)S(1)}, u32[]{:S(2)}, u32[]{:S(2)}) collective-permute-start(bf16[512,256]{1,0:T(8,128)(2,1)S(1)} %collective-permute-done.16.rest_4_), channel_id=1, source_target_pairs={{0,3},{1,0},{2,1},{3,2},{4,7},{5,4},{6,5},{7,6},{8,9},{9,10},{10,1... | collective-permute-start | bytes 786440 | tf_op jit(solution)/shard_map/ppermute | solution.py:51
  92.1 2.5 %collective-permute-start.25 = (bf16[256,512]{1,0:T(8,128)(2,1)S(1)}, bf16[256,512]{1,0:T(8,128)(2,1)S(1)}, u32[]{:S(2)}, u32[]{:S(2)}) collective-permute-start(bf16[256,512]{1,0:T(8,128)(2,1)S(1)} %collective-permute-done.19.rest_12_), channel_id=1, source_target_pairs={{0,96},{1,97},{2,98},{3,99},{4,100},{5,101},{6,102},{7,103},{8,40}... | collective-permute-start | bytes 786440 | tf_op jit(solution)/shard_map/ppermute | solution.py:51
  94.6 3.4 %collective-permute-done.23.rest_6_ = bf16[512,256]{1,0:T(8,128)(2,1)S(1)} collective-permute-done((bf16[512,256]{1,0:T(8,128)(2,1)S(1)}, bf16[512,256]{1,0:T(8,128)(2,1)S(1)}, u32[]{:S(2)}, u32[]{:S(2)}) %collective-permute-start.23) | collective-permute-done | bytes 262176 | tf_op jit(solution)/shard_map/ppermute | solution.py:51
  98.5 2.2 %collective-permute-done.24 = bf16[512,512]{1,0:T(8,128)(2,1)S(1)} collective-permute-done((bf16[512,512]{1,0:T(8,128)(2,1)S(1)}, bf16[512,512]{1,0:T(8,128)(2,1)S(1)}, u32[]{:S(2)}, u32[]{:S(2)}) %collective-permute-start.24) | collective-permute-done | bytes 524320 | tf_op jit(solution)/shard_map/ppermute | solution.py:51
  103.2 5.9 %collective-permute-done.26.rest_7_ = bf16[512,256]{1,0:T(8,128)(2,1)S(1)} collective-permute-done((bf16[512,256]{1,0:T(8,128)(2,1)S(1)}, bf16[512,256]{1,0:T(8,128)(2,1)S(1)}, u32[]{:S(2)}, u32[]{:S(2)}) %collective-permute-start.26) | collective-permute-done | bytes 262176 | tf_op jit(solution)/shard_map/ppermute | solution.py:51
  109.3 1.9 %square_part.1 = (f32[256,512]{1,0:T(8,128)S(1)}, bf16[256,512]{1,0:T(8,128)(2,1)S(1)}) custom-call(s32[5]{0:T(128)S(1)} %stack.23.where, bf16[512,256]{1,0:T(8,128)(2,1)S(1)} %pad_maximum_fusion.2.rest_0_, bf16[512,256]{1,0:T(8,128)(2,1)S(1)} %collective-permute-done.17.rest_1_, bf16[512,256]{1,0:T(8,128)(2,1)S(1)} %collective-permute-done.18.rest_2_, ...), custom_call_target="tpu_custom_call" | custom-call | flops 1073741824 | bytes 4194304 | tf_op jit(solution)/shard_map/square_part/pallas_call | solution.py:187
  112.9 3.3 %collective-permute-start.31 = (bf16[256,512]{1,0:T(8,128)(2,1)S(1)}, bf16[256,512]{1,0:T(8,128)(2,1)S(1)}, u32[]{:S(2)}, u32[]{:S(2)}) collective-permute-start(bf16[256,512]{1,0:T(8,128)(2,1)S(1)} %add_convert_fusion.rest_0_), channel_id=1, source_target_pairs={{0,3},{1,0},{2,1},{3,2},{4,7},{5,4},{6,5},{7,6},{8,9},{9,10},{10,1... | collective-permute-start | bytes 786440 | tf_op jit(solution)/shard_map/ppermute | solution.py:51
  116.2 5.9 %collective-permute-done.31.rest_2_ = bf16[256,512]{1,0:T(8,128)(2,1)S(1)} collective-permute-done((bf16[256,512]{1,0:T(8,128)(2,1)S(1)}, bf16[256,512]{1,0:T(8,128)(2,1)S(1)}, u32[]{:S(2)}, u32[]{:S(2)}) %collective-permute-start.31) | collective-permute-done | bytes 262176 | tf_op jit(solution)/shard_map/ppermute | solution.py:51
  125.4 1.7 %collective-permute-start.32 = (bf16[256,512]{1,0:T(8,128)(2,1)S(1)}, bf16[256,512]{1,0:T(8,128)(2,1)S(1)}, u32[]{:S(2)}, u32[]{:S(2)}) collective-permute-start(bf16[256,512]{1,0:T(8,128)(2,1)S(1)} %collective-permute-done.30.rest_1_), channel_id=1, source_target_pairs={{0,1},{1,2},{2,3},{3,0},{4,5},{5,6},{6,7},{7,4},{8,11},{9,8},{10,9... | collective-permute-start | bytes 786440 | tf_op jit(solution)/shard_map/ppermute | solution.py:51
  127.4 4.5 %collective-permute-done.33.rest_5_ = bf16[256,512]{1,0:T(8,128)(2,1)S(1)} collective-permute-done((bf16[256,512]{1,0:T(8,128)(2,1)S(1)}, bf16[256,512]{1,0:T(8,128)(2,1)S(1)}, u32[]{:S(2)}, u32[]{:S(2)}) %collective-permute-start.33) | collective-permute-done | bytes 262176 | tf_op jit(solution)/shard_map/ppermute | solution.py:51
  132.0 2.8 %collective-permute-done.32.rest_3_ = bf16[256,512]{1,0:T(8,128)(2,1)S(1)} collective-permute-done((bf16[256,512]{1,0:T(8,128)(2,1)S(1)}, bf16[256,512]{1,0:T(8,128)(2,1)S(1)}, u32[]{:S(2)}, u32[]{:S(2)}) %collective-permute-start.32) | collective-permute-done | bytes 262176 | tf_op jit(solution)/shard_map/ppermute | solution.py:51
  134.8 4.8 %collective-permute-done.35.rest_7_ = bf16[256,512]{1,0:T(8,128)(2,1)S(1)} collective-permute-done((bf16[256,512]{1,0:T(8,128)(2,1)S(1)}, bf16[256,512]{1,0:T(8,128)(2,1)S(1)}, u32[]{:S(2)}, u32[]{:S(2)}) %collective-permute-start.35) | collective-permute-done | bytes 262176 | tf_op jit(solution)/shard_map/ppermute | solution.py:51
  139.5 3.5 %apply_other.1 = bf16[256,1536]{1,0:T(8,128)(2,1)S(1)} custom-call(s32[5]{0:T(128)S(1)} %stack.23.where, bf16[256,512]{1,0:T(8,128)(2,1)S(1)} %add_convert_fusion.rest_0_, bf16[256,512]{1,0:T(8,128)(2,1)S(1)} %collective-permute-done.30.rest_1_, bf16[256,512]{1,0:T(8,128)(2,1)S(1)} %collective-permute-done.31.rest_2_, ...), custom_call_target="tpu_custom_call" | custom-call | flops 1610612736 | bytes 9175040 | tf_op jit(solution)/shard_map/apply_other/pallas_call | solution.py:204
  143.0 2.2 %collective-permute-start.36 = (bf16[256,1536]{1,0:T(8,128)(2,1)S(1)}, bf16[256,1536]{1,0:T(8,128)(2,1)S(1)}, u32[]{:S(2)}, u32[]{:S(2)}) collective-permute-start(bf16[256,1536]{1,0:T(8,128)(2,1)S(1)} %apply_other.1), channel_id=1, source_target_pairs={{0,16},{1,17},{2,18},{3,19},{4,20},{5,21},{6,22},{7,23},{8,24},{9,... | collective-permute-start | bytes 2359304 | tf_op jit(solution)/shard_map/ppermute | solution.py:51
  145.3 3.5 %apply_own.1 = f32[256,1536]{1,0:T(8,128)S(1)} custom-call(s32[5]{0:T(128)S(1)} %stack.23.where, bf16[256,512]{1,0:T(8,128)(2,1)S(1)} %add_convert_fusion.rest_0_, bf16[256,512]{1,0:T(8,128)(2,1)S(1)} %collective-permute-done.30.rest_1_, bf16[256,512]{1,0:T(8,128)(2,1)S(1)} %collective-permute-done.31.rest_2_, ...), custom_call_target="tpu_custom_call" | custom-call | flops 1610612736 | bytes 9175040 | tf_op jit(solution)/shard_map/apply_own/pallas_call | solution.py:204
  148.8 10.5 %collective-permute-done.36 = bf16[256,1536]{1,0:T(8,128)(2,1)S(1)} collective-permute-done((bf16[256,1536]{1,0:T(8,128)(2,1)S(1)}, bf16[256,1536]{1,0:T(8,128)(2,1)S(1)}, u32[]{:S(2)}, u32[]{:S(2)}) %collective-permute-start.36) | collective-permute-done | bytes 786464 | tf_op jit(solution)/shard_map/ppermute | solution.py:51
  (69 shorter events, 29.5 us)
Async XLA Ops:
  0.0 21.7 %collective-permute-start.2 = (bf16[256,1536]{1,0:T(8,128)(2,1)}, bf16[256,1536]{1,0:T(8,128)(2,1)S(1)}, u32[]{:S(2)}, u32[]{:S(2)}) collective-permute-start(bf16[256,1536]{1,0:T(8,128)(2,1)} %rest_8_.3), channel_id=1, source_target_pairs={{0,16},{1,17},{2,18},{3,19},{4,20},{5,21},{6,22},{7,23},{8,24},{9,... | collective-permute-start | bytes 2359304 | tf_op jit(solution)/shard_map/ppermute | solution.py:51
  3.3 20.5 %collective-permute-start.1 = (bf16[256,1536]{1,0:T(8,128)(2,1)}, bf16[256,1536]{1,0:T(8,128)(2,1)S(1)}, u32[]{:S(2)}, u32[]{:S(2)}) collective-permute-start(bf16[256,1536]{1,0:T(8,128)(2,1)} %rest_8_.3), channel_id=1, source_target_pairs={{0,96},{1,97},{2,98},{3,99},{4,100},{5,101},{6,102},{7,103},{8,40}... | collective-permute-start | bytes 2359304 | tf_op jit(solution)/shard_map/ppermute | solution.py:51
  6.0 18.4 %collective-permute-start = (bf16[256,1536]{1,0:T(8,128)(2,1)}, bf16[256,1536]{1,0:T(8,128)(2,1)}, u32[]{:S(2)}, u32[]{:S(2)}) collective-permute-start(bf16[256,1536]{1,0:T(8,128)(2,1)} %rest_8_.3), channel_id=1, source_target_pairs={{0,32},{1,33},{2,34},{3,35},{4,36},{5,37},{6,38},{7,39},{8,104},{9... | collective-permute-start | bytes 2359304 | tf_op jit(solution)/shard_map/ppermute | solution.py:51
  24.5 13.4 %collective-permute-start.4 = (bf16[256,1536]{1,0:T(8,128)(2,1)}, bf16[256,1536]{1,0:T(8,128)(2,1)S(1)}, u32[]{:S(2)}, u32[]{:S(2)}) collective-permute-start(bf16[256,1536]{1,0:T(8,128)(2,1)} %collective-permute-done.fore.rest_10_), channel_id=1, source_target_pairs={{0,32},{1,33},{2,34},{3,35},{4,36},{5,37},{6,38},{7,39},{8,104},{9... | collective-permute-start | bytes 2359304 | tf_op jit(solution)/shard_map/ppermute | solution.py:51
  25.0 13.0 %collective-permute-start.6 = (bf16[256,1536]{1,0:T(8,128)(2,1)S(1)}, bf16[256,1536]{1,0:T(8,128)(2,1)}, u32[]{:S(2)}, u32[]{:S(2)}) collective-permute-start(bf16[256,1536]{1,0:T(8,128)(2,1)S(1)} %collective-permute-done.1.back.rest_12_), channel_id=1, source_target_pairs={{0,8},{1,9},{2,10},{3,11},{4,12},{5,13},{6,14},{7,15},{8,0},{9,1},... | collective-permute-start | bytes 2359304 | tf_op jit(solution)/shard_map/ppermute | solution.py:51
  26.7 11.3 %collective-permute-start.7 = (bf16[256,1536]{1,0:T(8,128)(2,1)}, bf16[256,1536]{1,0:T(8,128)(2,1)}, u32[]{:S(2)}, u32[]{:S(2)}) collective-permute-start(bf16[256,1536]{1,0:T(8,128)(2,1)} %collective-permute-done.fore.rest_10_), channel_id=1, source_target_pairs={{0,8},{1,9},{2,10},{3,11},{4,12},{5,13},{6,14},{7,15},{8,0},{9,1},... | collective-permute-start | bytes 2359304 | tf_op jit(solution)/shard_map/ppermute | solution.py:51
  37.9 6.7 %collective-permute-start.5 = (bf16[256,1536]{1,0:T(8,128)(2,1)S(1)}, bf16[256,1536]{1,0:T(8,128)(2,1)S(1)}, u32[]{:S(2)}, u32[]{:S(2)}) collective-permute-start(bf16[256,1536]{1,0:T(8,128)(2,1)S(1)} %collective-permute-done.4.far.rest_14_), channel_id=1, source_target_pairs={{0,8},{1,9},{2,10},{3,11},{4,12},{5,13},{6,14},{7,15},{8,0},{9,1},... | collective-permute-start | bytes 2359304 | tf_op jit(solution)/shard_map/ppermute | solution.py:51
  46.4 8.0 %collective-permute-start.12 = (bf16[256,512]{1,0:T(8,128)(2,1)S(1)}, bf16[256,512]{1,0:T(8,128)(2,1)S(1)}, u32[]{:S(2)}, u32[]{:S(2)}) collective-permute-start(bf16[256,512]{1,0:T(8,128)(2,1)S(1)} %get-tuple-element.43), channel_id=1, source_target_pairs={{0,3},{1,0},{2,1},{3,2},{4,7},{5,4},{6,5},{7,6},{8,9},{9,10},{10,1... | collective-permute-start | bytes 786440 | tf_op jit(solution)/shard_map/ppermute | solution.py:51
  50.5 7.7 %collective-permute-start.8 = (bf16[256,512]{1,0:T(8,128)(2,1)S(1)}, bf16[256,512]{1,0:T(8,128)(2,1)S(1)}, u32[]{:S(2)}, u32[]{:S(2)}) collective-permute-start(bf16[256,512]{1,0:T(8,128)(2,1)S(1)} %get-tuple-element.38), channel_id=1, source_target_pairs={{0,3},{1,0},{2,1},{3,2},{4,7},{5,4},{6,5},{7,6},{8,9},{9,10},{10,1... | collective-permute-start | bytes 786440 | tf_op jit(solution)/shard_map/ppermute | solution.py:51
  50.9 10.1 %collective-permute-start.10 = (bf16[256,512]{1,0:T(8,128)(2,1)S(1)}, bf16[256,512]{1,0:T(8,128)(2,1)S(1)}, u32[]{:S(2)}, u32[]{:S(2)}) collective-permute-start(bf16[256,512]{1,0:T(8,128)(2,1)S(1)} %get-tuple-element.40), channel_id=1, source_target_pairs={{0,4},{1,5},{2,6},{3,7},{4,0},{5,1},{6,2},{7,3},{8,12},{9,13},{10,... | collective-permute-start | bytes 786440 | tf_op jit(solution)/shard_map/ppermute | solution.py:51
  54.4 9.1 %collective-permute-start.13 = (bf16[256,512]{1,0:T(8,128)(2,1)S(1)}, bf16[256,512]{1,0:T(8,128)(2,1)S(1)}, u32[]{:S(2)}, u32[]{:S(2)}) collective-permute-start(bf16[256,512]{1,0:T(8,128)(2,1)S(1)} %add_convert_fusion.3), channel_id=1, source_target_pairs={{0,3},{1,0},{2,1},{3,2},{4,7},{5,4},{6,5},{7,6},{8,9},{9,10},{10,1... | collective-permute-start | bytes 786440 | tf_op jit(solution)/shard_map/ppermute | solution.py:51
  58.3 9.4 %collective-permute-start.9 = (bf16[256,512]{1,0:T(8,128)(2,1)S(1)}, bf16[256,512]{1,0:T(8,128)(2,1)S(1)}, u32[]{:S(2)}, u32[]{:S(2)}) collective-permute-start(bf16[256,512]{1,0:T(8,128)(2,1)S(1)} %add_convert_fusion.5), channel_id=1, source_target_pairs={{0,3},{1,0},{2,1},{3,2},{4,7},{5,4},{6,5},{7,6},{8,9},{9,10},{10,1... | collective-permute-start | bytes 786440 | tf_op jit(solution)/shard_map/ppermute | solution.py:51
  61.1 7.7 %collective-permute-start.11 = (bf16[256,512]{1,0:T(8,128)(2,1)S(1)}, bf16[256,512]{1,0:T(8,128)(2,1)S(1)}, u32[]{:S(2)}, u32[]{:S(2)}) collective-permute-start(bf16[256,512]{1,0:T(8,128)(2,1)S(1)} %add_convert_fusion.4), channel_id=1, source_target_pairs={{0,1},{1,2},{2,3},{3,0},{4,5},{5,6},{6,7},{7,4},{8,11},{9,8},{10,9... | collective-permute-start | bytes 786440 | tf_op jit(solution)/shard_map/ppermute | solution.py:51
  70.2 8.4 %collective-permute-start.21 = (bf16[256,512]{1,0:T(8,128)(2,1)S(1)}, bf16[256,512]{1,0:T(8,128)(2,1)S(1)}, u32[]{:S(2)}, u32[]{:S(2)}) collective-permute-start(bf16[256,512]{1,0:T(8,128)(2,1)S(1)} %add_convert_fusion.1.rest_8_), channel_id=1, source_target_pairs={{0,96},{1,97},{2,98},{3,99},{4,100},{5,101},{6,102},{7,103},{8,40}... | collective-permute-start | bytes 786440 | tf_op jit(solution)/shard_map/ppermute | solution.py:51
  72.0 7.7 %collective-permute-start.20 = (bf16[256,512]{1,0:T(8,128)(2,1)S(1)}, bf16[256,512]{1,0:T(8,128)(2,1)S(1)}, u32[]{:S(2)}, u32[]{:S(2)}) collective-permute-start(bf16[256,512]{1,0:T(8,128)(2,1)S(1)} %add_convert_fusion.1.rest_8_), channel_id=1, source_target_pairs={{0,32},{1,33},{2,34},{3,35},{4,36},{5,37},{6,38},{7,39},{8,104},{9... | collective-permute-start | bytes 786440 | tf_op jit(solution)/shard_map/ppermute | solution.py:51
  72.4 9.2 %collective-permute-start.19 = (bf16[256,512]{1,0:T(8,128)(2,1)S(1)}, bf16[256,512]{1,0:T(8,128)(2,1)S(1)}, u32[]{:S(2)}, u32[]{:S(2)}) collective-permute-start(bf16[256,512]{1,0:T(8,128)(2,1)S(1)} %add_convert_fusion.1.rest_8_), channel_id=1, source_target_pairs={{0,4},{1,5},{2,6},{3,7},{4,0},{5,1},{6,2},{7,3},{8,12},{9,13},{10,... | collective-permute-start | bytes 786440 | tf_op jit(solution)/shard_map/ppermute | solution.py:51
  73.4 9.7 %collective-permute-start.18 = (bf16[512,256]{1,0:T(8,128)(2,1)S(1)}, bf16[512,256]{1,0:T(8,128)(2,1)S(1)}, u32[]{:S(2)}, u32[]{:S(2)}) collective-permute-start(bf16[512,256]{1,0:T(8,128)(2,1)S(1)} %pad_maximum_fusion.2.rest_0_), channel_id=1, source_target_pairs={{0,3},{1,0},{2,1},{3,2},{4,7},{5,4},{6,5},{7,6},{8,9},{9,10},{10,1... | collective-permute-start | bytes 786440 | tf_op jit(solution)/shard_map/ppermute | solution.py:51
  77.1 7.6 %collective-permute-start.17 = (bf16[512,256]{1,0:T(8,128)(2,1)S(1)}, bf16[512,256]{1,0:T(8,128)(2,1)S(1)}, u32[]{:S(2)}, u32[]{:S(2)}) collective-permute-start(bf16[512,256]{1,0:T(8,128)(2,1)S(1)} %pad_maximum_fusion.2.rest_0_), channel_id=1, source_target_pairs={{0,1},{1,2},{2,3},{3,0},{4,5},{5,6},{6,7},{7,4},{8,11},{9,8},{10,9... | collective-permute-start | bytes 786440 | tf_op jit(solution)/shard_map/ppermute | solution.py:51
  78.5 8.8 %collective-permute-start.16 = (bf16[512,256]{1,0:T(8,128)(2,1)S(1)}, bf16[512,256]{1,0:T(8,128)(2,1)S(1)}, u32[]{:S(2)}, u32[]{:S(2)}) collective-permute-start(bf16[512,256]{1,0:T(8,128)(2,1)S(1)} %pad_maximum_fusion.2.rest_0_), channel_id=1, source_target_pairs={{0,16},{1,17},{2,18},{3,19},{4,20},{5,21},{6,22},{7,23},{8,24},{9,... | collective-permute-start | bytes 786440 | tf_op jit(solution)/shard_map/ppermute | solution.py:51
  87.4 13.3 %collective-permute-start.24 = (bf16[512,512]{1,0:T(8,128)(2,1)S(1)}, bf16[512,512]{1,0:T(8,128)(2,1)S(1)}, u32[]{:S(2)}, u32[]{:S(2)}) collective-permute-start(bf16[512,512]{1,0:T(8,128)(2,1)S(1)} %pad_maximum_fusion.1), channel_id=1, source_target_pairs={{0,32},{1,33},{2,34},{3,35},{4,36},{5,37},{6,38},{7,39},{8,104},{9... | collective-permute-start | bytes 1572872 | tf_op jit(solution)/shard_map/ppermute | solution.py:51
  88.3 13.1 %collective-permute-start.22 = (bf16[1024,256]{1,0:T(8,128)(2,1)S(1)}, bf16[1024,256]{1,0:T(8,128)(2,1)S(1)}, u32[]{:S(2)}, u32[]{:S(2)}) collective-permute-start(bf16[1024,256]{1,0:T(8,128)(2,1)S(1)} %pad_maximum_fusion), channel_id=1, source_target_pairs={{0,1},{1,2},{2,3},{3,0},{4,5},{5,6},{6,7},{7,4},{8,11},{9,8},{10,9... | collective-permute-start | bytes 1572872 | tf_op jit(solution)/shard_map/ppermute | solution.py:51
  88.4 9.6 %collective-permute-start.23 = (bf16[512,256]{1,0:T(8,128)(2,1)S(1)}, bf16[512,256]{1,0:T(8,128)(2,1)S(1)}, u32[]{:S(2)}, u32[]{:S(2)}) collective-permute-start(bf16[512,256]{1,0:T(8,128)(2,1)S(1)} %collective-permute-done.16.rest_4_), channel_id=1, source_target_pairs={{0,3},{1,0},{2,1},{3,2},{4,7},{5,4},{6,5},{7,6},{8,9},{9,10},{10,1... | collective-permute-start | bytes 786440 | tf_op jit(solution)/shard_map/ppermute | solution.py:51
  101.5 7.7 %collective-permute-start.26 = (bf16[512,256]{1,0:T(8,128)(2,1)S(1)}, bf16[512,256]{1,0:T(8,128)(2,1)S(1)}, u32[]{:S(2)}, u32[]{:S(2)}) collective-permute-start(bf16[512,256]{1,0:T(8,128)(2,1)S(1)} %get-tuple-element.61.rest_5_), channel_id=1, source_target_pairs={{0,1},{1,2},{2,3},{3,0},{4,5},{5,6},{6,7},{7,4},{8,11},{9,8},{10,9... | collective-permute-start | bytes 786440 | tf_op jit(solution)/shard_map/ppermute | solution.py:51
  101.6 7.7 %collective-permute-start.27 = (bf16[256,512]{1,0:T(8,128)(2,1)S(1)}, bf16[256,512]{1,0:T(8,128)(2,1)S(1)}, u32[]{:S(2)}, u32[]{:S(2)}) collective-permute-start(bf16[256,512]{1,0:T(8,128)(2,1)S(1)} %get-tuple-element.59.rest_13_), channel_id=1, source_target_pairs={{0,32},{1,33},{2,34},{3,35},{4,36},{5,37},{6,38},{7,39},{8,104},{9... | collective-permute-start | bytes 786440 | tf_op jit(solution)/shard_map/ppermute | solution.py:51
  112.9 9.2 %collective-permute-start.31 = (bf16[256,512]{1,0:T(8,128)(2,1)S(1)}, bf16[256,512]{1,0:T(8,128)(2,1)S(1)}, u32[]{:S(2)}, u32[]{:S(2)}) collective-permute-start(bf16[256,512]{1,0:T(8,128)(2,1)S(1)} %add_convert_fusion.rest_0_), channel_id=1, source_target_pairs={{0,3},{1,0},{2,1},{3,2},{4,7},{5,4},{6,5},{7,6},{8,9},{9,10},{10,1... | collective-permute-start | bytes 786440 | tf_op jit(solution)/shard_map/ppermute | solution.py:51
  116.2 7.6 %collective-permute-start.30 = (bf16[256,512]{1,0:T(8,128)(2,1)S(1)}, bf16[256,512]{1,0:T(8,128)(2,1)S(1)}, u32[]{:S(2)}, u32[]{:S(2)}) collective-permute-start(bf16[256,512]{1,0:T(8,128)(2,1)S(1)} %add_convert_fusion.rest_0_), channel_id=1, source_target_pairs={{0,1},{1,2},{2,3},{3,0},{4,5},{5,6},{6,7},{7,4},{8,11},{9,8},{10,9... | collective-permute-start | bytes 786440 | tf_op jit(solution)/shard_map/ppermute | solution.py:51
  116.2 8.1 %collective-permute-start.29 = (bf16[256,512]{1,0:T(8,128)(2,1)S(1)}, bf16[256,512]{1,0:T(8,128)(2,1)S(1)}, u32[]{:S(2)}, u32[]{:S(2)}) collective-permute-start(bf16[256,512]{1,0:T(8,128)(2,1)S(1)} %add_convert_fusion.rest_0_), channel_id=1, source_target_pairs={{0,4},{1,5},{2,6},{3,7},{4,0},{5,1},{6,2},{7,3},{8,12},{9,13},{10,... | collective-permute-start | bytes 786440 | tf_op jit(solution)/shard_map/ppermute | solution.py:51
  124.4 7.6 %collective-permute-start.33 = (bf16[256,512]{1,0:T(8,128)(2,1)S(1)}, bf16[256,512]{1,0:T(8,128)(2,1)S(1)}, u32[]{:S(2)}, u32[]{:S(2)}) collective-permute-start(bf16[256,512]{1,0:T(8,128)(2,1)S(1)} %collective-permute-done.29.rest_4_), channel_id=1, source_target_pairs={{0,1},{1,2},{2,3},{3,0},{4,5},{5,6},{6,7},{7,4},{8,11},{9,8},{10,9... | collective-permute-start | bytes 786440 | tf_op jit(solution)/shard_map/ppermute | solution.py:51
  125.4 9.4 %collective-permute-start.32 = (bf16[256,512]{1,0:T(8,128)(2,1)S(1)}, bf16[256,512]{1,0:T(8,128)(2,1)S(1)}, u32[]{:S(2)}, u32[]{:S(2)}) collective-permute-start(bf16[256,512]{1,0:T(8,128)(2,1)S(1)} %collective-permute-done.30.rest_1_), channel_id=1, source_target_pairs={{0,1},{1,2},{2,3},{3,0},{4,5},{5,6},{6,7},{7,4},{8,11},{9,8},{10,9... | collective-permute-start | bytes 786440 | tf_op jit(solution)/shard_map/ppermute | solution.py:51
  127.2 7.6 %collective-permute-start.34 = (bf16[256,512]{1,0:T(8,128)(2,1)S(1)}, bf16[256,512]{1,0:T(8,128)(2,1)S(1)}, u32[]{:S(2)}, u32[]{:S(2)}) collective-permute-start(bf16[256,512]{1,0:T(8,128)(2,1)S(1)} %collective-permute-done.31.rest_2_), channel_id=1, source_target_pairs={{0,4},{1,5},{2,6},{3,7},{4,0},{5,1},{6,2},{7,3},{8,12},{9,13},{10,... | collective-permute-start | bytes 786440 | tf_op jit(solution)/shard_map/ppermute | solution.py:51
  132.0 7.6 %collective-permute-start.35 = (bf16[256,512]{1,0:T(8,128)(2,1)S(1)}, bf16[256,512]{1,0:T(8,128)(2,1)S(1)}, u32[]{:S(2)}, u32[]{:S(2)}) collective-permute-start(bf16[256,512]{1,0:T(8,128)(2,1)S(1)} %collective-permute-done.33.rest_5_), channel_id=1, source_target_pairs={{0,1},{1,2},{2,3},{3,0},{4,5},{5,6},{6,7},{7,4},{8,11},{9,8},{10,9... | collective-permute-start | bytes 786440 | tf_op jit(solution)/shard_map/ppermute | solution.py:51
  143.0 16.2 %collective-permute-start.36 = (bf16[256,1536]{1,0:T(8,128)(2,1)S(1)}, bf16[256,1536]{1,0:T(8,128)(2,1)S(1)}, u32[]{:S(2)}, u32[]{:S(2)}) collective-permute-start(bf16[256,1536]{1,0:T(8,128)(2,1)S(1)} %apply_other.1), channel_id=1, source_target_pairs={{0,16},{1,17},{2,18},{3,19},{4,20},{5,21},{6,22},{7,23},{8,24},{9,... | collective-permute-start | bytes 2359304 | tf_op jit(solution)/shard_map/ppermute | solution.py:51
  (9 other events, 29.4 us)

commit v3 on v2

--- a/solution.py
+++ b/solution.py
@@ -76,12 +76,17 @@
             out[r, q // 2, :, (q % 2) * BLOCK : (q % 2 + 1) * BLOCK] = part.astype(out.dtype)
 
 
-def gram_far_kernel(where, own, across, far, far_other, near, *rest):
+def gram_far_own_kernel(own, across, far, out):
+    for r, rows in enumerate((own, across)):
+        out[r] = nt(rows[...], far[...]).astype(out.dtype)
+
+
+def gram_far_kernel(where, own, across, far_other, far_own, near, *rest):
     outs, tiles = rest[:8], rest[8]
     x, yh, core, yl, z = (where[i] for i in range(5))
     for r, rows in enumerate((own, across)):
-        for q, cols in enumerate((far, far_other)):
-            tiles[r, :, q * BLOCK : (q + 1) * BLOCK] = nt(rows[...], cols[...]).astype(tiles.dtype)
+        tiles[r, :, :BLOCK] = far_own[r]
+        tiles[r, :, BLOCK:] = nt(rows[...], far_other[...]).astype(tiles.dtype)
     for index, out in enumerate(outs):
         dy, position = index // 4, index % 4
         row = lax.rem(yl + dy + yh, 2)
@@ -169,7 +174,20 @@
     )(own, other, fore, fore_other, back, back_other, across)
 
 
-def gram_far(where, own, across, far, far_other, near):
+def gram_far_own(own, across, far):
+    depth = own.shape[1]
+    return pl.pallas_call(
+        gram_far_own_kernel,
+        in_specs=[whole() for _ in range(3)],
+        out_specs=whole(),
+        out_shape=jax.ShapeDtypeStruct((2, BLOCK, BLOCK), jnp.bfloat16),
+        compiler_params=params(24),
+        cost_estimate=cost(2 * 2 * BLOCK * BLOCK * depth, 3 * BLOCK * depth * 2 + 2 * BLOCK * BLOCK * 2),
+        name="gram_far_own",
+    )(own, across, far)
+
+
+def gram_far(where, own, across, far_other, far_own, near):
     depth = own.shape[1]
     return pl.pallas_call(
         gram_far_kernel,
@@ -178,9 +196,9 @@
         out_shape=[jax.ShapeDtypeStruct((BLOCK, TILE), jnp.bfloat16) for _ in range(8)],
         scratch_shapes=[pltpu.VMEM((2, BLOCK, TILE), jnp.bfloat16)],
         compiler_params=params(24),
-        cost_estimate=cost(2 * 2 * BLOCK * TILE * depth, 4 * BLOCK * depth * 2 + 14 * BLOCK * TILE * 2),
+        cost_estimate=cost(2 * 2 * BLOCK * BLOCK * depth, 3 * BLOCK * depth * 2 + 15 * BLOCK * TILE * 2),
         name="gram_far",
-    )(where, own, across, far, far_other, near)
+    )(where, own, across, far_other, far_own, near)
 
 
 def square_part(where, left, right):
@@ -219,20 +237,20 @@
 
 def gather_rings(sides):
     first = [
-        [send(value, pair), send(value, ring + "_fore"), send(value, ring + "_back")]
+        [send(value, ring + "_back"), send(value, ring + "_fore"), send(value, pair)]
         for value, ring, pair in sides
     ]
     first = lax.optimization_barrier(first)
     second = [
         [
+            send(there, ring + "_back"),
             send(jnp.concatenate([there, fore], axis=0), ring + "_fore"),
-            send(there, ring + "_back"),
         ]
-        for (there, fore, back), (value, ring, pair) in zip(first, sides)
+        for (back, fore, there), (value, ring, pair) in zip(first, sides)
     ]
     second = lax.optimization_barrier(second)
     out = []
-    for (there, fore, back), (both, there_back), (value, ring, pair) in zip(first, second, sides):
+    for (back, fore, there), (there_back, both), (value, ring, pair) in zip(first, second, sides):
         count = value.shape[0]
         there_fore, far = both[:count], both[count:]
         there_far = send(there_fore, ring + "_fore")
@@ -241,11 +259,10 @@
 
 
 def gather_even(value, ring, pair):
-    there, fore, back = lax.optimization_barrier(
-        [send(value, pair), send(value, ring + "_fore"), send(value, ring + "_back")]
-    )
+    fore, back = send(value, ring + "_fore"), send(value, ring + "_back")
+    there = send(value, pair)
+    far = send(fore, ring + "_fore")
     there_fore = send(there, ring + "_fore")
-    far = send(fore, ring + "_fore")
     there_back = send(back, pair)
     there_far = send(there_fore, ring + "_fore")
     return [value, fore, back, far, there, there_fore, there_back, there_far]
@@ -268,14 +285,16 @@
     row, col = lax.axis_index("row"), lax.axis_index("col")
     where = jnp.stack([row >> 2, (row >> 1) & 1, row & 1, col >> 2, col & 3]).astype(jnp.int32)
 
-    fore, back, across, other = lax.optimization_barrier(
-        [send(iterate, move) for move in ("x_fore", "x_back", "yh", "core")]
+    other, across, back, fore = lax.optimization_barrier(
+        [send(iterate, move) for move in ("core", "yh", "x_back", "x_fore")]
     )
+    fore_other, back_other = send(back, "core"), send(fore, "core")
     far = send(fore, "x_fore")
-    fore_other, back_other = send(back, "core"), send(fore, "core")
     near = gram_near(iterate, other, fore, fore_other, back, back_other, across)
+    far, near = lax.optimization_barrier((far, near))
     far_other = send(far, "core")
-    gram = sum_over_col(gram_far(where, iterate, across, far, far_other, near))
+    far_own = gram_far_own(iterate, across, far)
+    gram = sum_over_col(gram_far(where, iterate, across, far_other, far_own, near))
 
     row_part = jnp.concatenate([gram[:, :BLOCK], send(gram[:, BLOCK:], "core")], axis=0)
     left, right = gather_rings([(row_part, "z", "yh"), (gram, "x", "yl")])

time: 162 us -> 154 us (0.951); the launches traced: 160 us -> 154 us
  waiting for transfers between devices: 94.2 us -> 87.8 us
  Pallas kernels: 15 us -> 11.4 us
  starting transfers between devices: 46 us -> 48.8 us
    ppermute x37, waiting for transfers between devices: 94.2 us -> 87.8 us  [send(): return lax.ppermute(value, ('row', 'col'), pairs(MOVES[move]))]
    ppermute x37, starting transfers between devices: 46 us -> 48.8 us  [send(): return lax.ppermute(value, ('row', 'col'), pairs(MOVES[move]))]
    pallas_call x2, Pallas kernels: 7 us -> 4.85 us  [apply_part(): pl.pallas_call(functools.partial(apply_kernel, other_rows), in_specs=[sme...]
    pallas_call x1, Pallas kernels: 4.31 us -> 2.63 us  [gram_near(): pl.pallas_call(gram_near_kernel, in_specs=[whole() for _ in range(7)], ou...]
    unnamed x8 -> x30, local copies, waits for them, and re-layouts: 3.14 us -> 4.08 us
  transfers between devices with their start and end apart: 37 -> 37, of which waited for: 30 -> 28; matrix products, arithmetic and copies ran while one was open for 0% -> 0% of each run, Pallas kernels for 5% -> 4%
where the time goes in v3:
time: 154 us
  waiting for transfers between devices  87.8 us (57%)
  starting transfers between devices  48.8 us (32%)
  Pallas kernels  11.4 us (7%)
  local copies, waits for them, and re-layouts  4.25 us (3%)
  other arithmetic  1.7 us (1%)
    ppermute x37, waiting for transfers between devices, send(): return lax.ppermute(value, ('row', 'col'), pairs(MOVES[move]))  87.8 us
    ppermute x37, starting transfers between devices, send(): return lax.ppermute(value, ('row', 'col'), pairs(MOVES[move]))  48.8 us
    pallas_call x2, Pallas kernels, apply_part(): pl.pallas_call(functools.partial(apply_kernel, other_rows), in_specs=[sme...  4.85 us
    unnamed x30, local copies, waits for them, and re-layouts  4.08 us
  transfers between devices with their start and end apart: 37, of which 28 were waited for; matrix products, arithmetic and copies ran while one was open for 0% of the time, Pallas kernels for 4%

profile of v3, /device:TPU:0, one launch (start us, length us, event | category | flops | bytes accessed | tf_op | source)
XLA Modules:
  0.0 154.1 jit_solution(4194241043080190324)
XLA Ops:
  3.2 3.3 %collective-permute-start.1 = (bf16[256,1536]{1,0:T(8,128)(2,1)}, bf16[256,1536]{1,0:T(8,128)(2,1)S(1)}, u32[]{:S(2)}, u32[]{:S(2)}) collective-permute-start(bf16[256,1536]{1,0:T(8,128)(2,1)} %rest_8_.3), channel_id=1, source_target_pairs={{0,16},{1,17},{2,18},{3,19},{4,20},{5,21},{6,22},{7,23},{8,24},{9,... | collective-permute-start | bytes 2359304 | tf_op jit(solution)/shard_map/ppermute | solution.py:51
  6.5 13.8 %collective-permute-done.3.fore.rest_10_ = bf16[256,1536]{1,0:T(8,128)(2,1)S(1)} collective-permute-done((bf16[256,1536]{1,0:T(8,128)(2,1)}, bf16[256,1536]{1,0:T(8,128)(2,1)S(1)}, u32[]{:S(2)}, u32[]{:S(2)}) %collective-permute-start.3) | collective-permute-done | bytes 786464 | tf_op jit(solution)/shard_map/ppermute | solution.py:51
  20.4 3.2 %collective-permute-done.1.across = bf16[256,1536]{1,0:T(8,128)(2,1)S(1)} collective-permute-done((bf16[256,1536]{1,0:T(8,128)(2,1)}, bf16[256,1536]{1,0:T(8,128)(2,1)S(1)}, u32[]{:S(2)}, u32[]{:S(2)}) %collective-permute-start.1) | collective-permute-done | bytes 786464 | tf_op jit(solution)/shard_map/ppermute | solution.py:51
  28.2 2.6 %gram_near.1.near = bf16[2,3,256,512]{3,2,1,0:T(8,128)(2,1)S(1)} custom-call(bf16[256,1536]{1,0:T(8,128)(2,1)S(1)} %copy-done, bf16[256,1536]{1,0:T(8,128)(2,1)S(1)} %collective-permute-done.other.rest_9_, bf16[256,1536]{1,0:T(8,128)(2,1)S(1)} %collective-permute-done.3.fore.rest_10_, bf16[256,1536]{1,0:T(8,128)(2,1)S(1)} %collective-permute-done.5.fore_other.rest_11_, ...), custom_call_target="tpu_custom_call" | custom-call | flops 2415919104 | bytes 7077888 | tf_op jit(solution)/shard_map/gram_near/pallas_call | solution.py:166
  32.1 5.3 %collective-permute-done.4.far.rest_14_ = bf16[256,1536]{1,0:T(8,128)(2,1)S(1)} collective-permute-done((bf16[256,1536]{1,0:T(8,128)(2,1)S(1)}, bf16[256,1536]{1,0:T(8,128)(2,1)S(1)}, u32[]{:S(2)}, u32[]{:S(2)}) %collective-permute-start.4) | collective-permute-done | bytes 786464 | tf_op jit(solution)/shard_map/ppermute | solution.py:51
  41.6 4.1 %collective-permute-start.12 = (bf16[256,512]{1,0:T(8,128)(2,1)S(1)}, bf16[256,512]{1,0:T(8,128)(2,1)S(1)}, u32[]{:S(2)}, u32[]{:S(2)}) collective-permute-start(bf16[256,512]{1,0:T(8,128)(2,1)S(1)} %get-tuple-element.44), channel_id=1, source_target_pairs={{0,3},{1,0},{2,1},{3,2},{4,7},{5,4},{6,5},{7,6},{8,9},{9,10},{10,1... | collective-permute-start | bytes 786440 | tf_op jit(solution)/shard_map/ppermute | solution.py:51
  47.7 1.9 %collective-permute-done.12 = bf16[256,512]{1,0:T(8,128)(2,1)S(1)} collective-permute-done((bf16[256,512]{1,0:T(8,128)(2,1)S(1)}, bf16[256,512]{1,0:T(8,128)(2,1)S(1)}, u32[]{:S(2)}, u32[]{:S(2)}) %collective-permute-start.12) | collective-permute-done | bytes 262176 | tf_op jit(solution)/shard_map/ppermute | solution.py:51
  49.7 3.8 %collective-permute-start.13 = (bf16[256,512]{1,0:T(8,128)(2,1)S(1)}, bf16[256,512]{1,0:T(8,128)(2,1)S(1)}, u32[]{:S(2)}, u32[]{:S(2)}) collective-permute-start(bf16[256,512]{1,0:T(8,128)(2,1)S(1)} %add_convert_fusion.3), channel_id=1, source_target_pairs={{0,3},{1,0},{2,1},{3,2},{4,7},{5,4},{6,5},{7,6},{8,9},{9,10},{10,1... | collective-permute-start | bytes 786440 | tf_op jit(solution)/shard_map/ppermute | solution.py:51
  53.5 2.7 %collective-permute-start.9 = (bf16[256,512]{1,0:T(8,128)(2,1)S(1)}, bf16[256,512]{1,0:T(8,128)(2,1)S(1)}, u32[]{:S(2)}, u32[]{:S(2)}) collective-permute-start(bf16[256,512]{1,0:T(8,128)(2,1)S(1)} %add_convert_fusion.5), channel_id=1, source_target_pairs={{0,3},{1,0},{2,1},{3,2},{4,7},{5,4},{6,5},{7,6},{8,9},{9,10},{10,1... | collective-permute-start | bytes 786440 | tf_op jit(solution)/shard_map/ppermute | solution.py:51
  56.4 2.3 %collective-permute-done.13 = bf16[256,512]{1,0:T(8,128)(2,1)S(1)} collective-permute-done((bf16[256,512]{1,0:T(8,128)(2,1)S(1)}, bf16[256,512]{1,0:T(8,128)(2,1)S(1)}, u32[]{:S(2)}, u32[]{:S(2)}) %collective-permute-start.13) | collective-permute-done | bytes 262176 | tf_op jit(solution)/shard_map/ppermute | solution.py:51
  60.5 2.5 %collective-permute-done.9 = bf16[256,512]{1,0:T(8,128)(2,1)S(1)} collective-permute-done((bf16[256,512]{1,0:T(8,128)(2,1)S(1)}, bf16[256,512]{1,0:T(8,128)(2,1)S(1)}, u32[]{:S(2)}, u32[]{:S(2)}) %collective-permute-start.9) | collective-permute-done | bytes 262176 | tf_op jit(solution)/shard_map/ppermute | solution.py:51
  64.0 1.7 %collective-permute-done.14 = bf16[256,512]{1,0:T(8,128)(2,1)S(1)} collective-permute-done((bf16[256,512]{1,0:T(8,128)(2,1)S(1)}, bf16[256,512]{1,0:T(8,128)(2,1)S(1)}, u32[]{:S(2)}, u32[]{:S(2)}) %collective-permute-start.14) | collective-permute-done | bytes 262176 | tf_op jit(solution)/shard_map/ppermute | solution.py:51
  65.9 1.7 %collective-permute-start.21 = (bf16[256,512]{1,0:T(8,128)(2,1)S(1)}, bf16[256,512]{1,0:T(8,128)(2,1)S(1)}, u32[]{:S(2)}, u32[]{:S(2)}) collective-permute-start(bf16[256,512]{1,0:T(8,128)(2,1)S(1)} %add_convert_fusion.1.rest_8_), channel_id=1, source_target_pairs={{0,4},{1,5},{2,6},{3,7},{4,0},{5,1},{6,2},{7,3},{8,12},{9,13},{10,... | collective-permute-start | bytes 786440 | tf_op jit(solution)/shard_map/ppermute | solution.py:51
  67.7 3.2 %collective-permute-start.19 = (bf16[256,512]{1,0:T(8,128)(2,1)S(1)}, bf16[256,512]{1,0:T(8,128)(2,1)S(1)}, u32[]{:S(2)}, u32[]{:S(2)}) collective-permute-start(bf16[256,512]{1,0:T(8,128)(2,1)S(1)} %add_convert_fusion.1.rest_8_), channel_id=1, source_target_pairs={{0,96},{1,97},{2,98},{3,99},{4,100},{5,101},{6,102},{7,103},{8,40}... | collective-permute-start | bytes 786440 | tf_op jit(solution)/shard_map/ppermute | solution.py:51
  71.0 3.0 %collective-permute-start.18 = (bf16[512,256]{1,0:T(8,128)(2,1)S(1)}, bf16[512,256]{1,0:T(8,128)(2,1)S(1)}, u32[]{:S(2)}, u32[]{:S(2)}) collective-permute-start(bf16[512,256]{1,0:T(8,128)(2,1)S(1)} %pad_maximum_fusion.2.rest_0_), channel_id=1, source_target_pairs={{0,16},{1,17},{2,18},{3,19},{4,20},{5,21},{6,22},{7,23},{8,24},{9,... | collective-permute-start | bytes 786440 | tf_op jit(solution)/shard_map/ppermute | solution.py:51
  74.0 4.0 %collective-permute-start.16 = (bf16[512,256]{1,0:T(8,128)(2,1)S(1)}, bf16[512,256]{1,0:T(8,128)(2,1)S(1)}, u32[]{:S(2)}, u32[]{:S(2)}) collective-permute-start(bf16[512,256]{1,0:T(8,128)(2,1)S(1)} %pad_maximum_fusion.2.rest_0_), channel_id=1, source_target_pairs={{0,3},{1,0},{2,1},{3,2},{4,7},{5,4},{6,5},{7,6},{8,9},{9,10},{10,1... | collective-permute-start | bytes 786440 | tf_op jit(solution)/shard_map/ppermute | solution.py:51
  78.0 2.4 %collective-permute-done.18.rest_4_ = bf16[512,256]{1,0:T(8,128)(2,1)S(1)} collective-permute-done((bf16[512,256]{1,0:T(8,128)(2,1)S(1)}, bf16[512,256]{1,0:T(8,128)(2,1)S(1)}, u32[]{:S(2)}, u32[]{:S(2)}) %collective-permute-start.18) | collective-permute-done | bytes 262176 | tf_op jit(solution)/shard_map/ppermute | solution.py:51
  80.4 3.8 %collective-permute-done.17.rest_1_ = bf16[512,256]{1,0:T(8,128)(2,1)S(1)} collective-permute-done((bf16[512,256]{1,0:T(8,128)(2,1)S(1)}, bf16[512,256]{1,0:T(8,128)(2,1)S(1)}, u32[]{:S(2)}, u32[]{:S(2)}) %collective-permute-start.17) | collective-permute-done | bytes 262176 | tf_op jit(solution)/shard_map/ppermute | solution.py:51
  84.4 3.2 %collective-permute-start.22 = (bf16[512,256]{1,0:T(8,128)(2,1)S(1)}, bf16[512,256]{1,0:T(8,128)(2,1)S(1)}, u32[]{:S(2)}, u32[]{:S(2)}) collective-permute-start(bf16[512,256]{1,0:T(8,128)(2,1)S(1)} %collective-permute-done.18.rest_4_), channel_id=1, source_target_pairs={{0,3},{1,0},{2,1},{3,2},{4,7},{5,4},{6,5},{7,6},{8,9},{9,10},{10,1... | collective-permute-start | bytes 786440 | tf_op jit(solution)/shard_map/ppermute | solution.py:51
  87.6 3.2 %collective-permute-start.24 = (bf16[256,512]{1,0:T(8,128)(2,1)S(1)}, bf16[256,512]{1,0:T(8,128)(2,1)S(1)}, u32[]{:S(2)}, u32[]{:S(2)}) collective-permute-start(bf16[256,512]{1,0:T(8,128)(2,1)S(1)} %collective-permute-done.21.rest_12_), channel_id=1, source_target_pairs={{0,96},{1,97},{2,98},{3,99},{4,100},{5,101},{6,102},{7,103},{8,40}... | collective-permute-start | bytes 786440 | tf_op jit(solution)/shard_map/ppermute | solution.py:51
  90.9 3.0 %collective-permute-done.22.rest_6_ = bf16[512,256]{1,0:T(8,128)(2,1)S(1)} collective-permute-done((bf16[512,256]{1,0:T(8,128)(2,1)S(1)}, bf16[512,256]{1,0:T(8,128)(2,1)S(1)}, u32[]{:S(2)}, u32[]{:S(2)}) %collective-permute-start.22) | collective-permute-done | bytes 262176 | tf_op jit(solution)/shard_map/ppermute | solution.py:51
  93.8 2.3 %collective-permute-done.24.rest_14_ = bf16[256,512]{1,0:T(8,128)(2,1)S(1)} collective-permute-done((bf16[256,512]{1,0:T(8,128)(2,1)S(1)}, bf16[256,512]{1,0:T(8,128)(2,1)S(1)}, u32[]{:S(2)}, u32[]{:S(2)}) %collective-permute-start.24) | collective-permute-done | bytes 262176 | tf_op jit(solution)/shard_map/ppermute | solution.py:51
  98.2 6.3 %collective-permute-done.26.rest_7_ = bf16[512,256]{1,0:T(8,128)(2,1)S(1)} collective-permute-done((bf16[512,256]{1,0:T(8,128)(2,1)S(1)}, bf16[512,256]{1,0:T(8,128)(2,1)S(1)}, u32[]{:S(2)}, u32[]{:S(2)}) %collective-permute-start.26) | collective-permute-done | bytes 262176 | tf_op jit(solution)/shard_map/ppermute | solution.py:51
  105.4 1.9 %square_part.1 = (f32[256,512]{1,0:T(8,128)S(1)}, bf16[256,512]{1,0:T(8,128)(2,1)S(1)}) custom-call(s32[5]{0:T(128)S(1)} %stack.23.where, bf16[512,256]{1,0:T(8,128)(2,1)S(1)} %pad_maximum_fusion.2.rest_0_, bf16[512,256]{1,0:T(8,128)(2,1)S(1)} %collective-permute-done.17.rest_1_, bf16[512,256]{1,0:T(8,128)(2,1)S(1)} %collective-permute-done.16.rest_2_, ...), custom_call_target="tpu_custom_call" | custom-call | flops 1073741824 | bytes 4194304 | tf_op jit(solution)/shard_map/square_part/pallas_call | solution.py:205
  109.3 3.2 %collective-permute-start.30 = (bf16[256,512]{1,0:T(8,128)(2,1)S(1)}, bf16[256,512]{1,0:T(8,128)(2,1)S(1)}, u32[]{:S(2)}, u32[]{:S(2)}) collective-permute-start(bf16[256,512]{1,0:T(8,128)(2,1)S(1)} %add_convert_fusion.rest_0_), channel_id=1, source_target_pairs={{0,3},{1,0},{2,1},{3,2},{4,7},{5,4},{6,5},{7,6},{8,9},{9,10},{10,1... | collective-permute-start | bytes 786440 | tf_op jit(solution)/shard_map/ppermute | solution.py:51
  112.6 5.2 %collective-permute-done.32.rest_4_ = bf16[256,512]{1,0:T(8,128)(2,1)S(1)} collective-permute-done((bf16[256,512]{1,0:T(8,128)(2,1)S(1)}, bf16[256,512]{1,0:T(8,128)(2,1)S(1)}, u32[]{:S(2)}, u32[]{:S(2)}) %collective-permute-start.32) | collective-permute-done | bytes 262176 | tf_op jit(solution)/shard_map/ppermute | solution.py:51
  120.5 4.8 %collective-permute-done.33.rest_5_ = bf16[256,512]{1,0:T(8,128)(2,1)S(1)} collective-permute-done((bf16[256,512]{1,0:T(8,128)(2,1)S(1)}, bf16[256,512]{1,0:T(8,128)(2,1)S(1)}, u32[]{:S(2)}, u32[]{:S(2)}) %collective-permute-start.33) | collective-permute-done | bytes 262176 | tf_op jit(solution)/shard_map/ppermute | solution.py:51
  125.4 2.0 %collective-permute-done.34.rest_6_ = bf16[256,512]{1,0:T(8,128)(2,1)S(1)} collective-permute-done((bf16[256,512]{1,0:T(8,128)(2,1)S(1)}, bf16[256,512]{1,0:T(8,128)(2,1)S(1)}, u32[]{:S(2)}, u32[]{:S(2)}) %collective-permute-start.34) | collective-permute-done | bytes 262176 | tf_op jit(solution)/shard_map/ppermute | solution.py:51
  128.2 4.8 %collective-permute-done.35.rest_7_ = bf16[256,512]{1,0:T(8,128)(2,1)S(1)} collective-permute-done((bf16[256,512]{1,0:T(8,128)(2,1)S(1)}, bf16[256,512]{1,0:T(8,128)(2,1)S(1)}, u32[]{:S(2)}, u32[]{:S(2)}) %collective-permute-start.35) | collective-permute-done | bytes 262176 | tf_op jit(solution)/shard_map/ppermute | solution.py:51
  133.0 2.4 %apply_other.1 = bf16[256,1536]{1,0:T(8,128)(2,1)S(1)} custom-call(s32[5]{0:T(128)S(1)} %stack.23.where, bf16[256,512]{1,0:T(8,128)(2,1)S(1)} %add_convert_fusion.rest_0_, bf16[256,512]{1,0:T(8,128)(2,1)S(1)} %collective-permute-done.29.rest_1_, bf16[256,512]{1,0:T(8,128)(2,1)S(1)} %collective-permute-done.30.rest_2_, ...), custom_call_target="tpu_custom_call" | custom-call | flops 1610612736 | bytes 9175040 | tf_op jit(solution)/shard_map/apply_other/pallas_call | solution.py:222
  136.1 2.4 %apply_own.1 = f32[256,1536]{1,0:T(8,128)S(1)} custom-call(s32[5]{0:T(128)S(1)} %stack.23.where, bf16[256,512]{1,0:T(8,128)(2,1)S(1)} %add_convert_fusion.rest_0_, bf16[256,512]{1,0:T(8,128)(2,1)S(1)} %collective-permute-done.29.rest_1_, bf16[256,512]{1,0:T(8,128)(2,1)S(1)} %collective-permute-done.30.rest_2_, ...), custom_call_target="tpu_custom_call" | custom-call | flops 1610612736 | bytes 9175040 | tf_op jit(solution)/shard_map/apply_own/pallas_call | solution.py:222
  138.5 14.5 %collective-permute-done.36 = bf16[256,1536]{1,0:T(8,128)(2,1)S(1)} collective-permute-done((bf16[256,1536]{1,0:T(8,128)(2,1)S(1)}, bf16[256,1536]{1,0:T(8,128)(2,1)S(1)}, u32[]{:S(2)}, u32[]{:S(2)}) %collective-permute-start.36) | collective-permute-done | bytes 786464 | tf_op jit(solution)/shard_map/ppermute | solution.py:51
  (92 shorter events, 29.2 us)
Async XLA Ops:
  0.0 20.4 %collective-permute-start.3 = (bf16[256,1536]{1,0:T(8,128)(2,1)}, bf16[256,1536]{1,0:T(8,128)(2,1)S(1)}, u32[]{:S(2)}, u32[]{:S(2)}) collective-permute-start(bf16[256,1536]{1,0:T(8,128)(2,1)} %rest_8_.3), channel_id=1, source_target_pairs={{0,32},{1,33},{2,34},{3,35},{4,36},{5,37},{6,38},{7,39},{8,104},{9... | collective-permute-start | bytes 2359304 | tf_op jit(solution)/shard_map/ppermute | solution.py:51
  1.6 18.8 %collective-permute-start.2 = (bf16[256,1536]{1,0:T(8,128)(2,1)}, bf16[256,1536]{1,0:T(8,128)(2,1)S(1)}, u32[]{:S(2)}, u32[]{:S(2)}) collective-permute-start(bf16[256,1536]{1,0:T(8,128)(2,1)} %rest_8_.3), channel_id=1, source_target_pairs={{0,96},{1,97},{2,98},{3,99},{4,100},{5,101},{6,102},{7,103},{8,40}... | collective-permute-start | bytes 2359304 | tf_op jit(solution)/shard_map/ppermute | solution.py:51
  3.2 20.3 %collective-permute-start.1 = (bf16[256,1536]{1,0:T(8,128)(2,1)}, bf16[256,1536]{1,0:T(8,128)(2,1)S(1)}, u32[]{:S(2)}, u32[]{:S(2)}) collective-permute-start(bf16[256,1536]{1,0:T(8,128)(2,1)} %rest_8_.3), channel_id=1, source_target_pairs={{0,16},{1,17},{2,18},{3,19},{4,20},{5,21},{6,22},{7,23},{8,24},{9,... | collective-permute-start | bytes 2359304 | tf_op jit(solution)/shard_map/ppermute | solution.py:51
  6.5 17.1 %collective-permute-start = (bf16[256,1536]{1,0:T(8,128)(2,1)}, bf16[256,1536]{1,0:T(8,128)(2,1)S(1)}, u32[]{:S(2)}, u32[]{:S(2)}) collective-permute-start(bf16[256,1536]{1,0:T(8,128)(2,1)} %rest_8_.3), channel_id=1, source_target_pairs={{0,8},{1,9},{2,10},{3,11},{4,12},{5,13},{6,14},{7,15},{8,0},{9,1},... | collective-permute-start | bytes 2359304 | tf_op jit(solution)/shard_map/ppermute | solution.py:51
  24.2 13.2 %collective-permute-start.4 = (bf16[256,1536]{1,0:T(8,128)(2,1)S(1)}, bf16[256,1536]{1,0:T(8,128)(2,1)S(1)}, u32[]{:S(2)}, u32[]{:S(2)}) collective-permute-start(bf16[256,1536]{1,0:T(8,128)(2,1)S(1)} %collective-permute-done.3.fore.rest_10_), channel_id=1, source_target_pairs={{0,32},{1,33},{2,34},{3,35},{4,36},{5,37},{6,38},{7,39},{8,104},{9... | collective-permute-start | bytes 2359304 | tf_op jit(solution)/shard_map/ppermute | solution.py:51
  41.6 8.0 %collective-permute-start.12 = (bf16[256,512]{1,0:T(8,128)(2,1)S(1)}, bf16[256,512]{1,0:T(8,128)(2,1)S(1)}, u32[]{:S(2)}, u32[]{:S(2)}) collective-permute-start(bf16[256,512]{1,0:T(8,128)(2,1)S(1)} %get-tuple-element.44), channel_id=1, source_target_pairs={{0,3},{1,0},{2,1},{3,2},{4,7},{5,4},{6,5},{7,6},{8,9},{9,10},{10,1... | collective-permute-start | bytes 786440 | tf_op jit(solution)/shard_map/ppermute | solution.py:51
  45.7 7.7 %collective-permute-start.8 = (bf16[256,512]{1,0:T(8,128)(2,1)S(1)}, bf16[256,512]{1,0:T(8,128)(2,1)S(1)}, u32[]{:S(2)}, u32[]{:S(2)}) collective-permute-start(bf16[256,512]{1,0:T(8,128)(2,1)S(1)} %get-tuple-element.39), channel_id=1, source_target_pairs={{0,3},{1,0},{2,1},{3,2},{4,7},{5,4},{6,5},{7,6},{8,9},{9,10},{10,1... | collective-permute-start | bytes 786440 | tf_op jit(solution)/shard_map/ppermute | solution.py:51
  46.2 10.1 %collective-permute-start.10 = (bf16[256,512]{1,0:T(8,128)(2,1)S(1)}, bf16[256,512]{1,0:T(8,128)(2,1)S(1)}, u32[]{:S(2)}, u32[]{:S(2)}) collective-permute-start(bf16[256,512]{1,0:T(8,128)(2,1)S(1)} %get-tuple-element.41), channel_id=1, source_target_pairs={{0,4},{1,5},{2,6},{3,7},{4,0},{5,1},{6,2},{7,3},{8,12},{9,13},{10,... | collective-permute-start | bytes 786440 | tf_op jit(solution)/shard_map/ppermute | solution.py:51
  49.7 9.1 %collective-permute-start.13 = (bf16[256,512]{1,0:T(8,128)(2,1)S(1)}, bf16[256,512]{1,0:T(8,128)(2,1)S(1)}, u32[]{:S(2)}, u32[]{:S(2)}) collective-permute-start(bf16[256,512]{1,0:T(8,128)(2,1)S(1)} %add_convert_fusion.3), channel_id=1, source_target_pairs={{0,3},{1,0},{2,1},{3,2},{4,7},{5,4},{6,5},{7,6},{8,9},{9,10},{10,1... | collective-permute-start | bytes 786440 | tf_op jit(solution)/shard_map/ppermute | solution.py:51
  53.5 9.4 %collective-permute-start.9 = (bf16[256,512]{1,0:T(8,128)(2,1)S(1)}, bf16[256,512]{1,0:T(8,128)(2,1)S(1)}, u32[]{:S(2)}, u32[]{:S(2)}) collective-permute-start(bf16[256,512]{1,0:T(8,128)(2,1)S(1)} %add_convert_fusion.5), channel_id=1, source_target_pairs={{0,3},{1,0},{2,1},{3,2},{4,7},{5,4},{6,5},{7,6},{8,9},{9,10},{10,1... | collective-permute-start | bytes 786440 | tf_op jit(solution)/shard_map/ppermute | solution.py:51
  56.3 7.7 %collective-permute-start.11 = (bf16[256,512]{1,0:T(8,128)(2,1)S(1)}, bf16[256,512]{1,0:T(8,128)(2,1)S(1)}, u32[]{:S(2)}, u32[]{:S(2)}) collective-permute-start(bf16[256,512]{1,0:T(8,128)(2,1)S(1)} %add_convert_fusion.4), channel_id=1, source_target_pairs={{0,1},{1,2},{2,3},{3,0},{4,5},{5,6},{6,7},{7,4},{8,11},{9,8},{10,9... | collective-permute-start | bytes 786440 | tf_op jit(solution)/shard_map/ppermute | solution.py:51
  58.8 6.9 %collective-permute-start.14 = (bf16[256,512]{1,0:T(8,128)(2,1)S(1)}, bf16[256,512]{1,0:T(8,128)(2,1)S(1)}, u32[]{:S(2)}, u32[]{:S(2)}) collective-permute-start(bf16[256,512]{1,0:T(8,128)(2,1)S(1)} %add_convert_fusion.2), channel_id=1, source_target_pairs={{0,4},{1,5},{2,6},{3,7},{4,0},{5,1},{6,2},{7,3},{8,12},{9,13},{10,... | collective-permute-start | bytes 786440 | tf_op jit(solution)/shard_map/ppermute | solution.py:51
  65.9 8.1 %collective-permute-start.21 = (bf16[256,512]{1,0:T(8,128)(2,1)S(1)}, bf16[256,512]{1,0:T(8,128)(2,1)S(1)}, u32[]{:S(2)}, u32[]{:S(2)}) collective-permute-start(bf16[256,512]{1,0:T(8,128)(2,1)S(1)} %add_convert_fusion.1.rest_8_), channel_id=1, source_target_pairs={{0,4},{1,5},{2,6},{3,7},{4,0},{5,1},{6,2},{7,3},{8,12},{9,13},{10,... | collective-permute-start | bytes 786440 | tf_op jit(solution)/shard_map/ppermute | solution.py:51
  67.6 10.3 %collective-permute-start.20 = (bf16[256,512]{1,0:T(8,128)(2,1)S(1)}, bf16[256,512]{1,0:T(8,128)(2,1)S(1)}, u32[]{:S(2)}, u32[]{:S(2)}) collective-permute-start(bf16[256,512]{1,0:T(8,128)(2,1)S(1)} %add_convert_fusion.1.rest_8_), channel_id=1, source_target_pairs={{0,32},{1,33},{2,34},{3,35},{4,36},{5,37},{6,38},{7,39},{8,104},{9... | collective-permute-start | bytes 786440 | tf_op jit(solution)/shard_map/ppermute | solution.py:51
  67.7 10.3 %collective-permute-start.19 = (bf16[256,512]{1,0:T(8,128)(2,1)S(1)}, bf16[256,512]{1,0:T(8,128)(2,1)S(1)}, u32[]{:S(2)}, u32[]{:S(2)}) collective-permute-start(bf16[256,512]{1,0:T(8,128)(2,1)S(1)} %add_convert_fusion.1.rest_8_), channel_id=1, source_target_pairs={{0,96},{1,97},{2,98},{3,99},{4,100},{5,101},{6,102},{7,103},{8,40}... | collective-permute-start | bytes 786440 | tf_op jit(solution)/shard_map/ppermute | solution.py:51
  71.0 9.4 %collective-permute-start.18 = (bf16[512,256]{1,0:T(8,128)(2,1)S(1)}, bf16[512,256]{1,0:T(8,128)(2,1)S(1)}, u32[]{:S(2)}, u32[]{:S(2)}) collective-permute-start(bf16[512,256]{1,0:T(8,128)(2,1)S(1)} %pad_maximum_fusion.2.rest_0_), channel_id=1, source_target_pairs={{0,16},{1,17},{2,18},{3,19},{4,20},{5,21},{6,22},{7,23},{8,24},{9,... | collective-permute-start | bytes 786440 | tf_op jit(solution)/shard_map/ppermute | solution.py:51
  74.0 10.2 %collective-permute-start.17 = (bf16[512,256]{1,0:T(8,128)(2,1)S(1)}, bf16[512,256]{1,0:T(8,128)(2,1)S(1)}, u32[]{:S(2)}, u32[]{:S(2)}) collective-permute-start(bf16[512,256]{1,0:T(8,128)(2,1)S(1)} %pad_maximum_fusion.2.rest_0_), channel_id=1, source_target_pairs={{0,1},{1,2},{2,3},{3,0},{4,5},{5,6},{6,7},{7,4},{8,11},{9,8},{10,9... | collective-permute-start | bytes 786440 | tf_op jit(solution)/shard_map/ppermute | solution.py:51
  74.0 10.2 %collective-permute-start.16 = (bf16[512,256]{1,0:T(8,128)(2,1)S(1)}, bf16[512,256]{1,0:T(8,128)(2,1)S(1)}, u32[]{:S(2)}, u32[]{:S(2)}) collective-permute-start(bf16[512,256]{1,0:T(8,128)(2,1)S(1)} %pad_maximum_fusion.2.rest_0_), channel_id=1, source_target_pairs={{0,3},{1,0},{2,1},{3,2},{4,7},{5,4},{6,5},{7,6},{8,9},{9,10},{10,1... | collective-permute-start | bytes 786440 | tf_op jit(solution)/shard_map/ppermute | solution.py:51
  84.2 12.3 %collective-permute-start.25 = (bf16[512,512]{1,0:T(8,128)(2,1)S(1)}, bf16[512,512]{1,0:T(8,128)(2,1)S(1)}, u32[]{:S(2)}, u32[]{:S(2)}) collective-permute-start(bf16[512,512]{1,0:T(8,128)(2,1)S(1)} %pad_maximum_fusion.1), channel_id=1, source_target_pairs={{0,32},{1,33},{2,34},{3,35},{4,36},{5,37},{6,38},{7,39},{8,104},{9... | collective-permute-start | bytes 1572872 | tf_op jit(solution)/shard_map/ppermute | solution.py:51
  84.3 12.5 %collective-permute-start.23 = (bf16[1024,256]{1,0:T(8,128)(2,1)S(1)}, bf16[1024,256]{1,0:T(8,128)(2,1)S(1)}, u32[]{:S(2)}, u32[]{:S(2)}) collective-permute-start(bf16[1024,256]{1,0:T(8,128)(2,1)S(1)} %pad_maximum_fusion), channel_id=1, source_target_pairs={{0,1},{1,2},{2,3},{3,0},{4,5},{5,6},{6,7},{7,4},{8,11},{9,8},{10,9... | collective-permute-start | bytes 1572872 | tf_op jit(solution)/shard_map/ppermute | solution.py:51
  84.4 9.4 %collective-permute-start.22 = (bf16[512,256]{1,0:T(8,128)(2,1)S(1)}, bf16[512,256]{1,0:T(8,128)(2,1)S(1)}, u32[]{:S(2)}, u32[]{:S(2)}) collective-permute-start(bf16[512,256]{1,0:T(8,128)(2,1)S(1)} %collective-permute-done.18.rest_4_), channel_id=1, source_target_pairs={{0,3},{1,0},{2,1},{3,2},{4,7},{5,4},{6,5},{7,6},{8,9},{9,10},{10,1... | collective-permute-start | bytes 786440 | tf_op jit(solution)/shard_map/ppermute | solution.py:51
  87.6 8.4 %collective-permute-start.24 = (bf16[256,512]{1,0:T(8,128)(2,1)S(1)}, bf16[256,512]{1,0:T(8,128)(2,1)S(1)}, u32[]{:S(2)}, u32[]{:S(2)}) collective-permute-start(bf16[256,512]{1,0:T(8,128)(2,1)S(1)} %collective-permute-done.21.rest_12_), channel_id=1, source_target_pairs={{0,96},{1,97},{2,98},{3,99},{4,100},{5,101},{6,102},{7,103},{8,40}... | collective-permute-start | bytes 786440 | tf_op jit(solution)/shard_map/ppermute | solution.py:51
  96.8 7.7 %collective-permute-start.26 = (bf16[512,256]{1,0:T(8,128)(2,1)S(1)}, bf16[512,256]{1,0:T(8,128)(2,1)S(1)}, u32[]{:S(2)}, u32[]{:S(2)}) collective-permute-start(bf16[512,256]{1,0:T(8,128)(2,1)S(1)} %get-tuple-element.59.rest_5_), channel_id=1, source_target_pairs={{0,1},{1,2},{2,3},{3,0},{4,5},{5,6},{6,7},{7,4},{8,11},{9,8},{10,9... | collective-permute-start | bytes 786440 | tf_op jit(solution)/shard_map/ppermute | solution.py:51
  97.0 8.4 %collective-permute-start.27 = (bf16[256,512]{1,0:T(8,128)(2,1)S(1)}, bf16[256,512]{1,0:T(8,128)(2,1)S(1)}, u32[]{:S(2)}, u32[]{:S(2)}) collective-permute-start(bf16[256,512]{1,0:T(8,128)(2,1)S(1)} %get-tuple-element.57.rest_13_), channel_id=1, source_target_pairs={{0,32},{1,33},{2,34},{3,35},{4,36},{5,37},{6,38},{7,39},{8,104},{9... | collective-permute-start | bytes 786440 | tf_op jit(solution)/shard_map/ppermute | solution.py:51
  109.1 8.7 %collective-permute-start.32 = (bf16[256,512]{1,0:T(8,128)(2,1)S(1)}, bf16[256,512]{1,0:T(8,128)(2,1)S(1)}, u32[]{:S(2)}, u32[]{:S(2)}) collective-permute-start(bf16[256,512]{1,0:T(8,128)(2,1)S(1)} %add_convert_fusion.rest_0_), channel_id=1, source_target_pairs={{0,4},{1,5},{2,6},{3,7},{4,0},{5,1},{6,2},{7,3},{8,12},{9,13},{10,... | collective-permute-start | bytes 786440 | tf_op jit(solution)/shard_map/ppermute | solution.py:51
  109.3 9.1 %collective-permute-start.30 = (bf16[256,512]{1,0:T(8,128)(2,1)S(1)}, bf16[256,512]{1,0:T(8,128)(2,1)S(1)}, u32[]{:S(2)}, u32[]{:S(2)}) collective-permute-start(bf16[256,512]{1,0:T(8,128)(2,1)S(1)} %add_convert_fusion.rest_0_), channel_id=1, source_target_pairs={{0,3},{1,0},{2,1},{3,2},{4,7},{5,4},{6,5},{7,6},{8,9},{9,10},{10,1... | collective-permute-start | bytes 786440 | tf_op jit(solution)/shard_map/ppermute | solution.py:51
  112.5 7.6 %collective-permute-start.29 = (bf16[256,512]{1,0:T(8,128)(2,1)S(1)}, bf16[256,512]{1,0:T(8,128)(2,1)S(1)}, u32[]{:S(2)}, u32[]{:S(2)}) collective-permute-start(bf16[256,512]{1,0:T(8,128)(2,1)S(1)} %add_convert_fusion.rest_0_), channel_id=1, source_target_pairs={{0,1},{1,2},{2,3},{3,0},{4,5},{5,6},{6,7},{7,4},{8,11},{9,8},{10,9... | collective-permute-start | bytes 786440 | tf_op jit(solution)/shard_map/ppermute | solution.py:51
  117.8 7.6 %collective-permute-start.33 = (bf16[256,512]{1,0:T(8,128)(2,1)S(1)}, bf16[256,512]{1,0:T(8,128)(2,1)S(1)}, u32[]{:S(2)}, u32[]{:S(2)}) collective-permute-start(bf16[256,512]{1,0:T(8,128)(2,1)S(1)} %collective-permute-done.32.rest_4_), channel_id=1, source_target_pairs={{0,1},{1,2},{2,3},{3,0},{4,5},{5,6},{6,7},{7,4},{8,11},{9,8},{10,9... | collective-permute-start | bytes 786440 | tf_op jit(solution)/shard_map/ppermute | solution.py:51
  118.5 8.9 %collective-permute-start.34 = (bf16[256,512]{1,0:T(8,128)(2,1)S(1)}, bf16[256,512]{1,0:T(8,128)(2,1)S(1)}, u32[]{:S(2)}, u32[]{:S(2)}) collective-permute-start(bf16[256,512]{1,0:T(8,128)(2,1)S(1)} %collective-permute-done.30.rest_2_), channel_id=1, source_target_pairs={{0,4},{1,5},{2,6},{3,7},{4,0},{5,1},{6,2},{7,3},{8,12},{9,13},{10,... | collective-permute-start | bytes 786440 | tf_op jit(solution)/shard_map/ppermute | solution.py:51
  120.1 8.1 %collective-permute-start.31 = (bf16[256,512]{1,0:T(8,128)(2,1)S(1)}, bf16[256,512]{1,0:T(8,128)(2,1)S(1)}, u32[]{:S(2)}, u32[]{:S(2)}) collective-permute-start(bf16[256,512]{1,0:T(8,128)(2,1)S(1)} %collective-permute-done.29.rest_1_), channel_id=1, source_target_pairs={{0,1},{1,2},{2,3},{3,0},{4,5},{5,6},{6,7},{7,4},{8,11},{9,8},{10,9... | collective-permute-start | bytes 786440 | tf_op jit(solution)/shard_map/ppermute | solution.py:51
  125.4 7.6 %collective-permute-start.35 = (bf16[256,512]{1,0:T(8,128)(2,1)S(1)}, bf16[256,512]{1,0:T(8,128)(2,1)S(1)}, u32[]{:S(2)}, u32[]{:S(2)}) collective-permute-start(bf16[256,512]{1,0:T(8,128)(2,1)S(1)} %collective-permute-done.33.rest_5_), channel_id=1, source_target_pairs={{0,1},{1,2},{2,3},{3,0},{4,5},{5,6},{6,7},{7,4},{8,11},{9,8},{10,9... | collective-permute-start | bytes 786440 | tf_op jit(solution)/shard_map/ppermute | solution.py:51
  135.4 17.6 %collective-permute-start.36 = (bf16[256,1536]{1,0:T(8,128)(2,1)S(1)}, bf16[256,1536]{1,0:T(8,128)(2,1)S(1)}, u32[]{:S(2)}, u32[]{:S(2)}) collective-permute-start(bf16[256,1536]{1,0:T(8,128)(2,1)S(1)} %apply_other.1), channel_id=1, source_target_pairs={{0,16},{1,17},{2,18},{3,19},{4,20},{5,21},{6,22},{7,23},{8,24},{9,... | collective-permute-start | bytes 2359304 | tf_op jit(solution)/shard_map/ppermute | solution.py:51
  (20 other events, 169.6 us)

commit v4 on v3

--- a/solution.py
+++ b/solution.py
@@ -240,7 +240,7 @@
         [send(value, ring + "_back"), send(value, ring + "_fore"), send(value, pair)]
         for value, ring, pair in sides
     ]
-    first = lax.optimization_barrier(first)
+    first = [lax.optimization_barrier(part) for part in first]
     second = [
         [
             send(there, ring + "_back"),
@@ -248,7 +248,7 @@
         ]
         for (back, fore, there), (value, ring, pair) in zip(first, sides)
     ]
-    second = lax.optimization_barrier(second)
+    second = [lax.optimization_barrier(part) for part in second]
     out = []
     for (back, fore, there), (there_back, both), (value, ring, pair) in zip(first, second, sides):
         count = value.shape[0]
@@ -285,6 +285,7 @@
     row, col = lax.axis_index("row"), lax.axis_index("col")
     where = jnp.stack([row >> 2, (row >> 1) & 1, row & 1, col >> 2, col & 3]).astype(jnp.int32)
 
+    iterate, where = lax.optimization_barrier((iterate, where))
     other, across, back, fore = lax.optimization_barrier(
         [send(iterate, move) for move in ("core", "yh", "x_back", "x_fore")]
     )

time: 154 us -> 154 us (level)
  waiting for transfers between devices: 87.8 us -> 95.8 us
  starting transfers between devices: 48.8 us -> 43 us
  local copies, waits for them, and re-layouts: 4.25 us -> 1.31 us
    ppermute x37, waiting for transfers between devices: 87.8 us -> 95.8 us  [send(): return lax.ppermute(value, ('row', 'col'), pairs(MOVES[move]))]
    ppermute x37, starting transfers between devices: 48.8 us -> 43 us  [send(): return lax.ppermute(value, ('row', 'col'), pairs(MOVES[move]))]
    unnamed x30 -> x4, local copies, waits for them, and re-layouts: 4.08 us -> 1.14 us
  transfers between devices with their start and end apart: 37 -> 37, of which waited for: 28 -> 26; matrix products, arithmetic and copies ran while one was open for 0% -> 0% of each run, Pallas kernels for 4% -> 4%
where the time goes in v4:
time: 154 us; the launch traced here: 153 us
  waiting for transfers between devices  95.8 us (62%)
  starting transfers between devices  43 us (28%)
  Pallas kernels  11.4 us (7%)
  other arithmetic  1.7 us (1%)
    ppermute x37, waiting for transfers between devices, send(): return lax.ppermute(value, ('row', 'col'), pairs(MOVES[move]))  95.8 us
    ppermute x37, starting transfers between devices, send(): return lax.ppermute(value, ('row', 'col'), pairs(MOVES[move]))  43 us
    pallas_call x2, Pallas kernels, apply_part(): pl.pallas_call(functools.partial(apply_kernel, other_rows), in_specs=[sme...  4.85 us
  transfers between devices with their start and end apart: 37, of which 26 were waited for; matrix products, arithmetic and copies ran while one was open for 0% of the time, Pallas kernels for 4%

profile of v4, /device:TPU:0, one launch (start us, length us, event | category | flops | bytes accessed | tf_op | source)
XLA Modules:
  0.0 153.4 jit_solution(10888864859946147695)
XLA Ops:
  3.3 3.3 %collective-permute-start.1 = (bf16[256,1536]{1,0:T(8,128)(2,1)}, bf16[256,1536]{1,0:T(8,128)(2,1)S(1)}, u32[]{:S(2)}, u32[]{:S(2)}) collective-permute-start(bf16[256,1536]{1,0:T(8,128)(2,1)} %rest_8_.1), channel_id=1, source_target_pairs={{0,16},{1,17},{2,18},{3,19},{4,20},{5,21},{6,22},{7,23},{8,24},{9,... | collective-permute-start | bytes 2359304 | tf_op jit(solution)/shard_map/ppermute | solution.py:51
  6.6 13.8 %collective-permute-done.3.fore.rest_10_ = bf16[256,1536]{1,0:T(8,128)(2,1)S(1)} collective-permute-done((bf16[256,1536]{1,0:T(8,128)(2,1)}, bf16[256,1536]{1,0:T(8,128)(2,1)S(1)}, u32[]{:S(2)}, u32[]{:S(2)}) %collective-permute-start.3) | collective-permute-done | bytes 786464 | tf_op jit(solution)/shard_map/ppermute | solution.py:51
  20.4 3.2 %collective-permute-done.1.across = bf16[256,1536]{1,0:T(8,128)(2,1)S(1)} collective-permute-done((bf16[256,1536]{1,0:T(8,128)(2,1)}, bf16[256,1536]{1,0:T(8,128)(2,1)S(1)}, u32[]{:S(2)}, u32[]{:S(2)}) %collective-permute-start.1) | collective-permute-done | bytes 786464 | tf_op jit(solution)/shard_map/ppermute | solution.py:51
  28.2 2.7 %gram_near.1.near = bf16[2,3,256,512]{3,2,1,0:T(8,128)(2,1)S(1)} custom-call(bf16[256,1536]{1,0:T(8,128)(2,1)S(1)} %copy-done, bf16[256,1536]{1,0:T(8,128)(2,1)S(1)} %collective-permute-done.other.rest_9_, bf16[256,1536]{1,0:T(8,128)(2,1)S(1)} %collective-permute-done.3.fore.rest_10_, bf16[256,1536]{1,0:T(8,128)(2,1)S(1)} %collective-permute-done.5.fore_other.rest_11_, ...), custom_call_target="tpu_custom_call" | custom-call | flops 2415919104 | bytes 7077888 | tf_op jit(solution)/shard_map/gram_near/pallas_call | solution.py:166
  30.9 6.5 %collective-permute-done.4.far.rest_14_ = bf16[256,1536]{1,0:T(8,128)(2,1)S(1)} collective-permute-done((bf16[256,1536]{1,0:T(8,128)(2,1)S(1)}, bf16[256,1536]{1,0:T(8,128)(2,1)S(1)}, u32[]{:S(2)}, u32[]{:S(2)}) %collective-permute-start.4) | collective-permute-done | bytes 786464 | tf_op jit(solution)/shard_map/ppermute | solution.py:51
  38.0 1.7 %collective-permute-done.7.far_other.rest_15_ = bf16[256,1536]{1,0:T(8,128)(2,1)S(1)} collective-permute-done((bf16[256,1536]{1,0:T(8,128)(2,1)S(1)}, bf16[256,1536]{1,0:T(8,128)(2,1)S(1)}, u32[]{:S(2)}, u32[]{:S(2)}) %collective-permute-start.7) | collective-permute-done | bytes 786464 | tf_op jit(solution)/shard_map/ppermute | solution.py:51
  41.0 4.1 %collective-permute-start.12 = (bf16[256,512]{1,0:T(8,128)(2,1)S(1)}, bf16[256,512]{1,0:T(8,128)(2,1)S(1)}, u32[]{:S(2)}, u32[]{:S(2)}) collective-permute-start(bf16[256,512]{1,0:T(8,128)(2,1)S(1)} %get-tuple-element.48), channel_id=1, source_target_pairs={{0,3},{1,0},{2,1},{3,2},{4,7},{5,4},{6,5},{7,6},{8,9},{9,10},{10,1... | collective-permute-start | bytes 786440 | tf_op jit(solution)/shard_map/ppermute | solution.py:51
  47.1 1.9 %collective-permute-done.12 = bf16[256,512]{1,0:T(8,128)(2,1)S(1)} collective-permute-done((bf16[256,512]{1,0:T(8,128)(2,1)S(1)}, bf16[256,512]{1,0:T(8,128)(2,1)S(1)}, u32[]{:S(2)}, u32[]{:S(2)}) %collective-permute-start.12) | collective-permute-done | bytes 262176 | tf_op jit(solution)/shard_map/ppermute | solution.py:51
  49.1 3.8 %collective-permute-start.13 = (bf16[256,512]{1,0:T(8,128)(2,1)S(1)}, bf16[256,512]{1,0:T(8,128)(2,1)S(1)}, u32[]{:S(2)}, u32[]{:S(2)}) collective-permute-start(bf16[256,512]{1,0:T(8,128)(2,1)S(1)} %add_convert_fusion.3), channel_id=1, source_target_pairs={{0,3},{1,0},{2,1},{3,2},{4,7},{5,4},{6,5},{7,6},{8,9},{9,10},{10,1... | collective-permute-start | bytes 786440 | tf_op jit(solution)/shard_map/ppermute | solution.py:51
  53.0 2.7 %collective-permute-start.9 = (bf16[256,512]{1,0:T(8,128)(2,1)S(1)}, bf16[256,512]{1,0:T(8,128)(2,1)S(1)}, u32[]{:S(2)}, u32[]{:S(2)}) collective-permute-start(bf16[256,512]{1,0:T(8,128)(2,1)S(1)} %add_convert_fusion.5), channel_id=1, source_target_pairs={{0,3},{1,0},{2,1},{3,2},{4,7},{5,4},{6,5},{7,6},{8,9},{9,10},{10,1... | collective-permute-start | bytes 786440 | tf_op jit(solution)/shard_map/ppermute | solution.py:51
  55.8 2.8 %collective-permute-done.13 = bf16[256,512]{1,0:T(8,128)(2,1)S(1)} collective-permute-done((bf16[256,512]{1,0:T(8,128)(2,1)S(1)}, bf16[256,512]{1,0:T(8,128)(2,1)S(1)}, u32[]{:S(2)}, u32[]{:S(2)}) %collective-permute-start.13) | collective-permute-done | bytes 262176 | tf_op jit(solution)/shard_map/ppermute | solution.py:51
  60.3 2.1 %collective-permute-done.9 = bf16[256,512]{1,0:T(8,128)(2,1)S(1)} collective-permute-done((bf16[256,512]{1,0:T(8,128)(2,1)S(1)}, bf16[256,512]{1,0:T(8,128)(2,1)S(1)}, u32[]{:S(2)}, u32[]{:S(2)}) %collective-permute-start.9) | collective-permute-done | bytes 262176 | tf_op jit(solution)/shard_map/ppermute | solution.py:51
  63.4 3.0 %collective-permute-done.14 = bf16[256,512]{1,0:T(8,128)(2,1)S(1)} collective-permute-done((bf16[256,512]{1,0:T(8,128)(2,1)S(1)}, bf16[256,512]{1,0:T(8,128)(2,1)S(1)}, u32[]{:S(2)}, u32[]{:S(2)}) %collective-permute-start.14) | collective-permute-done | bytes 262176 | tf_op jit(solution)/shard_map/ppermute | solution.py:51
  68.3 3.2 %collective-permute-start.22 = (bf16[256,512]{1,0:T(8,128)(2,1)S(1)}, bf16[256,512]{1,0:T(8,128)(2,1)S(1)}, u32[]{:S(2)}, u32[]{:S(2)}) collective-permute-start(bf16[256,512]{1,0:T(8,128)(2,1)S(1)} %add_convert_fusion.1.rest_8_), channel_id=1, source_target_pairs={{0,96},{1,97},{2,98},{3,99},{4,100},{5,101},{6,102},{7,103},{8,40}... | collective-permute-start | bytes 786440 | tf_op jit(solution)/shard_map/ppermute | solution.py:51
  71.6 3.0 %collective-permute-start.18 = (bf16[512,256]{1,0:T(8,128)(2,1)S(1)}, bf16[512,256]{1,0:T(8,128)(2,1)S(1)}, u32[]{:S(2)}, u32[]{:S(2)}) collective-permute-start(bf16[512,256]{1,0:T(8,128)(2,1)S(1)} %pad_maximum_fusion.2.rest_0_), channel_id=1, source_target_pairs={{0,16},{1,17},{2,18},{3,19},{4,20},{5,21},{6,22},{7,23},{8,24},{9,... | collective-permute-start | bytes 786440 | tf_op jit(solution)/shard_map/ppermute | solution.py:51
  74.6 4.1 %collective-permute-start.16 = (bf16[512,256]{1,0:T(8,128)(2,1)S(1)}, bf16[512,256]{1,0:T(8,128)(2,1)S(1)}, u32[]{:S(2)}, u32[]{:S(2)}) collective-permute-start(bf16[512,256]{1,0:T(8,128)(2,1)S(1)} %pad_maximum_fusion.2.rest_0_), channel_id=1, source_target_pairs={{0,3},{1,0},{2,1},{3,2},{4,7},{5,4},{6,5},{7,6},{8,9},{9,10},{10,1... | collective-permute-start | bytes 786440 | tf_op jit(solution)/shard_map/ppermute | solution.py:51
  78.8 2.2 %collective-permute-done.18.rest_4_ = bf16[512,256]{1,0:T(8,128)(2,1)S(1)} collective-permute-done((bf16[512,256]{1,0:T(8,128)(2,1)S(1)}, bf16[512,256]{1,0:T(8,128)(2,1)S(1)}, u32[]{:S(2)}, u32[]{:S(2)}) %collective-permute-start.18) | collective-permute-done | bytes 262176 | tf_op jit(solution)/shard_map/ppermute | solution.py:51
  81.0 4.5 %collective-permute-done.17.rest_1_ = bf16[512,256]{1,0:T(8,128)(2,1)S(1)} collective-permute-done((bf16[512,256]{1,0:T(8,128)(2,1)S(1)}, bf16[512,256]{1,0:T(8,128)(2,1)S(1)}, u32[]{:S(2)}, u32[]{:S(2)}) %collective-permute-start.17) | collective-permute-done | bytes 262176 | tf_op jit(solution)/shard_map/ppermute | solution.py:51
  85.9 3.7 %collective-permute-start.19 = (bf16[512,256]{1,0:T(8,128)(2,1)S(1)}, bf16[512,256]{1,0:T(8,128)(2,1)S(1)}, u32[]{:S(2)}, u32[]{:S(2)}) collective-permute-start(bf16[512,256]{1,0:T(8,128)(2,1)S(1)} %collective-permute-done.18.rest_4_), channel_id=1, source_target_pairs={{0,3},{1,0},{2,1},{3,2},{4,7},{5,4},{6,5},{7,6},{8,9},{9,10},{10,1... | collective-permute-start | bytes 786440 | tf_op jit(solution)/shard_map/ppermute | solution.py:51
  89.6 2.5 %collective-permute-done.25.rest_14_ = bf16[256,512]{1,0:T(8,128)(2,1)S(1)} collective-permute-done((bf16[256,512]{1,0:T(8,128)(2,1)S(1)}, bf16[256,512]{1,0:T(8,128)(2,1)S(1)}, u32[]{:S(2)}, u32[]{:S(2)}) %collective-permute-start.25) | collective-permute-done | bytes 262176 | tf_op jit(solution)/shard_map/ppermute | solution.py:51
  92.2 2.9 %collective-permute-done.19.rest_6_ = bf16[512,256]{1,0:T(8,128)(2,1)S(1)} collective-permute-done((bf16[512,256]{1,0:T(8,128)(2,1)S(1)}, bf16[512,256]{1,0:T(8,128)(2,1)S(1)}, u32[]{:S(2)}, u32[]{:S(2)}) %collective-permute-start.19) | collective-permute-done | bytes 262176 | tf_op jit(solution)/shard_map/ppermute | solution.py:51
  95.1 3.4 %collective-permute-done.20 = bf16[1024,256]{1,0:T(8,128)(2,1)S(1)} collective-permute-done((bf16[1024,256]{1,0:T(8,128)(2,1)S(1)}, bf16[1024,256]{1,0:T(8,128)(2,1)S(1)}, u32[]{:S(2)}, u32[]{:S(2)}) %collective-permute-start.20) | collective-permute-done | bytes 524320 | tf_op jit(solution)/shard_map/ppermute | solution.py:51
  99.8 6.5 %collective-permute-done.21.rest_7_ = bf16[512,256]{1,0:T(8,128)(2,1)S(1)} collective-permute-done((bf16[512,256]{1,0:T(8,128)(2,1)S(1)}, bf16[512,256]{1,0:T(8,128)(2,1)S(1)}, u32[]{:S(2)}, u32[]{:S(2)}) %collective-permute-start.21) | collective-permute-done | bytes 262176 | tf_op jit(solution)/shard_map/ppermute | solution.py:51
  106.3 1.9 %square_part.1 = (f32[256,512]{1,0:T(8,128)S(1)}, bf16[256,512]{1,0:T(8,128)(2,1)S(1)}) custom-call(s32[5]{0:T(128)S(1)} %stack.23.where, bf16[512,256]{1,0:T(8,128)(2,1)S(1)} %pad_maximum_fusion.2.rest_0_, bf16[512,256]{1,0:T(8,128)(2,1)S(1)} %collective-permute-done.17.rest_1_, bf16[512,256]{1,0:T(8,128)(2,1)S(1)} %collective-permute-done.16.rest_2_, ...), custom_call_target="tpu_custom_call" | custom-call | flops 1073741824 | bytes 4194304 | tf_op jit(solution)/shard_map/square_part/pallas_call | solution.py:205
  110.2 2.0 %collective-permute-start.29 = (bf16[256,512]{1,0:T(8,128)(2,1)S(1)}, bf16[256,512]{1,0:T(8,128)(2,1)S(1)}, u32[]{:S(2)}, u32[]{:S(2)}) collective-permute-start(bf16[256,512]{1,0:T(8,128)(2,1)S(1)} %add_convert_fusion.rest_0_), channel_id=1, source_target_pairs={{0,1},{1,2},{2,3},{3,0},{4,5},{5,6},{6,7},{7,4},{8,11},{9,8},{10,9... | collective-permute-start | bytes 786440 | tf_op jit(solution)/shard_map/ppermute | solution.py:51
  112.2 6.2 %collective-permute-done.32.rest_4_ = bf16[256,512]{1,0:T(8,128)(2,1)S(1)} collective-permute-done((bf16[256,512]{1,0:T(8,128)(2,1)S(1)}, bf16[256,512]{1,0:T(8,128)(2,1)S(1)}, u32[]{:S(2)}, u32[]{:S(2)}) %collective-permute-start.32) | collective-permute-done | bytes 262176 | tf_op jit(solution)/shard_map/ppermute | solution.py:51
  120.2 5.8 %collective-permute-done.33.rest_5_ = bf16[256,512]{1,0:T(8,128)(2,1)S(1)} collective-permute-done((bf16[256,512]{1,0:T(8,128)(2,1)S(1)}, bf16[256,512]{1,0:T(8,128)(2,1)S(1)}, u32[]{:S(2)}, u32[]{:S(2)}) %collective-permute-start.33) | collective-permute-done | bytes 262176 | tf_op jit(solution)/shard_map/ppermute | solution.py:51
  127.1 1.7 %collective-permute-done.31.rest_3_ = bf16[256,512]{1,0:T(8,128)(2,1)S(1)} collective-permute-done((bf16[256,512]{1,0:T(8,128)(2,1)S(1)}, bf16[256,512]{1,0:T(8,128)(2,1)S(1)}, u32[]{:S(2)}, u32[]{:S(2)}) %collective-permute-start.31) | collective-permute-done | bytes 262176 | tf_op jit(solution)/shard_map/ppermute | solution.py:51
  128.8 4.8 %collective-permute-done.35.rest_7_ = bf16[256,512]{1,0:T(8,128)(2,1)S(1)} collective-permute-done((bf16[256,512]{1,0:T(8,128)(2,1)S(1)}, bf16[256,512]{1,0:T(8,128)(2,1)S(1)}, u32[]{:S(2)}, u32[]{:S(2)}) %collective-permute-start.35) | collective-permute-done | bytes 262176 | tf_op jit(solution)/shard_map/ppermute | solution.py:51
  133.6 2.4 %apply_other.1 = bf16[256,1536]{1,0:T(8,128)(2,1)S(1)} custom-call(s32[5]{0:T(128)S(1)} %stack.23.where, bf16[256,512]{1,0:T(8,128)(2,1)S(1)} %add_convert_fusion.rest_0_, bf16[256,512]{1,0:T(8,128)(2,1)S(1)} %collective-permute-done.29.rest_1_, bf16[256,512]{1,0:T(8,128)(2,1)S(1)} %collective-permute-done.30.rest_2_, ...), custom_call_target="tpu_custom_call" | custom-call | flops 1610612736 | bytes 9175040 | tf_op jit(solution)/shard_map/apply_other/pallas_call | solution.py:222
  136.9 2.4 %apply_own.1 = f32[256,1536]{1,0:T(8,128)S(1)} custom-call(s32[5]{0:T(128)S(1)} %stack.23.where, bf16[256,512]{1,0:T(8,128)(2,1)S(1)} %add_convert_fusion.rest_0_, bf16[256,512]{1,0:T(8,128)(2,1)S(1)} %collective-permute-done.29.rest_1_, bf16[256,512]{1,0:T(8,128)(2,1)S(1)} %collective-permute-done.30.rest_2_, ...), custom_call_target="tpu_custom_call" | custom-call | flops 1610612736 | bytes 9175040 | tf_op jit(solution)/shard_map/apply_own/pallas_call | solution.py:222
  139.4 12.9 %collective-permute-done.36 = bf16[256,1536]{1,0:T(8,128)(2,1)S(1)} collective-permute-done((bf16[256,1536]{1,0:T(8,128)(2,1)S(1)}, bf16[256,1536]{1,0:T(8,128)(2,1)S(1)}, u32[]{:S(2)}, u32[]{:S(2)}) %collective-permute-start.36) | collective-permute-done | bytes 786464 | tf_op jit(solution)/shard_map/ppermute | solution.py:51
  (66 shorter events, 25.4 us)
Async XLA Ops:
  0.1 20.4 %collective-permute-start.3 = (bf16[256,1536]{1,0:T(8,128)(2,1)}, bf16[256,1536]{1,0:T(8,128)(2,1)S(1)}, u32[]{:S(2)}, u32[]{:S(2)}) collective-permute-start(bf16[256,1536]{1,0:T(8,128)(2,1)} %rest_8_.1), channel_id=1, source_target_pairs={{0,32},{1,33},{2,34},{3,35},{4,36},{5,37},{6,38},{7,39},{8,104},{9... | collective-permute-start | bytes 2359304 | tf_op jit(solution)/shard_map/ppermute | solution.py:51
  1.7 18.8 %collective-permute-start.2 = (bf16[256,1536]{1,0:T(8,128)(2,1)}, bf16[256,1536]{1,0:T(8,128)(2,1)S(1)}, u32[]{:S(2)}, u32[]{:S(2)}) collective-permute-start(bf16[256,1536]{1,0:T(8,128)(2,1)} %rest_8_.1), channel_id=1, source_target_pairs={{0,96},{1,97},{2,98},{3,99},{4,100},{5,101},{6,102},{7,103},{8,40}... | collective-permute-start | bytes 2359304 | tf_op jit(solution)/shard_map/ppermute | solution.py:51
  3.3 20.3 %collective-permute-start.1 = (bf16[256,1536]{1,0:T(8,128)(2,1)}, bf16[256,1536]{1,0:T(8,128)(2,1)S(1)}, u32[]{:S(2)}, u32[]{:S(2)}) collective-permute-start(bf16[256,1536]{1,0:T(8,128)(2,1)} %rest_8_.1), channel_id=1, source_target_pairs={{0,16},{1,17},{2,18},{3,19},{4,20},{5,21},{6,22},{7,23},{8,24},{9,... | collective-permute-start | bytes 2359304 | tf_op jit(solution)/shard_map/ppermute | solution.py:51
  6.6 17.1 %collective-permute-start = (bf16[256,1536]{1,0:T(8,128)(2,1)}, bf16[256,1536]{1,0:T(8,128)(2,1)S(1)}, u32[]{:S(2)}, u32[]{:S(2)}) collective-permute-start(bf16[256,1536]{1,0:T(8,128)(2,1)} %rest_8_.1), channel_id=1, source_target_pairs={{0,8},{1,9},{2,10},{3,11},{4,12},{5,13},{6,14},{7,15},{8,0},{9,1},... | collective-permute-start | bytes 2359304 | tf_op jit(solution)/shard_map/ppermute | solution.py:51
  24.2 13.2 %collective-permute-start.4 = (bf16[256,1536]{1,0:T(8,128)(2,1)S(1)}, bf16[256,1536]{1,0:T(8,128)(2,1)S(1)}, u32[]{:S(2)}, u32[]{:S(2)}) collective-permute-start(bf16[256,1536]{1,0:T(8,128)(2,1)S(1)} %collective-permute-done.3.fore.rest_10_), channel_id=1, source_target_pairs={{0,32},{1,33},{2,34},{3,35},{4,36},{5,37},{6,38},{7,39},{8,104},{9... | collective-permute-start | bytes 2359304 | tf_op jit(solution)/shard_map/ppermute | solution.py:51
  41.0 8.0 %collective-permute-start.12 = (bf16[256,512]{1,0:T(8,128)(2,1)S(1)}, bf16[256,512]{1,0:T(8,128)(2,1)S(1)}, u32[]{:S(2)}, u32[]{:S(2)}) collective-permute-start(bf16[256,512]{1,0:T(8,128)(2,1)S(1)} %get-tuple-element.48), channel_id=1, source_target_pairs={{0,3},{1,0},{2,1},{3,2},{4,7},{5,4},{6,5},{7,6},{8,9},{9,10},{10,1... | collective-permute-start | bytes 786440 | tf_op jit(solution)/shard_map/ppermute | solution.py:51
  45.2 7.7 %collective-permute-start.8 = (bf16[256,512]{1,0:T(8,128)(2,1)S(1)}, bf16[256,512]{1,0:T(8,128)(2,1)S(1)}, u32[]{:S(2)}, u32[]{:S(2)}) collective-permute-start(bf16[256,512]{1,0:T(8,128)(2,1)S(1)} %get-tuple-element.43), channel_id=1, source_target_pairs={{0,3},{1,0},{2,1},{3,2},{4,7},{5,4},{6,5},{7,6},{8,9},{9,10},{10,1... | collective-permute-start | bytes 786440 | tf_op jit(solution)/shard_map/ppermute | solution.py:51
  45.6 10.1 %collective-permute-start.10 = (bf16[256,512]{1,0:T(8,128)(2,1)S(1)}, bf16[256,512]{1,0:T(8,128)(2,1)S(1)}, u32[]{:S(2)}, u32[]{:S(2)}) collective-permute-start(bf16[256,512]{1,0:T(8,128)(2,1)S(1)} %get-tuple-element.45), channel_id=1, source_target_pairs={{0,4},{1,5},{2,6},{3,7},{4,0},{5,1},{6,2},{7,3},{8,12},{9,13},{10,... | collective-permute-start | bytes 786440 | tf_op jit(solution)/shard_map/ppermute | solution.py:51
  49.1 9.5 %collective-permute-start.13 = (bf16[256,512]{1,0:T(8,128)(2,1)S(1)}, bf16[256,512]{1,0:T(8,128)(2,1)S(1)}, u32[]{:S(2)}, u32[]{:S(2)}) collective-permute-start(bf16[256,512]{1,0:T(8,128)(2,1)S(1)} %add_convert_fusion.3), channel_id=1, source_target_pairs={{0,3},{1,0},{2,1},{3,2},{4,7},{5,4},{6,5},{7,6},{8,9},{9,10},{10,1... | collective-permute-start | bytes 786440 | tf_op jit(solution)/shard_map/ppermute | solution.py:51
  53.0 9.4 %collective-permute-start.9 = (bf16[256,512]{1,0:T(8,128)(2,1)S(1)}, bf16[256,512]{1,0:T(8,128)(2,1)S(1)}, u32[]{:S(2)}, u32[]{:S(2)}) collective-permute-start(bf16[256,512]{1,0:T(8,128)(2,1)S(1)} %add_convert_fusion.5), channel_id=1, source_target_pairs={{0,3},{1,0},{2,1},{3,2},{4,7},{5,4},{6,5},{7,6},{8,9},{9,10},{10,1... | collective-permute-start | bytes 786440 | tf_op jit(solution)/shard_map/ppermute | solution.py:51
  55.8 7.7 %collective-permute-start.11 = (bf16[256,512]{1,0:T(8,128)(2,1)S(1)}, bf16[256,512]{1,0:T(8,128)(2,1)S(1)}, u32[]{:S(2)}, u32[]{:S(2)}) collective-permute-start(bf16[256,512]{1,0:T(8,128)(2,1)S(1)} %add_convert_fusion.4), channel_id=1, source_target_pairs={{0,1},{1,2},{2,3},{3,0},{4,5},{5,6},{6,7},{7,4},{8,11},{9,8},{10,9... | collective-permute-start | bytes 786440 | tf_op jit(solution)/shard_map/ppermute | solution.py:51
  58.7 7.7 %collective-permute-start.14 = (bf16[256,512]{1,0:T(8,128)(2,1)S(1)}, bf16[256,512]{1,0:T(8,128)(2,1)S(1)}, u32[]{:S(2)}, u32[]{:S(2)}) collective-permute-start(bf16[256,512]{1,0:T(8,128)(2,1)S(1)} %add_convert_fusion.2), channel_id=1, source_target_pairs={{0,4},{1,5},{2,6},{3,7},{4,0},{5,1},{6,2},{7,3},{8,12},{9,13},{10,... | collective-permute-start | bytes 786440 | tf_op jit(solution)/shard_map/ppermute | solution.py:51
  66.5 8.0 %collective-permute-start.24 = (bf16[256,512]{1,0:T(8,128)(2,1)S(1)}, bf16[256,512]{1,0:T(8,128)(2,1)S(1)}, u32[]{:S(2)}, u32[]{:S(2)}) collective-permute-start(bf16[256,512]{1,0:T(8,128)(2,1)S(1)} %add_convert_fusion.1.rest_8_), channel_id=1, source_target_pairs={{0,4},{1,5},{2,6},{3,7},{4,0},{5,1},{6,2},{7,3},{8,12},{9,13},{10,... | collective-permute-start | bytes 786440 | tf_op jit(solution)/shard_map/ppermute | solution.py:51
  68.2 10.4 %collective-permute-start.23 = (bf16[256,512]{1,0:T(8,128)(2,1)S(1)}, bf16[256,512]{1,0:T(8,128)(2,1)S(1)}, u32[]{:S(2)}, u32[]{:S(2)}) collective-permute-start(bf16[256,512]{1,0:T(8,128)(2,1)S(1)} %add_convert_fusion.1.rest_8_), channel_id=1, source_target_pairs={{0,32},{1,33},{2,34},{3,35},{4,36},{5,37},{6,38},{7,39},{8,104},{9... | collective-permute-start | bytes 786440 | tf_op jit(solution)/shard_map/ppermute | solution.py:51
  68.3 10.3 %collective-permute-start.22 = (bf16[256,512]{1,0:T(8,128)(2,1)S(1)}, bf16[256,512]{1,0:T(8,128)(2,1)S(1)}, u32[]{:S(2)}, u32[]{:S(2)}) collective-permute-start(bf16[256,512]{1,0:T(8,128)(2,1)S(1)} %add_convert_fusion.1.rest_8_), channel_id=1, source_target_pairs={{0,96},{1,97},{2,98},{3,99},{4,100},{5,101},{6,102},{7,103},{8,40}... | collective-permute-start | bytes 786440 | tf_op jit(solution)/shard_map/ppermute | solution.py:51
  71.6 9.4 %collective-permute-start.18 = (bf16[512,256]{1,0:T(8,128)(2,1)S(1)}, bf16[512,256]{1,0:T(8,128)(2,1)S(1)}, u32[]{:S(2)}, u32[]{:S(2)}) collective-permute-start(bf16[512,256]{1,0:T(8,128)(2,1)S(1)} %pad_maximum_fusion.2.rest_0_), channel_id=1, source_target_pairs={{0,16},{1,17},{2,18},{3,19},{4,20},{5,21},{6,22},{7,23},{8,24},{9,... | collective-permute-start | bytes 786440 | tf_op jit(solution)/shard_map/ppermute | solution.py:51
  74.6 11.0 %collective-permute-start.17 = (bf16[512,256]{1,0:T(8,128)(2,1)S(1)}, bf16[512,256]{1,0:T(8,128)(2,1)S(1)}, u32[]{:S(2)}, u32[]{:S(2)}) collective-permute-start(bf16[512,256]{1,0:T(8,128)(2,1)S(1)} %pad_maximum_fusion.2.rest_0_), channel_id=1, source_target_pairs={{0,1},{1,2},{2,3},{3,0},{4,5},{5,6},{6,7},{7,4},{8,11},{9,8},{10,9... | collective-permute-start | bytes 786440 | tf_op jit(solution)/shard_map/ppermute | solution.py:51
  74.6 11.0 %collective-permute-start.16 = (bf16[512,256]{1,0:T(8,128)(2,1)S(1)}, bf16[512,256]{1,0:T(8,128)(2,1)S(1)}, u32[]{:S(2)}, u32[]{:S(2)}) collective-permute-start(bf16[512,256]{1,0:T(8,128)(2,1)S(1)} %pad_maximum_fusion.2.rest_0_), channel_id=1, source_target_pairs={{0,3},{1,0},{2,1},{3,2},{4,7},{5,4},{6,5},{7,6},{8,9},{9,10},{10,1... | collective-permute-start | bytes 786440 | tf_op jit(solution)/shard_map/ppermute | solution.py:51
  78.7 13.4 %collective-permute-start.26 = (bf16[512,512]{1,0:T(8,128)(2,1)S(1)}, bf16[512,512]{1,0:T(8,128)(2,1)S(1)}, u32[]{:S(2)}, u32[]{:S(2)}) collective-permute-start(bf16[512,512]{1,0:T(8,128)(2,1)S(1)} %pad_maximum_fusion.1), channel_id=1, source_target_pairs={{0,32},{1,33},{2,34},{3,35},{4,36},{5,37},{6,38},{7,39},{8,104},{9... | collective-permute-start | bytes 1572872 | tf_op jit(solution)/shard_map/ppermute | solution.py:51
  85.6 13.0 %collective-permute-start.20 = (bf16[1024,256]{1,0:T(8,128)(2,1)S(1)}, bf16[1024,256]{1,0:T(8,128)(2,1)S(1)}, u32[]{:S(2)}, u32[]{:S(2)}) collective-permute-start(bf16[1024,256]{1,0:T(8,128)(2,1)S(1)} %pad_maximum_fusion), channel_id=1, source_target_pairs={{0,1},{1,2},{2,3},{3,0},{4,5},{5,6},{6,7},{7,4},{8,11},{9,8},{10,9... | collective-permute-start | bytes 1572872 | tf_op jit(solution)/shard_map/ppermute | solution.py:51
  85.6 6.4 %collective-permute-start.25 = (bf16[256,512]{1,0:T(8,128)(2,1)S(1)}, bf16[256,512]{1,0:T(8,128)(2,1)S(1)}, u32[]{:S(2)}, u32[]{:S(2)}) collective-permute-start(bf16[256,512]{1,0:T(8,128)(2,1)S(1)} %collective-permute-done.24.rest_12_), channel_id=1, source_target_pairs={{0,96},{1,97},{2,98},{3,99},{4,100},{5,101},{6,102},{7,103},{8,40}... | collective-permute-start | bytes 786440 | tf_op jit(solution)/shard_map/ppermute | solution.py:51
  85.9 9.3 %collective-permute-start.19 = (bf16[512,256]{1,0:T(8,128)(2,1)S(1)}, bf16[512,256]{1,0:T(8,128)(2,1)S(1)}, u32[]{:S(2)}, u32[]{:S(2)}) collective-permute-start(bf16[512,256]{1,0:T(8,128)(2,1)S(1)} %collective-permute-done.18.rest_4_), channel_id=1, source_target_pairs={{0,3},{1,0},{2,1},{3,2},{4,7},{5,4},{6,5},{7,6},{8,9},{9,10},{10,1... | collective-permute-start | bytes 786440 | tf_op jit(solution)/shard_map/ppermute | solution.py:51
  92.1 7.7 %collective-permute-start.27 = (bf16[256,512]{1,0:T(8,128)(2,1)S(1)}, bf16[256,512]{1,0:T(8,128)(2,1)S(1)}, u32[]{:S(2)}, u32[]{:S(2)}) collective-permute-start(bf16[256,512]{1,0:T(8,128)(2,1)S(1)} %get-tuple-element.61.rest_13_), channel_id=1, source_target_pairs={{0,32},{1,33},{2,34},{3,35},{4,36},{5,37},{6,38},{7,39},{8,104},{9... | collective-permute-start | bytes 786440 | tf_op jit(solution)/shard_map/ppermute | solution.py:51
  98.6 7.7 %collective-permute-start.21 = (bf16[512,256]{1,0:T(8,128)(2,1)S(1)}, bf16[512,256]{1,0:T(8,128)(2,1)S(1)}, u32[]{:S(2)}, u32[]{:S(2)}) collective-permute-start(bf16[512,256]{1,0:T(8,128)(2,1)S(1)} %get-tuple-element.63.rest_5_), channel_id=1, source_target_pairs={{0,1},{1,2},{2,3},{3,0},{4,5},{5,6},{6,7},{7,4},{8,11},{9,8},{10,9... | collective-permute-start | bytes 786440 | tf_op jit(solution)/shard_map/ppermute | solution.py:51
  110.0 8.4 %collective-permute-start.32 = (bf16[256,512]{1,0:T(8,128)(2,1)S(1)}, bf16[256,512]{1,0:T(8,128)(2,1)S(1)}, u32[]{:S(2)}, u32[]{:S(2)}) collective-permute-start(bf16[256,512]{1,0:T(8,128)(2,1)S(1)} %add_convert_fusion.rest_0_), channel_id=1, source_target_pairs={{0,4},{1,5},{2,6},{3,7},{4,0},{5,1},{6,2},{7,3},{8,12},{9,13},{10,... | collective-permute-start | bytes 786440 | tf_op jit(solution)/shard_map/ppermute | solution.py:51
  110.2 8.4 %collective-permute-start.30 = (bf16[256,512]{1,0:T(8,128)(2,1)S(1)}, bf16[256,512]{1,0:T(8,128)(2,1)S(1)}, u32[]{:S(2)}, u32[]{:S(2)}) collective-permute-start(bf16[256,512]{1,0:T(8,128)(2,1)S(1)} %add_convert_fusion.rest_0_), channel_id=1, source_target_pairs={{0,3},{1,0},{2,1},{3,2},{4,7},{5,4},{6,5},{7,6},{8,9},{9,10},{10,1... | collective-permute-start | bytes 786440 | tf_op jit(solution)/shard_map/ppermute | solution.py:51
  110.2 10.0 %collective-permute-start.29 = (bf16[256,512]{1,0:T(8,128)(2,1)S(1)}, bf16[256,512]{1,0:T(8,128)(2,1)S(1)}, u32[]{:S(2)}, u32[]{:S(2)}) collective-permute-start(bf16[256,512]{1,0:T(8,128)(2,1)S(1)} %add_convert_fusion.rest_0_), channel_id=1, source_target_pairs={{0,1},{1,2},{2,3},{3,0},{4,5},{5,6},{6,7},{7,4},{8,11},{9,8},{10,9... | collective-permute-start | bytes 786440 | tf_op jit(solution)/shard_map/ppermute | solution.py:51
  118.4 7.6 %collective-permute-start.33 = (bf16[256,512]{1,0:T(8,128)(2,1)S(1)}, bf16[256,512]{1,0:T(8,128)(2,1)S(1)}, u32[]{:S(2)}, u32[]{:S(2)}) collective-permute-start(bf16[256,512]{1,0:T(8,128)(2,1)S(1)} %collective-permute-done.32.rest_4_), channel_id=1, source_target_pairs={{0,1},{1,2},{2,3},{3,0},{4,5},{5,6},{6,7},{7,4},{8,11},{9,8},{10,9... | collective-permute-start | bytes 786440 | tf_op jit(solution)/shard_map/ppermute | solution.py:51
  118.6 8.5 %collective-permute-start.34 = (bf16[256,512]{1,0:T(8,128)(2,1)S(1)}, bf16[256,512]{1,0:T(8,128)(2,1)S(1)}, u32[]{:S(2)}, u32[]{:S(2)}) collective-permute-start(bf16[256,512]{1,0:T(8,128)(2,1)S(1)} %collective-permute-done.30.rest_2_), channel_id=1, source_target_pairs={{0,4},{1,5},{2,6},{3,7},{4,0},{5,1},{6,2},{7,3},{8,12},{9,13},{10,... | collective-permute-start | bytes 786440 | tf_op jit(solution)/shard_map/ppermute | solution.py:51
  120.2 8.6 %collective-permute-start.31 = (bf16[256,512]{1,0:T(8,128)(2,1)S(1)}, bf16[256,512]{1,0:T(8,128)(2,1)S(1)}, u32[]{:S(2)}, u32[]{:S(2)}) collective-permute-start(bf16[256,512]{1,0:T(8,128)(2,1)S(1)} %collective-permute-done.29.rest_1_), channel_id=1, source_target_pairs={{0,1},{1,2},{2,3},{3,0},{4,5},{5,6},{6,7},{7,4},{8,11},{9,8},{10,9... | collective-permute-start | bytes 786440 | tf_op jit(solution)/shard_map/ppermute | solution.py:51
  126.0 7.6 %collective-permute-start.35 = (bf16[256,512]{1,0:T(8,128)(2,1)S(1)}, bf16[256,512]{1,0:T(8,128)(2,1)S(1)}, u32[]{:S(2)}, u32[]{:S(2)}) collective-permute-start(bf16[256,512]{1,0:T(8,128)(2,1)S(1)} %collective-permute-done.33.rest_5_), channel_id=1, source_target_pairs={{0,1},{1,2},{2,3},{3,0},{4,5},{5,6},{6,7},{7,4},{8,11},{9,8},{10,9... | collective-permute-start | bytes 786440 | tf_op jit(solution)/shard_map/ppermute | solution.py:51
  136.0 16.3 %collective-permute-start.36 = (bf16[256,1536]{1,0:T(8,128)(2,1)S(1)}, bf16[256,1536]{1,0:T(8,128)(2,1)S(1)}, u32[]{:S(2)}, u32[]{:S(2)}) collective-permute-start(bf16[256,1536]{1,0:T(8,128)(2,1)S(1)} %apply_other.1), channel_id=1, source_target_pairs={{0,16},{1,17},{2,18},{3,19},{4,20},{5,21},{6,22},{7,23},{8,24},{9,... | collective-permute-start | bytes 2359304 | tf_op jit(solution)/shard_map/ppermute | solution.py:51
  (7 other events, 39.5 us)

commit v5 on v2

v5 whole, which is shorter than its diff:
```python
import functools
import math

import jax
import jax.numpy as jnp
from jax import lax
from jax.experimental import pallas as pl
from jax.experimental.pallas import tpu as pltpu
from jax.sharding import PartitionSpec as P

linear_coef = 3.4445
cubic_coef = -4.775
quintic_coef = 2.0315

NX, NY, NC, NZ = 4, 2, 2, 4
BLOCK = 256
TILE = 2 * BLOCK
MIB = 1 << 20


def pairs(move):
    out = []
    for x in range(NX):
        for yh in range(NY):
            for core in range(NC):
                for yl in range(NY):
                    for z in range(NZ):
                        source = ((x * 2 + yh) * 2 + core) * 8 + yl * 4 + z
                        a, b, c, d, e = move(x, yh, core, yl, z)
                        a, e = a % NX, e % NZ
                        out.append((source, ((a * 2 + b) * 2 + c) * 8 + d * 4 + e))
    return out


def way(core):
    return 1 - 2 * core


def mask(position, core):
    return (0, 1 + 2 * core, 3 - 2 * core, 2)[position]


MOVES = {
    "core": lambda x, yh, c, yl, z: (x, yh, 1 - c, yl, z),
    "yh": lambda x, yh, c, yl, z: (x, 1 - yh, c, yl, z),
    "yl": lambda x, yh, c, yl, z: (x, yh, c, 1 - yl, z),
    "x_fore": lambda x, yh, c, yl, z: (x + way(c), yh, c, yl, z),
    "x_back": lambda x, yh, c, yl, z: (x - way(c), yh, c, yl, z),
    "x_first": lambda x, yh, c, yl, z: (x ^ mask(1, c), yh, c, yl, z),
    "x_second": lambda x, yh, c, yl, z: (x ^ mask(2, c), yh, c, yl, z),
    "z_first": lambda x, yh, c, yl, z: (x, yh, c, yl, z ^ mask(1, c)),
    "z_second": lambda x, yh, c, yl, z: (x, yh, c, yl, z ^ mask(2, c)),
}


def send(value, move):
    return lax.ppermute(value, ("row", "col"), pairs(MOVES[move]))


def place(delta, core):
    delta = lax.rem(delta + 8, 4)
    side = jnp.where(delta == 3 - 2 * core, 1, 2)
    return jnp.where(delta == 0, 0, jnp.where(delta == 2, 3, side))


def partner(difference, core):
    side = jnp.where(difference == 1 + 2 * core, 1, 2)
    return jnp.where(difference == 0, 0, jnp.where(difference == 2, 3, side))


def nt(left, right):
    return lax.dot_general(left, right, (((1,), (1,)), ((), ())), preferred_element_type=jnp.float32)


def nn(left, right):
    return lax.dot_general(left, right, (((1,), (0,)), ((), ())), preferred_element_type=jnp.float32)


def gram_near_kernel(own, other, across, across_other, fore, back, out):
    for r, rows in enumerate((own, other, across, across_other)):
        for q, cols in enumerate((own, fore, back)):
            part = nt(rows[...], cols[...])
            out[r // 2, q, (r % 2) * BLOCK : (r % 2 + 1) * BLOCK] = part.astype(out.dtype)


def gram_far_kernel(where, own, other, across, across_other, far, near, *rest):
    outs, tiles = rest[:6], rest[6]
    x, yh, core, yl, z = (where[i] for i in range(5))
    for r, rows in enumerate((own, other, across, across_other)):
        part = nt(rows[...], far[...])
        tiles[r // 2, (r % 2) * BLOCK : (r % 2 + 1) * BLOCK] = part.astype(tiles.dtype)
    for index in range(8):
        dy, position = index // 4, index % 4
        row = lax.rem(yl + dy + yh, 2)
        col = place((z ^ mask(position, core)) - x, core)
        out, start = outs[dy * 3 + min(position, 2)], TILE * (position == 3)

        @pl.when(col == 3)
        def _():
            out[start : start + TILE] = tiles[row]

        @pl.when(col != 3)
        def _():
            out[start : start + TILE] = near[row, jnp.minimum(col, 2)]


def piece(refs, index):
    dy, position = index // 4, index % 4
    ref = refs[dy * 3 + min(position, 2)]
    if position < 2:
        return ref[...]
    count = ref.shape[0] // 2
    return ref[(position - 2) * count : (position - 1) * count]


def square_kernel(where, *rest):
    left, right, (mine, theirs), (held,) = rest[:6], rest[6:12], rest[12:14], rest[14:]
    x, yh, core, yl, z = (where[i] for i in range(5))
    for index in range(8):
        held[index // 4, index % 4] = piece(right, index)
    total = jnp.zeros((TILE, TILE), jnp.float32)
    for index in range(8):
        row = lax.rem(yh + index // 4 + yl, 2)
        col = partner(z ^ mask(index % 4, core) ^ x, core)
        total += nn(piece(left, index), held[row, col])
    mine[...] = total[:BLOCK]
    theirs[:, :BLOCK] = total[BLOCK:, BLOCK:].astype(theirs.dtype)
    theirs[:, BLOCK:] = total[BLOCK:, :BLOCK].astype(theirs.dtype)


def apply_kernel(other_rows, where, *rest):
    mixing, blocks, (out, held) = rest[:6], rest[6:14], rest[14:]
    x, yh, core, yl, z = (where[i] for i in range(5))
    which = lax.rem(yh + yl + int(other_rows), 2)
    for dy in range(2):

        @pl.when(which == dy)
        def _():
            for position in range(4):
                col = place((z ^ mask(position, core)) - x, core)
                held[col] = piece(mixing, dy * 4 + position)

    for start in range(0, out.shape[1], TILE):
        columns = slice(start, start + TILE)
        total = jnp.zeros((BLOCK, TILE), jnp.float32)
        for position in range(4):
            for half in range(2):
                total += nn(
                    held[position, :, half * BLOCK : (half + 1) * BLOCK],
                    blocks[position * 2 + half][:, columns],
                )
        if not other_rows:
            total = total + linear_coef * blocks[0][:, columns].astype(jnp.float32)
        out[:, columns] = total.astype(out.dtype)


def params(mib):
    return pltpu.CompilerParams(vmem_limit_bytes=mib * MIB)


def smem():
    return pl.BlockSpec(memory_space=pltpu.SMEM)


def whole():
    return pl.BlockSpec(memory_space=pltpu.VMEM)


def cost(flops, moved):
    return pl.CostEstimate(flops=flops, bytes_accessed=moved, transcendentals=0)


def gram_near(own, other, across, across_other, fore, back):
    depth = own.shape[1]
    return pl.pallas_call(
        gram_near_kernel,
        in_specs=[whole() for _ in range(6)],
        out_specs=whole(),
        out_shape=jax.ShapeDtypeStruct((2, 3, TILE, BLOCK), jnp.bfloat16),
        compiler_params=params(24),
        cost_estimate=cost(2 * 6 * BLOCK * TILE * depth, 6 * BLOCK * depth * 2 + 6 * BLOCK * TILE * 2),
        name="gram_near",
    )(own, other, across, across_other, fore, back)


def gram_far(where, own, other, across, across_other, far, near):
    depth = own.shape[1]
    shapes = [(TILE * (2 if position == 2 else 1), BLOCK) for _ in range(2) for position in range(3)]
    return pl.pallas_call(
        gram_far_kernel,
        in_specs=[smem()] + [whole() for _ in range(6)],
        out_specs=[whole() for _ in range(6)],
        out_shape=[jax.ShapeDtypeStruct(shape, jnp.bfloat16) for shape in shapes],
        scratch_shapes=[pltpu.VMEM((2, TILE, BLOCK), jnp.bfloat16)],
        compiler_params=params(24),
        cost_estimate=cost(2 * 2 * BLOCK * TILE * depth, 5 * BLOCK * depth * 2 + 14 * BLOCK * TILE * 2),
        name="gram_far",
    )(where, own, other, across, across_other, far, near)


def square_part(where, left, right):
    return pl.pallas_call(
        square_kernel,
        in_specs=[smem()] + [whole() for _ in range(12)],
        out_specs=[whole(), whole()],
        out_shape=[
            jax.ShapeDtypeStruct((BLOCK, TILE), jnp.float32),
            jax.ShapeDtypeStruct((BLOCK, TILE), jnp.bfloat16),
        ],
        scratch_shapes=[pltpu.VMEM((2, 4, BLOCK, TILE), jnp.bfloat16)],
        compiler_params=params(24),
        cost_estimate=cost(2 * 8 * TILE * TILE * BLOCK, 16 * BLOCK * TILE * 2),
        name="square_part",
    )(where, *left, *right)


def apply_part(other_rows, where, mixing, blocks):
    depth = blocks[0].shape[1]
    return pl.pallas_call(
        functools.partial(apply_kernel, other_rows),
        in_specs=[smem()] + [whole() for _ in range(14)],
        out_specs=whole(),
        out_shape=jax.ShapeDtypeStruct((BLOCK, depth), jnp.bfloat16 if other_rows else jnp.float32),
        scratch_shapes=[pltpu.VMEM((4, BLOCK, TILE), jnp.bfloat16)],
        compiler_params=params(24),
        cost_estimate=cost(2 * 8 * BLOCK * BLOCK * depth, 9 * BLOCK * depth * 2 + 8 * BLOCK * TILE * 2),
        name="apply_other" if other_rows else "apply_own",
    )(where, *mixing, *blocks)


def add(left, right):
    return (left.astype(jnp.float32) + right.astype(jnp.float32)).astype(jnp.bfloat16)


def gather_rings(sides):
    out = []
    for value, ring, pair in sides:
        first, there = lax.optimization_barrier([send(value, ring + "_first"), send(value, pair)])
        second, there_first = lax.optimization_barrier(
            [
                send(jnp.concatenate([value, first], axis=0), ring + "_second"),
                send(there, ring + "_first"),
            ]
        )
        there_second = send(jnp.concatenate([there, there_first], axis=0), ring + "_second")
        out.append([value, first, second, there, there_first, there_second])
    return out


def gather_even(value, ring, pair):
    there, first = send(value, pair), send(value, ring + "_first")
    second = send(jnp.concatenate([value, first], axis=0), ring + "_second")
    there_first = send(first, pair)
    there_second = send(jnp.concatenate([there, there_first], axis=0), ring + "_second")
    return [value, first, second, there, there_first, there_second]


def sum_over_col(tiles):
    own, first, second, there, there_first, there_second = tiles
    count = own.shape[0]
    there_pair = send(there_second, "z_second")
    pair = send(second, "z_second")
    there_from = send(add(there_first, there_pair[count:]), "z_first")
    first_from = send(add(first, pair[count:]), "z_first")
    there_sum = there.astype(jnp.float32) + there_pair[:count].astype(jnp.float32)
    there_sum = (there_sum + there_from.astype(jnp.float32)).astype(jnp.bfloat16)
    total = own.astype(jnp.float32) + pair[:count].astype(jnp.float32)
    total = total + first_from.astype(jnp.float32)
    total = total + send(there_sum, "yl").astype(jnp.float32)
    return total.astype(jnp.bfloat16)


def on_device(iterate):
    total_cols = iterate.shape[1] * lax.axis_size("col")
    row, col = lax.axis_index("row"), lax.axis_index("col")
    where = jnp.stack([row >> 2, (row >> 1) & 1, row & 1, col >> 2, col & 3]).astype(jnp.int32)
    iterate, where = lax.optimization_barrier((iterate, where))

    other, across, back, fore = lax.optimization_barrier(
        [send(iterate, move) for move in ("core", "yh", "x_back", "x_fore")]
    )
    across_other = send(across, "core")
    far = send(fore, "x_fore")
    rows = (iterate, other, across, across_other)
    near = gram_near(*rows, fore, back)
    gram_left = sum_over_col(gram_far(where, *rows, far, near))

    gram = jnp.concatenate([gram_left[:BLOCK], send(gram_left[BLOCK:], "core")], axis=1)
    left, right = gather_rings([(gram_left, "z", "yh"), (gram, "x", "yl")])
    mine, theirs = square_part(where, left, right)
    square = mine + send(theirs, "core").astype(jnp.float32)
    mixing = (cubic_coef * gram.astype(jnp.float32) + quintic_coef * square).astype(jnp.bfloat16)

    pieces = gather_even(mixing, "z", "yl")
    fore_other, back_other, far_other = (send(v, "core") for v in (back, fore, far))
    blocks = [iterate, other, fore, fore_other, back, back_other, far, far_other]
    applied_other = apply_part(True, where, pieces, blocks)
    applied = apply_part(False, where, pieces, blocks)
    update = applied + send(applied_other, "yh").astype(jnp.float32)
    return (math.sqrt(total_cols) * update).astype(jnp.bfloat16)


def solution(mesh):
    return jax.shard_map(
        on_device,
        mesh=mesh,
        in_specs=(P("row", "col"),),
        out_specs=P("row", "col"),
        check_vma=False,
    )
```

time: 162 us -> 159 us (0.981); the launches traced: 160 us -> 159 us
  waiting for transfers between devices: 94.2 us -> 108 us
  starting transfers between devices: 46 us -> 36.7 us
  Pallas kernels: 15 us -> 11.2 us
  local copies, waits for them, and re-layouts: 3.32 us -> 1.24 us
    ppermute x37 -> x32, waiting for transfers between devices: 94.2 us -> 108 us  [send(): return lax.ppermute(value, ('row', 'col'), pairs(MOVES[move]))]
    ppermute x37 -> x32, starting transfers between devices: 46 us -> 36.7 us  [send(): return lax.ppermute(value, ('row', 'col'), pairs(MOVES[move]))]
    pallas_call x2, Pallas kernels: 7 us -> 4.84 us  [apply_part(): pl.pallas_call(functools.partial(apply_kernel, other_rows), in_specs=[sme...]
    unnamed x8 -> x4, local copies, waits for them, and re-layouts: 3.14 us -> 1.14 us
    pallas_call x1, Pallas kernels: 4.31 us -> 2.66 us  [gram_near(): pl.pallas_call(gram_near_kernel, in_specs=[whole() for _ in range(6)], ou...]
  transfers between devices with their start and end apart: 37 -> 32, of which waited for: 30 -> 22; matrix products, arithmetic and copies ran while one was open for 0% -> 0% of each run, Pallas kernels for 5% -> 3%
where the time goes in v5:
time: 159 us
  waiting for transfers between devices  108 us (68%)
  starting transfers between devices  36.7 us (23%)
  Pallas kernels  11.2 us (7%)
  other arithmetic  1.83 us (1%)
    ppermute x32, waiting for transfers between devices, send(): return lax.ppermute(value, ('row', 'col'), pairs(MOVES[move]))  108 us
    ppermute x32, starting transfers between devices, send(): return lax.ppermute(value, ('row', 'col'), pairs(MOVES[move]))  36.7 us
    pallas_call x2, Pallas kernels, apply_part(): pl.pallas_call(functools.partial(apply_kernel, other_rows), in_specs=[sme...  4.84 us
  transfers between devices with their start and end apart: 32, of which 22 were waited for; matrix products, arithmetic and copies ran while one was open for 0% of the time, Pallas kernels for 3%

profile of v5, /device:TPU:0, one launch (start us, length us, event | category | flops | bytes accessed | tf_op | source)
XLA Modules:
  0.0 159.1 jit_solution(10588631258417651111)
XLA Ops:
  0.1 3.4 %collective-permute-start.1 = (bf16[256,1536]{1,0:T(8,128)(2,1)}, bf16[256,1536]{1,0:T(8,128)(2,1)S(1)}, u32[]{:S(2)}, u32[]{:S(2)}) collective-permute-start(bf16[256,1536]{1,0:T(8,128)(2,1)} %rest_6_.1), channel_id=1, source_target_pairs={{0,16},{1,17},{2,18},{3,19},{4,20},{5,21},{6,22},{7,23},{8,24},{9,... | collective-permute-start | bytes 2359304 | tf_op jit(solution)/shard_map/ppermute | solution.py:57
  3.5 2.8 %collective-permute-start.2 = (bf16[256,1536]{1,0:T(8,128)(2,1)}, bf16[256,1536]{1,0:T(8,128)(2,1)S(1)}, u32[]{:S(2)}, u32[]{:S(2)}) collective-permute-start(bf16[256,1536]{1,0:T(8,128)(2,1)} %rest_6_.1), channel_id=1, source_target_pairs={{0,96},{1,97},{2,98},{3,99},{4,100},{5,101},{6,102},{7,103},{8,40}... | collective-permute-start | bytes 2359304 | tf_op jit(solution)/shard_map/ppermute | solution.py:57
  6.2 15.6 %collective-permute-done.1.across = bf16[256,1536]{1,0:T(8,128)(2,1)S(1)} collective-permute-done((bf16[256,1536]{1,0:T(8,128)(2,1)}, bf16[256,1536]{1,0:T(8,128)(2,1)S(1)}, u32[]{:S(2)}, u32[]{:S(2)}) %collective-permute-start.1) | collective-permute-done | bytes 786464 | tf_op jit(solution)/shard_map/ppermute | solution.py:57
  21.8 2.1 %collective-permute-done.2.back.rest_10_ = bf16[256,1536]{1,0:T(8,128)(2,1)S(1)} collective-permute-done((bf16[256,1536]{1,0:T(8,128)(2,1)}, bf16[256,1536]{1,0:T(8,128)(2,1)S(1)}, u32[]{:S(2)}, u32[]{:S(2)}) %collective-permute-start.2) | collective-permute-done | bytes 786464 | tf_op jit(solution)/shard_map/ppermute | solution.py:57
  27.9 2.7 %gram_near.1.near = bf16[2,3,512,256]{3,2,1,0:T(8,128)(2,1)S(1)} custom-call(bf16[256,1536]{1,0:T(8,128)(2,1)S(1)} %copy-done, bf16[256,1536]{1,0:T(8,128)(2,1)S(1)} %collective-permute-done.other.rest_7_, bf16[256,1536]{1,0:T(8,128)(2,1)S(1)} %collective-permute-done.1.across, bf16[256,1536]{1,0:T(8,128)(2,1)S(1)} %collective-permute-done.4.across_other, ...), custom_call_target="tpu_custom_call" | custom-call | flops 2415919104 | bytes 6291456 | tf_op jit(solution)/shard_map/gram_near/pallas_call | solution.py:175
  30.6 7.1 %collective-permute-done.5.far.rest_12_ = bf16[256,1536]{1,0:T(8,128)(2,1)S(1)} collective-permute-done((bf16[256,1536]{1,0:T(8,128)(2,1)S(1)}, bf16[256,1536]{1,0:T(8,128)(2,1)S(1)}, u32[]{:S(2)}, u32[]{:S(2)}) %collective-permute-start.5) | collective-permute-done | bytes 786464 | tf_op jit(solution)/shard_map/ppermute | solution.py:57
  37.7 1.8 %gram_far.1 = (bf16[512,256]{1,0:T(8,128)(2,1)S(1)}, bf16[512,256]{1,0:T(8,128)(2,1)S(1)}, bf16[1024,256]{1,0:T(8,128)(2,1)S(1)}, bf16[512,256]{1,0:T(8,128)(2,1...) custom-call(s32[5]{0:T(128)S(1)} %stack.23.where, bf16[256,1536]{1,0:T(8,128)(2,1)S(1)} %copy-done, ...), custom_call_target="tpu_custom_call" | custom-call | flops 805306368 | bytes 7602176 | tf_op jit(solution)/shard_map/gram_far/pallas_call | solution.py:189
  39.5 4.1 %collective-permute-start.8 = (bf16[1024,256]{1,0:T(8,128)(2,1)S(1)}, bf16[1024,256]{1,0:T(8,128)(2,1)S(1)}, u32[]{:S(2)}, u32[]{:S(2)}) collective-permute-start(bf16[1024,256]{1,0:T(8,128)(2,1)S(1)} %get-tuple-element.37), channel_id=1, source_target_pairs={{0,3},{1,2},{2,1},{3,0},{4,7},{5,6},{6,5},{7,4},{8,9},{9,8},{10,11... | collective-permute-start | bytes 1572872 | tf_op jit(solution)/shard_map/ppermute | solution.py:57
  43.7 7.1 %collective-permute-done.8 = bf16[1024,256]{1,0:T(8,128)(2,1)S(1)} collective-permute-done((bf16[1024,256]{1,0:T(8,128)(2,1)S(1)}, bf16[1024,256]{1,0:T(8,128)(2,1)S(1)}, u32[]{:S(2)}, u32[]{:S(2)}) %collective-permute-start.8) | collective-permute-done | bytes 524320 | tf_op jit(solution)/shard_map/ppermute | solution.py:57
  50.9 9.9 %collective-permute-done.6 = bf16[1024,256]{1,0:T(8,128)(2,1)S(1)} collective-permute-done((bf16[1024,256]{1,0:T(8,128)(2,1)S(1)}, bf16[1024,256]{1,0:T(8,128)(2,1)S(1)}, u32[]{:S(2)}, u32[]{:S(2)}) %collective-permute-start.6) | collective-permute-done | bytes 524320 | tf_op jit(solution)/shard_map/ppermute | solution.py:57
  61.9 5.5 %collective-permute-done.7 = bf16[512,256]{1,0:T(8,128)(2,1)S(1)} collective-permute-done((bf16[512,256]{1,0:T(8,128)(2,1)S(1)}, bf16[512,256]{1,0:T(8,128)(2,1)S(1)}, u32[]{:S(2)}, u32[]{:S(2)}) %collective-permute-start.7) | collective-permute-done | bytes 262176 | tf_op jit(solution)/shard_map/ppermute | solution.py:57
  67.8 2.1 %collective-permute-start.12 = (bf16[512,256]{1,0:T(8,128)(2,1)S(1)}, bf16[512,256]{1,0:T(8,128)(2,1)S(1)}, u32[]{:S(2)}, u32[]{:S(2)}) collective-permute-start(bf16[512,256]{1,0:T(8,128)(2,1)S(1)} %add_convert_fusion.1.rest_0_), channel_id=1, source_target_pairs={{0,1},{1,0},{2,3},{3,2},{4,5},{5,4},{6,7},{7,6},{8,11},{9,10},{10,... | collective-permute-start | bytes 786440 | tf_op jit(solution)/shard_map/ppermute | solution.py:57
  72.0 2.3 %collective-permute-done.12.rest_1_ = bf16[512,256]{1,0:T(8,128)(2,1)S(1)} collective-permute-done((bf16[512,256]{1,0:T(8,128)(2,1)S(1)}, bf16[512,256]{1,0:T(8,128)(2,1)S(1)}, u32[]{:S(2)}, u32[]{:S(2)}) %collective-permute-start.12) | collective-permute-done | bytes 262176 | tf_op jit(solution)/shard_map/ppermute | solution.py:57
  74.3 5.7 %collective-permute-done.13.rest_3_ = bf16[512,256]{1,0:T(8,128)(2,1)S(1)} collective-permute-done((bf16[512,256]{1,0:T(8,128)(2,1)S(1)}, bf16[512,256]{1,0:T(8,128)(2,1)S(1)}, u32[]{:S(2)}, u32[]{:S(2)}) %collective-permute-start.13) | collective-permute-done | bytes 262176 | tf_op jit(solution)/shard_map/ppermute | solution.py:57
  80.0 4.3 %collective-permute-start.14 = (bf16[1024,256]{1,0:T(8,128)(2,1)S(1)}, bf16[1024,256]{1,0:T(8,128)(2,1)S(1)}, u32[]{:S(2)}, u32[]{:S(2)}) collective-permute-start(bf16[1024,256]{1,0:T(8,128)(2,1)S(1)} %pad_maximum_fusion), channel_id=1, source_target_pairs={{0,3},{1,2},{2,1},{3,0},{4,7},{5,6},{6,5},{7,4},{8,9},{9,8},{10,11... | collective-permute-start | bytes 1572872 | tf_op jit(solution)/shard_map/ppermute | solution.py:57
  84.4 2.1 %collective-permute-start.15 = (bf16[512,256]{1,0:T(8,128)(2,1)S(1)}, bf16[512,256]{1,0:T(8,128)(2,1)S(1)}, u32[]{:S(2)}, u32[]{:S(2)}) collective-permute-start(bf16[512,256]{1,0:T(8,128)(2,1)S(1)} %collective-permute-done.13.rest_3_), channel_id=1, source_target_pairs={{0,1},{1,0},{2,3},{3,2},{4,5},{5,4},{6,7},{7,6},{8,11},{9,10},{10,... | collective-permute-start | bytes 786440 | tf_op jit(solution)/shard_map/ppermute | solution.py:57
  86.5 5.6 %collective-permute-done.15.rest_4_ = bf16[512,256]{1,0:T(8,128)(2,1)S(1)} collective-permute-done((bf16[512,256]{1,0:T(8,128)(2,1)S(1)}, bf16[512,256]{1,0:T(8,128)(2,1)S(1)}, u32[]{:S(2)}, u32[]{:S(2)}) %collective-permute-start.15) | collective-permute-done | bytes 262176 | tf_op jit(solution)/shard_map/ppermute | solution.py:57
  92.2 2.1 %collective-permute-done.14.rest_2_ = bf16[1024,256]{1,0:T(8,128)(2,1)S(1)} collective-permute-done((bf16[1024,256]{1,0:T(8,128)(2,1)S(1)}, bf16[1024,256]{1,0:T(8,128)(2,1)S(1)}, u32[]{:S(2)}, u32[]{:S(2)}) %collective-permute-start.14) | collective-permute-done | bytes 524320 | tf_op jit(solution)/shard_map/ppermute | solution.py:57
  94.3 3.0 %collective-permute-start.16 = (bf16[1024,256]{1,0:T(8,128)(2,1)S(1)}, bf16[1024,256]{1,0:T(8,128)(2,1)S(1)}, u32[]{:S(2)}, u32[]{:S(2)}) collective-permute-start(bf16[1024,256]{1,0:T(8,128)(2,1)S(1)} %pad_maximum_fusion.1), channel_id=1, source_target_pairs={{0,3},{1,2},{2,1},{3,0},{4,7},{5,6},{6,5},{7,4},{8,9},{9,8},{10,11... | collective-permute-start | bytes 1572872 | tf_op jit(solution)/shard_map/ppermute | solution.py:57
  97.7 7.0 %collective-permute-done.16.rest_5_ = bf16[1024,256]{1,0:T(8,128)(2,1)S(1)} collective-permute-done((bf16[1024,256]{1,0:T(8,128)(2,1)S(1)}, bf16[1024,256]{1,0:T(8,128)(2,1)S(1)}, u32[]{:S(2)}, u32[]{:S(2)}) %collective-permute-start.16) | collective-permute-done | bytes 524320 | tf_op jit(solution)/shard_map/ppermute | solution.py:57
  104.8 3.0 %collective-permute-done.21.rest_11_ = bf16[512,512]{1,0:T(8,128)(2,1)S(1)} collective-permute-done((bf16[512,512]{1,0:T(8,128)(2,1)S(1)}, bf16[512,512]{1,0:T(8,128)(2,1)S(1)}, u32[]{:S(2)}, u32[]{:S(2)}) %collective-permute-start.21) | collective-permute-done | bytes 524320 | tf_op jit(solution)/shard_map/ppermute | solution.py:57
  107.8 1.9 %square_part.1 = (f32[256,512]{1,0:T(8,128)S(1)}, bf16[256,512]{1,0:T(8,128)(2,1)S(1)}) custom-call(s32[5]{0:T(128)S(1)} %stack.23.where, bf16[512,256]{1,0:T(8,128)(2,1)S(1)} %add_convert_fusion.1.rest_0_, bf16[512,256]{1,0:T(8,128)(2,1)S(1)} %collective-permute-done.12.rest_1_, bf16[1024,256]{1,0:T(8,128)(2,1)S(1)} %collective-permute-done.14.rest_2_, ...), custom_call_target="tpu_custom_call" | custom-call | flops 1073741824 | bytes 4194304 | tf_op jit(solution)/shard_map/square_part/pallas_call | solution.py:202
  112.6 5.3 %collective-permute-done.23.rest_1_ = bf16[256,512]{1,0:T(8,128)(2,1)S(1)} collective-permute-done((bf16[256,512]{1,0:T(8,128)(2,1)S(1)}, bf16[256,512]{1,0:T(8,128)(2,1)S(1)}, u32[]{:S(2)}, u32[]{:S(2)}) %collective-permute-start.23) | collective-permute-done | bytes 262176 | tf_op jit(solution)/shard_map/ppermute | solution.py:57
  120.5 2.6 %collective-permute-start.24 = (bf16[512,512]{1,0:T(8,128)(2,1)S(1)}, bf16[512,512]{1,0:T(8,128)(2,1)S(1)}, u32[]{:S(2)}, u32[]{:S(2)}) collective-permute-start(bf16[512,512]{1,0:T(8,128)(2,1)S(1)} %pad_maximum_fusion.4), channel_id=1, source_target_pairs={{0,3},{1,2},{2,1},{3,0},{4,7},{5,6},{6,5},{7,4},{8,9},{9,8},{10,11... | collective-permute-start | bytes 1572872 | tf_op jit(solution)/shard_map/ppermute | solution.py:57
  123.0 3.4 %collective-permute-done.26.rest_4_ = bf16[256,512]{1,0:T(8,128)(2,1)S(1)} collective-permute-done((bf16[256,512]{1,0:T(8,128)(2,1)S(1)}, bf16[256,512]{1,0:T(8,128)(2,1)S(1)}, u32[]{:S(2)}, u32[]{:S(2)}) %collective-permute-start.26) | collective-permute-done | bytes 262176 | tf_op jit(solution)/shard_map/ppermute | solution.py:57
  126.5 2.1 %collective-permute-start.27 = (bf16[512,512]{1,0:T(8,128)(2,1)S(1)}, bf16[512,512]{1,0:T(8,128)(2,1)S(1)}, u32[]{:S(2)}, u32[]{:S(2)}) collective-permute-start(bf16[512,512]{1,0:T(8,128)(2,1)S(1)} %pad_maximum_fusion.5), channel_id=1, source_target_pairs={{0,3},{1,2},{2,1},{3,0},{4,7},{5,6},{6,5},{7,4},{8,9},{9,8},{10,11... | collective-permute-start | bytes 1572872 | tf_op jit(solution)/shard_map/ppermute | solution.py:57
  128.6 2.3 %collective-permute-done.24.rest_2_ = bf16[512,512]{1,0:T(8,128)(2,1)S(1)} collective-permute-done((bf16[512,512]{1,0:T(8,128)(2,1)S(1)}, bf16[512,512]{1,0:T(8,128)(2,1)S(1)}, u32[]{:S(2)}, u32[]{:S(2)}) %collective-permute-start.24) | collective-permute-done | bytes 524320 | tf_op jit(solution)/shard_map/ppermute | solution.py:57
  130.9 6.0 %collective-permute-done.27.rest_5_ = bf16[512,512]{1,0:T(8,128)(2,1)S(1)} collective-permute-done((bf16[512,512]{1,0:T(8,128)(2,1)S(1)}, bf16[512,512]{1,0:T(8,128)(2,1)S(1)}, u32[]{:S(2)}, u32[]{:S(2)}) %collective-permute-start.27) | collective-permute-done | bytes 524320 | tf_op jit(solution)/shard_map/ppermute | solution.py:57
  136.9 2.4 %apply_other.1 = bf16[256,1536]{1,0:T(8,128)(2,1)S(1)} custom-call(s32[5]{0:T(128)S(1)} %stack.23.where, bf16[256,512]{1,0:T(8,128)(2,1)S(1)} %add_convert_fusion.rest_0_, bf16[256,512]{1,0:T(8,128)(2,1)S(1)} %collective-permute-done.23.rest_1_, bf16[512,512]{1,0:T(8,128)(2,1)S(1)} %collective-permute-done.24.rest_2_, ...), custom_call_target="tpu_custom_call" | custom-call | flops 1610612736 | bytes 9175040 | tf_op jit(solution)/shard_map/apply_other/pallas_call | solution.py:219
  139.4 3.0 %collective-permute-start.31 = (bf16[256,1536]{1,0:T(8,128)(2,1)S(1)}, bf16[256,1536]{1,0:T(8,128)(2,1)S(1)}, u32[]{:S(2)}, u32[]{:S(2)}) collective-permute-start(bf16[256,1536]{1,0:T(8,128)(2,1)S(1)} %apply_other.1), channel_id=1, source_target_pairs={{0,16},{1,17},{2,18},{3,19},{4,20},{5,21},{6,22},{7,23},{8,24},{9,... | collective-permute-start | bytes 2359304 | tf_op jit(solution)/shard_map/ppermute | solution.py:57
  142.3 2.4 %apply_own.1 = f32[256,1536]{1,0:T(8,128)S(1)} custom-call(s32[5]{0:T(128)S(1)} %stack.23.where, bf16[256,512]{1,0:T(8,128)(2,1)S(1)} %add_convert_fusion.rest_0_, bf16[256,512]{1,0:T(8,128)(2,1)S(1)} %collective-permute-done.23.rest_1_, bf16[512,512]{1,0:T(8,128)(2,1)S(1)} %collective-permute-done.24.rest_2_, ...), custom_call_target="tpu_custom_call" | custom-call | flops 1610612736 | bytes 9175040 | tf_op jit(solution)/shard_map/apply_own/pallas_call | solution.py:219
  144.7 13.3 %collective-permute-done.31 = bf16[256,1536]{1,0:T(8,128)(2,1)S(1)} collective-permute-done((bf16[256,1536]{1,0:T(8,128)(2,1)S(1)}, bf16[256,1536]{1,0:T(8,128)(2,1)S(1)}, u32[]{:S(2)}, u32[]{:S(2)}) %collective-permute-start.31) | collective-permute-done | bytes 786464 | tf_op jit(solution)/shard_map/ppermute | solution.py:57
  (56 shorter events, 15.3 us)
Async XLA Ops:
  0.1 6.1 %collective-permute-start = (bf16[256,1536]{1,0:T(8,128)(2,1)}, bf16[256,1536]{1,0:T(8,128)(2,1)S(1)}, u32[]{:S(2)}, u32[]{:S(2)}) collective-permute-start(bf16[256,1536]{1,0:T(8,128)(2,1)} %rest_6_.1), channel_id=1, source_target_pairs={{0,8},{1,9},{2,10},{3,11},{4,12},{5,13},{6,14},{7,15},{8,0},{9,1},... | collective-permute-start | bytes 2359304 | tf_op jit(solution)/shard_map/ppermute | solution.py:57
  0.1 21.7 %collective-permute-start.1 = (bf16[256,1536]{1,0:T(8,128)(2,1)}, bf16[256,1536]{1,0:T(8,128)(2,1)S(1)}, u32[]{:S(2)}, u32[]{:S(2)}) collective-permute-start(bf16[256,1536]{1,0:T(8,128)(2,1)} %rest_6_.1), channel_id=1, source_target_pairs={{0,16},{1,17},{2,18},{3,19},{4,20},{5,21},{6,22},{7,23},{8,24},{9,... | collective-permute-start | bytes 2359304 | tf_op jit(solution)/shard_map/ppermute | solution.py:57
  3.5 20.4 %collective-permute-start.2 = (bf16[256,1536]{1,0:T(8,128)(2,1)}, bf16[256,1536]{1,0:T(8,128)(2,1)S(1)}, u32[]{:S(2)}, u32[]{:S(2)}) collective-permute-start(bf16[256,1536]{1,0:T(8,128)(2,1)} %rest_6_.1), channel_id=1, source_target_pairs={{0,96},{1,97},{2,98},{3,99},{4,100},{5,101},{6,102},{7,103},{8,40}... | collective-permute-start | bytes 2359304 | tf_op jit(solution)/shard_map/ppermute | solution.py:57
  6.2 18.3 %collective-permute-start.3 = (bf16[256,1536]{1,0:T(8,128)(2,1)}, bf16[256,1536]{1,0:T(8,128)(2,1)S(1)}, u32[]{:S(2)}, u32[]{:S(2)}) collective-permute-start(bf16[256,1536]{1,0:T(8,128)(2,1)} %rest_6_.1), channel_id=1, source_target_pairs={{0,32},{1,33},{2,34},{3,35},{4,36},{5,37},{6,38},{7,39},{8,104},{9... | collective-permute-start | bytes 2359304 | tf_op jit(solution)/shard_map/ppermute | solution.py:57
  24.5 2.3 %collective-permute-start.4 = (bf16[256,1536]{1,0:T(8,128)(2,1)S(1)}, bf16[256,1536]{1,0:T(8,128)(2,1)S(1)}, u32[]{:S(2)}, u32[]{:S(2)}) collective-permute-start(bf16[256,1536]{1,0:T(8,128)(2,1)S(1)} %collective-permute-done.1.across), channel_id=1, source_target_pairs={{0,8},{1,9},{2,10},{3,11},{4,12},{5,13},{6,14},{7,15},{8,0},{9,1},... | collective-permute-start | bytes 2359304 | tf_op jit(solution)/shard_map/ppermute | solution.py:57
  24.5 13.2 %collective-permute-start.5 = (bf16[256,1536]{1,0:T(8,128)(2,1)S(1)}, bf16[256,1536]{1,0:T(8,128)(2,1)S(1)}, u32[]{:S(2)}, u32[]{:S(2)}) collective-permute-start(bf16[256,1536]{1,0:T(8,128)(2,1)S(1)} %collective-permute-done.3.fore.rest_8_), channel_id=1, source_target_pairs={{0,32},{1,33},{2,34},{3,35},{4,36},{5,37},{6,38},{7,39},{8,104},{9... | collective-permute-start | bytes 2359304 | tf_op jit(solution)/shard_map/ppermute | solution.py:57
  39.5 11.3 %collective-permute-start.8 = (bf16[1024,256]{1,0:T(8,128)(2,1)S(1)}, bf16[1024,256]{1,0:T(8,128)(2,1)S(1)}, u32[]{:S(2)}, u32[]{:S(2)}) collective-permute-start(bf16[1024,256]{1,0:T(8,128)(2,1)S(1)} %get-tuple-element.37), channel_id=1, source_target_pairs={{0,3},{1,2},{2,1},{3,0},{4,7},{5,6},{6,5},{7,4},{8,9},{9,8},{10,11... | collective-permute-start | bytes 1572872 | tf_op jit(solution)/shard_map/ppermute | solution.py:57
  43.6 17.2 %collective-permute-start.6 = (bf16[1024,256]{1,0:T(8,128)(2,1)S(1)}, bf16[1024,256]{1,0:T(8,128)(2,1)S(1)}, u32[]{:S(2)}, u32[]{:S(2)}) collective-permute-start(bf16[1024,256]{1,0:T(8,128)(2,1)S(1)} %get-tuple-element.34), channel_id=1, source_target_pairs={{0,3},{1,2},{2,1},{3,0},{4,7},{5,6},{6,5},{7,4},{8,9},{9,8},{10,11... | collective-permute-start | bytes 1572872 | tf_op jit(solution)/shard_map/ppermute | solution.py:57
  50.8 10.2 %collective-permute-start.9 = (bf16[512,256]{1,0:T(8,128)(2,1)S(1)}, bf16[512,256]{1,0:T(8,128)(2,1)S(1)}, u32[]{:S(2)}, u32[]{:S(2)}) collective-permute-start(bf16[512,256]{1,0:T(8,128)(2,1)S(1)} %add_convert_fusion.3), channel_id=1, source_target_pairs={{0,1},{1,0},{2,3},{3,2},{4,5},{5,4},{6,7},{7,6},{8,11},{9,10},{10,... | collective-permute-start | bytes 786440 | tf_op jit(solution)/shard_map/ppermute | solution.py:57
  60.9 6.5 %collective-permute-start.7 = (bf16[512,256]{1,0:T(8,128)(2,1)S(1)}, bf16[512,256]{1,0:T(8,128)(2,1)S(1)}, u32[]{:S(2)}, u32[]{:S(2)}) collective-permute-start(bf16[512,256]{1,0:T(8,128)(2,1)S(1)} %add_convert_fusion.4), channel_id=1, source_target_pairs={{0,1},{1,0},{2,3},{3,2},{4,5},{5,4},{6,7},{7,6},{8,11},{9,10},{10,... | collective-permute-start | bytes 786440 | tf_op jit(solution)/shard_map/ppermute | solution.py:57
  61.1 6.5 %collective-permute-start.10 = (bf16[512,256]{1,0:T(8,128)(2,1)S(1)}, bf16[512,256]{1,0:T(8,128)(2,1)S(1)}, u32[]{:S(2)}, u32[]{:S(2)}) collective-permute-start(bf16[512,256]{1,0:T(8,128)(2,1)S(1)} %add_convert_fusion.2), channel_id=1, source_target_pairs={{0,4},{1,5},{2,6},{3,7},{4,0},{5,1},{6,2},{7,3},{8,12},{9,13},{10,... | collective-permute-start | bytes 786440 | tf_op jit(solution)/shard_map/ppermute | solution.py:57
  67.7 3.1 %collective-permute-start.11 = (bf16[256,256]{1,0:T(8,128)(2,1)S(1)}, bf16[256,256]{1,0:T(8,128)(2,1)S(1)}, u32[]{:S(2)}, u32[]{:S(2)}) collective-permute-start(bf16[256,256]{1,0:T(8,128)(2,1)S(1)} %get-tuple-element.50), channel_id=1, source_target_pairs={{0,8},{1,9},{2,10},{3,11},{4,12},{5,13},{6,14},{7,15},{8,0},{9,1},... | collective-permute-start | bytes 393224 | tf_op jit(solution)/shard_map/ppermute | solution.py:57
  67.8 6.5 %collective-permute-start.12 = (bf16[512,256]{1,0:T(8,128)(2,1)S(1)}, bf16[512,256]{1,0:T(8,128)(2,1)S(1)}, u32[]{:S(2)}, u32[]{:S(2)}) collective-permute-start(bf16[512,256]{1,0:T(8,128)(2,1)S(1)} %add_convert_fusion.1.rest_0_), channel_id=1, source_target_pairs={{0,1},{1,0},{2,3},{3,2},{4,5},{5,4},{6,7},{7,6},{8,11},{9,10},{10,... | collective-permute-start | bytes 786440 | tf_op jit(solution)/shard_map/ppermute | solution.py:57
  69.9 10.1 %collective-permute-start.13 = (bf16[512,256]{1,0:T(8,128)(2,1)S(1)}, bf16[512,256]{1,0:T(8,128)(2,1)S(1)}, u32[]{:S(2)}, u32[]{:S(2)}) collective-permute-start(bf16[512,256]{1,0:T(8,128)(2,1)S(1)} %add_convert_fusion.1.rest_0_), channel_id=1, source_target_pairs={{0,16},{1,17},{2,18},{3,19},{4,20},{5,21},{6,22},{7,23},{8,24},{9,... | collective-permute-start | bytes 786440 | tf_op jit(solution)/shard_map/ppermute | solution.py:57
  70.9 13.4 %collective-permute-start.17 = (bf16[256,512]{1,0:T(8,128)(2,1)S(1)}, bf16[256,512]{1,0:T(8,128)(2,1)S(1)}, u32[]{:S(2)}, u32[]{:S(2)}) collective-permute-start(bf16[256,512]{1,0:T(8,128)(2,1)S(1)} %pad_maximum_fusion.6.rest_6_), channel_id=1, source_target_pairs={{0,32},{1,33},{2,34},{3,35},{4,36},{5,37},{6,38},{7,39},{8,104},{9... | collective-permute-start | bytes 786440 | tf_op jit(solution)/shard_map/ppermute | solution.py:57
  71.0 13.3 %collective-permute-start.18 = (bf16[256,512]{1,0:T(8,128)(2,1)S(1)}, bf16[256,512]{1,0:T(8,128)(2,1)S(1)}, u32[]{:S(2)}, u32[]{:S(2)}) collective-permute-start(bf16[256,512]{1,0:T(8,128)(2,1)S(1)} %pad_maximum_fusion.6.rest_6_), channel_id=1, source_target_pairs={{0,4},{1,5},{2,6},{3,7},{4,0},{5,1},{6,2},{7,3},{8,12},{9,13},{10,... | collective-permute-start | bytes 786440 | tf_op jit(solution)/shard_map/ppermute | solution.py:57
  80.0 14.2 %collective-permute-start.14 = (bf16[1024,256]{1,0:T(8,128)(2,1)S(1)}, bf16[1024,256]{1,0:T(8,128)(2,1)S(1)}, u32[]{:S(2)}, u32[]{:S(2)}) collective-permute-start(bf16[1024,256]{1,0:T(8,128)(2,1)S(1)} %pad_maximum_fusion), channel_id=1, source_target_pairs={{0,3},{1,2},{2,1},{3,0},{4,7},{5,6},{6,5},{7,4},{8,9},{9,8},{10,11... | collective-permute-start | bytes 1572872 | tf_op jit(solution)/shard_map/ppermute | solution.py:57
  84.3 12.9 %collective-permute-start.19 = (bf16[512,512]{1,0:T(8,128)(2,1)S(1)}, bf16[512,512]{1,0:T(8,128)(2,1)S(1)}, u32[]{:S(2)}, u32[]{:S(2)}) collective-permute-start(bf16[512,512]{1,0:T(8,128)(2,1)S(1)} %pad_maximum_fusion.2), channel_id=1, source_target_pairs={{0,96},{1,97},{2,98},{3,99},{4,100},{5,101},{6,102},{7,103},{8,40}... | collective-permute-start | bytes 1572872 | tf_op jit(solution)/shard_map/ppermute | solution.py:57
  84.4 7.7 %collective-permute-start.15 = (bf16[512,256]{1,0:T(8,128)(2,1)S(1)}, bf16[512,256]{1,0:T(8,128)(2,1)S(1)}, u32[]{:S(2)}, u32[]{:S(2)}) collective-permute-start(bf16[512,256]{1,0:T(8,128)(2,1)S(1)} %collective-permute-done.13.rest_3_), channel_id=1, source_target_pairs={{0,1},{1,0},{2,3},{3,2},{4,5},{5,4},{6,7},{7,6},{8,11},{9,10},{10,... | collective-permute-start | bytes 786440 | tf_op jit(solution)/shard_map/ppermute | solution.py:57
  86.5 10.7 %collective-permute-start.20 = (bf16[256,512]{1,0:T(8,128)(2,1)S(1)}, bf16[256,512]{1,0:T(8,128)(2,1)S(1)}, u32[]{:S(2)}, u32[]{:S(2)}) collective-permute-start(bf16[256,512]{1,0:T(8,128)(2,1)S(1)} %collective-permute-done.18.rest_9_), channel_id=1, source_target_pairs={{0,32},{1,33},{2,34},{3,35},{4,36},{5,37},{6,38},{7,39},{8,104},{9... | collective-permute-start | bytes 786440 | tf_op jit(solution)/shard_map/ppermute | solution.py:57
  94.3 10.5 %collective-permute-start.16 = (bf16[1024,256]{1,0:T(8,128)(2,1)S(1)}, bf16[1024,256]{1,0:T(8,128)(2,1)S(1)}, u32[]{:S(2)}, u32[]{:S(2)}) collective-permute-start(bf16[1024,256]{1,0:T(8,128)(2,1)S(1)} %pad_maximum_fusion.1), channel_id=1, source_target_pairs={{0,3},{1,2},{2,1},{3,0},{4,7},{5,6},{6,5},{7,4},{8,9},{9,8},{10,11... | collective-permute-start | bytes 1572872 | tf_op jit(solution)/shard_map/ppermute | solution.py:57
  97.3 10.5 %collective-permute-start.21 = (bf16[512,512]{1,0:T(8,128)(2,1)S(1)}, bf16[512,512]{1,0:T(8,128)(2,1)S(1)}, u32[]{:S(2)}, u32[]{:S(2)}) collective-permute-start(bf16[512,512]{1,0:T(8,128)(2,1)S(1)} %pad_maximum_fusion.3), channel_id=1, source_target_pairs={{0,96},{1,97},{2,98},{3,99},{4,100},{5,101},{6,102},{7,103},{8,40}... | collective-permute-start | bytes 1572872 | tf_op jit(solution)/shard_map/ppermute | solution.py:57
  109.7 1.6 %collective-permute-start.22 = (bf16[256,512]{1,0:T(8,128)(2,1)S(1)}, bf16[256,512]{1,0:T(8,128)(2,1)S(1)}, u32[]{:S(2)}, u32[]{:S(2)}) collective-permute-start(bf16[256,512]{1,0:T(8,128)(2,1)S(1)} %get-tuple-element.48), channel_id=1, source_target_pairs={{0,8},{1,9},{2,10},{3,11},{4,12},{5,13},{6,14},{7,15},{8,0},{9,1},... | collective-permute-start | bytes 786440 | tf_op jit(solution)/shard_map/ppermute | solution.py:57
  111.4 6.5 %collective-permute-start.23 = (bf16[256,512]{1,0:T(8,128)(2,1)S(1)}, bf16[256,512]{1,0:T(8,128)(2,1)S(1)}, u32[]{:S(2)}, u32[]{:S(2)}) collective-permute-start(bf16[256,512]{1,0:T(8,128)(2,1)S(1)} %add_convert_fusion.rest_0_), channel_id=1, source_target_pairs={{0,1},{1,0},{2,3},{3,2},{4,5},{5,4},{6,7},{7,6},{8,11},{9,10},{10,... | collective-permute-start | bytes 786440 | tf_op jit(solution)/shard_map/ppermute | solution.py:57
  111.5 9.0 %collective-permute-start.25 = (bf16[256,512]{1,0:T(8,128)(2,1)S(1)}, bf16[256,512]{1,0:T(8,128)(2,1)S(1)}, u32[]{:S(2)}, u32[]{:S(2)}) collective-permute-start(bf16[256,512]{1,0:T(8,128)(2,1)S(1)} %add_convert_fusion.rest_0_), channel_id=1, source_target_pairs={{0,4},{1,5},{2,6},{3,7},{4,0},{5,1},{6,2},{7,3},{8,12},{9,13},{10,... | collective-permute-start | bytes 786440 | tf_op jit(solution)/shard_map/ppermute | solution.py:57
  117.9 8.5 %collective-permute-start.26 = (bf16[256,512]{1,0:T(8,128)(2,1)S(1)}, bf16[256,512]{1,0:T(8,128)(2,1)S(1)}, u32[]{:S(2)}, u32[]{:S(2)}) collective-permute-start(bf16[256,512]{1,0:T(8,128)(2,1)S(1)} %collective-permute-done.23.rest_1_), channel_id=1, source_target_pairs={{0,4},{1,5},{2,6},{3,7},{4,0},{5,1},{6,2},{7,3},{8,12},{9,13},{10,... | collective-permute-start | bytes 786440 | tf_op jit(solution)/shard_map/ppermute | solution.py:57
  118.9 9.6 %collective-permute-start.29 = (bf16[256,1536]{1,0:T(8,128)(2,1)S(1)}, bf16[256,1536]{1,0:T(8,128)(2,1)S(1)}, u32[]{:S(2)}, u32[]{:S(2)}) collective-permute-start(bf16[256,1536]{1,0:T(8,128)(2,1)S(1)} %collective-permute-done.3.fore.rest_8_), channel_id=1, source_target_pairs={{0,8},{1,9},{2,10},{3,11},{4,12},{5,13},{6,14},{7,15},{8,0},{9,1},... | collective-permute-start | bytes 2359304 | tf_op jit(solution)/shard_map/ppermute | solution.py:57
  118.9 9.6 %collective-permute-start.28 = (bf16[256,1536]{1,0:T(8,128)(2,1)S(1)}, bf16[256,1536]{1,0:T(8,128)(2,1)S(1)}, u32[]{:S(2)}, u32[]{:S(2)}) collective-permute-start(bf16[256,1536]{1,0:T(8,128)(2,1)S(1)} %collective-permute-done.2.back.rest_10_), channel_id=1, source_target_pairs={{0,8},{1,9},{2,10},{3,11},{4,12},{5,13},{6,14},{7,15},{8,0},{9,1},... | collective-permute-start | bytes 2359304 | tf_op jit(solution)/shard_map/ppermute | solution.py:57
  119.4 9.1 %collective-permute-start.30 = (bf16[256,1536]{1,0:T(8,128)(2,1)S(1)}, bf16[256,1536]{1,0:T(8,128)(2,1)S(1)}, u32[]{:S(2)}, u32[]{:S(2)}) collective-permute-start(bf16[256,1536]{1,0:T(8,128)(2,1)S(1)} %collective-permute-done.5.far.rest_12_), channel_id=1, source_target_pairs={{0,8},{1,9},{2,10},{3,11},{4,12},{5,13},{6,14},{7,15},{8,0},{9,1},... | collective-permute-start | bytes 2359304 | tf_op jit(solution)/shard_map/ppermute | solution.py:57
  120.5 10.4 %collective-permute-start.24 = (bf16[512,512]{1,0:T(8,128)(2,1)S(1)}, bf16[512,512]{1,0:T(8,128)(2,1)S(1)}, u32[]{:S(2)}, u32[]{:S(2)}) collective-permute-start(bf16[512,512]{1,0:T(8,128)(2,1)S(1)} %pad_maximum_fusion.4), channel_id=1, source_target_pairs={{0,3},{1,2},{2,1},{3,0},{4,7},{5,6},{6,5},{7,4},{8,9},{9,8},{10,11... | collective-permute-start | bytes 1572872 | tf_op jit(solution)/shard_map/ppermute | solution.py:57
  126.5 10.5 %collective-permute-start.27 = (bf16[512,512]{1,0:T(8,128)(2,1)S(1)}, bf16[512,512]{1,0:T(8,128)(2,1)S(1)}, u32[]{:S(2)}, u32[]{:S(2)}) collective-permute-start(bf16[512,512]{1,0:T(8,128)(2,1)S(1)} %pad_maximum_fusion.5), channel_id=1, source_target_pairs={{0,3},{1,2},{2,1},{3,0},{4,7},{5,6},{6,5},{7,4},{8,9},{9,8},{10,11... | collective-permute-start | bytes 1572872 | tf_op jit(solution)/shard_map/ppermute | solution.py:57
  139.4 18.7 %collective-permute-start.31 = (bf16[256,1536]{1,0:T(8,128)(2,1)S(1)}, bf16[256,1536]{1,0:T(8,128)(2,1)S(1)}, u32[]{:S(2)}, u32[]{:S(2)}) collective-permute-start(bf16[256,1536]{1,0:T(8,128)(2,1)S(1)} %apply_other.1), channel_id=1, source_target_pairs={{0,16},{1,17},{2,18},{3,19},{4,20},{5,21},{6,22},{7,23},{8,24},{9,... | collective-permute-start | bytes 2359304 | tf_op jit(solution)/shard_map/ppermute | solution.py:57
  (2 other events, 26.7 us)

commit v6 on v4

--- a/solution.py
+++ b/solution.py
@@ -15,6 +15,7 @@
 NX, NY, NC, NZ = 4, 2, 2, 4
 BLOCK = 256
 TILE = 2 * BLOCK
+STRIP = 384
 MIB = 1 << 20
 
 
@@ -69,36 +70,31 @@
     return lax.dot_general(left, right, (((1,), (0,)), ((), ())), preferred_element_type=jnp.float32)
 
 
-def gram_near_kernel(own, other, fore, fore_other, back, back_other, across, out):
-    for r, rows in enumerate((own, across)):
-        for q, cols in enumerate((own, other, fore, fore_other, back, back_other)):
+def gram_near_kernel(own, other, across, across_other, fore, out):
+    for r, rows in enumerate((own, other, across, across_other)):
+        for q, cols in enumerate((own, fore)):
             part = nt(rows[...], cols[...])
-            out[r, q // 2, :, (q % 2) * BLOCK : (q % 2 + 1) * BLOCK] = part.astype(out.dtype)
-
-
-def gram_far_own_kernel(own, across, far, out):
-    for r, rows in enumerate((own, across)):
-        out[r] = nt(rows[...], far[...]).astype(out.dtype)
-
-
-def gram_far_kernel(where, own, across, far_other, far_own, near, *rest):
+            out[r // 2, q, (r % 2) * BLOCK : (r % 2 + 1) * BLOCK] = part.astype(out.dtype)
+
+
+def gram_far_kernel(where, own, other, across, across_other, back, far, near, *rest):
     outs, tiles = rest[:8], rest[8]
     x, yh, core, yl, z = (where[i] for i in range(5))
-    for r, rows in enumerate((own, across)):
-        tiles[r, :, :BLOCK] = far_own[r]
-        tiles[r, :, BLOCK:] = nt(rows[...], far_other[...]).astype(tiles.dtype)
+    for r, rows in enumerate((own, other, across, across_other)):
+        for q, cols in enumerate((back, far)):
+            part = nt(rows[...], cols[...])
+            tiles[r // 2, q, (r % 2) * BLOCK : (r % 2 + 1) * BLOCK] = part.astype(tiles.dtype)
     for index, out in enumerate(outs):
-        dy, position = index // 4, index % 4
-        row = lax.rem(yl + dy + yh, 2)
-        col = place(z + ahead(position, core) - x, core)
-
-        @pl.when(col == 3)
+        row = lax.rem(yl + index // 4 + yh, 2)
+        col = place(z + ahead(index % 4, core) - x, core)
+
+        @pl.when(col >= 2)
         def _():
-            out[...] = tiles[row]
-
-        @pl.when(col != 3)
+            out[...] = tiles[row, jnp.maximum(col - 2, 0)]
+
+        @pl.when(col < 2)
         def _():
-            out[...] = near[row, jnp.minimum(col, 2)]
+            out[...] = near[row, jnp.minimum(col, 1)]
 
 
 def square_kernel(where, *rest):
@@ -118,9 +114,8 @@
     theirs[:, BLOCK:] = total[BLOCK:, :BLOCK].astype(theirs.dtype)
 
 
-def apply_kernel(other_rows, where, *rest):
-    mixing, blocks, rest = rest[:8], rest[8:16], rest[16:]
-    out, held = rest[-2:]
+def apply_kernel(other_rows, begin, where, *rest):
+    mixing, blocks, (out, held) = rest[:8], rest[8:16], rest[16:]
     x, yh, core, yl, z = (where[i] for i in range(5))
     which = lax.rem(yh + yl + int(other_rows), 2)
     for dy in range(2):
@@ -131,9 +126,9 @@
                 col = place(z + ahead(position, core) - x, core)
                 held[col] = mixing[dy * 4 + position][...]
 
-    for start in range(0, out.shape[1], TILE):
-        columns = slice(start, start + TILE)
-        total = jnp.zeros((BLOCK, TILE), jnp.float32)
+    for start in range(0, out.shape[1], STRIP):
+        columns = slice(begin + start, begin + start + STRIP)
+        total = jnp.zeros((BLOCK, STRIP), jnp.float32)
         for position in range(4):
             for half in range(2):
                 total += nn(
@@ -142,7 +137,7 @@
                 )
         if not other_rows:
             total = total + linear_coef * blocks[0][:, columns].astype(jnp.float32)
-        out[:, columns] = total.astype(out.dtype)
+        out[:, start : start + STRIP] = total.astype(out.dtype)
 
 
 def params(mib):
@@ -161,44 +156,31 @@
     return pl.CostEstimate(flops=flops, bytes_accessed=moved, transcendentals=0)
 
 
-def gram_near(own, other, fore, fore_other, back, back_other, across):
+def gram_near(own, other, across, across_other, fore):
     depth = own.shape[1]
     return pl.pallas_call(
         gram_near_kernel,
-        in_specs=[whole() for _ in range(7)],
+        in_specs=[whole() for _ in range(5)],
         out_specs=whole(),
-        out_shape=jax.ShapeDtypeStruct((2, 3, BLOCK, TILE), jnp.bfloat16),
+        out_shape=jax.ShapeDtypeStruct((2, 2, TILE, BLOCK), jnp.bfloat16),
         compiler_params=params(24),
-        cost_estimate=cost(2 * 6 * BLOCK * TILE * depth, 7 * BLOCK * depth * 2 + 6 * BLOCK * TILE * 2),
+        cost_estimate=cost(2 * 4 * BLOCK * TILE * depth, 5 * BLOCK * depth * 2 + 4 * BLOCK * TILE * 2),
         name="gram_near",
-    )(own, other, fore, fore_other, back, back_other, across)
-
-
-def gram_far_own(own, across, far):
-    depth = own.shape[1]
-    return pl.pallas_call(
-        gram_far_own_kernel,
-        in_specs=[whole() for _ in range(3)],
-        out_specs=whole(),
-        out_shape=jax.ShapeDtypeStruct((2, BLOCK, BLOCK), jnp.bfloat16),
-        compiler_params=params(24),
-        cost_estimate=cost(2 * 2 * BLOCK * BLOCK * depth, 3 * BLOCK * depth * 2 + 2 * BLOCK * BLOCK * 2),
-        name="gram_far_own",
-    )(own, across, far)
-
-
-def gram_far(where, own, across, far_other, far_own, near):
+    )(own, other, across, across_other, fore)
+
+
+def gram_far(where, own, other, across, across_other, back, far, near):
     depth = own.shape[1]
     return pl.pallas_call(
         gram_far_kernel,
-        in_specs=[smem()] + [whole() for _ in range(5)],
+        in_specs=[smem()] + [whole() for _ in range(7)],
         out_specs=[whole() for _ in range(8)],
-        out_shape=[jax.ShapeDtypeStruct((BLOCK, TILE), jnp.bfloat16) for _ in range(8)],
-        scratch_shapes=[pltpu.VMEM((2, BLOCK, TILE), jnp.bfloat16)],
+        out_shape=[jax.ShapeDtypeStruct((TILE, BLOCK), jnp.bfloat16) for _ in range(8)],
+        scratch_shapes=[pltpu.VMEM((2, 2, TILE, BLOCK), jnp.bfloat16)],
         compiler_params=params(24),
-        cost_estimate=cost(2 * 2 * BLOCK * BLOCK * depth, 3 * BLOCK * depth * 2 + 15 * BLOCK * TILE * 2),
+        cost_estimate=cost(2 * 4 * BLOCK * TILE * depth, 6 * BLOCK * depth * 2 + 12 * BLOCK * TILE * 2),
         name="gram_far",
-    )(where, own, across, far_other, far_own, near)
+    )(where, own, other, across, across_other, back, far, near)
 
 
 def square_part(where, left, right):
@@ -217,16 +199,15 @@
     )(where, *left, *right)
 
 
-def apply_part(other_rows, where, mixing, blocks):
-    depth = blocks[0].shape[1]
+def apply_part(other_rows, begin, width, where, mixing, blocks):
     return pl.pallas_call(
-        functools.partial(apply_kernel, other_rows),
+        functools.partial(apply_kernel, other_rows, begin),
         in_specs=[smem()] + [whole() for _ in range(16)],
         out_specs=whole(),
-        out_shape=jax.ShapeDtypeStruct((BLOCK, depth), jnp.bfloat16 if other_rows else jnp.float32),
+        out_shape=jax.ShapeDtypeStruct((BLOCK, width), jnp.bfloat16 if other_rows else jnp.float32),
         scratch_shapes=[pltpu.VMEM((4, BLOCK, TILE), jnp.bfloat16)],
         compiler_params=params(24),
-        cost_estimate=cost(2 * 8 * BLOCK * BLOCK * depth, 9 * BLOCK * depth * 2 + 8 * BLOCK * TILE * 2),
+        cost_estimate=cost(2 * 8 * BLOCK * BLOCK * width, 9 * BLOCK * width * 2 + 8 * BLOCK * TILE * 2),
         name="apply_other" if other_rows else "apply_own",
     )(where, *mixing, *blocks)
 
@@ -284,30 +265,35 @@
     total_cols = iterate.shape[1] * lax.axis_size("col")
     row, col = lax.axis_index("row"), lax.axis_index("col")
     where = jnp.stack([row >> 2, (row >> 1) & 1, row & 1, col >> 2, col & 3]).astype(jnp.int32)
-
     iterate, where = lax.optimization_barrier((iterate, where))
-    other, across, back, fore = lax.optimization_barrier(
-        [send(iterate, move) for move in ("core", "yh", "x_back", "x_fore")]
+
+    half = BLOCK // 2
+    other, across_top, fore, iterate = lax.optimization_barrier(
+        [send(iterate, "core"), send(iterate[:half], "yh"), send(iterate, "x_fore"), iterate]
     )
-    fore_other, back_other = send(back, "core"), send(fore, "core")
-    far = send(fore, "x_fore")
-    near = gram_near(iterate, other, fore, fore_other, back, back_other, across)
-    far, near = lax.optimization_barrier((far, near))
-    far_other = send(far, "core")
-    far_own = gram_far_own(iterate, across, far)
-    gram = sum_over_col(gram_far(where, iterate, across, far_other, far_own, near))
-
-    row_part = jnp.concatenate([gram[:, :BLOCK], send(gram[:, BLOCK:], "core")], axis=0)
-    left, right = gather_rings([(row_part, "z", "yh"), (gram, "x", "yl")])
+    across_low, back, far = lax.optimization_barrier(
+        [send(iterate[half:], "yh"), send(iterate, "x_back"), send(fore, "x_fore")]
+    )
+    across = jnp.concatenate([across_top, across_low], axis=0)
+    rows = (iterate, other, across, send(across, "core"))
+    near = gram_near(*rows, fore)
+    gram_left = sum_over_col(gram_far(where, *rows, back, far, near))
+
+    gram = jnp.concatenate([gram_left[:BLOCK], send(gram_left[BLOCK:], "core")], axis=1)
+    left, right = gather_rings([(gram_left, "z", "yh"), (gram, "x", "yl")])
     mine, theirs = square_part(where, left, right)
     square = mine + send(theirs, "core").astype(jnp.float32)
     mixing = (cubic_coef * gram.astype(jnp.float32) + quintic_coef * square).astype(jnp.bfloat16)
 
     pieces = gather_even(mixing, "z", "yl")
+    fore_other, back_other, far_other = (send(v, "core") for v in (back, fore, far))
     blocks = [iterate, other, fore, fore_other, back, back_other, far, far_other]
-    applied_other = apply_part(True, where, pieces, blocks)
-    applied = apply_part(False, where, pieces, blocks)
-    update = applied + send(applied_other, "yh").astype(jnp.float32)
+    depth = iterate.shape[1]
+    swapped = []
+    for begin in (0, depth // 2):
+        swapped.append(send(apply_part(True, begin, depth // 2, where, pieces, blocks), "yh"))
+    applied = apply_part(False, 0, depth, where, pieces, blocks)
+    update = applied + jnp.concatenate(swapped, axis=1).astype(jnp.float32)
     return (math.sqrt(total_cols) * update).astype(jnp.bfloat16)
 
 

time: 154 us -> 156 us (1.013)
  waiting for transfers between devices: 95.8 us -> 88.2 us
  starting transfers between devices: 43 us -> 50.2 us
  Pallas kernels: 11.4 us -> 13.1 us
    ppermute x37 -> x40, waiting for transfers between devices: 95.8 us -> 88.2 us  [send(): return lax.ppermute(value, ('row', 'col'), pairs(MOVES[move]))]
    ppermute x37 -> x40, starting transfers between devices: 43 us -> 50.2 us  [send(): return lax.ppermute(value, ('row', 'col'), pairs(MOVES[move]))]
    slice x1 -> x3, local copies, waits for them, and re-layouts: 0.02 us -> 2.09 us  [the longest x1 1.05 us: on_device(): iterate[:half]]
  transfers between devices with their start and end apart: 37 -> 40, of which waited for: 26 -> 28; matrix products, arithmetic and copies ran while one was open for 0% -> 2% of each run, Pallas kernels for 4% -> 4%
where the time goes in v6:
time: 156 us
  waiting for transfers between devices  88.2 us (57%)
  starting transfers between devices  50.2 us (32%)
  Pallas kernels  13.1 us (8%)
  local copies, waits for them, and re-layouts  2.3 us (1%)
  other arithmetic  1.7 us (1%)
    ppermute x40, waiting for transfers between devices, send(): return lax.ppermute(value, ('row', 'col'), pairs(MOVES[move]))  88.2 us
    ppermute x40, starting transfers between devices, send(): return lax.ppermute(value, ('row', 'col'), pairs(MOVES[move]))  50.2 us
    pallas_call x3, Pallas kernels, apply_part(): pl.pallas_call(functools.partial(apply_kernel, other_rows, begin), in_spe...  6.78 us
  transfers between devices with their start and end apart: 40, of which 28 were waited for; matrix products, arithmetic and copies ran while one was open for 2% of the time, Pallas kernels for 4%

profile of v6, /device:TPU:0, one launch (start us, length us, event | category | flops | bytes accessed | tf_op | source)
XLA Modules:
  0.0 155.8 jit_solution(16943123100809940491)
XLA Ops:
  2.8 3.3 %collective-permute-start.1 = (bf16[128,1536]{1,0:T(8,128)(2,1)S(1)}, bf16[128,1536]{1,0:T(8,128)(2,1)S(1)}, u32[]{:S(2)}, u32[]{:S(2)}) collective-permute-start(bf16[128,1536]{1,0:T(8,128)(2,1)S(1)} %slice.24), channel_id=1, source_target_pairs={{0,16},{1,17},{2,18},{3,19},{4,20},{5,21},{6,22},{7,23},{8,24},{9,... | collective-permute-start | bytes 1179656 | tf_op jit(solution)/shard_map/ppermute | solution.py:52
  6.1 9.9 %collective-permute-done.1 = bf16[128,1536]{1,0:T(8,128)(2,1)S(1)} collective-permute-done((bf16[128,1536]{1,0:T(8,128)(2,1)S(1)}, bf16[128,1536]{1,0:T(8,128)(2,1)S(1)}, u32[]{:S(2)}, u32[]{:S(2)}) %collective-permute-start.1) | collective-permute-done | bytes 393248 | tf_op jit(solution)/shard_map/ppermute | solution.py:52
  19.1 3.3 %collective-permute-start.3 = (bf16[128,1536]{1,0:T(8,128)(2,1)S(1)}, bf16[128,1536]{1,0:T(8,128)(2,1)S(1)}, u32[]{:S(2)}, u32[]{:S(2)}) collective-permute-start(bf16[128,1536]{1,0:T(8,128)(2,1)S(1)} %slice.25), channel_id=1, source_target_pairs={{0,16},{1,17},{2,18},{3,19},{4,20},{5,21},{6,22},{7,23},{8,24},{9,... | collective-permute-start | bytes 1179656 | tf_op jit(solution)/shard_map/ppermute | solution.py:52
  22.4 10.1 %collective-permute-done.3 = bf16[128,1536]{1,0:T(8,128)(2,1)S(1)} collective-permute-done((bf16[128,1536]{1,0:T(8,128)(2,1)S(1)}, bf16[128,1536]{1,0:T(8,128)(2,1)S(1)}, u32[]{:S(2)}, u32[]{:S(2)}) %collective-permute-start.3) | collective-permute-done | bytes 393248 | tf_op jit(solution)/shard_map/ppermute | solution.py:52
  32.5 3.2 %collective-permute-done.4.back.rest_12_ = bf16[256,1536]{1,0:T(8,128)(2,1)S(1)} collective-permute-done((bf16[256,1536]{1,0:T(8,128)(2,1)}, bf16[256,1536]{1,0:T(8,128)(2,1)S(1)}, u32[]{:S(2)}, u32[]{:S(2)}) %collective-permute-start.4) | collective-permute-done | bytes 786464 | tf_op jit(solution)/shard_map/ppermute | solution.py:52
  37.2 2.3 %collective-permute-done.6.across_other = bf16[256,1536]{1,0:T(8,128)(2,1)S(1)} collective-permute-done((bf16[256,1536]{1,0:T(8,128)(2,1)S(1)}, bf16[256,1536]{1,0:T(8,128)(2,1)S(1)}, u32[]{:S(2)}, u32[]{:S(2)}) %collective-permute-start.6) | collective-permute-done | bytes 786464 | tf_op jit(solution)/shard_map/ppermute | solution.py:52
  41.3 2.6 %gram_far.1 = (bf16[512,256]{1,0:T(8,128)(2,1)S(1)}, bf16[512,256]{1,0:T(8,128)(2,1)S(1)}, bf16[512,256]{1,0:T(8,128)(2,1)S(1)}, bf16[512,256]{1,0:T(8,128)(2,1)...) custom-call(s32[5]{0:T(128)S(1)} %stack.23.where, ...), custom_call_target="tpu_custom_call" | custom-call | flops 1610612736 | bytes 7864320 | tf_op jit(solution)/shard_map/gram_far/pallas_call | solution.py:174
  43.9 4.1 %collective-permute-start.11 = (bf16[512,256]{1,0:T(8,128)(2,1)S(1)}, bf16[512,256]{1,0:T(8,128)(2,1)S(1)}, u32[]{:S(2)}, u32[]{:S(2)}) collective-permute-start(bf16[512,256]{1,0:T(8,128)(2,1)S(1)} %get-tuple-element.50), channel_id=1, source_target_pairs={{0,3},{1,0},{2,1},{3,2},{4,7},{5,4},{6,5},{7,6},{8,9},{9,10},{10,1... | collective-permute-start | bytes 786440 | tf_op jit(solution)/shard_map/ppermute | solution.py:52
  52.0 3.8 %collective-permute-start.12 = (bf16[512,256]{1,0:T(8,128)(2,1)S(1)}, bf16[512,256]{1,0:T(8,128)(2,1)S(1)}, u32[]{:S(2)}, u32[]{:S(2)}) collective-permute-start(bf16[512,256]{1,0:T(8,128)(2,1)S(1)} %add_convert_fusion.3), channel_id=1, source_target_pairs={{0,3},{1,0},{2,1},{3,2},{4,7},{5,4},{6,5},{7,6},{8,9},{9,10},{10,1... | collective-permute-start | bytes 786440 | tf_op jit(solution)/shard_map/ppermute | solution.py:52
  55.9 2.7 %collective-permute-start.8 = (bf16[512,256]{1,0:T(8,128)(2,1)S(1)}, bf16[512,256]{1,0:T(8,128)(2,1)S(1)}, u32[]{:S(2)}, u32[]{:S(2)}) collective-permute-start(bf16[512,256]{1,0:T(8,128)(2,1)S(1)} %add_convert_fusion.5), channel_id=1, source_target_pairs={{0,3},{1,0},{2,1},{3,2},{4,7},{5,4},{6,5},{7,6},{8,9},{9,10},{10,1... | collective-permute-start | bytes 786440 | tf_op jit(solution)/shard_map/ppermute | solution.py:52
  58.8 2.8 %collective-permute-done.12 = bf16[512,256]{1,0:T(8,128)(2,1)S(1)} collective-permute-done((bf16[512,256]{1,0:T(8,128)(2,1)S(1)}, bf16[512,256]{1,0:T(8,128)(2,1)S(1)}, u32[]{:S(2)}, u32[]{:S(2)}) %collective-permute-start.12) | collective-permute-done | bytes 262176 | tf_op jit(solution)/shard_map/ppermute | solution.py:52
  63.2 2.1 %collective-permute-done.8 = bf16[512,256]{1,0:T(8,128)(2,1)S(1)} collective-permute-done((bf16[512,256]{1,0:T(8,128)(2,1)S(1)}, bf16[512,256]{1,0:T(8,128)(2,1)S(1)}, u32[]{:S(2)}, u32[]{:S(2)}) %collective-permute-start.8) | collective-permute-done | bytes 262176 | tf_op jit(solution)/shard_map/ppermute | solution.py:52
  68.2 3.8 %collective-permute-start.15 = (bf16[512,256]{1,0:T(8,128)(2,1)S(1)}, bf16[512,256]{1,0:T(8,128)(2,1)S(1)}, u32[]{:S(2)}, u32[]{:S(2)}) collective-permute-start(bf16[512,256]{1,0:T(8,128)(2,1)S(1)} %add_convert_fusion.1.rest_0_), channel_id=1, source_target_pairs={{0,3},{1,0},{2,1},{3,2},{4,7},{5,4},{6,5},{7,6},{8,9},{9,10},{10,1... | collective-permute-start | bytes 786440 | tf_op jit(solution)/shard_map/ppermute | solution.py:52
  72.1 3.3 %collective-permute-start.17 = (bf16[512,256]{1,0:T(8,128)(2,1)S(1)}, bf16[512,256]{1,0:T(8,128)(2,1)S(1)}, u32[]{:S(2)}, u32[]{:S(2)}) collective-permute-start(bf16[512,256]{1,0:T(8,128)(2,1)S(1)} %add_convert_fusion.1.rest_0_), channel_id=1, source_target_pairs={{0,16},{1,17},{2,18},{3,19},{4,20},{5,21},{6,22},{7,23},{8,24},{9,... | collective-permute-start | bytes 786440 | tf_op jit(solution)/shard_map/ppermute | solution.py:52
  75.4 2.2 %collective-permute-start.21 = (bf16[256,512]{1,0:T(8,128)(2,1)S(1)}, bf16[256,512]{1,0:T(8,128)(2,1)S(1)}, u32[]{:S(2)}, u32[]{:S(2)}) collective-permute-start(bf16[256,512]{1,0:T(8,128)(2,1)S(1)} %pad_maximum_fusion.2.rest_8_), channel_id=1, source_target_pairs={{0,96},{1,97},{2,98},{3,99},{4,100},{5,101},{6,102},{7,103},{8,40}... | collective-permute-start | bytes 786440 | tf_op jit(solution)/shard_map/ppermute | solution.py:52
  80.1 2.7 %collective-permute-done.17.rest_4_ = bf16[512,256]{1,0:T(8,128)(2,1)S(1)} collective-permute-done((bf16[512,256]{1,0:T(8,128)(2,1)S(1)}, bf16[512,256]{1,0:T(8,128)(2,1)S(1)}, u32[]{:S(2)}, u32[]{:S(2)}) %collective-permute-start.17) | collective-permute-done | bytes 262176 | tf_op jit(solution)/shard_map/ppermute | solution.py:52
  85.2 3.0 %collective-permute-done.23.rest_12_ = bf16[256,512]{1,0:T(8,128)(2,1)S(1)} collective-permute-done((bf16[256,512]{1,0:T(8,128)(2,1)S(1)}, bf16[256,512]{1,0:T(8,128)(2,1)S(1)}, u32[]{:S(2)}, u32[]{:S(2)}) %collective-permute-start.23) | collective-permute-done | bytes 262176 | tf_op jit(solution)/shard_map/ppermute | solution.py:52
  89.4 3.2 %collective-permute-start.24 = (bf16[256,512]{1,0:T(8,128)(2,1)S(1)}, bf16[256,512]{1,0:T(8,128)(2,1)S(1)}, u32[]{:S(2)}, u32[]{:S(2)}) collective-permute-start(bf16[256,512]{1,0:T(8,128)(2,1)S(1)} %collective-permute-done.23.rest_12_), channel_id=1, source_target_pairs={{0,96},{1,97},{2,98},{3,99},{4,100},{5,101},{6,102},{7,103},{8,40}... | collective-permute-start | bytes 786440 | tf_op jit(solution)/shard_map/ppermute | solution.py:52
  92.5 2.2 %collective-permute-done.18.rest_6_ = bf16[512,256]{1,0:T(8,128)(2,1)S(1)} collective-permute-done((bf16[512,256]{1,0:T(8,128)(2,1)S(1)}, bf16[512,256]{1,0:T(8,128)(2,1)S(1)}, u32[]{:S(2)}, u32[]{:S(2)}) %collective-permute-start.18) | collective-permute-done | bytes 262176 | tf_op jit(solution)/shard_map/ppermute | solution.py:52
  94.9 3.7 %collective-permute-done.24.rest_14_ = bf16[256,512]{1,0:T(8,128)(2,1)S(1)} collective-permute-done((bf16[256,512]{1,0:T(8,128)(2,1)S(1)}, bf16[256,512]{1,0:T(8,128)(2,1)S(1)}, u32[]{:S(2)}, u32[]{:S(2)}) %collective-permute-start.24) | collective-permute-done | bytes 262176 | tf_op jit(solution)/shard_map/ppermute | solution.py:52
  98.6 2.9 %collective-permute-done.25 = bf16[512,512]{1,0:T(8,128)(2,1)S(1)} collective-permute-done((bf16[512,512]{1,0:T(8,128)(2,1)S(1)}, bf16[512,512]{1,0:T(8,128)(2,1)S(1)}, u32[]{:S(2)}, u32[]{:S(2)}) %collective-permute-start.25) | collective-permute-done | bytes 524320 | tf_op jit(solution)/shard_map/ppermute | solution.py:52
  102.5 6.7 %collective-permute-done.26.rest_15_ = bf16[256,512]{1,0:T(8,128)(2,1)S(1)} collective-permute-done((bf16[256,512]{1,0:T(8,128)(2,1)S(1)}, bf16[256,512]{1,0:T(8,128)(2,1)S(1)}, u32[]{:S(2)}, u32[]{:S(2)}) %collective-permute-start.26) | collective-permute-done | bytes 262176 | tf_op jit(solution)/shard_map/ppermute | solution.py:52
  114.3 3.2 %collective-permute-start.29 = (bf16[256,512]{1,0:T(8,128)(2,1)S(1)}, bf16[256,512]{1,0:T(8,128)(2,1)S(1)}, u32[]{:S(2)}, u32[]{:S(2)}) collective-permute-start(bf16[256,512]{1,0:T(8,128)(2,1)S(1)} %add_convert_fusion.rest_0_), channel_id=1, source_target_pairs={{0,3},{1,0},{2,1},{3,2},{4,7},{5,4},{6,5},{7,6},{8,9},{9,10},{10,1... | collective-permute-start | bytes 786440 | tf_op jit(solution)/shard_map/ppermute | solution.py:52
  117.5 3.8 %collective-permute-done.31.rest_4_ = bf16[256,512]{1,0:T(8,128)(2,1)S(1)} collective-permute-done((bf16[256,512]{1,0:T(8,128)(2,1)S(1)}, bf16[256,512]{1,0:T(8,128)(2,1)S(1)}, u32[]{:S(2)}, u32[]{:S(2)}) %collective-permute-start.31) | collective-permute-done | bytes 262176 | tf_op jit(solution)/shard_map/ppermute | solution.py:52
  121.3 2.6 %collective-permute-done.28.rest_1_ = bf16[256,512]{1,0:T(8,128)(2,1)S(1)} collective-permute-done((bf16[256,512]{1,0:T(8,128)(2,1)S(1)}, bf16[256,512]{1,0:T(8,128)(2,1)S(1)}, u32[]{:S(2)}, u32[]{:S(2)}) %collective-permute-start.28) | collective-permute-done | bytes 262176 | tf_op jit(solution)/shard_map/ppermute | solution.py:52
  125.0 3.9 %collective-permute-done.32.rest_5_ = bf16[256,512]{1,0:T(8,128)(2,1)S(1)} collective-permute-done((bf16[256,512]{1,0:T(8,128)(2,1)S(1)}, bf16[256,512]{1,0:T(8,128)(2,1)S(1)}, u32[]{:S(2)}, u32[]{:S(2)}) %collective-permute-start.32) | collective-permute-done | bytes 262176 | tf_op jit(solution)/shard_map/ppermute | solution.py:52
  128.9 2.8 %collective-permute-done.30.rest_3_ = bf16[256,512]{1,0:T(8,128)(2,1)S(1)} collective-permute-done((bf16[256,512]{1,0:T(8,128)(2,1)S(1)}, bf16[256,512]{1,0:T(8,128)(2,1)S(1)}, u32[]{:S(2)}, u32[]{:S(2)}) %collective-permute-start.30) | collective-permute-done | bytes 262176 | tf_op jit(solution)/shard_map/ppermute | solution.py:52
  131.7 4.8 %collective-permute-done.34.rest_7_ = bf16[256,512]{1,0:T(8,128)(2,1)S(1)} collective-permute-done((bf16[256,512]{1,0:T(8,128)(2,1)S(1)}, bf16[256,512]{1,0:T(8,128)(2,1)S(1)}, u32[]{:S(2)}, u32[]{:S(2)}) %collective-permute-start.34) | collective-permute-done | bytes 262176 | tf_op jit(solution)/shard_map/ppermute | solution.py:52
  138.4 1.9 %collective-permute-start.38 = (bf16[256,768]{1,0:T(8,128)(2,1)S(1)}, bf16[256,768]{1,0:T(8,128)(2,1)S(1)}, u32[]{:S(2)}, u32[]{:S(2)}) collective-permute-start(bf16[256,768]{1,0:T(8,128)(2,1)S(1)} %apply_other.2), channel_id=1, source_target_pairs={{0,16},{1,17},{2,18},{3,19},{4,20},{5,21},{6,22},{7,23},{8,24},{9,... | collective-permute-start | bytes 1179656 | tf_op jit(solution)/shard_map/ppermute | solution.py:52
  144.0 3.0 %apply_own.1 = f32[256,1536]{1,0:T(8,128)S(1)} custom-call(s32[5]{0:T(128)S(1)} %stack.23.where, bf16[256,512]{1,0:T(8,128)(2,1)S(1)} %add_convert_fusion.rest_0_, bf16[256,512]{1,0:T(8,128)(2,1)S(1)} %collective-permute-done.28.rest_1_, bf16[256,512]{1,0:T(8,128)(2,1)S(1)} %collective-permute-done.29.rest_2_, ...), custom_call_target="tpu_custom_call" | custom-call | flops 1610612736 | bytes 9175040 | tf_op jit(solution)/shard_map/apply_own/pallas_call | solution.py:203
  147.0 3.5 %collective-permute-done.38 = bf16[256,768]{1,0:T(8,128)(2,1)S(1)} collective-permute-done((bf16[256,768]{1,0:T(8,128)(2,1)S(1)}, bf16[256,768]{1,0:T(8,128)(2,1)S(1)}, u32[]{:S(2)}, u32[]{:S(2)}) %collective-permute-start.38) | collective-permute-done | bytes 393248 | tf_op jit(solution)/shard_map/ppermute | solution.py:52
  150.5 4.2 %collective-permute-done.39 = bf16[256,768]{1,0:T(8,128)(2,1)S(1)} collective-permute-done((bf16[256,768]{1,0:T(8,128)(2,1)S(1)}, bf16[256,768]{1,0:T(8,128)(2,1)S(1)}, u32[]{:S(2)}, u32[]{:S(2)}) %collective-permute-start.39) | collective-permute-done | bytes 393248 | tf_op jit(solution)/shard_map/ppermute | solution.py:52
  (74 shorter events, 37.9 us)
Async XLA Ops:
  0.1 16.0 %collective-permute-start = (bf16[256,1536]{1,0:T(8,128)(2,1)}, bf16[256,1536]{1,0:T(8,128)(2,1)S(1)}, u32[]{:S(2)}, u32[]{:S(2)}) collective-permute-start(bf16[256,1536]{1,0:T(8,128)(2,1)} %rest_8_.2), channel_id=1, source_target_pairs={{0,8},{1,9},{2,10},{3,11},{4,12},{5,13},{6,14},{7,15},{8,0},{9,1},... | collective-permute-start | bytes 2359304 | tf_op jit(solution)/shard_map/ppermute | solution.py:52
  0.1 15.9 %collective-permute-start.2 = (bf16[256,1536]{1,0:T(8,128)(2,1)}, bf16[256,1536]{1,0:T(8,128)(2,1)S(1)}, u32[]{:S(2)}, u32[]{:S(2)}) collective-permute-start(bf16[256,1536]{1,0:T(8,128)(2,1)} %rest_8_.2), channel_id=1, source_target_pairs={{0,32},{1,33},{2,34},{3,35},{4,36},{5,37},{6,38},{7,39},{8,104},{9... | collective-permute-start | bytes 2359304 | tf_op jit(solution)/shard_map/ppermute | solution.py:52
  2.8 13.2 %collective-permute-start.1 = (bf16[128,1536]{1,0:T(8,128)(2,1)S(1)}, bf16[128,1536]{1,0:T(8,128)(2,1)S(1)}, u32[]{:S(2)}, u32[]{:S(2)}) collective-permute-start(bf16[128,1536]{1,0:T(8,128)(2,1)S(1)} %slice.24), channel_id=1, source_target_pairs={{0,16},{1,17},{2,18},{3,19},{4,20},{5,21},{6,22},{7,23},{8,24},{9,... | collective-permute-start | bytes 1179656 | tf_op jit(solution)/shard_map/ppermute | solution.py:52
  16.0 19.7 %collective-permute-start.4 = (bf16[256,1536]{1,0:T(8,128)(2,1)}, bf16[256,1536]{1,0:T(8,128)(2,1)S(1)}, u32[]{:S(2)}, u32[]{:S(2)}) collective-permute-start(bf16[256,1536]{1,0:T(8,128)(2,1)} %rest_8_.2), channel_id=1, source_target_pairs={{0,96},{1,97},{2,98},{3,99},{4,100},{5,101},{6,102},{7,103},{8,40}... | collective-permute-start | bytes 2359304 | tf_op jit(solution)/shard_map/ppermute | solution.py:52
  17.7 19.4 %collective-permute-start.5 = (bf16[256,1536]{1,0:T(8,128)(2,1)S(1)}, bf16[256,1536]{1,0:T(8,128)(2,1)S(1)}, u32[]{:S(2)}, u32[]{:S(2)}) collective-permute-start(bf16[256,1536]{1,0:T(8,128)(2,1)S(1)} %collective-permute-done.2.fore.rest_10_), channel_id=1, source_target_pairs={{0,32},{1,33},{2,34},{3,35},{4,36},{5,37},{6,38},{7,39},{8,104},{9... | collective-permute-start | bytes 2359304 | tf_op jit(solution)/shard_map/ppermute | solution.py:52
  19.1 13.4 %collective-permute-start.3 = (bf16[128,1536]{1,0:T(8,128)(2,1)S(1)}, bf16[128,1536]{1,0:T(8,128)(2,1)S(1)}, u32[]{:S(2)}, u32[]{:S(2)}) collective-permute-start(bf16[128,1536]{1,0:T(8,128)(2,1)S(1)} %slice.25), channel_id=1, source_target_pairs={{0,16},{1,17},{2,18},{3,19},{4,20},{5,21},{6,22},{7,23},{8,24},{9,... | collective-permute-start | bytes 1179656 | tf_op jit(solution)/shard_map/ppermute | solution.py:52
  43.9 8.0 %collective-permute-start.11 = (bf16[512,256]{1,0:T(8,128)(2,1)S(1)}, bf16[512,256]{1,0:T(8,128)(2,1)S(1)}, u32[]{:S(2)}, u32[]{:S(2)}) collective-permute-start(bf16[512,256]{1,0:T(8,128)(2,1)S(1)} %get-tuple-element.50), channel_id=1, source_target_pairs={{0,3},{1,0},{2,1},{3,2},{4,7},{5,4},{6,5},{7,6},{8,9},{9,10},{10,1... | collective-permute-start | bytes 786440 | tf_op jit(solution)/shard_map/ppermute | solution.py:52
  48.1 7.7 %collective-permute-start.7 = (bf16[512,256]{1,0:T(8,128)(2,1)S(1)}, bf16[512,256]{1,0:T(8,128)(2,1)S(1)}, u32[]{:S(2)}, u32[]{:S(2)}) collective-permute-start(bf16[512,256]{1,0:T(8,128)(2,1)S(1)} %get-tuple-element.45), channel_id=1, source_target_pairs={{0,3},{1,0},{2,1},{3,2},{4,7},{5,4},{6,5},{7,6},{8,9},{9,10},{10,1... | collective-permute-start | bytes 786440 | tf_op jit(solution)/shard_map/ppermute | solution.py:52
  48.5 10.1 %collective-permute-start.9 = (bf16[512,256]{1,0:T(8,128)(2,1)S(1)}, bf16[512,256]{1,0:T(8,128)(2,1)S(1)}, u32[]{:S(2)}, u32[]{:S(2)}) collective-permute-start(bf16[512,256]{1,0:T(8,128)(2,1)S(1)} %get-tuple-element.47), channel_id=1, source_target_pairs={{0,4},{1,5},{2,6},{3,7},{4,0},{5,1},{6,2},{7,3},{8,12},{9,13},{10,... | collective-permute-start | bytes 786440 | tf_op jit(solution)/shard_map/ppermute | solution.py:52
  52.0 9.5 %collective-permute-start.12 = (bf16[512,256]{1,0:T(8,128)(2,1)S(1)}, bf16[512,256]{1,0:T(8,128)(2,1)S(1)}, u32[]{:S(2)}, u32[]{:S(2)}) collective-permute-start(bf16[512,256]{1,0:T(8,128)(2,1)S(1)} %add_convert_fusion.3), channel_id=1, source_target_pairs={{0,3},{1,0},{2,1},{3,2},{4,7},{5,4},{6,5},{7,6},{8,9},{9,10},{10,1... | collective-permute-start | bytes 786440 | tf_op jit(solution)/shard_map/ppermute | solution.py:52
  55.9 9.4 %collective-permute-start.8 = (bf16[512,256]{1,0:T(8,128)(2,1)S(1)}, bf16[512,256]{1,0:T(8,128)(2,1)S(1)}, u32[]{:S(2)}, u32[]{:S(2)}) collective-permute-start(bf16[512,256]{1,0:T(8,128)(2,1)S(1)} %add_convert_fusion.5), channel_id=1, source_target_pairs={{0,3},{1,0},{2,1},{3,2},{4,7},{5,4},{6,5},{7,6},{8,9},{9,10},{10,1... | collective-permute-start | bytes 786440 | tf_op jit(solution)/shard_map/ppermute | solution.py:52
  58.7 7.7 %collective-permute-start.10 = (bf16[512,256]{1,0:T(8,128)(2,1)S(1)}, bf16[512,256]{1,0:T(8,128)(2,1)S(1)}, u32[]{:S(2)}, u32[]{:S(2)}) collective-permute-start(bf16[512,256]{1,0:T(8,128)(2,1)S(1)} %add_convert_fusion.4), channel_id=1, source_target_pairs={{0,1},{1,2},{2,3},{3,0},{4,5},{5,6},{6,7},{7,4},{8,11},{9,8},{10,9... | collective-permute-start | bytes 786440 | tf_op jit(solution)/shard_map/ppermute | solution.py:52
  68.2 10.4 %collective-permute-start.15 = (bf16[512,256]{1,0:T(8,128)(2,1)S(1)}, bf16[512,256]{1,0:T(8,128)(2,1)S(1)}, u32[]{:S(2)}, u32[]{:S(2)}) collective-permute-start(bf16[512,256]{1,0:T(8,128)(2,1)S(1)} %add_convert_fusion.1.rest_0_), channel_id=1, source_target_pairs={{0,3},{1,0},{2,1},{3,2},{4,7},{5,4},{6,5},{7,6},{8,9},{9,10},{10,1... | collective-permute-start | bytes 786440 | tf_op jit(solution)/shard_map/ppermute | solution.py:52
  72.1 8.1 %collective-permute-start.16 = (bf16[512,256]{1,0:T(8,128)(2,1)S(1)}, bf16[512,256]{1,0:T(8,128)(2,1)S(1)}, u32[]{:S(2)}, u32[]{:S(2)}) collective-permute-start(bf16[512,256]{1,0:T(8,128)(2,1)S(1)} %add_convert_fusion.1.rest_0_), channel_id=1, source_target_pairs={{0,1},{1,2},{2,3},{3,0},{4,5},{5,6},{6,7},{7,4},{8,11},{9,8},{10,9... | collective-permute-start | bytes 786440 | tf_op jit(solution)/shard_map/ppermute | solution.py:52
  72.1 10.7 %collective-permute-start.17 = (bf16[512,256]{1,0:T(8,128)(2,1)S(1)}, bf16[512,256]{1,0:T(8,128)(2,1)S(1)}, u32[]{:S(2)}, u32[]{:S(2)}) collective-permute-start(bf16[512,256]{1,0:T(8,128)(2,1)S(1)} %add_convert_fusion.1.rest_0_), channel_id=1, source_target_pairs={{0,16},{1,17},{2,18},{3,19},{4,20},{5,21},{6,22},{7,23},{8,24},{9,... | collective-permute-start | bytes 786440 | tf_op jit(solution)/shard_map/ppermute | solution.py:52
  75.4 8.8 %collective-permute-start.21 = (bf16[256,512]{1,0:T(8,128)(2,1)S(1)}, bf16[256,512]{1,0:T(8,128)(2,1)S(1)}, u32[]{:S(2)}, u32[]{:S(2)}) collective-permute-start(bf16[256,512]{1,0:T(8,128)(2,1)S(1)} %pad_maximum_fusion.2.rest_8_), channel_id=1, source_target_pairs={{0,96},{1,97},{2,98},{3,99},{4,100},{5,101},{6,102},{7,103},{8,40}... | collective-permute-start | bytes 786440 | tf_op jit(solution)/shard_map/ppermute | solution.py:52
  78.6 9.6 %collective-permute-start.23 = (bf16[256,512]{1,0:T(8,128)(2,1)S(1)}, bf16[256,512]{1,0:T(8,128)(2,1)S(1)}, u32[]{:S(2)}, u32[]{:S(2)}) collective-permute-start(bf16[256,512]{1,0:T(8,128)(2,1)S(1)} %pad_maximum_fusion.2.rest_8_), channel_id=1, source_target_pairs={{0,4},{1,5},{2,6},{3,7},{4,0},{5,1},{6,2},{7,3},{8,12},{9,13},{10,... | collective-permute-start | bytes 786440 | tf_op jit(solution)/shard_map/ppermute | solution.py:52
  82.9 11.9 %collective-permute-start.19 = (bf16[1024,256]{1,0:T(8,128)(2,1)S(1)}, bf16[1024,256]{1,0:T(8,128)(2,1)S(1)}, u32[]{:S(2)}, u32[]{:S(2)}) collective-permute-start(bf16[1024,256]{1,0:T(8,128)(2,1)S(1)} %pad_maximum_fusion), channel_id=1, source_target_pairs={{0,1},{1,2},{2,3},{3,0},{4,5},{5,6},{6,7},{7,4},{8,11},{9,8},{10,9... | collective-permute-start | bytes 1572872 | tf_op jit(solution)/shard_map/ppermute | solution.py:52
  88.2 13.3 %collective-permute-start.25 = (bf16[512,512]{1,0:T(8,128)(2,1)S(1)}, bf16[512,512]{1,0:T(8,128)(2,1)S(1)}, u32[]{:S(2)}, u32[]{:S(2)}) collective-permute-start(bf16[512,512]{1,0:T(8,128)(2,1)S(1)} %pad_maximum_fusion.1), channel_id=1, source_target_pairs={{0,32},{1,33},{2,34},{3,35},{4,36},{5,37},{6,38},{7,39},{8,104},{9... | collective-permute-start | bytes 1572872 | tf_op jit(solution)/shard_map/ppermute | solution.py:52
  89.4 9.2 %collective-permute-start.24 = (bf16[256,512]{1,0:T(8,128)(2,1)S(1)}, bf16[256,512]{1,0:T(8,128)(2,1)S(1)}, u32[]{:S(2)}, u32[]{:S(2)}) collective-permute-start(bf16[256,512]{1,0:T(8,128)(2,1)S(1)} %collective-permute-done.23.rest_12_), channel_id=1, source_target_pairs={{0,96},{1,97},{2,98},{3,99},{4,100},{5,101},{6,102},{7,103},{8,40}... | collective-permute-start | bytes 786440 | tf_op jit(solution)/shard_map/ppermute | solution.py:52
  94.8 7.7 %collective-permute-start.20 = (bf16[512,256]{1,0:T(8,128)(2,1)S(1)}, bf16[512,256]{1,0:T(8,128)(2,1)S(1)}, u32[]{:S(2)}, u32[]{:S(2)}) collective-permute-start(bf16[512,256]{1,0:T(8,128)(2,1)S(1)} %get-tuple-element.65.rest_5_), channel_id=1, source_target_pairs={{0,1},{1,2},{2,3},{3,0},{4,5},{5,6},{6,7},{7,4},{8,11},{9,8},{10,9... | collective-permute-start | bytes 786440 | tf_op jit(solution)/shard_map/ppermute | solution.py:52
  101.6 7.7 %collective-permute-start.26 = (bf16[256,512]{1,0:T(8,128)(2,1)S(1)}, bf16[256,512]{1,0:T(8,128)(2,1)S(1)}, u32[]{:S(2)}, u32[]{:S(2)}) collective-permute-start(bf16[256,512]{1,0:T(8,128)(2,1)S(1)} %get-tuple-element.63.rest_13_), channel_id=1, source_target_pairs={{0,32},{1,33},{2,34},{3,35},{4,36},{5,37},{6,38},{7,39},{8,104},{9... | collective-permute-start | bytes 786440 | tf_op jit(solution)/shard_map/ppermute | solution.py:52
  101.6 12.7 %collective-permute-start.36 = (bf16[256,1536]{1,0:T(8,128)(2,1)S(1)}, bf16[256,1536]{1,0:T(8,128)(2,1)S(1)}, u32[]{:S(2)}, u32[]{:S(2)}) collective-permute-start(bf16[256,1536]{1,0:T(8,128)(2,1)S(1)} %collective-permute-done.2.fore.rest_10_), channel_id=1, source_target_pairs={{0,8},{1,9},{2,10},{3,11},{4,12},{5,13},{6,14},{7,15},{8,0},{9,1},... | collective-permute-start | bytes 2359304 | tf_op jit(solution)/shard_map/ppermute | solution.py:52
  111.2 17.7 %collective-permute-start.35 = (bf16[256,1536]{1,0:T(8,128)(2,1)S(1)}, bf16[256,1536]{1,0:T(8,128)(2,1)S(1)}, u32[]{:S(2)}, u32[]{:S(2)}) collective-permute-start(bf16[256,1536]{1,0:T(8,128)(2,1)S(1)} %collective-permute-done.4.back.rest_12_), channel_id=1, source_target_pairs={{0,8},{1,9},{2,10},{3,11},{4,12},{5,13},{6,14},{7,15},{8,0},{9,1},... | collective-permute-start | bytes 2359304 | tf_op jit(solution)/shard_map/ppermute | solution.py:52
  111.7 17.2 %collective-permute-start.37 = (bf16[256,1536]{1,0:T(8,128)(2,1)S(1)}, bf16[256,1536]{1,0:T(8,128)(2,1)S(1)}, u32[]{:S(2)}, u32[]{:S(2)}) collective-permute-start(bf16[256,1536]{1,0:T(8,128)(2,1)S(1)} %collective-permute-done.5.far.rest_14_), channel_id=1, source_target_pairs={{0,8},{1,9},{2,10},{3,11},{4,12},{5,13},{6,14},{7,15},{8,0},{9,1},... | collective-permute-start | bytes 2359304 | tf_op jit(solution)/shard_map/ppermute | solution.py:52
  112.9 8.4 %collective-permute-start.31 = (bf16[256,512]{1,0:T(8,128)(2,1)S(1)}, bf16[256,512]{1,0:T(8,128)(2,1)S(1)}, u32[]{:S(2)}, u32[]{:S(2)}) collective-permute-start(bf16[256,512]{1,0:T(8,128)(2,1)S(1)} %add_convert_fusion.rest_0_), channel_id=1, source_target_pairs={{0,4},{1,5},{2,6},{3,7},{4,0},{5,1},{6,2},{7,3},{8,12},{9,13},{10,... | collective-permute-start | bytes 786440 | tf_op jit(solution)/shard_map/ppermute | solution.py:52
  114.3 9.6 %collective-permute-start.28 = (bf16[256,512]{1,0:T(8,128)(2,1)S(1)}, bf16[256,512]{1,0:T(8,128)(2,1)S(1)}, u32[]{:S(2)}, u32[]{:S(2)}) collective-permute-start(bf16[256,512]{1,0:T(8,128)(2,1)S(1)} %add_convert_fusion.rest_0_), channel_id=1, source_target_pairs={{0,1},{1,2},{2,3},{3,0},{4,5},{5,6},{6,7},{7,4},{8,11},{9,8},{10,9... | collective-permute-start | bytes 786440 | tf_op jit(solution)/shard_map/ppermute | solution.py:52
  114.3 9.6 %collective-permute-start.29 = (bf16[256,512]{1,0:T(8,128)(2,1)S(1)}, bf16[256,512]{1,0:T(8,128)(2,1)S(1)}, u32[]{:S(2)}, u32[]{:S(2)}) collective-permute-start(bf16[256,512]{1,0:T(8,128)(2,1)S(1)} %add_convert_fusion.rest_0_), channel_id=1, source_target_pairs={{0,3},{1,0},{2,1},{3,2},{4,7},{5,4},{6,5},{7,6},{8,9},{9,10},{10,1... | collective-permute-start | bytes 786440 | tf_op jit(solution)/shard_map/ppermute | solution.py:52
  123.9 7.8 %collective-permute-start.30 = (bf16[256,512]{1,0:T(8,128)(2,1)S(1)}, bf16[256,512]{1,0:T(8,128)(2,1)S(1)}, u32[]{:S(2)}, u32[]{:S(2)}) collective-permute-start(bf16[256,512]{1,0:T(8,128)(2,1)S(1)} %collective-permute-done.28.rest_1_), channel_id=1, source_target_pairs={{0,1},{1,2},{2,3},{3,0},{4,5},{5,6},{6,7},{7,4},{8,11},{9,8},{10,9... | collective-permute-start | bytes 786440 | tf_op jit(solution)/shard_map/ppermute | solution.py:52
  123.9 7.8 %collective-permute-start.33 = (bf16[256,512]{1,0:T(8,128)(2,1)S(1)}, bf16[256,512]{1,0:T(8,128)(2,1)S(1)}, u32[]{:S(2)}, u32[]{:S(2)}) collective-permute-start(bf16[256,512]{1,0:T(8,128)(2,1)S(1)} %collective-permute-done.29.rest_2_), channel_id=1, source_target_pairs={{0,4},{1,5},{2,6},{3,7},{4,0},{5,1},{6,2},{7,3},{8,12},{9,13},{10,... | collective-permute-start | bytes 786440 | tf_op jit(solution)/shard_map/ppermute | solution.py:52
  138.4 12.1 %collective-permute-start.38 = (bf16[256,768]{1,0:T(8,128)(2,1)S(1)}, bf16[256,768]{1,0:T(8,128)(2,1)S(1)}, u32[]{:S(2)}, u32[]{:S(2)}) collective-permute-start(bf16[256,768]{1,0:T(8,128)(2,1)S(1)} %apply_other.2), channel_id=1, source_target_pairs={{0,16},{1,17},{2,18},{3,19},{4,20},{5,21},{6,22},{7,23},{8,24},{9,... | collective-permute-start | bytes 1179656 | tf_op jit(solution)/shard_map/ppermute | solution.py:52
  142.2 12.5 %collective-permute-start.39 = (bf16[256,768]{1,0:T(8,128)(2,1)S(1)}, bf16[256,768]{1,0:T(8,128)(2,1)S(1)}, u32[]{:S(2)}, u32[]{:S(2)}) collective-permute-start(bf16[256,768]{1,0:T(8,128)(2,1)S(1)} %apply_other.3), channel_id=1, source_target_pairs={{0,16},{1,17},{2,18},{3,19},{4,20},{5,21},{6,22},{7,23},{8,24},{9,... | collective-permute-start | bytes 1179656 | tf_op jit(solution)/shard_map/ppermute | solution.py:52
  (9 other events, 82.5 us)

commit v7 on v6

--- a/solution.py
+++ b/solution.py
@@ -70,31 +70,17 @@
     return lax.dot_general(left, right, (((1,), (0,)), ((), ())), preferred_element_type=jnp.float32)
 
 
-def gram_near_kernel(own, other, across, across_other, fore, out):
-    for r, rows in enumerate((own, other, across, across_other)):
-        for q, cols in enumerate((own, fore)):
-            part = nt(rows[...], cols[...])
-            out[r // 2, q, (r % 2) * BLOCK : (r % 2 + 1) * BLOCK] = part.astype(out.dtype)
-
-
-def gram_far_kernel(where, own, other, across, across_other, back, far, near, *rest):
+def gram_kernel(where, own, other, across, across_other, fore, back, far, *rest):
     outs, tiles = rest[:8], rest[8]
     x, yh, core, yl, z = (where[i] for i in range(5))
     for r, rows in enumerate((own, other, across, across_other)):
-        for q, cols in enumerate((back, far)):
+        for q, cols in enumerate((own, fore, back, far)):
             part = nt(rows[...], cols[...])
             tiles[r // 2, q, (r % 2) * BLOCK : (r % 2 + 1) * BLOCK] = part.astype(tiles.dtype)
     for index, out in enumerate(outs):
         row = lax.rem(yl + index // 4 + yh, 2)
         col = place(z + ahead(index % 4, core) - x, core)
-
-        @pl.when(col >= 2)
-        def _():
-            out[...] = tiles[row, jnp.maximum(col - 2, 0)]
-
-        @pl.when(col < 2)
-        def _():
-            out[...] = near[row, jnp.minimum(col, 1)]
+        out[...] = tiles[row, col]
 
 
 def square_kernel(where, *rest):
@@ -156,31 +142,18 @@
     return pl.CostEstimate(flops=flops, bytes_accessed=moved, transcendentals=0)
 
 
-def gram_near(own, other, across, across_other, fore):
+def gram_tiles(where, own, other, across, across_other, fore, back, far):
     depth = own.shape[1]
     return pl.pallas_call(
-        gram_near_kernel,
-        in_specs=[whole() for _ in range(5)],
-        out_specs=whole(),
-        out_shape=jax.ShapeDtypeStruct((2, 2, TILE, BLOCK), jnp.bfloat16),
-        compiler_params=params(24),
-        cost_estimate=cost(2 * 4 * BLOCK * TILE * depth, 5 * BLOCK * depth * 2 + 4 * BLOCK * TILE * 2),
-        name="gram_near",
-    )(own, other, across, across_other, fore)
-
-
-def gram_far(where, own, other, across, across_other, back, far, near):
-    depth = own.shape[1]
-    return pl.pallas_call(
-        gram_far_kernel,
+        gram_kernel,
         in_specs=[smem()] + [whole() for _ in range(7)],
         out_specs=[whole() for _ in range(8)],
         out_shape=[jax.ShapeDtypeStruct((TILE, BLOCK), jnp.bfloat16) for _ in range(8)],
-        scratch_shapes=[pltpu.VMEM((2, 2, TILE, BLOCK), jnp.bfloat16)],
+        scratch_shapes=[pltpu.VMEM((2, 4, TILE, BLOCK), jnp.bfloat16)],
         compiler_params=params(24),
-        cost_estimate=cost(2 * 4 * BLOCK * TILE * depth, 6 * BLOCK * depth * 2 + 12 * BLOCK * TILE * 2),
-        name="gram_far",
-    )(where, own, other, across, across_other, back, far, near)
+        cost_estimate=cost(2 * 8 * BLOCK * TILE * depth, 7 * BLOCK * depth * 2 + 8 * BLOCK * TILE * 2),
+        name="gram_tiles",
+    )(where, own, other, across, across_other, fore, back, far)
 
 
 def square_part(where, left, right):
@@ -216,29 +189,6 @@
     return (left.astype(jnp.float32) + right.astype(jnp.float32)).astype(jnp.bfloat16)
 
 
-def gather_rings(sides):
-    first = [
-        [send(value, ring + "_back"), send(value, ring + "_fore"), send(value, pair)]
-        for value, ring, pair in sides
-    ]
-    first = [lax.optimization_barrier(part) for part in first]
-    second = [
-        [
-            send(there, ring + "_back"),
-            send(jnp.concatenate([there, fore], axis=0), ring + "_fore"),
-        ]
-        for (back, fore, there), (value, ring, pair) in zip(first, sides)
-    ]
-    second = [lax.optimization_barrier(part) for part in second]
-    out = []
-    for (back, fore, there), (there_back, both), (value, ring, pair) in zip(first, second, sides):
-        count = value.shape[0]
-        there_fore, far = both[:count], both[count:]
-        there_far = send(there_fore, ring + "_fore")
-        out.append([value, fore, back, far, there, there_fore, there_back, there_far])
-    return out
-
-
 def gather_even(value, ring, pair):
     fore, back = send(value, ring + "_fore"), send(value, ring + "_back")
     there = send(value, pair)
@@ -268,19 +218,19 @@
     iterate, where = lax.optimization_barrier((iterate, where))
 
     half = BLOCK // 2
-    other, across_top, fore, iterate = lax.optimization_barrier(
-        [send(iterate, "core"), send(iterate[:half], "yh"), send(iterate, "x_fore"), iterate]
+    across = send(iterate, "yh")
+    other, back, low = lax.optimization_barrier(
+        [send(iterate, "core"), send(iterate, "x_back"), send(iterate[half:], "x_fore")]
     )
-    across_low, back, far = lax.optimization_barrier(
-        [send(iterate[half:], "yh"), send(iterate, "x_back"), send(fore, "x_fore")]
-    )
-    across = jnp.concatenate([across_top, across_low], axis=0)
+    top = send(iterate[:half], "x_fore")
+    far = [send(top, "x_fore"), send(low, "x_fore")]
+    fore = jnp.concatenate([top, low], axis=0)
+    far = jnp.concatenate(far, axis=0)
     rows = (iterate, other, across, send(across, "core"))
-    near = gram_near(*rows, fore)
-    gram_left = sum_over_col(gram_far(where, *rows, back, far, near))
+    gram_left = sum_over_col(gram_tiles(where, *rows, fore, back, far))
 
     gram = jnp.concatenate([gram_left[:BLOCK], send(gram_left[BLOCK:], "core")], axis=1)
-    left, right = gather_rings([(gram_left, "z", "yh"), (gram, "x", "yl")])
+    left, right = gather_even(gram_left, "z", "yh"), gather_even(gram, "x", "yl")
     mine, theirs = square_part(where, left, right)
     square = mine + send(theirs, "core").astype(jnp.float32)
     mixing = (cubic_coef * gram.astype(jnp.float32) + quintic_coef * square).astype(jnp.bfloat16)

time: 156 us -> 140 us (0.90)
  waiting for transfers between devices: 88.2 us -> 77.9 us
  starting transfers between devices: 50.2 us -> 46.4 us
    ppermute x40 -> x43, waiting for transfers between devices: 88.2 us -> 77.9 us  [send(): return lax.ppermute(value, ('row', 'col'), pairs(MOVES[move]))]
    ppermute x40 -> x43, starting transfers between devices: 50.2 us -> 46.4 us  [send(): return lax.ppermute(value, ('row', 'col'), pairs(MOVES[move]))]
    pallas_call x2 -> x1, Pallas kernels: 4.44 us -> 4.16 us  [gram_tiles(): pl.pallas_call(gram_kernel, in_specs=[smem()] + [whole() for _ in range(7...]
  transfers between devices with their start and end apart: 40 -> 43, of which waited for: 28 -> 25; matrix products, arithmetic and copies ran while one was open for 2% -> 1% of each run, Pallas kernels for 4% -> 5%
where the time goes in v7:
time: 140 us
  waiting for transfers between devices  77.9 us (56%)
  starting transfers between devices  46.4 us (33%)
  Pallas kernels  12.9 us (9%)
  other arithmetic  1.62 us (1%)
    ppermute x43, waiting for transfers between devices, send(): return lax.ppermute(value, ('row', 'col'), pairs(MOVES[move]))  77.9 us
    ppermute x43, starting transfers between devices, send(): return lax.ppermute(value, ('row', 'col'), pairs(MOVES[move]))  46.4 us
    pallas_call x3, Pallas kernels, apply_part(): pl.pallas_call(functools.partial(apply_kernel, other_rows, begin), in_spe...  6.78 us
    pallas_call x1, Pallas kernels, gram_tiles(): pl.pallas_call(gram_kernel, in_specs=[smem()] + [whole() for _ in range(7...  4.16 us
  transfers between devices with their start and end apart: 43, of which 25 were waited for; matrix products, arithmetic and copies ran while one was open for 1% of the time, Pallas kernels for 5%

profile of v7, /device:TPU:0, one launch (start us, length us, event | category | flops | bytes accessed | tf_op | source)
XLA Modules:
  0.0 140.3 jit_solution(1916867740499077505)
XLA Ops:
  0.1 3.3 %collective-permute-start.3 = (bf16[256,1536]{1,0:T(8,128)(2,1)}, bf16[256,1536]{1,0:T(8,128)(2,1)S(1)}, u32[]{:S(2)}, u32[]{:S(2)}) collective-permute-start(bf16[256,1536]{1,0:T(8,128)(2,1)} %rest_8_.2), channel_id=1, source_target_pairs={{0,16},{1,17},{2,18},{3,19},{4,20},{5,21},{6,22},{7,23},{8,24},{9,... | collective-permute-start | bytes 2359304 | tf_op jit(solution)/shard_map/ppermute | solution.py:52
  3.4 2.8 %collective-permute-start.1 = (bf16[256,1536]{1,0:T(8,128)(2,1)}, bf16[256,1536]{1,0:T(8,128)(2,1)S(1)}, u32[]{:S(2)}, u32[]{:S(2)}) collective-permute-start(bf16[256,1536]{1,0:T(8,128)(2,1)} %rest_8_.2), channel_id=1, source_target_pairs={{0,96},{1,97},{2,98},{3,99},{4,100},{5,101},{6,102},{7,103},{8,40}... | collective-permute-start | bytes 2359304 | tf_op jit(solution)/shard_map/ppermute | solution.py:52
  8.1 11.4 %collective-permute-done.5 = bf16[128,1536]{1,0:T(8,128)(2,1)S(1)} collective-permute-done((bf16[128,1536]{1,0:T(8,128)(2,1)S(1)}, bf16[128,1536]{1,0:T(8,128)(2,1)S(1)}, u32[]{:S(2)}, u32[]{:S(2)}) %collective-permute-start.5) | collective-permute-done | bytes 393248 | tf_op jit(solution)/shard_map/ppermute | solution.py:52
  21.2 2.6 %collective-permute-done.2 = bf16[128,1536]{1,0:T(8,128)(2,1)S(1)} collective-permute-done((bf16[128,1536]{1,0:T(8,128)(2,1)S(1)}, bf16[128,1536]{1,0:T(8,128)(2,1)S(1)}, u32[]{:S(2)}, u32[]{:S(2)}) %collective-permute-start.2) | collective-permute-done | bytes 393248 | tf_op jit(solution)/shard_map/ppermute | solution.py:52
  24.4 4.2 %collective-permute-done.6 = bf16[128,1536]{1,0:T(8,128)(2,1)S(1)} collective-permute-done((bf16[128,1536]{1,0:T(8,128)(2,1)S(1)}, bf16[128,1536]{1,0:T(8,128)(2,1)S(1)}, u32[]{:S(2)}, u32[]{:S(2)}) %collective-permute-start.6) | collective-permute-done | bytes 393248 | tf_op jit(solution)/shard_map/ppermute | solution.py:52
  28.6 4.2 %collective-permute-done.7 = bf16[128,1536]{1,0:T(8,128)(2,1)S(1)} collective-permute-done((bf16[128,1536]{1,0:T(8,128)(2,1)S(1)}, bf16[128,1536]{1,0:T(8,128)(2,1)S(1)}, u32[]{:S(2)}, u32[]{:S(2)}) %collective-permute-start.7) | collective-permute-done | bytes 393248 | tf_op jit(solution)/shard_map/ppermute | solution.py:52
  32.8 4.2 %gram_tiles.1 = (bf16[512,256]{1,0:T(8,128)(2,1)S(1)}, bf16[512,256]{1,0:T(8,128)(2,1)S(1)}, bf16[512,256]{1,0:T(8,128)(2,1)S(1)}, bf16[512,256]{1,0:T(8,128)(2,...) custom-call(s32[5]{0:T(128)S(1)} %stack.23.where, ...), custom_call_target="tpu_custom_call" | custom-call | flops 3221225472 | bytes 7602176 | tf_op jit(solution)/shard_map/gram_tiles/pallas_call | solution.py:147
  37.0 4.1 %collective-permute-start.12 = (bf16[512,256]{1,0:T(8,128)(2,1)S(1)}, bf16[512,256]{1,0:T(8,128)(2,1)S(1)}, u32[]{:S(2)}, u32[]{:S(2)}) collective-permute-start(bf16[512,256]{1,0:T(8,128)(2,1)S(1)} %get-tuple-element.32), channel_id=1, source_target_pairs={{0,3},{1,0},{2,1},{3,2},{4,7},{5,4},{6,5},{7,6},{8,9},{9,10},{10,1... | collective-permute-start | bytes 786440 | tf_op jit(solution)/shard_map/ppermute | solution.py:52
  42.2 2.8 %collective-permute-done.12 = bf16[512,256]{1,0:T(8,128)(2,1)S(1)} collective-permute-done((bf16[512,256]{1,0:T(8,128)(2,1)S(1)}, bf16[512,256]{1,0:T(8,128)(2,1)S(1)}, u32[]{:S(2)}, u32[]{:S(2)}) %collective-permute-start.12) | collective-permute-done | bytes 262176 | tf_op jit(solution)/shard_map/ppermute | solution.py:52
  45.1 3.8 %collective-permute-start.13 = (bf16[512,256]{1,0:T(8,128)(2,1)S(1)}, bf16[512,256]{1,0:T(8,128)(2,1)S(1)}, u32[]{:S(2)}, u32[]{:S(2)}) collective-permute-start(bf16[512,256]{1,0:T(8,128)(2,1)S(1)} %add_convert_fusion.3), channel_id=1, source_target_pairs={{0,3},{1,0},{2,1},{3,2},{4,7},{5,4},{6,5},{7,6},{8,9},{9,10},{10,1... | collective-permute-start | bytes 786440 | tf_op jit(solution)/shard_map/ppermute | solution.py:52
  48.9 2.7 %collective-permute-start.9 = (bf16[512,256]{1,0:T(8,128)(2,1)S(1)}, bf16[512,256]{1,0:T(8,128)(2,1)S(1)}, u32[]{:S(2)}, u32[]{:S(2)}) collective-permute-start(bf16[512,256]{1,0:T(8,128)(2,1)S(1)} %add_convert_fusion.5), channel_id=1, source_target_pairs={{0,3},{1,0},{2,1},{3,2},{4,7},{5,4},{6,5},{7,6},{8,9},{9,10},{10,1... | collective-permute-start | bytes 786440 | tf_op jit(solution)/shard_map/ppermute | solution.py:52
  51.8 2.9 %collective-permute-done.13 = bf16[512,256]{1,0:T(8,128)(2,1)S(1)} collective-permute-done((bf16[512,256]{1,0:T(8,128)(2,1)S(1)}, bf16[512,256]{1,0:T(8,128)(2,1)S(1)}, u32[]{:S(2)}, u32[]{:S(2)}) %collective-permute-start.13) | collective-permute-done | bytes 262176 | tf_op jit(solution)/shard_map/ppermute | solution.py:52
  55.5 2.8 %collective-permute-done.9 = bf16[512,256]{1,0:T(8,128)(2,1)S(1)} collective-permute-done((bf16[512,256]{1,0:T(8,128)(2,1)S(1)}, bf16[512,256]{1,0:T(8,128)(2,1)S(1)}, u32[]{:S(2)}, u32[]{:S(2)}) %collective-permute-start.9) | collective-permute-done | bytes 262176 | tf_op jit(solution)/shard_map/ppermute | solution.py:52
  62.7 3.7 %collective-permute-start.17 = (bf16[512,256]{1,0:T(8,128)(2,1)S(1)}, bf16[512,256]{1,0:T(8,128)(2,1)S(1)}, u32[]{:S(2)}, u32[]{:S(2)}) collective-permute-start(bf16[512,256]{1,0:T(8,128)(2,1)S(1)} %add_convert_fusion.1.rest_0_), channel_id=1, source_target_pairs={{0,3},{1,0},{2,1},{3,2},{4,7},{5,4},{6,5},{7,6},{8,9},{9,10},{10,1... | collective-permute-start | bytes 786440 | tf_op jit(solution)/shard_map/ppermute | solution.py:52
  67.3 4.8 %collective-permute-done.19.rest_4_ = bf16[512,256]{1,0:T(8,128)(2,1)S(1)} collective-permute-done((bf16[512,256]{1,0:T(8,128)(2,1)S(1)}, bf16[512,256]{1,0:T(8,128)(2,1)S(1)}, u32[]{:S(2)}, u32[]{:S(2)}) %collective-permute-start.19) | collective-permute-done | bytes 262176 | tf_op jit(solution)/shard_map/ppermute | solution.py:52
  73.9 2.4 %collective-permute-start.21 = (bf16[512,256]{1,0:T(8,128)(2,1)S(1)}, bf16[512,256]{1,0:T(8,128)(2,1)S(1)}, u32[]{:S(2)}, u32[]{:S(2)}) collective-permute-start(bf16[512,256]{1,0:T(8,128)(2,1)S(1)} %collective-permute-done.17.rest_2_), channel_id=1, source_target_pairs={{0,16},{1,17},{2,18},{3,19},{4,20},{5,21},{6,22},{7,23},{8,24},{9,... | collective-permute-start | bytes 786440 | tf_op jit(solution)/shard_map/ppermute | solution.py:52
  76.5 3.2 %collective-permute-done.23.rest_9_ = bf16[256,512]{1,0:T(8,128)(2,1)S(1)} collective-permute-done((bf16[256,512]{1,0:T(8,128)(2,1)S(1)}, bf16[256,512]{1,0:T(8,128)(2,1)S(1)}, u32[]{:S(2)}, u32[]{:S(2)}) %collective-permute-start.23) | collective-permute-done | bytes 262176 | tf_op jit(solution)/shard_map/ppermute | solution.py:52
  80.5 4.1 %collective-permute-done.21.rest_6_ = bf16[512,256]{1,0:T(8,128)(2,1)S(1)} collective-permute-done((bf16[512,256]{1,0:T(8,128)(2,1)S(1)}, bf16[512,256]{1,0:T(8,128)(2,1)S(1)}, u32[]{:S(2)}, u32[]{:S(2)}) %collective-permute-start.21) | collective-permute-done | bytes 262176 | tf_op jit(solution)/shard_map/ppermute | solution.py:52
  86.1 2.6 %collective-permute-done.28.rest_14_ = bf16[256,512]{1,0:T(8,128)(2,1)S(1)} collective-permute-done((bf16[256,512]{1,0:T(8,128)(2,1)S(1)}, bf16[256,512]{1,0:T(8,128)(2,1)S(1)}, u32[]{:S(2)}, u32[]{:S(2)}) %collective-permute-start.28) | collective-permute-done | bytes 262176 | tf_op jit(solution)/shard_map/ppermute | solution.py:52
  88.6 3.6 %collective-permute-done.22.rest_7_ = bf16[512,256]{1,0:T(8,128)(2,1)S(1)} collective-permute-done((bf16[512,256]{1,0:T(8,128)(2,1)S(1)}, bf16[512,256]{1,0:T(8,128)(2,1)S(1)}, u32[]{:S(2)}, u32[]{:S(2)}) %collective-permute-start.22) | collective-permute-done | bytes 262176 | tf_op jit(solution)/shard_map/ppermute | solution.py:52
  92.2 1.9 %square_part.1 = (f32[256,512]{1,0:T(8,128)S(1)}, bf16[256,512]{1,0:T(8,128)(2,1)S(1)}) custom-call(s32[5]{0:T(128)S(1)} %stack.23.where, bf16[512,256]{1,0:T(8,128)(2,1)S(1)} %add_convert_fusion.1.rest_0_, bf16[512,256]{1,0:T(8,128)(2,1)S(1)} %collective-permute-done.16.rest_1_, bf16[512,256]{1,0:T(8,128)(2,1)S(1)} %collective-permute-done.17.rest_2_, ...), custom_call_target="tpu_custom_call" | custom-call | flops 1073741824 | bytes 4194304 | tf_op jit(solution)/shard_map/square_part/pallas_call | solution.py:160
  96.8 3.2 %collective-permute-start.32 = (bf16[256,512]{1,0:T(8,128)(2,1)S(1)}, bf16[256,512]{1,0:T(8,128)(2,1)S(1)}, u32[]{:S(2)}, u32[]{:S(2)}) collective-permute-start(bf16[256,512]{1,0:T(8,128)(2,1)S(1)} %add_convert_fusion.rest_0_), channel_id=1, source_target_pairs={{0,3},{1,0},{2,1},{3,2},{4,7},{5,4},{6,5},{7,6},{8,9},{9,10},{10,1... | collective-permute-start | bytes 786440 | tf_op jit(solution)/shard_map/ppermute | solution.py:52
  100.0 4.3 %collective-permute-done.34.rest_4_ = bf16[256,512]{1,0:T(8,128)(2,1)S(1)} collective-permute-done((bf16[256,512]{1,0:T(8,128)(2,1)S(1)}, bf16[256,512]{1,0:T(8,128)(2,1)S(1)}, u32[]{:S(2)}, u32[]{:S(2)}) %collective-permute-start.34) | collective-permute-done | bytes 262176 | tf_op jit(solution)/shard_map/ppermute | solution.py:52
  104.3 3.2 %collective-permute-start.35 = (bf16[256,512]{1,0:T(8,128)(2,1)S(1)}, bf16[256,512]{1,0:T(8,128)(2,1)S(1)}, u32[]{:S(2)}, u32[]{:S(2)}) collective-permute-start(bf16[256,512]{1,0:T(8,128)(2,1)S(1)} %collective-permute-done.34.rest_4_), channel_id=1, source_target_pairs={{0,1},{1,2},{2,3},{3,0},{4,5},{5,6},{6,7},{7,4},{8,11},{9,8},{10,9... | collective-permute-start | bytes 786440 | tf_op jit(solution)/shard_map/ppermute | solution.py:52
  109.7 2.2 %collective-permute-done.35.rest_5_ = bf16[256,512]{1,0:T(8,128)(2,1)S(1)} collective-permute-done((bf16[256,512]{1,0:T(8,128)(2,1)S(1)}, bf16[256,512]{1,0:T(8,128)(2,1)S(1)}, u32[]{:S(2)}, u32[]{:S(2)}) %collective-permute-start.35) | collective-permute-done | bytes 262176 | tf_op jit(solution)/shard_map/ppermute | solution.py:52
  111.9 2.0 %collective-permute-start.37 = (bf16[256,512]{1,0:T(8,128)(2,1)S(1)}, bf16[256,512]{1,0:T(8,128)(2,1)S(1)}, u32[]{:S(2)}, u32[]{:S(2)}) collective-permute-start(bf16[256,512]{1,0:T(8,128)(2,1)S(1)} %collective-permute-done.35.rest_5_), channel_id=1, source_target_pairs={{0,1},{1,2},{2,3},{3,0},{4,5},{5,6},{6,7},{7,4},{8,11},{9,8},{10,9... | collective-permute-start | bytes 786440 | tf_op jit(solution)/shard_map/ppermute | solution.py:52
  115.8 3.7 %collective-permute-done.37.rest_7_ = bf16[256,512]{1,0:T(8,128)(2,1)S(1)} collective-permute-done((bf16[256,512]{1,0:T(8,128)(2,1)S(1)}, bf16[256,512]{1,0:T(8,128)(2,1)S(1)}, u32[]{:S(2)}, u32[]{:S(2)}) %collective-permute-start.37) | collective-permute-done | bytes 262176 | tf_op jit(solution)/shard_map/ppermute | solution.py:52
  121.4 2.5 %collective-permute-start.41 = (bf16[256,768]{1,0:T(8,128)(2,1)S(1)}, bf16[256,768]{1,0:T(8,128)(2,1)S(1)}, u32[]{:S(2)}, u32[]{:S(2)}) collective-permute-start(bf16[256,768]{1,0:T(8,128)(2,1)S(1)} %apply_other.2), channel_id=1, source_target_pairs={{0,16},{1,17},{2,18},{3,19},{4,20},{5,21},{6,22},{7,23},{8,24},{9,... | collective-permute-start | bytes 1179656 | tf_op jit(solution)/shard_map/ppermute | solution.py:52
  123.9 1.9 %apply_other.3 = bf16[256,768]{1,0:T(8,128)(2,1)S(1)} custom-call(s32[5]{0:T(128)S(1)} %stack.23.where, bf16[256,512]{1,0:T(8,128)(2,1)S(1)} %add_convert_fusion.rest_0_, bf16[256,512]{1,0:T(8,128)(2,1)S(1)} %collective-permute-done.31.rest_1_, bf16[256,512]{1,0:T(8,128)(2,1)S(1)} %collective-permute-done.32.rest_2_, ...), custom_call_target="tpu_custom_call" | custom-call | flops 805306368 | bytes 5636096 | tf_op jit(solution)/shard_map/apply_other/pallas_call | solution.py:176
  127.0 3.0 %apply_own.1 = f32[256,1536]{1,0:T(8,128)S(1)} custom-call(s32[5]{0:T(128)S(1)} %stack.23.where, bf16[256,512]{1,0:T(8,128)(2,1)S(1)} %add_convert_fusion.rest_0_, bf16[256,512]{1,0:T(8,128)(2,1)S(1)} %collective-permute-done.31.rest_1_, bf16[256,512]{1,0:T(8,128)(2,1)S(1)} %collective-permute-done.32.rest_2_, ...), custom_call_target="tpu_custom_call" | custom-call | flops 1610612736 | bytes 9175040 | tf_op jit(solution)/shard_map/apply_own/pallas_call | solution.py:176
  130.0 5.0 %collective-permute-done.41 = bf16[256,768]{1,0:T(8,128)(2,1)S(1)} collective-permute-done((bf16[256,768]{1,0:T(8,128)(2,1)S(1)}, bf16[256,768]{1,0:T(8,128)(2,1)S(1)}, u32[]{:S(2)}, u32[]{:S(2)}) %collective-permute-start.41) | collective-permute-done | bytes 393248 | tf_op jit(solution)/shard_map/ppermute | solution.py:52
  135.0 4.2 %collective-permute-done.42 = bf16[256,768]{1,0:T(8,128)(2,1)S(1)} collective-permute-done((bf16[256,768]{1,0:T(8,128)(2,1)S(1)}, bf16[256,768]{1,0:T(8,128)(2,1)S(1)}, u32[]{:S(2)}, u32[]{:S(2)}) %collective-permute-start.42) | collective-permute-done | bytes 393248 | tf_op jit(solution)/shard_map/ppermute | solution.py:52
  (76 shorter events, 26.7 us)
Async XLA Ops:
  0.1 21.0 %collective-permute-start.3 = (bf16[256,1536]{1,0:T(8,128)(2,1)}, bf16[256,1536]{1,0:T(8,128)(2,1)S(1)}, u32[]{:S(2)}, u32[]{:S(2)}) collective-permute-start(bf16[256,1536]{1,0:T(8,128)(2,1)} %rest_8_.2), channel_id=1, source_target_pairs={{0,16},{1,17},{2,18},{3,19},{4,20},{5,21},{6,22},{7,23},{8,24},{9,... | collective-permute-start | bytes 2359304 | tf_op jit(solution)/shard_map/ppermute | solution.py:52
  3.4 20.4 %collective-permute-start.1 = (bf16[256,1536]{1,0:T(8,128)(2,1)}, bf16[256,1536]{1,0:T(8,128)(2,1)S(1)}, u32[]{:S(2)}, u32[]{:S(2)}) collective-permute-start(bf16[256,1536]{1,0:T(8,128)(2,1)} %rest_8_.2), channel_id=1, source_target_pairs={{0,96},{1,97},{2,98},{3,99},{4,100},{5,101},{6,102},{7,103},{8,40}... | collective-permute-start | bytes 2359304 | tf_op jit(solution)/shard_map/ppermute | solution.py:52
  6.1 17.7 %collective-permute-start = (bf16[256,1536]{1,0:T(8,128)(2,1)}, bf16[256,1536]{1,0:T(8,128)(2,1)S(1)}, u32[]{:S(2)}, u32[]{:S(2)}) collective-permute-start(bf16[256,1536]{1,0:T(8,128)(2,1)} %rest_8_.2), channel_id=1, source_target_pairs={{0,8},{1,9},{2,10},{3,11},{4,12},{5,13},{6,14},{7,15},{8,0},{9,1},... | collective-permute-start | bytes 2359304 | tf_op jit(solution)/shard_map/ppermute | solution.py:52
  7.3 12.3 %collective-permute-start.5 = (bf16[128,1536]{1,0:T(8,128)(2,1)S(1)}, bf16[128,1536]{1,0:T(8,128)(2,1)S(1)}, u32[]{:S(2)}, u32[]{:S(2)}) collective-permute-start(bf16[128,1536]{1,0:T(8,128)(2,1)S(1)} %get-tuple-element.35), channel_id=1, source_target_pairs={{0,32},{1,33},{2,34},{3,35},{4,36},{5,37},{6,38},{7,39},{8,104},{9... | collective-permute-start | bytes 1179656 | tf_op jit(solution)/shard_map/ppermute | solution.py:52
  7.4 16.4 %collective-permute-start.2 = (bf16[128,1536]{1,0:T(8,128)(2,1)S(1)}, bf16[128,1536]{1,0:T(8,128)(2,1)S(1)}, u32[]{:S(2)}, u32[]{:S(2)}) collective-permute-start(bf16[128,1536]{1,0:T(8,128)(2,1)S(1)} %get-tuple-element.36), channel_id=1, source_target_pairs={{0,32},{1,33},{2,34},{3,35},{4,36},{5,37},{6,38},{7,39},{8,104},{9... | collective-permute-start | bytes 1179656 | tf_op jit(solution)/shard_map/ppermute | solution.py:52
  19.6 9.0 %collective-permute-start.6 = (bf16[128,1536]{1,0:T(8,128)(2,1)S(1)}, bf16[128,1536]{1,0:T(8,128)(2,1)S(1)}, u32[]{:S(2)}, u32[]{:S(2)}) collective-permute-start(bf16[128,1536]{1,0:T(8,128)(2,1)S(1)} %collective-permute-done.5), channel_id=1, source_target_pairs={{0,32},{1,33},{2,34},{3,35},{4,36},{5,37},{6,38},{7,39},{8,104},{9... | collective-permute-start | bytes 1179656 | tf_op jit(solution)/shard_map/ppermute | solution.py:52
  21.1 11.7 %collective-permute-start.4 = (bf16[256,1536]{1,0:T(8,128)(2,1)S(1)}, bf16[256,1536]{1,0:T(8,128)(2,1)S(1)}, u32[]{:S(2)}, u32[]{:S(2)}) collective-permute-start(bf16[256,1536]{1,0:T(8,128)(2,1)S(1)} %collective-permute-done.3.across), channel_id=1, source_target_pairs={{0,8},{1,9},{2,10},{3,11},{4,12},{5,13},{6,14},{7,15},{8,0},{9,1},... | collective-permute-start | bytes 2359304 | tf_op jit(solution)/shard_map/ppermute | solution.py:52
  23.8 9.0 %collective-permute-start.7 = (bf16[128,1536]{1,0:T(8,128)(2,1)S(1)}, bf16[128,1536]{1,0:T(8,128)(2,1)S(1)}, u32[]{:S(2)}, u32[]{:S(2)}) collective-permute-start(bf16[128,1536]{1,0:T(8,128)(2,1)S(1)} %collective-permute-done.2), channel_id=1, source_target_pairs={{0,32},{1,33},{2,34},{3,35},{4,36},{5,37},{6,38},{7,39},{8,104},{9... | collective-permute-start | bytes 1179656 | tf_op jit(solution)/shard_map/ppermute | solution.py:52
  37.0 8.0 %collective-permute-start.12 = (bf16[512,256]{1,0:T(8,128)(2,1)S(1)}, bf16[512,256]{1,0:T(8,128)(2,1)S(1)}, u32[]{:S(2)}, u32[]{:S(2)}) collective-permute-start(bf16[512,256]{1,0:T(8,128)(2,1)S(1)} %get-tuple-element.32), channel_id=1, source_target_pairs={{0,3},{1,0},{2,1},{3,2},{4,7},{5,4},{6,5},{7,6},{8,9},{9,10},{10,1... | collective-permute-start | bytes 786440 | tf_op jit(solution)/shard_map/ppermute | solution.py:52
  41.1 7.7 %collective-permute-start.8 = (bf16[512,256]{1,0:T(8,128)(2,1)S(1)}, bf16[512,256]{1,0:T(8,128)(2,1)S(1)}, u32[]{:S(2)}, u32[]{:S(2)}) collective-permute-start(bf16[512,256]{1,0:T(8,128)(2,1)S(1)} %get-tuple-element.27), channel_id=1, source_target_pairs={{0,3},{1,0},{2,1},{3,2},{4,7},{5,4},{6,5},{7,6},{8,9},{9,10},{10,1... | collective-permute-start | bytes 786440 | tf_op jit(solution)/shard_map/ppermute | solution.py:52
  41.5 10.1 %collective-permute-start.10 = (bf16[512,256]{1,0:T(8,128)(2,1)S(1)}, bf16[512,256]{1,0:T(8,128)(2,1)S(1)}, u32[]{:S(2)}, u32[]{:S(2)}) collective-permute-start(bf16[512,256]{1,0:T(8,128)(2,1)S(1)} %get-tuple-element.29), channel_id=1, source_target_pairs={{0,4},{1,5},{2,6},{3,7},{4,0},{5,1},{6,2},{7,3},{8,12},{9,13},{10,... | collective-permute-start | bytes 786440 | tf_op jit(solution)/shard_map/ppermute | solution.py:52
  45.1 9.6 %collective-permute-start.13 = (bf16[512,256]{1,0:T(8,128)(2,1)S(1)}, bf16[512,256]{1,0:T(8,128)(2,1)S(1)}, u32[]{:S(2)}, u32[]{:S(2)}) collective-permute-start(bf16[512,256]{1,0:T(8,128)(2,1)S(1)} %add_convert_fusion.3), channel_id=1, source_target_pairs={{0,3},{1,0},{2,1},{3,2},{4,7},{5,4},{6,5},{7,6},{8,9},{9,10},{10,1... | collective-permute-start | bytes 786440 | tf_op jit(solution)/shard_map/ppermute | solution.py:52
  48.9 9.4 %collective-permute-start.9 = (bf16[512,256]{1,0:T(8,128)(2,1)S(1)}, bf16[512,256]{1,0:T(8,128)(2,1)S(1)}, u32[]{:S(2)}, u32[]{:S(2)}) collective-permute-start(bf16[512,256]{1,0:T(8,128)(2,1)S(1)} %add_convert_fusion.5), channel_id=1, source_target_pairs={{0,3},{1,0},{2,1},{3,2},{4,7},{5,4},{6,5},{7,6},{8,9},{9,10},{10,1... | collective-permute-start | bytes 786440 | tf_op jit(solution)/shard_map/ppermute | solution.py:52
  51.7 7.7 %collective-permute-start.11 = (bf16[512,256]{1,0:T(8,128)(2,1)S(1)}, bf16[512,256]{1,0:T(8,128)(2,1)S(1)}, u32[]{:S(2)}, u32[]{:S(2)}) collective-permute-start(bf16[512,256]{1,0:T(8,128)(2,1)S(1)} %add_convert_fusion.4), channel_id=1, source_target_pairs={{0,1},{1,2},{2,3},{3,0},{4,5},{5,6},{6,7},{7,4},{8,11},{9,8},{10,9... | collective-permute-start | bytes 786440 | tf_op jit(solution)/shard_map/ppermute | solution.py:52
  61.5 10.7 %collective-permute-start.19 = (bf16[512,256]{1,0:T(8,128)(2,1)S(1)}, bf16[512,256]{1,0:T(8,128)(2,1)S(1)}, u32[]{:S(2)}, u32[]{:S(2)}) collective-permute-start(bf16[512,256]{1,0:T(8,128)(2,1)S(1)} %add_convert_fusion.1.rest_0_), channel_id=1, source_target_pairs={{0,16},{1,17},{2,18},{3,19},{4,20},{5,21},{6,22},{7,23},{8,24},{9,... | collective-permute-start | bytes 786440 | tf_op jit(solution)/shard_map/ppermute | solution.py:52
  62.7 9.6 %collective-permute-start.17 = (bf16[512,256]{1,0:T(8,128)(2,1)S(1)}, bf16[512,256]{1,0:T(8,128)(2,1)S(1)}, u32[]{:S(2)}, u32[]{:S(2)}) collective-permute-start(bf16[512,256]{1,0:T(8,128)(2,1)S(1)} %add_convert_fusion.1.rest_0_), channel_id=1, source_target_pairs={{0,3},{1,0},{2,1},{3,2},{4,7},{5,4},{6,5},{7,6},{8,9},{9,10},{10,1... | collective-permute-start | bytes 786440 | tf_op jit(solution)/shard_map/ppermute | solution.py:52
  66.4 10.0 %collective-permute-start.26 = (bf16[256,512]{1,0:T(8,128)(2,1)S(1)}, bf16[256,512]{1,0:T(8,128)(2,1)S(1)}, u32[]{:S(2)}, u32[]{:S(2)}) collective-permute-start(bf16[256,512]{1,0:T(8,128)(2,1)S(1)} %pad_maximum_fusion.rest_8_), channel_id=1, source_target_pairs={{0,4},{1,5},{2,6},{3,7},{4,0},{5,1},{6,2},{7,3},{8,12},{9,13},{10,... | collective-permute-start | bytes 786440 | tf_op jit(solution)/shard_map/ppermute | solution.py:52
  67.2 9.1 %collective-permute-start.24 = (bf16[256,512]{1,0:T(8,128)(2,1)S(1)}, bf16[256,512]{1,0:T(8,128)(2,1)S(1)}, u32[]{:S(2)}, u32[]{:S(2)}) collective-permute-start(bf16[256,512]{1,0:T(8,128)(2,1)S(1)} %pad_maximum_fusion.rest_8_), channel_id=1, source_target_pairs={{0,96},{1,97},{2,98},{3,99},{4,100},{5,101},{6,102},{7,103},{8,40}... | collective-permute-start | bytes 786440 | tf_op jit(solution)/shard_map/ppermute | solution.py:52
  72.2 8.2 %collective-permute-start.20 = (bf16[512,256]{1,0:T(8,128)(2,1)S(1)}, bf16[512,256]{1,0:T(8,128)(2,1)S(1)}, u32[]{:S(2)}, u32[]{:S(2)}) collective-permute-start(bf16[512,256]{1,0:T(8,128)(2,1)S(1)} %collective-permute-done.19.rest_4_), channel_id=1, source_target_pairs={{0,1},{1,2},{2,3},{3,0},{4,5},{5,6},{6,7},{7,4},{8,11},{9,8},{10,9... | collective-permute-start | bytes 786440 | tf_op jit(solution)/shard_map/ppermute | solution.py:52
  73.9 10.7 %collective-permute-start.21 = (bf16[512,256]{1,0:T(8,128)(2,1)S(1)}, bf16[512,256]{1,0:T(8,128)(2,1)S(1)}, u32[]{:S(2)}, u32[]{:S(2)}) collective-permute-start(bf16[512,256]{1,0:T(8,128)(2,1)S(1)} %collective-permute-done.17.rest_2_), channel_id=1, source_target_pairs={{0,16},{1,17},{2,18},{3,19},{4,20},{5,21},{6,22},{7,23},{8,24},{9,... | collective-permute-start | bytes 786440 | tf_op jit(solution)/shard_map/ppermute | solution.py:52
  76.3 8.3 %collective-permute-start.27 = (bf16[256,512]{1,0:T(8,128)(2,1)S(1)}, bf16[256,512]{1,0:T(8,128)(2,1)S(1)}, u32[]{:S(2)}, u32[]{:S(2)}) collective-permute-start(bf16[256,512]{1,0:T(8,128)(2,1)S(1)} %collective-permute-done.26.rest_12_), channel_id=1, source_target_pairs={{0,32},{1,33},{2,34},{3,35},{4,36},{5,37},{6,38},{7,39},{8,104},{9... | collective-permute-start | bytes 786440 | tf_op jit(solution)/shard_map/ppermute | solution.py:52
  76.4 8.3 %collective-permute-start.18 = (bf16[512,256]{1,0:T(8,128)(2,1)S(1)}, bf16[512,256]{1,0:T(8,128)(2,1)S(1)}, u32[]{:S(2)}, u32[]{:S(2)}) collective-permute-start(bf16[512,256]{1,0:T(8,128)(2,1)S(1)} %collective-permute-done.16.rest_1_), channel_id=1, source_target_pairs={{0,1},{1,2},{2,3},{3,0},{4,5},{5,6},{6,7},{7,4},{8,11},{9,8},{10,9... | collective-permute-start | bytes 786440 | tf_op jit(solution)/shard_map/ppermute | solution.py:52
  79.7 8.9 %collective-permute-start.28 = (bf16[256,512]{1,0:T(8,128)(2,1)S(1)}, bf16[256,512]{1,0:T(8,128)(2,1)S(1)}, u32[]{:S(2)}, u32[]{:S(2)}) collective-permute-start(bf16[256,512]{1,0:T(8,128)(2,1)S(1)} %collective-permute-done.24.rest_10_), channel_id=1, source_target_pairs={{0,4},{1,5},{2,6},{3,7},{4,0},{5,1},{6,2},{7,3},{8,12},{9,13},{10,... | collective-permute-start | bytes 786440 | tf_op jit(solution)/shard_map/ppermute | solution.py:52
  80.4 8.2 %collective-permute-start.25 = (bf16[256,512]{1,0:T(8,128)(2,1)S(1)}, bf16[256,512]{1,0:T(8,128)(2,1)S(1)}, u32[]{:S(2)}, u32[]{:S(2)}) collective-permute-start(bf16[256,512]{1,0:T(8,128)(2,1)S(1)} %collective-permute-done.23.rest_9_), channel_id=1, source_target_pairs={{0,32},{1,33},{2,34},{3,35},{4,36},{5,37},{6,38},{7,39},{8,104},{9... | collective-permute-start | bytes 786440 | tf_op jit(solution)/shard_map/ppermute | solution.py:52
  84.7 15.3 %collective-permute-start.39 = (bf16[256,1536]{1,0:T(8,128)(2,1)S(1)}, bf16[256,1536]{1,0:T(8,128)(2,1)S(1)}, u32[]{:S(2)}, u32[]{:S(2)}) collective-permute-start(bf16[256,1536]{1,0:T(8,128)(2,1)S(1)} %constant_dynamic-update-slice_fusion.fore.rest_10_), channel_id=1, source_target_pairs={{0,8},{1,9},{2,10},{3,11},{4,12},{5,13},{6,14},{7,15},{8,0},{9,1},... | collective-permute-start | bytes 2359304 | tf_op jit(solution)/shard_map/ppermute | solution.py:52
  94.2 19.6 %collective-permute-start.38 = (bf16[256,1536]{1,0:T(8,128)(2,1)S(1)}, bf16[256,1536]{1,0:T(8,128)(2,1)S(1)}, u32[]{:S(2)}, u32[]{:S(2)}) collective-permute-start(bf16[256,1536]{1,0:T(8,128)(2,1)S(1)} %collective-permute-done.1.back.rest_12_), channel_id=1, source_target_pairs={{0,8},{1,9},{2,10},{3,11},{4,12},{5,13},{6,14},{7,15},{8,0},{9,1},... | collective-permute-start | bytes 2359304 | tf_op jit(solution)/shard_map/ppermute | solution.py:52
  94.7 19.1 %collective-permute-start.40 = (bf16[256,1536]{1,0:T(8,128)(2,1)S(1)}, bf16[256,1536]{1,0:T(8,128)(2,1)S(1)}, u32[]{:S(2)}, u32[]{:S(2)}) collective-permute-start(bf16[256,1536]{1,0:T(8,128)(2,1)S(1)} %constant_dynamic-update-slice_fusion.2.far.rest_14_), channel_id=1, source_target_pairs={{0,8},{1,9},{2,10},{3,11},{4,12},{5,13},{6,14},{7,15},{8,0},{9,1},... | collective-permute-start | bytes 2359304 | tf_op jit(solution)/shard_map/ppermute | solution.py:52
  95.9 8.4 %collective-permute-start.34 = (bf16[256,512]{1,0:T(8,128)(2,1)S(1)}, bf16[256,512]{1,0:T(8,128)(2,1)S(1)}, u32[]{:S(2)}, u32[]{:S(2)}) collective-permute-start(bf16[256,512]{1,0:T(8,128)(2,1)S(1)} %add_convert_fusion.rest_0_), channel_id=1, source_target_pairs={{0,4},{1,5},{2,6},{3,7},{4,0},{5,1},{6,2},{7,3},{8,12},{9,13},{10,... | collective-permute-start | bytes 786440 | tf_op jit(solution)/shard_map/ppermute | solution.py:52
  96.8 10.7 %collective-permute-start.32 = (bf16[256,512]{1,0:T(8,128)(2,1)S(1)}, bf16[256,512]{1,0:T(8,128)(2,1)S(1)}, u32[]{:S(2)}, u32[]{:S(2)}) collective-permute-start(bf16[256,512]{1,0:T(8,128)(2,1)S(1)} %add_convert_fusion.rest_0_), channel_id=1, source_target_pairs={{0,3},{1,0},{2,1},{3,2},{4,7},{5,4},{6,5},{7,6},{8,9},{9,10},{10,1... | collective-permute-start | bytes 786440 | tf_op jit(solution)/shard_map/ppermute | solution.py:52
  100.0 8.2 %collective-permute-start.31 = (bf16[256,512]{1,0:T(8,128)(2,1)S(1)}, bf16[256,512]{1,0:T(8,128)(2,1)S(1)}, u32[]{:S(2)}, u32[]{:S(2)}) collective-permute-start(bf16[256,512]{1,0:T(8,128)(2,1)S(1)} %add_convert_fusion.rest_0_), channel_id=1, source_target_pairs={{0,1},{1,2},{2,3},{3,0},{4,5},{5,6},{6,7},{7,4},{8,11},{9,8},{10,9... | collective-permute-start | bytes 786440 | tf_op jit(solution)/shard_map/ppermute | solution.py:52
  121.4 13.6 %collective-permute-start.41 = (bf16[256,768]{1,0:T(8,128)(2,1)S(1)}, bf16[256,768]{1,0:T(8,128)(2,1)S(1)}, u32[]{:S(2)}, u32[]{:S(2)}) collective-permute-start(bf16[256,768]{1,0:T(8,128)(2,1)S(1)} %apply_other.2), channel_id=1, source_target_pairs={{0,16},{1,17},{2,18},{3,19},{4,20},{5,21},{6,22},{7,23},{8,24},{9,... | collective-permute-start | bytes 1179656 | tf_op jit(solution)/shard_map/ppermute | solution.py:52
  125.8 13.4 %collective-permute-start.42 = (bf16[256,768]{1,0:T(8,128)(2,1)S(1)}, bf16[256,768]{1,0:T(8,128)(2,1)S(1)}, u32[]{:S(2)}, u32[]{:S(2)}) collective-permute-start(bf16[256,768]{1,0:T(8,128)(2,1)S(1)} %apply_other.3), channel_id=1, source_target_pairs={{0,16},{1,17},{2,18},{3,19},{4,20},{5,21},{6,22},{7,23},{8,24},{9,... | collective-permute-start | bytes 1179656 | tf_op jit(solution)/shard_map/ppermute | solution.py:52
  (12 other events, 98.9 us)

commit v8 on v7

--- a/solution.py
+++ b/solution.py
@@ -41,6 +41,8 @@
     "core": lambda x, yh, c, yl, z: (x, yh, 1 - c, yl, z),
     "yh": lambda x, yh, c, yl, z: (x, 1 - yh, c, yl, z),
     "yl": lambda x, yh, c, yl, z: (x, yh, c, 1 - yl, z),
+    "turn": lambda x, yh, c, yl, z: (x, yl, c, yh, z),
+    "turn_yl": lambda x, yh, c, yl, z: (x, yl, c, 1 - yh, z),
     "x_fore": lambda x, yh, c, yl, z: (x + way(c), yh, c, yl, z),
     "x_back": lambda x, yh, c, yl, z: (x - way(c), yh, c, yl, z),
     "z_fore": lambda x, yh, c, yl, z: (x, yh, c, yl, z + way(c)),
@@ -95,32 +97,24 @@
             row = lax.rem(yh + dy + yl, 2)
             col = place(z + ahead(position, core) - x, core)
             total += nn(left[dy * 4 + position][...], held[row, col])
-    mine[...] = total[:BLOCK]
-    theirs[:, :BLOCK] = total[BLOCK:, BLOCK:].astype(theirs.dtype)
-    theirs[:, BLOCK:] = total[BLOCK:, :BLOCK].astype(theirs.dtype)
+    mine[...] = total[:, :BLOCK]
+    theirs[:BLOCK] = total[BLOCK:, BLOCK:].astype(theirs.dtype)
+    theirs[BLOCK:] = total[:BLOCK, BLOCK:].astype(theirs.dtype)
 
 
 def apply_kernel(other_rows, begin, where, *rest):
     mixing, blocks, (out, held) = rest[:8], rest[8:16], rest[16:]
     x, yh, core, yl, z = (where[i] for i in range(5))
-    which = lax.rem(yh + yl + int(other_rows), 2)
-    for dy in range(2):
-
-        @pl.when(which == dy)
-        def _():
-            for position in range(4):
-                col = place(z + ahead(position, core) - x, core)
-                held[col] = mixing[dy * 4 + position][...]
+    for index in range(8):
+        row = lax.rem(yl + index // 4 + yh, 2)
+        col = place(z + ahead(index % 4, core) - x, core)
+        held[row, col] = mixing[index][int(other_rows) * BLOCK : (int(other_rows) + 1) * BLOCK]
 
     for start in range(0, out.shape[1], STRIP):
         columns = slice(begin + start, begin + start + STRIP)
         total = jnp.zeros((BLOCK, STRIP), jnp.float32)
-        for position in range(4):
-            for half in range(2):
-                total += nn(
-                    held[position, :, half * BLOCK : (half + 1) * BLOCK],
-                    blocks[position * 2 + half][:, columns],
-                )
+        for index in range(8):
+            total += nn(held[index // 4, index % 4], blocks[index][:, columns])
         if not other_rows:
             total = total + linear_coef * blocks[0][:, columns].astype(jnp.float32)
         out[:, start : start + STRIP] = total.astype(out.dtype)
@@ -162,8 +156,8 @@
         in_specs=[smem()] + [whole() for _ in range(16)],
         out_specs=[whole(), whole()],
         out_shape=[
-            jax.ShapeDtypeStruct((BLOCK, TILE), jnp.float32),
-            jax.ShapeDtypeStruct((BLOCK, TILE), jnp.bfloat16),
+            jax.ShapeDtypeStruct((TILE, BLOCK), jnp.float32),
+            jax.ShapeDtypeStruct((TILE, BLOCK), jnp.bfloat16),
         ],
         scratch_shapes=[pltpu.VMEM((2, 4, BLOCK, TILE), jnp.bfloat16)],
         compiler_params=params(24),
@@ -178,7 +172,7 @@
         in_specs=[smem()] + [whole() for _ in range(16)],
         out_specs=whole(),
         out_shape=jax.ShapeDtypeStruct((BLOCK, width), jnp.bfloat16 if other_rows else jnp.float32),
-        scratch_shapes=[pltpu.VMEM((4, BLOCK, TILE), jnp.bfloat16)],
+        scratch_shapes=[pltpu.VMEM((2, 4, BLOCK, BLOCK), jnp.bfloat16)],
         compiler_params=params(24),
         cost_estimate=cost(2 * 8 * BLOCK * BLOCK * width, 9 * BLOCK * width * 2 + 8 * BLOCK * TILE * 2),
         name="apply_other" if other_rows else "apply_own",
@@ -189,9 +183,9 @@
     return (left.astype(jnp.float32) + right.astype(jnp.float32)).astype(jnp.bfloat16)
 
 
-def gather_even(value, ring, pair):
+def gather_even(value, ring, pair, there=None):
     fore, back = send(value, ring + "_fore"), send(value, ring + "_back")
-    there = send(value, pair)
+    there = send(value, pair) if there is None else there
     far = send(fore, ring + "_fore")
     there_fore = send(there, ring + "_fore")
     there_back = send(back, pair)
@@ -229,19 +223,22 @@
     rows = (iterate, other, across, send(across, "core"))
     gram_left = sum_over_col(gram_tiles(where, *rows, fore, back, far))
 
+    across_fore, across_back = send(across, "x_fore"), send(across, "x_back")
+    gram_left, across_fore, across_back = lax.optimization_barrier((gram_left, across_fore, across_back))
+    across_far = send(across_fore, "x_fore")
     gram = jnp.concatenate([gram_left[:BLOCK], send(gram_left[BLOCK:], "core")], axis=1)
     left, right = gather_even(gram_left, "z", "yh"), gather_even(gram, "x", "yl")
     mine, theirs = square_part(where, left, right)
     square = mine + send(theirs, "core").astype(jnp.float32)
-    mixing = (cubic_coef * gram.astype(jnp.float32) + quintic_coef * square).astype(jnp.bfloat16)
-
-    pieces = gather_even(mixing, "z", "yl")
-    fore_other, back_other, far_other = (send(v, "core") for v in (back, fore, far))
-    blocks = [iterate, other, fore, fore_other, back, back_other, far, far_other]
+    mixing = (cubic_coef * gram_left.astype(jnp.float32) + quintic_coef * square).astype(jnp.bfloat16)
+
+    there = send(mixing, "turn_yl")
+    pieces = gather_even(send(mixing, "turn"), "z", "yl", there)
+    blocks = [iterate, fore, back, far, across, across_fore, across_back, across_far]
     depth = iterate.shape[1]
     swapped = []
     for begin in (0, depth // 2):
-        swapped.append(send(apply_part(True, begin, depth // 2, where, pieces, blocks), "yh"))
+        swapped.append(send(apply_part(True, begin, depth // 2, where, pieces, blocks), "core"))
     applied = apply_part(False, 0, depth, where, pieces, blocks)
     update = applied + jnp.concatenate(swapped, axis=1).astype(jnp.float32)
     return (math.sqrt(total_cols) * update).astype(jnp.bfloat16)

time: 140 us -> 137 us (0.979); the launches traced: 140 us -> 135 us
  waiting for transfers between devices: 77.9 us -> 72.6 us
    ppermute x43 -> x44, waiting for transfers between devices: 77.9 us -> 72.6 us  [send(): return lax.ppermute(value, ('row', 'col'), pairs(MOVES[move]))]
    ppermute x43 -> x44, starting transfers between devices: 46.4 us -> 46.9 us  [send(): return lax.ppermute(value, ('row', 'col'), pairs(MOVES[move]))]
  transfers between devices with their start and end apart: 43 -> 44, of which waited for: 25 -> 27; matrix products, arithmetic and copies ran while one was open for 1% -> 1% of each run, Pallas kernels for 5% -> 4%
where the time goes in v8:
time: 137 us; the launch traced here: 135 us
  waiting for transfers between devices  72.6 us (53%)
  starting transfers between devices  46.9 us (34%)
  Pallas kernels  12.8 us (9%)
  other arithmetic  1.62 us (1%)
  local copies, waits for them, and re-layouts  1.38 us (1%)
    ppermute x44, waiting for transfers between devices, send(): return lax.ppermute(value, ('row', 'col'), pairs(MOVES[move]))  72.6 us
    ppermute x44, starting transfers between devices, send(): return lax.ppermute(value, ('row', 'col'), pairs(MOVES[move]))  46.9 us
    pallas_call x3, Pallas kernels, apply_part(): pl.pallas_call(functools.partial(apply_kernel, other_rows, begin), in_spe...  6.7 us
    pallas_call x1, Pallas kernels, gram_tiles(): pl.pallas_call(gram_kernel, in_specs=[smem()] + [whole() for _ in range(7...  4.14 us
  transfers between devices with their start and end apart: 44, of which 27 were waited for; matrix products, arithmetic and copies ran while one was open for 1% of the time, Pallas kernels for 4%

profile of v8, /device:TPU:0, one launch (start us, length us, event | category | flops | bytes accessed | tf_op | source)
XLA Modules:
  0.0 135.5 jit_solution(5376309523730194106)
XLA Ops:
  0.1 3.3 %collective-permute-start.3 = (bf16[256,1536]{1,0:T(8,128)(2,1)}, bf16[256,1536]{1,0:T(8,128)(2,1)S(1)}, u32[]{:S(2)}, u32[]{:S(2)}) collective-permute-start(bf16[256,1536]{1,0:T(8,128)(2,1)} %rest_8_.2), channel_id=1, source_target_pairs={{0,16},{1,17},{2,18},{3,19},{4,20},{5,21},{6,22},{7,23},{8,24},{9,... | collective-permute-start | bytes 2359304 | tf_op jit(solution)/shard_map/ppermute | solution.py:54
  3.4 2.8 %collective-permute-start.1 = (bf16[256,1536]{1,0:T(8,128)(2,1)}, bf16[256,1536]{1,0:T(8,128)(2,1)S(1)}, u32[]{:S(2)}, u32[]{:S(2)}) collective-permute-start(bf16[256,1536]{1,0:T(8,128)(2,1)} %rest_8_.2), channel_id=1, source_target_pairs={{0,96},{1,97},{2,98},{3,99},{4,100},{5,101},{6,102},{7,103},{8,40}... | collective-permute-start | bytes 2359304 | tf_op jit(solution)/shard_map/ppermute | solution.py:54
  8.1 11.4 %collective-permute-done.5 = bf16[128,1536]{1,0:T(8,128)(2,1)S(1)} collective-permute-done((bf16[128,1536]{1,0:T(8,128)(2,1)S(1)}, bf16[128,1536]{1,0:T(8,128)(2,1)S(1)}, u32[]{:S(2)}, u32[]{:S(2)}) %collective-permute-start.5) | collective-permute-done | bytes 393248 | tf_op jit(solution)/shard_map/ppermute | solution.py:54
  21.2 2.6 %collective-permute-done.2 = bf16[128,1536]{1,0:T(8,128)(2,1)S(1)} collective-permute-done((bf16[128,1536]{1,0:T(8,128)(2,1)S(1)}, bf16[128,1536]{1,0:T(8,128)(2,1)S(1)}, u32[]{:S(2)}, u32[]{:S(2)}) %collective-permute-start.2) | collective-permute-done | bytes 393248 | tf_op jit(solution)/shard_map/ppermute | solution.py:54
  24.4 4.2 %collective-permute-done.6 = bf16[128,1536]{1,0:T(8,128)(2,1)S(1)} collective-permute-done((bf16[128,1536]{1,0:T(8,128)(2,1)S(1)}, bf16[128,1536]{1,0:T(8,128)(2,1)S(1)}, u32[]{:S(2)}, u32[]{:S(2)}) %collective-permute-start.6) | collective-permute-done | bytes 393248 | tf_op jit(solution)/shard_map/ppermute | solution.py:54
  28.6 4.2 %collective-permute-done.7 = bf16[128,1536]{1,0:T(8,128)(2,1)S(1)} collective-permute-done((bf16[128,1536]{1,0:T(8,128)(2,1)S(1)}, bf16[128,1536]{1,0:T(8,128)(2,1)S(1)}, u32[]{:S(2)}, u32[]{:S(2)}) %collective-permute-start.7) | collective-permute-done | bytes 393248 | tf_op jit(solution)/shard_map/ppermute | solution.py:54
  32.8 4.1 %gram_tiles.1 = (bf16[512,256]{1,0:T(8,128)(2,1)S(1)}, bf16[512,256]{1,0:T(8,128)(2,1)S(1)}, bf16[512,256]{1,0:T(8,128)(2,1)S(1)}, bf16[512,256]{1,0:T(8,128)(2,...) custom-call(s32[5]{0:T(128)S(1)} %stack.23.where, ...), custom_call_target="tpu_custom_call" | custom-call | flops 3221225472 | bytes 7602176 | tf_op jit(solution)/shard_map/gram_tiles/pallas_call | solution.py:141
  37.0 4.1 %collective-permute-start.12 = (bf16[512,256]{1,0:T(8,128)(2,1)S(1)}, bf16[512,256]{1,0:T(8,128)(2,1)S(1)}, u32[]{:S(2)}, u32[]{:S(2)}) collective-permute-start(bf16[512,256]{1,0:T(8,128)(2,1)S(1)} %get-tuple-element.35), channel_id=1, source_target_pairs={{0,3},{1,0},{2,1},{3,2},{4,7},{5,4},{6,5},{7,6},{8,9},{9,10},{10,1... | collective-permute-start | bytes 786440 | tf_op jit(solution)/shard_map/ppermute | solution.py:54
  45.1 3.8 %collective-permute-start.13 = (bf16[512,256]{1,0:T(8,128)(2,1)S(1)}, bf16[512,256]{1,0:T(8,128)(2,1)S(1)}, u32[]{:S(2)}, u32[]{:S(2)}) collective-permute-start(bf16[512,256]{1,0:T(8,128)(2,1)S(1)} %add_convert_fusion.3), channel_id=1, source_target_pairs={{0,3},{1,0},{2,1},{3,2},{4,7},{5,4},{6,5},{7,6},{8,9},{9,10},{10,1... | collective-permute-start | bytes 786440 | tf_op jit(solution)/shard_map/ppermute | solution.py:54
  48.9 2.7 %collective-permute-start.9 = (bf16[512,256]{1,0:T(8,128)(2,1)S(1)}, bf16[512,256]{1,0:T(8,128)(2,1)S(1)}, u32[]{:S(2)}, u32[]{:S(2)}) collective-permute-start(bf16[512,256]{1,0:T(8,128)(2,1)S(1)} %add_convert_fusion.5), channel_id=1, source_target_pairs={{0,3},{1,0},{2,1},{3,2},{4,7},{5,4},{6,5},{7,6},{8,9},{9,10},{10,1... | collective-permute-start | bytes 786440 | tf_op jit(solution)/shard_map/ppermute | solution.py:54
  51.8 1.7 %collective-permute-start.11 = (bf16[512,256]{1,0:T(8,128)(2,1)S(1)}, bf16[512,256]{1,0:T(8,128)(2,1)S(1)}, u32[]{:S(2)}, u32[]{:S(2)}) collective-permute-start(bf16[512,256]{1,0:T(8,128)(2,1)S(1)} %add_convert_fusion.4), channel_id=1, source_target_pairs={{0,1},{1,2},{2,3},{3,0},{4,5},{5,6},{6,7},{7,4},{8,11},{9,8},{10,9... | collective-permute-start | bytes 786440 | tf_op jit(solution)/shard_map/ppermute | solution.py:54
  54.3 3.6 %collective-permute-done.9 = bf16[512,256]{1,0:T(8,128)(2,1)S(1)} collective-permute-done((bf16[512,256]{1,0:T(8,128)(2,1)S(1)}, bf16[512,256]{1,0:T(8,128)(2,1)S(1)}, u32[]{:S(2)}, u32[]{:S(2)}) %collective-permute-start.9) | collective-permute-done | bytes 262176 | tf_op jit(solution)/shard_map/ppermute | solution.py:54
  59.4 1.7 %collective-permute-done.14 = bf16[512,256]{1,0:T(8,128)(2,1)S(1)} collective-permute-done((bf16[512,256]{1,0:T(8,128)(2,1)S(1)}, bf16[512,256]{1,0:T(8,128)(2,1)S(1)}, u32[]{:S(2)}, u32[]{:S(2)}) %collective-permute-start.14) | collective-permute-done | bytes 262176 | tf_op jit(solution)/shard_map/ppermute | solution.py:54
  62.3 1.7 %collective-permute-start.18 = (bf16[512,256]{1,0:T(8,128)(2,1)S(1)}, bf16[512,256]{1,0:T(8,128)(2,1)S(1)}, u32[]{:S(2)}, u32[]{:S(2)}) collective-permute-start(bf16[512,256]{1,0:T(8,128)(2,1)S(1)} %add_convert_fusion.1.rest_0_), channel_id=1, source_target_pairs={{0,3},{1,0},{2,1},{3,2},{4,7},{5,4},{6,5},{7,6},{8,9},{9,10},{10,1... | collective-permute-start | bytes 786440 | tf_op jit(solution)/shard_map/ppermute | solution.py:54
  65.7 3.0 %collective-permute-start.26 = (bf16[256,512]{1,0:T(8,128)(2,1)S(1)}, bf16[256,512]{1,0:T(8,128)(2,1)S(1)}, u32[]{:S(2)}, u32[]{:S(2)}) collective-permute-start(bf16[256,512]{1,0:T(8,128)(2,1)S(1)} %pad_maximum_fusion.rest_8_), channel_id=1, source_target_pairs={{0,96},{1,97},{2,98},{3,99},{4,100},{5,101},{6,102},{7,103},{8,40}... | collective-permute-start | bytes 786440 | tf_op jit(solution)/shard_map/ppermute | solution.py:54
  68.7 3.6 %collective-permute-done.20.rest_4_ = bf16[512,256]{1,0:T(8,128)(2,1)S(1)} collective-permute-done((bf16[512,256]{1,0:T(8,128)(2,1)S(1)}, bf16[512,256]{1,0:T(8,128)(2,1)S(1)}, u32[]{:S(2)}, u32[]{:S(2)}) %collective-permute-start.20) | collective-permute-done | bytes 262176 | tf_op jit(solution)/shard_map/ppermute | solution.py:54
  72.3 1.6 %collective-permute-start.21 = (bf16[512,256]{1,0:T(8,128)(2,1)S(1)}, bf16[512,256]{1,0:T(8,128)(2,1)S(1)}, u32[]{:S(2)}, u32[]{:S(2)}) collective-permute-start(bf16[512,256]{1,0:T(8,128)(2,1)S(1)} %collective-permute-done.20.rest_4_), channel_id=1, source_target_pairs={{0,1},{1,2},{2,3},{3,0},{4,5},{5,6},{6,7},{7,4},{8,11},{9,8},{10,9... | collective-permute-start | bytes 786440 | tf_op jit(solution)/shard_map/ppermute | solution.py:54
  77.4 2.4 %collective-permute-done.25.rest_9_ = bf16[256,512]{1,0:T(8,128)(2,1)S(1)} collective-permute-done((bf16[256,512]{1,0:T(8,128)(2,1)S(1)}, bf16[256,512]{1,0:T(8,128)(2,1)S(1)}, u32[]{:S(2)}, u32[]{:S(2)}) %collective-permute-start.25) | collective-permute-done | bytes 262176 | tf_op jit(solution)/shard_map/ppermute | solution.py:54
  81.3 3.3 %collective-permute-done.22.rest_6_ = bf16[512,256]{1,0:T(8,128)(2,1)S(1)} collective-permute-done((bf16[512,256]{1,0:T(8,128)(2,1)S(1)}, bf16[512,256]{1,0:T(8,128)(2,1)S(1)}, u32[]{:S(2)}, u32[]{:S(2)}) %collective-permute-start.22) | collective-permute-done | bytes 262176 | tf_op jit(solution)/shard_map/ppermute | solution.py:54
  86.2 1.8 %collective-permute-done.30.rest_14_ = bf16[256,512]{1,0:T(8,128)(2,1)S(1)} collective-permute-done((bf16[256,512]{1,0:T(8,128)(2,1)S(1)}, bf16[256,512]{1,0:T(8,128)(2,1)S(1)}, u32[]{:S(2)}, u32[]{:S(2)}) %collective-permute-start.30) | collective-permute-done | bytes 262176 | tf_op jit(solution)/shard_map/ppermute | solution.py:54
  88.1 4.0 %collective-permute-done.23.rest_7_ = bf16[512,256]{1,0:T(8,128)(2,1)S(1)} collective-permute-done((bf16[512,256]{1,0:T(8,128)(2,1)S(1)}, bf16[512,256]{1,0:T(8,128)(2,1)S(1)}, u32[]{:S(2)}, u32[]{:S(2)}) %collective-permute-start.23) | collective-permute-done | bytes 262176 | tf_op jit(solution)/shard_map/ppermute | solution.py:54
  92.6 1.9 %square_part.1 = (f32[512,256]{1,0:T(8,128)S(1)}, bf16[512,256]{1,0:T(8,128)(2,1)S(1)}) custom-call(s32[5]{0:T(128)S(1)} %stack.23.where, bf16[512,256]{1,0:T(8,128)(2,1)S(1)} %add_convert_fusion.1.rest_0_, bf16[512,256]{1,0:T(8,128)(2,1)S(1)} %collective-permute-done.17.rest_1_, bf16[512,256]{1,0:T(8,128)(2,1)S(1)} %collective-permute-done.18.rest_2_, ...), custom_call_target="tpu_custom_call" | custom-call | flops 1073741824 | bytes 4194304 | tf_op jit(solution)/shard_map/square_part/pallas_call | solution.py:154
  98.4 7.8 %collective-permute-done.37.rest_4_ = bf16[512,256]{1,0:T(8,128)(2,1)S(1)} collective-permute-done((bf16[512,256]{1,0:T(8,128)(2,1)S(1)}, bf16[512,256]{1,0:T(8,128)(2,1)S(1)}, u32[]{:S(2)}, u32[]{:S(2)}) %collective-permute-start.37) | collective-permute-done | bytes 262176 | tf_op jit(solution)/shard_map/ppermute | solution.py:54
  106.9 2.5 %collective-permute-start.35 = (bf16[512,256]{1,0:T(8,128)(2,1)S(1)}, bf16[512,256]{1,0:T(8,128)(2,1)S(1)}, u32[]{:S(2)}, u32[]{:S(2)}) collective-permute-start(bf16[512,256]{1,0:T(8,128)(2,1)S(1)} %collective-permute-done.33.rest_0_), channel_id=1, source_target_pairs={{0,3},{1,0},{2,1},{3,2},{4,7},{5,4},{6,5},{7,6},{8,9},{9,10},{10,1... | collective-permute-start | bytes 786440 | tf_op jit(solution)/shard_map/ppermute | solution.py:54
  109.4 6.4 %collective-permute-done.38.rest_5_ = bf16[512,256]{1,0:T(8,128)(2,1)S(1)} collective-permute-done((bf16[512,256]{1,0:T(8,128)(2,1)S(1)}, bf16[512,256]{1,0:T(8,128)(2,1)S(1)}, u32[]{:S(2)}, u32[]{:S(2)}) %collective-permute-start.38) | collective-permute-done | bytes 262176 | tf_op jit(solution)/shard_map/ppermute | solution.py:54
  116.2 1.8 %collective-permute-start.39 = (bf16[512,256]{1,0:T(8,128)(2,1)S(1)}, bf16[512,256]{1,0:T(8,128)(2,1)S(1)}, u32[]{:S(2)}, u32[]{:S(2)}) collective-permute-start(bf16[512,256]{1,0:T(8,128)(2,1)S(1)} %collective-permute-done.35.rest_2_), channel_id=1, source_target_pairs={{0,4},{1,5},{2,6},{3,7},{4,0},{5,1},{6,2},{7,3},{8,12},{9,13},{10,... | collective-permute-start | bytes 786440 | tf_op jit(solution)/shard_map/ppermute | solution.py:54
  120.0 3.4 %collective-permute-done.40.rest_7_ = bf16[512,256]{1,0:T(8,128)(2,1)S(1)} collective-permute-done((bf16[512,256]{1,0:T(8,128)(2,1)S(1)}, bf16[512,256]{1,0:T(8,128)(2,1)S(1)}, u32[]{:S(2)}, u32[]{:S(2)}) %collective-permute-start.40) | collective-permute-done | bytes 262176 | tf_op jit(solution)/shard_map/ppermute | solution.py:54
  123.4 1.7 %collective-permute-done.39.rest_6_ = bf16[512,256]{1,0:T(8,128)(2,1)S(1)} collective-permute-done((bf16[512,256]{1,0:T(8,128)(2,1)S(1)}, bf16[512,256]{1,0:T(8,128)(2,1)S(1)}, u32[]{:S(2)}, u32[]{:S(2)}) %collective-permute-start.39) | collective-permute-done | bytes 262176 | tf_op jit(solution)/shard_map/ppermute | solution.py:54
  125.1 1.9 %collective-permute-done.36.rest_3_ = bf16[512,256]{1,0:T(8,128)(2,1)S(1)} collective-permute-done((bf16[512,256]{1,0:T(8,128)(2,1)S(1)}, bf16[512,256]{1,0:T(8,128)(2,1)S(1)}, u32[]{:S(2)}, u32[]{:S(2)}) %collective-permute-start.36) | collective-permute-done | bytes 262176 | tf_op jit(solution)/shard_map/ppermute | solution.py:54
  127.0 1.9 %apply_other.2 = bf16[256,768]{1,0:T(8,128)(2,1)S(1)} custom-call(s32[5]{0:T(128)S(1)} %stack.23.where, bf16[512,256]{1,0:T(8,128)(2,1)S(1)} %collective-permute-done.33.rest_0_, bf16[512,256]{1,0:T(8,128)(2,1)S(1)} %collective-permute-done.34.rest_1_, bf16[512,256]{1,0:T(8,128)(2,1)S(1)} %collective-permute-done.35.rest_2_, ...), custom_call_target="tpu_custom_call" | custom-call | flops 805306368 | bytes 5636096 | tf_op jit(solution)/shard_map/apply_other/pallas_call | solution.py:170
  128.9 1.9 %apply_other.3 = bf16[256,768]{1,0:T(8,128)(2,1)S(1)} custom-call(s32[5]{0:T(128)S(1)} %stack.23.where, bf16[512,256]{1,0:T(8,128)(2,1)S(1)} %collective-permute-done.33.rest_0_, bf16[512,256]{1,0:T(8,128)(2,1)S(1)} %collective-permute-done.34.rest_1_, bf16[512,256]{1,0:T(8,128)(2,1)S(1)} %collective-permute-done.35.rest_2_, ...), custom_call_target="tpu_custom_call" | custom-call | flops 805306368 | bytes 5636096 | tf_op jit(solution)/shard_map/apply_other/pallas_call | solution.py:170
  131.4 3.0 %apply_own.1 = f32[256,1536]{1,0:T(8,128)S(1)} custom-call(s32[5]{0:T(128)S(1)} %stack.23.where, bf16[512,256]{1,0:T(8,128)(2,1)S(1)} %collective-permute-done.33.rest_0_, bf16[512,256]{1,0:T(8,128)(2,1)S(1)} %collective-permute-done.34.rest_1_, bf16[512,256]{1,0:T(8,128)(2,1)S(1)} %collective-permute-done.35.rest_2_, ...), custom_call_target="tpu_custom_call" | custom-call | flops 1610612736 | bytes 9175040 | tf_op jit(solution)/shard_map/apply_own/pallas_call | solution.py:170
  (78 shorter events, 29.4 us)
Async XLA Ops:
  0.1 21.0 %collective-permute-start.3 = (bf16[256,1536]{1,0:T(8,128)(2,1)}, bf16[256,1536]{1,0:T(8,128)(2,1)S(1)}, u32[]{:S(2)}, u32[]{:S(2)}) collective-permute-start(bf16[256,1536]{1,0:T(8,128)(2,1)} %rest_8_.2), channel_id=1, source_target_pairs={{0,16},{1,17},{2,18},{3,19},{4,20},{5,21},{6,22},{7,23},{8,24},{9,... | collective-permute-start | bytes 2359304 | tf_op jit(solution)/shard_map/ppermute | solution.py:54
  3.4 20.4 %collective-permute-start.1 = (bf16[256,1536]{1,0:T(8,128)(2,1)}, bf16[256,1536]{1,0:T(8,128)(2,1)S(1)}, u32[]{:S(2)}, u32[]{:S(2)}) collective-permute-start(bf16[256,1536]{1,0:T(8,128)(2,1)} %rest_8_.2), channel_id=1, source_target_pairs={{0,96},{1,97},{2,98},{3,99},{4,100},{5,101},{6,102},{7,103},{8,40}... | collective-permute-start | bytes 2359304 | tf_op jit(solution)/shard_map/ppermute | solution.py:54
  6.1 17.7 %collective-permute-start = (bf16[256,1536]{1,0:T(8,128)(2,1)}, bf16[256,1536]{1,0:T(8,128)(2,1)S(1)}, u32[]{:S(2)}, u32[]{:S(2)}) collective-permute-start(bf16[256,1536]{1,0:T(8,128)(2,1)} %rest_8_.2), channel_id=1, source_target_pairs={{0,8},{1,9},{2,10},{3,11},{4,12},{5,13},{6,14},{7,15},{8,0},{9,1},... | collective-permute-start | bytes 2359304 | tf_op jit(solution)/shard_map/ppermute | solution.py:54
  7.3 12.3 %collective-permute-start.5 = (bf16[128,1536]{1,0:T(8,128)(2,1)S(1)}, bf16[128,1536]{1,0:T(8,128)(2,1)S(1)}, u32[]{:S(2)}, u32[]{:S(2)}) collective-permute-start(bf16[128,1536]{1,0:T(8,128)(2,1)S(1)} %get-tuple-element.41), channel_id=1, source_target_pairs={{0,32},{1,33},{2,34},{3,35},{4,36},{5,37},{6,38},{7,39},{8,104},{9... | collective-permute-start | bytes 1179656 | tf_op jit(solution)/shard_map/ppermute | solution.py:54
  7.4 16.4 %collective-permute-start.2 = (bf16[128,1536]{1,0:T(8,128)(2,1)S(1)}, bf16[128,1536]{1,0:T(8,128)(2,1)S(1)}, u32[]{:S(2)}, u32[]{:S(2)}) collective-permute-start(bf16[128,1536]{1,0:T(8,128)(2,1)S(1)} %get-tuple-element.42), channel_id=1, source_target_pairs={{0,32},{1,33},{2,34},{3,35},{4,36},{5,37},{6,38},{7,39},{8,104},{9... | collective-permute-start | bytes 1179656 | tf_op jit(solution)/shard_map/ppermute | solution.py:54
  19.6 9.0 %collective-permute-start.6 = (bf16[128,1536]{1,0:T(8,128)(2,1)S(1)}, bf16[128,1536]{1,0:T(8,128)(2,1)S(1)}, u32[]{:S(2)}, u32[]{:S(2)}) collective-permute-start(bf16[128,1536]{1,0:T(8,128)(2,1)S(1)} %collective-permute-done.5), channel_id=1, source_target_pairs={{0,32},{1,33},{2,34},{3,35},{4,36},{5,37},{6,38},{7,39},{8,104},{9... | collective-permute-start | bytes 1179656 | tf_op jit(solution)/shard_map/ppermute | solution.py:54
  21.1 11.7 %collective-permute-start.4 = (bf16[256,1536]{1,0:T(8,128)(2,1)S(1)}, bf16[256,1536]{1,0:T(8,128)(2,1)S(1)}, u32[]{:S(2)}, u32[]{:S(2)}) collective-permute-start(bf16[256,1536]{1,0:T(8,128)(2,1)S(1)} %collective-permute-done.3.across.rest_12_), channel_id=1, source_target_pairs={{0,8},{1,9},{2,10},{3,11},{4,12},{5,13},{6,14},{7,15},{8,0},{9,1},... | collective-permute-start | bytes 2359304 | tf_op jit(solution)/shard_map/ppermute | solution.py:54
  23.8 9.0 %collective-permute-start.7 = (bf16[128,1536]{1,0:T(8,128)(2,1)S(1)}, bf16[128,1536]{1,0:T(8,128)(2,1)S(1)}, u32[]{:S(2)}, u32[]{:S(2)}) collective-permute-start(bf16[128,1536]{1,0:T(8,128)(2,1)S(1)} %collective-permute-done.2), channel_id=1, source_target_pairs={{0,32},{1,33},{2,34},{3,35},{4,36},{5,37},{6,38},{7,39},{8,104},{9... | collective-permute-start | bytes 1179656 | tf_op jit(solution)/shard_map/ppermute | solution.py:54
  37.0 8.0 %collective-permute-start.12 = (bf16[512,256]{1,0:T(8,128)(2,1)S(1)}, bf16[512,256]{1,0:T(8,128)(2,1)S(1)}, u32[]{:S(2)}, u32[]{:S(2)}) collective-permute-start(bf16[512,256]{1,0:T(8,128)(2,1)S(1)} %get-tuple-element.35), channel_id=1, source_target_pairs={{0,3},{1,0},{2,1},{3,2},{4,7},{5,4},{6,5},{7,6},{8,9},{9,10},{10,1... | collective-permute-start | bytes 786440 | tf_op jit(solution)/shard_map/ppermute | solution.py:54
  41.5 19.8 %collective-permute-start.16 = (bf16[256,1536]{1,0:T(8,128)(2,1)S(1)}, bf16[256,1536]{1,0:T(8,128)(2,1)S(1)}, u32[]{:S(2)}, u32[]{:S(2)}) collective-permute-start(bf16[256,1536]{1,0:T(8,128)(2,1)S(1)} %collective-permute-done.3.across.rest_12_), channel_id=1, source_target_pairs={{0,96},{1,97},{2,98},{3,99},{4,100},{5,101},{6,102},{7,103},{8,40}... | collective-permute-start | bytes 2359304 | tf_op jit(solution)/shard_map/ppermute | solution.py:54
  43.0 18.5 %collective-permute-start.15 = (bf16[256,1536]{1,0:T(8,128)(2,1)S(1)}, bf16[256,1536]{1,0:T(8,128)(2,1)S(1)}, u32[]{:S(2)}, u32[]{:S(2)}) collective-permute-start(bf16[256,1536]{1,0:T(8,128)(2,1)S(1)} %collective-permute-done.3.across.rest_12_), channel_id=1, source_target_pairs={{0,32},{1,33},{2,34},{3,35},{4,36},{5,37},{6,38},{7,39},{8,104},{9... | collective-permute-start | bytes 2359304 | tf_op jit(solution)/shard_map/ppermute | solution.py:54
  43.5 8.2 %collective-permute-start.10 = (bf16[512,256]{1,0:T(8,128)(2,1)S(1)}, bf16[512,256]{1,0:T(8,128)(2,1)S(1)}, u32[]{:S(2)}, u32[]{:S(2)}) collective-permute-start(bf16[512,256]{1,0:T(8,128)(2,1)S(1)} %get-tuple-element.32), channel_id=1, source_target_pairs={{0,4},{1,5},{2,6},{3,7},{4,0},{5,1},{6,2},{7,3},{8,12},{9,13},{10,... | collective-permute-start | bytes 786440 | tf_op jit(solution)/shard_map/ppermute | solution.py:54
  45.1 8.4 %collective-permute-start.13 = (bf16[512,256]{1,0:T(8,128)(2,1)S(1)}, bf16[512,256]{1,0:T(8,128)(2,1)S(1)}, u32[]{:S(2)}, u32[]{:S(2)}) collective-permute-start(bf16[512,256]{1,0:T(8,128)(2,1)S(1)} %add_convert_fusion.3), channel_id=1, source_target_pairs={{0,3},{1,0},{2,1},{3,2},{4,7},{5,4},{6,5},{7,6},{8,9},{9,10},{10,1... | collective-permute-start | bytes 786440 | tf_op jit(solution)/shard_map/ppermute | solution.py:54
  48.9 9.0 %collective-permute-start.9 = (bf16[512,256]{1,0:T(8,128)(2,1)S(1)}, bf16[512,256]{1,0:T(8,128)(2,1)S(1)}, u32[]{:S(2)}, u32[]{:S(2)}) collective-permute-start(bf16[512,256]{1,0:T(8,128)(2,1)S(1)} %add_convert_fusion.5), channel_id=1, source_target_pairs={{0,3},{1,0},{2,1},{3,2},{4,7},{5,4},{6,5},{7,6},{8,9},{9,10},{10,1... | collective-permute-start | bytes 786440 | tf_op jit(solution)/shard_map/ppermute | solution.py:54
  61.6 10.7 %collective-permute-start.20 = (bf16[512,256]{1,0:T(8,128)(2,1)S(1)}, bf16[512,256]{1,0:T(8,128)(2,1)S(1)}, u32[]{:S(2)}, u32[]{:S(2)}) collective-permute-start(bf16[512,256]{1,0:T(8,128)(2,1)S(1)} %add_convert_fusion.1.rest_0_), channel_id=1, source_target_pairs={{0,16},{1,17},{2,18},{3,19},{4,20},{5,21},{6,22},{7,23},{8,24},{9,... | collective-permute-start | bytes 786440 | tf_op jit(solution)/shard_map/ppermute | solution.py:54
  62.3 10.0 %collective-permute-start.18 = (bf16[512,256]{1,0:T(8,128)(2,1)S(1)}, bf16[512,256]{1,0:T(8,128)(2,1)S(1)}, u32[]{:S(2)}, u32[]{:S(2)}) collective-permute-start(bf16[512,256]{1,0:T(8,128)(2,1)S(1)} %add_convert_fusion.1.rest_0_), channel_id=1, source_target_pairs={{0,3},{1,0},{2,1},{3,2},{4,7},{5,4},{6,5},{7,6},{8,9},{9,10},{10,1... | collective-permute-start | bytes 786440 | tf_op jit(solution)/shard_map/ppermute | solution.py:54
  64.0 9.9 %collective-permute-start.17 = (bf16[512,256]{1,0:T(8,128)(2,1)S(1)}, bf16[512,256]{1,0:T(8,128)(2,1)S(1)}, u32[]{:S(2)}, u32[]{:S(2)}) collective-permute-start(bf16[512,256]{1,0:T(8,128)(2,1)S(1)} %add_convert_fusion.1.rest_0_), channel_id=1, source_target_pairs={{0,1},{1,2},{2,3},{3,0},{4,5},{5,6},{6,7},{7,4},{8,11},{9,8},{10,9... | collective-permute-start | bytes 786440 | tf_op jit(solution)/shard_map/ppermute | solution.py:54
  64.3 11.5 %collective-permute-start.28 = (bf16[256,512]{1,0:T(8,128)(2,1)S(1)}, bf16[256,512]{1,0:T(8,128)(2,1)S(1)}, u32[]{:S(2)}, u32[]{:S(2)}) collective-permute-start(bf16[256,512]{1,0:T(8,128)(2,1)S(1)} %pad_maximum_fusion.rest_8_), channel_id=1, source_target_pairs={{0,4},{1,5},{2,6},{3,7},{4,0},{5,1},{6,2},{7,3},{8,12},{9,13},{10,... | collective-permute-start | bytes 786440 | tf_op jit(solution)/shard_map/ppermute | solution.py:54
  65.7 10.9 %collective-permute-start.26 = (bf16[256,512]{1,0:T(8,128)(2,1)S(1)}, bf16[256,512]{1,0:T(8,128)(2,1)S(1)}, u32[]{:S(2)}, u32[]{:S(2)}) collective-permute-start(bf16[256,512]{1,0:T(8,128)(2,1)S(1)} %pad_maximum_fusion.rest_8_), channel_id=1, source_target_pairs={{0,96},{1,97},{2,98},{3,99},{4,100},{5,101},{6,102},{7,103},{8,40}... | collective-permute-start | bytes 786440 | tf_op jit(solution)/shard_map/ppermute | solution.py:54
  72.3 8.3 %collective-permute-start.21 = (bf16[512,256]{1,0:T(8,128)(2,1)S(1)}, bf16[512,256]{1,0:T(8,128)(2,1)S(1)}, u32[]{:S(2)}, u32[]{:S(2)}) collective-permute-start(bf16[512,256]{1,0:T(8,128)(2,1)S(1)} %collective-permute-done.20.rest_4_), channel_id=1, source_target_pairs={{0,1},{1,2},{2,3},{3,0},{4,5},{5,6},{6,7},{7,4},{8,11},{9,8},{10,9... | collective-permute-start | bytes 786440 | tf_op jit(solution)/shard_map/ppermute | solution.py:54
  73.9 10.6 %collective-permute-start.22 = (bf16[512,256]{1,0:T(8,128)(2,1)S(1)}, bf16[512,256]{1,0:T(8,128)(2,1)S(1)}, u32[]{:S(2)}, u32[]{:S(2)}) collective-permute-start(bf16[512,256]{1,0:T(8,128)(2,1)S(1)} %collective-permute-done.18.rest_2_), channel_id=1, source_target_pairs={{0,16},{1,17},{2,18},{3,19},{4,20},{5,21},{6,22},{7,23},{8,24},{9,... | collective-permute-start | bytes 786440 | tf_op jit(solution)/shard_map/ppermute | solution.py:54
  75.8 8.8 %collective-permute-start.29 = (bf16[256,512]{1,0:T(8,128)(2,1)S(1)}, bf16[256,512]{1,0:T(8,128)(2,1)S(1)}, u32[]{:S(2)}, u32[]{:S(2)}) collective-permute-start(bf16[256,512]{1,0:T(8,128)(2,1)S(1)} %collective-permute-done.28.rest_12_), channel_id=1, source_target_pairs={{0,32},{1,33},{2,34},{3,35},{4,36},{5,37},{6,38},{7,39},{8,104},{9... | collective-permute-start | bytes 786440 | tf_op jit(solution)/shard_map/ppermute | solution.py:54
  76.6 9.6 %collective-permute-start.19 = (bf16[512,256]{1,0:T(8,128)(2,1)S(1)}, bf16[512,256]{1,0:T(8,128)(2,1)S(1)}, u32[]{:S(2)}, u32[]{:S(2)}) collective-permute-start(bf16[512,256]{1,0:T(8,128)(2,1)S(1)} %collective-permute-done.17.rest_1_), channel_id=1, source_target_pairs={{0,1},{1,2},{2,3},{3,0},{4,5},{5,6},{6,7},{7,4},{8,11},{9,8},{10,9... | collective-permute-start | bytes 786440 | tf_op jit(solution)/shard_map/ppermute | solution.py:54
  79.9 8.1 %collective-permute-start.30 = (bf16[256,512]{1,0:T(8,128)(2,1)S(1)}, bf16[256,512]{1,0:T(8,128)(2,1)S(1)}, u32[]{:S(2)}, u32[]{:S(2)}) collective-permute-start(bf16[256,512]{1,0:T(8,128)(2,1)S(1)} %collective-permute-done.26.rest_10_), channel_id=1, source_target_pairs={{0,4},{1,5},{2,6},{3,7},{4,0},{5,1},{6,2},{7,3},{8,12},{9,13},{10,... | collective-permute-start | bytes 786440 | tf_op jit(solution)/shard_map/ppermute | solution.py:54
  84.6 8.1 %collective-permute-start.31 = (bf16[256,512]{1,0:T(8,128)(2,1)S(1)}, bf16[256,512]{1,0:T(8,128)(2,1)S(1)}, u32[]{:S(2)}, u32[]{:S(2)}) collective-permute-start(bf16[256,512]{1,0:T(8,128)(2,1)S(1)} %collective-permute-done.29.rest_13_), channel_id=1, source_target_pairs={{0,32},{1,33},{2,34},{3,35},{4,36},{5,37},{6,38},{7,39},{8,104},{9... | collective-permute-start | bytes 786440 | tf_op jit(solution)/shard_map/ppermute | solution.py:54
  96.3 9.9 %collective-permute-start.37 = (bf16[512,256]{1,0:T(8,128)(2,1)S(1)}, bf16[512,256]{1,0:T(8,128)(2,1)S(1)}, u32[]{:S(2)}, u32[]{:S(2)}) collective-permute-start(bf16[512,256]{1,0:T(8,128)(2,1)S(1)} %add_convert_fusion), channel_id=1, source_target_pairs={{0,4},{1,5},{2,6},{3,7},{4,20},{5,21},{6,22},{7,23},{8,12},{9,13},... | collective-permute-start | bytes 786440 | tf_op jit(solution)/shard_map/ppermute | solution.py:54
  97.0 9.9 %collective-permute-start.33 = (bf16[512,256]{1,0:T(8,128)(2,1)S(1)}, bf16[512,256]{1,0:T(8,128)(2,1)S(1)}, u32[]{:S(2)}, u32[]{:S(2)}) collective-permute-start(bf16[512,256]{1,0:T(8,128)(2,1)S(1)} %add_convert_fusion), channel_id=1, source_target_pairs={{0,0},{1,1},{2,2},{3,3},{4,16},{5,17},{6,18},{7,19},{8,8},{9,9},{1... | collective-permute-start | bytes 786440 | tf_op jit(solution)/shard_map/ppermute | solution.py:54
  97.7 22.3 %collective-permute-start.41 = (bf16[256,1536]{1,0:T(8,128)(2,1)S(1)}, bf16[256,1536]{1,0:T(8,128)(2,1)S(1)}, u32[]{:S(2)}, u32[]{:S(2)}) collective-permute-start(bf16[256,1536]{1,0:T(8,128)(2,1)S(1)} %collective-permute-done.15.rest_13_), channel_id=1, source_target_pairs={{0,32},{1,33},{2,34},{3,35},{4,36},{5,37},{6,38},{7,39},{8,104},{9... | collective-permute-start | bytes 2359304 | tf_op jit(solution)/shard_map/ppermute | solution.py:54
  106.2 9.6 %collective-permute-start.38 = (bf16[512,256]{1,0:T(8,128)(2,1)S(1)}, bf16[512,256]{1,0:T(8,128)(2,1)S(1)}, u32[]{:S(2)}, u32[]{:S(2)}) collective-permute-start(bf16[512,256]{1,0:T(8,128)(2,1)S(1)} %collective-permute-done.37.rest_4_), channel_id=1, source_target_pairs={{0,1},{1,2},{2,3},{3,0},{4,5},{5,6},{6,7},{7,4},{8,11},{9,8},{10,9... | collective-permute-start | bytes 786440 | tf_op jit(solution)/shard_map/ppermute | solution.py:54
  106.9 9.3 %collective-permute-start.35 = (bf16[512,256]{1,0:T(8,128)(2,1)S(1)}, bf16[512,256]{1,0:T(8,128)(2,1)S(1)}, u32[]{:S(2)}, u32[]{:S(2)}) collective-permute-start(bf16[512,256]{1,0:T(8,128)(2,1)S(1)} %collective-permute-done.33.rest_0_), channel_id=1, source_target_pairs={{0,3},{1,0},{2,1},{3,2},{4,7},{5,4},{6,5},{7,6},{8,9},{9,10},{10,1... | collective-permute-start | bytes 786440 | tf_op jit(solution)/shard_map/ppermute | solution.py:54
  109.4 10.0 %collective-permute-start.34 = (bf16[512,256]{1,0:T(8,128)(2,1)S(1)}, bf16[512,256]{1,0:T(8,128)(2,1)S(1)}, u32[]{:S(2)}, u32[]{:S(2)}) collective-permute-start(bf16[512,256]{1,0:T(8,128)(2,1)S(1)} %collective-permute-done.33.rest_0_), channel_id=1, source_target_pairs={{0,1},{1,2},{2,3},{3,0},{4,5},{5,6},{6,7},{7,4},{8,11},{9,8},{10,9... | collective-permute-start | bytes 786440 | tf_op jit(solution)/shard_map/ppermute | solution.py:54
  116.2 8.9 %collective-permute-start.39 = (bf16[512,256]{1,0:T(8,128)(2,1)S(1)}, bf16[512,256]{1,0:T(8,128)(2,1)S(1)}, u32[]{:S(2)}, u32[]{:S(2)}) collective-permute-start(bf16[512,256]{1,0:T(8,128)(2,1)S(1)} %collective-permute-done.35.rest_2_), channel_id=1, source_target_pairs={{0,4},{1,5},{2,6},{3,7},{4,0},{5,1},{6,2},{7,3},{8,12},{9,13},{10,... | collective-permute-start | bytes 786440 | tf_op jit(solution)/shard_map/ppermute | solution.py:54
  (13 other events, 99.8 us)

commit v9 on v8

--- a/solution.py
+++ b/solution.py
@@ -15,7 +15,7 @@
 NX, NY, NC, NZ = 4, 2, 2, 4
 BLOCK = 256
 TILE = 2 * BLOCK
-STRIP = 384
+STRIP = 768
 MIB = 1 << 20
 
 
@@ -72,13 +72,24 @@
     return lax.dot_general(left, right, (((1,), (0,)), ((), ())), preferred_element_type=jnp.float32)
 
 
-def gram_kernel(where, own, other, across, across_other, fore, back, far, *rest):
+def gram_near_kernel(own, other, fore, back, out):
+    for r, rows in enumerate((own, other)):
+        for q, cols in enumerate((own, fore, back)):
+            part = nt(rows[...], cols[...])
+            out[q, r * BLOCK : (r + 1) * BLOCK] = part.astype(out.dtype)
+
+
+def gram_kernel(where, own, other, across, across_other, fore, back, far, near, *rest):
     outs, tiles = rest[:8], rest[8]
     x, yh, core, yl, z = (where[i] for i in range(5))
-    for r, rows in enumerate((own, other, across, across_other)):
+    tiles[0, :3] = near[...]
+    for r, rows in enumerate((own, other)):
+        part = nt(rows[...], far[...])
+        tiles[0, 3, r * BLOCK : (r + 1) * BLOCK] = part.astype(tiles.dtype)
+    for r, rows in enumerate((across, across_other)):
         for q, cols in enumerate((own, fore, back, far)):
             part = nt(rows[...], cols[...])
-            tiles[r // 2, q, (r % 2) * BLOCK : (r % 2 + 1) * BLOCK] = part.astype(tiles.dtype)
+            tiles[1, q, r * BLOCK : (r + 1) * BLOCK] = part.astype(tiles.dtype)
     for index, out in enumerate(outs):
         row = lax.rem(yl + index // 4 + yh, 2)
         col = place(z + ahead(index % 4, core) - x, core)
@@ -102,22 +113,21 @@
     theirs[BLOCK:] = total[:BLOCK, BLOCK:].astype(theirs.dtype)
 
 
-def apply_kernel(other_rows, begin, where, *rest):
-    mixing, blocks, (out, held) = rest[:8], rest[8:16], rest[16:]
+def apply_kernel(begin, where, *rest):
+    mixing, blocks, (mine, theirs, held) = rest[:8], rest[8:16], rest[16:]
     x, yh, core, yl, z = (where[i] for i in range(5))
     for index in range(8):
         row = lax.rem(yl + index // 4 + yh, 2)
         col = place(z + ahead(index % 4, core) - x, core)
-        held[row, col] = mixing[index][int(other_rows) * BLOCK : (int(other_rows) + 1) * BLOCK]
-
-    for start in range(0, out.shape[1], STRIP):
+        lanes = pl.ds(pl.multiple_of((row * 4 + col) * BLOCK, BLOCK), BLOCK)
+        held[:, lanes] = mixing[index][...]
+
+    for start in range(0, mine.shape[1], STRIP):
         columns = slice(begin + start, begin + start + STRIP)
-        total = jnp.zeros((BLOCK, STRIP), jnp.float32)
-        for index in range(8):
-            total += nn(held[index // 4, index % 4], blocks[index][:, columns])
-        if not other_rows:
-            total = total + linear_coef * blocks[0][:, columns].astype(jnp.float32)
-        out[:, start : start + STRIP] = total.astype(out.dtype)
+        total = nn(held[...], jnp.concatenate([block[:, columns] for block in blocks], axis=0))
+        theirs[:, start : start + STRIP] = total[BLOCK:].astype(theirs.dtype)
+        total = total[:BLOCK] + linear_coef * blocks[0][:, columns].astype(jnp.float32)
+        mine[:, start : start + STRIP] = total
 
 
 def params(mib):
@@ -136,18 +146,31 @@
     return pl.CostEstimate(flops=flops, bytes_accessed=moved, transcendentals=0)
 
 
-def gram_tiles(where, own, other, across, across_other, fore, back, far):
+def gram_near(own, other, fore, back):
     depth = own.shape[1]
     return pl.pallas_call(
+        gram_near_kernel,
+        in_specs=[whole() for _ in range(4)],
+        out_specs=whole(),
+        out_shape=jax.ShapeDtypeStruct((3, TILE, BLOCK), jnp.bfloat16),
+        compiler_params=params(24),
+        cost_estimate=cost(2 * 3 * BLOCK * TILE * depth, 4 * BLOCK * depth * 2 + 3 * BLOCK * TILE * 2),
+        name="gram_near",
+    )(own, other, fore, back)
+
+
+def gram_tiles(where, own, other, across, across_other, fore, back, far, near):
+    depth = own.shape[1]
+    return pl.pallas_call(
         gram_kernel,
-        in_specs=[smem()] + [whole() for _ in range(7)],
+        in_specs=[smem()] + [whole() for _ in range(8)],
         out_specs=[whole() for _ in range(8)],
         out_shape=[jax.ShapeDtypeStruct((TILE, BLOCK), jnp.bfloat16) for _ in range(8)],
         scratch_shapes=[pltpu.VMEM((2, 4, TILE, BLOCK), jnp.bfloat16)],
         compiler_params=params(24),
-        cost_estimate=cost(2 * 8 * BLOCK * TILE * depth, 7 * BLOCK * depth * 2 + 8 * BLOCK * TILE * 2),
+        cost_estimate=cost(2 * 5 * BLOCK * TILE * depth, 7 * BLOCK * depth * 2 + 11 * BLOCK * TILE * 2),
         name="gram_tiles",
-    )(where, own, other, across, across_other, fore, back, far)
+    )(where, own, other, across, across_other, fore, back, far, near)
 
 
 def square_part(where, left, right):
@@ -166,16 +189,19 @@
     )(where, *left, *right)
 
 
-def apply_part(other_rows, begin, width, where, mixing, blocks):
-    return pl.pallas_call(
-        functools.partial(apply_kernel, other_rows, begin),
+def apply_part(begin, width, where, mixing, blocks):
+    return pl.pallas_call(
+        functools.partial(apply_kernel, begin),
         in_specs=[smem()] + [whole() for _ in range(16)],
-        out_specs=whole(),
-        out_shape=jax.ShapeDtypeStruct((BLOCK, width), jnp.bfloat16 if other_rows else jnp.float32),
-        scratch_shapes=[pltpu.VMEM((2, 4, BLOCK, BLOCK), jnp.bfloat16)],
-        compiler_params=params(24),
-        cost_estimate=cost(2 * 8 * BLOCK * BLOCK * width, 9 * BLOCK * width * 2 + 8 * BLOCK * TILE * 2),
-        name="apply_other" if other_rows else "apply_own",
+        out_specs=[whole(), whole()],
+        out_shape=[
+            jax.ShapeDtypeStruct((BLOCK, width), jnp.float32),
+            jax.ShapeDtypeStruct((BLOCK, width), jnp.bfloat16),
+        ],
+        scratch_shapes=[pltpu.VMEM((TILE, 8 * BLOCK), jnp.bfloat16)],
+        compiler_params=params(24),
+        cost_estimate=cost(2 * 8 * TILE * BLOCK * width, 11 * BLOCK * width * 2 + 8 * BLOCK * TILE * 2),
+        name="apply_part",
     )(where, *mixing, *blocks)
 
 
@@ -219,9 +245,11 @@
     top = send(iterate[:half], "x_fore")
     far = [send(top, "x_fore"), send(low, "x_fore")]
     fore = jnp.concatenate([top, low], axis=0)
+    near = gram_near(iterate, other, fore, back)
+    far[0], near = lax.optimization_barrier((far[0], near))
     far = jnp.concatenate(far, axis=0)
     rows = (iterate, other, across, send(across, "core"))
-    gram_left = sum_over_col(gram_tiles(where, *rows, fore, back, far))
+    gram_left = sum_over_col(gram_tiles(where, *rows, fore, back, far, near))
 
     across_fore, across_back = send(across, "x_fore"), send(across, "x_back")
     gram_left, across_fore, across_back = lax.optimization_barrier((gram_left, across_fore, across_back))
@@ -236,12 +264,11 @@
     pieces = gather_even(send(mixing, "turn"), "z", "yl", there)
     blocks = [iterate, fore, back, far, across, across_fore, across_back, across_far]
     depth = iterate.shape[1]
-    swapped = []
+    update = []
     for begin in (0, depth // 2):
-        swapped.append(send(apply_part(True, begin, depth // 2, where, pieces, blocks), "core"))
-    applied = apply_part(False, 0, depth, where, pieces, blocks)
-    update = applied + jnp.concatenate(swapped, axis=1).astype(jnp.float32)
-    return (math.sqrt(total_cols) * update).astype(jnp.bfloat16)
+        mine, theirs = apply_part(begin, depth // 2, where, pieces, blocks)
+        update.append(mine + send(theirs, "core").astype(jnp.float32))
+    return (math.sqrt(total_cols) * jnp.concatenate(update, axis=1)).astype(jnp.bfloat16)
 
 
 def solution(mesh):

time: 137 us -> 135 us (0.985)
  waiting for transfers between devices: 72.6 us -> 61.6 us
  starting transfers between devices: 46.9 us -> 56.6 us
    ppermute x44, waiting for transfers between devices: 72.6 us -> 61.6 us  [send(): return lax.ppermute(value, ('row', 'col'), pairs(MOVES[move]))]
    ppermute x44, starting transfers between devices: 46.9 us -> 56.6 us  [send(): return lax.ppermute(value, ('row', 'col'), pairs(MOVES[move]))]
  transfers between devices with their start and end apart: 44 -> 44, of which waited for: 27 -> 25; matrix products, arithmetic and copies ran while one was open for 1% -> 1% of each run, Pallas kernels for 4% -> 3%
where the time goes in v9:
time: 135 us; the launch traced here: 133 us
  waiting for transfers between devices  61.6 us (46%)
  starting transfers between devices  56.6 us (42%)
  Pallas kernels  11.6 us (9%)
  other arithmetic  1.68 us (1%)
  local copies, waits for them, and re-layouts  1.38 us (1%)
    ppermute x44, waiting for transfers between devices, send(): return lax.ppermute(value, ('row', 'col'), pairs(MOVES[move]))  61.6 us
    ppermute x44, starting transfers between devices, send(): return lax.ppermute(value, ('row', 'col'), pairs(MOVES[move]))  56.6 us
    pallas_call x2, Pallas kernels, apply_part(): pl.pallas_call(functools.partial(apply_kernel, begin), in_specs=[smem()]...  5.31 us
    pallas_call x1, Pallas kernels, gram_tiles(): pl.pallas_call(gram_kernel, in_specs=[smem()] + [whole() for _ in range(8...  2.97 us
  transfers between devices with their start and end apart: 44, of which 25 were waited for; matrix products, arithmetic and copies ran while one was open for 1% of the time, Pallas kernels for 3%

profile of v9, /device:TPU:0, one launch (start us, length us, event | category | flops | bytes accessed | tf_op | source)
XLA Modules:
  0.0 133.2 jit_solution(10272296503729943337)
XLA Ops:
  0.1 2.9 %collective-permute-start.1 = (bf16[256,1536]{1,0:T(8,128)(2,1)}, bf16[256,1536]{1,0:T(8,128)(2,1)S(1)}, u32[]{:S(2)}, u32[]{:S(2)}) collective-permute-start(bf16[256,1536]{1,0:T(8,128)(2,1)} %rest_8_.1), channel_id=1, source_target_pairs={{0,96},{1,97},{2,98},{3,99},{4,100},{5,101},{6,102},{7,103},{8,40}... | collective-permute-start | bytes 2359304 | tf_op jit(solution)/shard_map/ppermute | solution.py:54
  3.0 3.2 %collective-permute-start.3 = (bf16[256,1536]{1,0:T(8,128)(2,1)}, bf16[256,1536]{1,0:T(8,128)(2,1)S(1)}, u32[]{:S(2)}, u32[]{:S(2)}) collective-permute-start(bf16[256,1536]{1,0:T(8,128)(2,1)} %rest_8_.1), channel_id=1, source_target_pairs={{0,16},{1,17},{2,18},{3,19},{4,20},{5,21},{6,22},{7,23},{8,24},{9,... | collective-permute-start | bytes 2359304 | tf_op jit(solution)/shard_map/ppermute | solution.py:54
  8.2 9.0 %collective-permute-done.5 = bf16[128,1536]{1,0:T(8,128)(2,1)S(1)} collective-permute-done((bf16[128,1536]{1,0:T(8,128)(2,1)S(1)}, bf16[128,1536]{1,0:T(8,128)(2,1)S(1)}, u32[]{:S(2)}, u32[]{:S(2)}) %collective-permute-start.5) | collective-permute-done | bytes 393248 | tf_op jit(solution)/shard_map/ppermute | solution.py:54
  17.7 3.8 %collective-permute-done.2 = bf16[128,1536]{1,0:T(8,128)(2,1)S(1)} collective-permute-done((bf16[128,1536]{1,0:T(8,128)(2,1)S(1)}, bf16[128,1536]{1,0:T(8,128)(2,1)S(1)}, u32[]{:S(2)}, u32[]{:S(2)}) %collective-permute-start.2) | collective-permute-done | bytes 393248 | tf_op jit(solution)/shard_map/ppermute | solution.py:54
  26.3 4.2 %collective-permute-done.7 = bf16[128,1536]{1,0:T(8,128)(2,1)S(1)} collective-permute-done((bf16[128,1536]{1,0:T(8,128)(2,1)S(1)}, bf16[128,1536]{1,0:T(8,128)(2,1)S(1)}, u32[]{:S(2)}, u32[]{:S(2)}) %collective-permute-start.7) | collective-permute-done | bytes 393248 | tf_op jit(solution)/shard_map/ppermute | solution.py:54
  30.5 3.0 %gram_tiles.1 = (bf16[512,256]{1,0:T(8,128)(2,1)S(1)}, bf16[512,256]{1,0:T(8,128)(2,1)S(1)}, bf16[512,256]{1,0:T(8,128)(2,1)S(1)}, bf16[512,256]{1,0:T(8,128)(2,...) custom-call(s32[5]{0:T(128)S(1)} %stack.23.where, ...), custom_call_target="tpu_custom_call" | custom-call | flops 2013265920 | bytes 8388608 | tf_op jit(solution)/shard_map/gram_tiles/pallas_call | solution.py:164
  33.5 4.2 %collective-permute-start.12 = (bf16[512,256]{1,0:T(8,128)(2,1)S(1)}, bf16[512,256]{1,0:T(8,128)(2,1)S(1)}, u32[]{:S(2)}, u32[]{:S(2)}) collective-permute-start(bf16[512,256]{1,0:T(8,128)(2,1)S(1)} %get-tuple-element.43), channel_id=1, source_target_pairs={{0,3},{1,0},{2,1},{3,2},{4,7},{5,4},{6,5},{7,6},{8,9},{9,10},{10,1... | collective-permute-start | bytes 786440 | tf_op jit(solution)/shard_map/ppermute | solution.py:54
  38.1 3.2 %collective-permute-start.16 = (bf16[256,1536]{1,0:T(8,128)(2,1)S(1)}, bf16[256,1536]{1,0:T(8,128)(2,1)S(1)}, u32[]{:S(2)}, u32[]{:S(2)}) collective-permute-start(bf16[256,1536]{1,0:T(8,128)(2,1)S(1)} %collective-permute-done.3.across.rest_12_), channel_id=1, source_target_pairs={{0,96},{1,97},{2,98},{3,99},{4,100},{5,101},{6,102},{7,103},{8,40}... | collective-permute-start | bytes 2359304 | tf_op jit(solution)/shard_map/ppermute | solution.py:54
  43.0 2.4 %collective-permute-start.13 = (bf16[512,256]{1,0:T(8,128)(2,1)S(1)}, bf16[512,256]{1,0:T(8,128)(2,1)S(1)}, u32[]{:S(2)}, u32[]{:S(2)}) collective-permute-start(bf16[512,256]{1,0:T(8,128)(2,1)S(1)} %add_convert_fusion.3), channel_id=1, source_target_pairs={{0,3},{1,0},{2,1},{3,2},{4,7},{5,4},{6,5},{7,6},{8,9},{9,10},{10,1... | collective-permute-start | bytes 786440 | tf_op jit(solution)/shard_map/ppermute | solution.py:54
  45.5 2.7 %collective-permute-start.9 = (bf16[512,256]{1,0:T(8,128)(2,1)S(1)}, bf16[512,256]{1,0:T(8,128)(2,1)S(1)}, u32[]{:S(2)}, u32[]{:S(2)}) collective-permute-start(bf16[512,256]{1,0:T(8,128)(2,1)S(1)} %add_convert_fusion.5), channel_id=1, source_target_pairs={{0,3},{1,0},{2,1},{3,2},{4,7},{5,4},{6,5},{7,6},{8,9},{9,10},{10,1... | collective-permute-start | bytes 786440 | tf_op jit(solution)/shard_map/ppermute | solution.py:54
  49.4 2.0 %collective-permute-done.13 = bf16[512,256]{1,0:T(8,128)(2,1)S(1)} collective-permute-done((bf16[512,256]{1,0:T(8,128)(2,1)S(1)}, bf16[512,256]{1,0:T(8,128)(2,1)S(1)}, u32[]{:S(2)}, u32[]{:S(2)}) %collective-permute-start.13) | collective-permute-done | bytes 262176 | tf_op jit(solution)/shard_map/ppermute | solution.py:54
  51.5 1.7 %collective-permute-start.14 = (bf16[512,256]{1,0:T(8,128)(2,1)S(1)}, bf16[512,256]{1,0:T(8,128)(2,1)S(1)}, u32[]{:S(2)}, u32[]{:S(2)}) collective-permute-start(bf16[512,256]{1,0:T(8,128)(2,1)S(1)} %add_convert_fusion.2), channel_id=1, source_target_pairs={{0,4},{1,5},{2,6},{3,7},{4,0},{5,1},{6,2},{7,3},{8,12},{9,13},{10,... | collective-permute-start | bytes 786440 | tf_op jit(solution)/shard_map/ppermute | solution.py:54
  53.2 1.8 %collective-permute-done.9 = bf16[512,256]{1,0:T(8,128)(2,1)S(1)} collective-permute-done((bf16[512,256]{1,0:T(8,128)(2,1)S(1)}, bf16[512,256]{1,0:T(8,128)(2,1)S(1)}, u32[]{:S(2)}, u32[]{:S(2)}) %collective-permute-start.9) | collective-permute-done | bytes 262176 | tf_op jit(solution)/shard_map/ppermute | solution.py:54
  55.9 2.1 %collective-permute-done.14 = bf16[512,256]{1,0:T(8,128)(2,1)S(1)} collective-permute-done((bf16[512,256]{1,0:T(8,128)(2,1)S(1)}, bf16[512,256]{1,0:T(8,128)(2,1)S(1)}, u32[]{:S(2)}, u32[]{:S(2)}) %collective-permute-start.14) | collective-permute-done | bytes 262176 | tf_op jit(solution)/shard_map/ppermute | solution.py:54
  59.8 3.2 %collective-permute-start.20 = (bf16[512,256]{1,0:T(8,128)(2,1)S(1)}, bf16[512,256]{1,0:T(8,128)(2,1)S(1)}, u32[]{:S(2)}, u32[]{:S(2)}) collective-permute-start(bf16[512,256]{1,0:T(8,128)(2,1)S(1)} %add_convert_fusion.1.rest_0_), channel_id=1, source_target_pairs={{0,16},{1,17},{2,18},{3,19},{4,20},{5,21},{6,22},{7,23},{8,24},{9,... | collective-permute-start | bytes 786440 | tf_op jit(solution)/shard_map/ppermute | solution.py:54
  63.0 1.6 %collective-permute-start.17 = (bf16[512,256]{1,0:T(8,128)(2,1)S(1)}, bf16[512,256]{1,0:T(8,128)(2,1)S(1)}, u32[]{:S(2)}, u32[]{:S(2)}) collective-permute-start(bf16[512,256]{1,0:T(8,128)(2,1)S(1)} %add_convert_fusion.1.rest_0_), channel_id=1, source_target_pairs={{0,1},{1,2},{2,3},{3,0},{4,5},{5,6},{6,7},{7,4},{8,11},{9,8},{10,9... | collective-permute-start | bytes 786440 | tf_op jit(solution)/shard_map/ppermute | solution.py:54
  67.0 3.4 %collective-permute-done.20.rest_4_ = bf16[512,256]{1,0:T(8,128)(2,1)S(1)} collective-permute-done((bf16[512,256]{1,0:T(8,128)(2,1)S(1)}, bf16[512,256]{1,0:T(8,128)(2,1)S(1)}, u32[]{:S(2)}, u32[]{:S(2)}) %collective-permute-start.20) | collective-permute-done | bytes 262176 | tf_op jit(solution)/shard_map/ppermute | solution.py:54
  73.6 2.2 %collective-permute-done.28.rest_12_ = bf16[256,512]{1,0:T(8,128)(2,1)S(1)} collective-permute-done((bf16[256,512]{1,0:T(8,128)(2,1)S(1)}, bf16[256,512]{1,0:T(8,128)(2,1)S(1)}, u32[]{:S(2)}, u32[]{:S(2)}) %collective-permute-start.28) | collective-permute-done | bytes 262176 | tf_op jit(solution)/shard_map/ppermute | solution.py:54
  75.9 1.8 %collective-permute-start.22 = (bf16[512,256]{1,0:T(8,128)(2,1)S(1)}, bf16[512,256]{1,0:T(8,128)(2,1)S(1)}, u32[]{:S(2)}, u32[]{:S(2)}) collective-permute-start(bf16[512,256]{1,0:T(8,128)(2,1)S(1)} %collective-permute-done.18.rest_2_), channel_id=1, source_target_pairs={{0,16},{1,17},{2,18},{3,19},{4,20},{5,21},{6,22},{7,23},{8,24},{9,... | collective-permute-start | bytes 786440 | tf_op jit(solution)/shard_map/ppermute | solution.py:54
  77.7 2.0 %collective-permute-done.21.rest_5_ = bf16[512,256]{1,0:T(8,128)(2,1)S(1)} collective-permute-done((bf16[512,256]{1,0:T(8,128)(2,1)S(1)}, bf16[512,256]{1,0:T(8,128)(2,1)S(1)}, u32[]{:S(2)}, u32[]{:S(2)}) %collective-permute-start.21) | collective-permute-done | bytes 262176 | tf_op jit(solution)/shard_map/ppermute | solution.py:54
  80.4 2.1 %collective-permute-done.19.rest_3_ = bf16[512,256]{1,0:T(8,128)(2,1)S(1)} collective-permute-done((bf16[512,256]{1,0:T(8,128)(2,1)S(1)}, bf16[512,256]{1,0:T(8,128)(2,1)S(1)}, u32[]{:S(2)}, u32[]{:S(2)}) %collective-permute-start.19) | collective-permute-done | bytes 262176 | tf_op jit(solution)/shard_map/ppermute | solution.py:54
  83.5 3.1 %collective-permute-done.22.rest_6_ = bf16[512,256]{1,0:T(8,128)(2,1)S(1)} collective-permute-done((bf16[512,256]{1,0:T(8,128)(2,1)S(1)}, bf16[512,256]{1,0:T(8,128)(2,1)S(1)}, u32[]{:S(2)}, u32[]{:S(2)}) %collective-permute-start.22) | collective-permute-done | bytes 262176 | tf_op jit(solution)/shard_map/ppermute | solution.py:54
  86.6 3.6 %collective-permute-done.30.rest_14_ = bf16[256,512]{1,0:T(8,128)(2,1)S(1)} collective-permute-done((bf16[256,512]{1,0:T(8,128)(2,1)S(1)}, bf16[256,512]{1,0:T(8,128)(2,1)S(1)}, u32[]{:S(2)}, u32[]{:S(2)}) %collective-permute-start.30) | collective-permute-done | bytes 262176 | tf_op jit(solution)/shard_map/ppermute | solution.py:54
  91.0 1.9 %square_part.1 = (f32[512,256]{1,0:T(8,128)S(1)}, bf16[512,256]{1,0:T(8,128)(2,1)S(1)}) custom-call(s32[5]{0:T(128)S(1)} %stack.23.where, bf16[512,256]{1,0:T(8,128)(2,1)S(1)} %add_convert_fusion.1.rest_0_, bf16[512,256]{1,0:T(8,128)(2,1)S(1)} %collective-permute-done.17.rest_1_, bf16[512,256]{1,0:T(8,128)(2,1)S(1)} %collective-permute-done.18.rest_2_, ...), custom_call_target="tpu_custom_call" | custom-call | flops 1073741824 | bytes 4194304 | tf_op jit(solution)/shard_map/square_part/pallas_call | solution.py:177
  95.5 3.7 %collective-permute-start.37 = (bf16[512,256]{1,0:T(8,128)(2,1)S(1)}, bf16[512,256]{1,0:T(8,128)(2,1)S(1)}, u32[]{:S(2)}, u32[]{:S(2)}) collective-permute-start(bf16[512,256]{1,0:T(8,128)(2,1)S(1)} %add_convert_fusion), channel_id=1, source_target_pairs={{0,4},{1,5},{2,6},{3,7},{4,20},{5,21},{6,22},{7,23},{8,12},{9,13},... | collective-permute-start | bytes 786440 | tf_op jit(solution)/shard_map/ppermute | solution.py:54
  100.4 2.0 %collective-permute-start.35 = (bf16[512,256]{1,0:T(8,128)(2,1)S(1)}, bf16[512,256]{1,0:T(8,128)(2,1)S(1)}, u32[]{:S(2)}, u32[]{:S(2)}) collective-permute-start(bf16[512,256]{1,0:T(8,128)(2,1)S(1)} %collective-permute-done.33.rest_0_), channel_id=1, source_target_pairs={{0,3},{1,0},{2,1},{3,2},{4,7},{5,4},{6,5},{7,6},{8,9},{9,10},{10,1... | collective-permute-start | bytes 786440 | tf_op jit(solution)/shard_map/ppermute | solution.py:54
  102.4 4.1 %collective-permute-done.37.rest_4_ = bf16[512,256]{1,0:T(8,128)(2,1)S(1)} collective-permute-done((bf16[512,256]{1,0:T(8,128)(2,1)S(1)}, bf16[512,256]{1,0:T(8,128)(2,1)S(1)}, u32[]{:S(2)}, u32[]{:S(2)}) %collective-permute-start.37) | collective-permute-done | bytes 262176 | tf_op jit(solution)/shard_map/ppermute | solution.py:54
  106.5 1.6 %collective-permute-start.38 = (bf16[512,256]{1,0:T(8,128)(2,1)S(1)}, bf16[512,256]{1,0:T(8,128)(2,1)S(1)}, u32[]{:S(2)}, u32[]{:S(2)}) collective-permute-start(bf16[512,256]{1,0:T(8,128)(2,1)S(1)} %collective-permute-done.37.rest_4_), channel_id=1, source_target_pairs={{0,1},{1,2},{2,3},{3,0},{4,5},{5,6},{6,7},{7,4},{8,11},{9,8},{10,9... | collective-permute-start | bytes 786440 | tf_op jit(solution)/shard_map/ppermute | solution.py:54
  109.4 7.7 %collective-permute-start.39 = (bf16[512,256]{1,0:T(8,128)(2,1)S(1)}, bf16[512,256]{1,0:T(8,128)(2,1)S(1)}, u32[]{:S(2)}, u32[]{:S(2)}) collective-permute-start(bf16[512,256]{1,0:T(8,128)(2,1)S(1)} %collective-permute-done.35.rest_2_), channel_id=1, source_target_pairs={{0,4},{1,5},{2,6},{3,7},{4,0},{5,1},{6,2},{7,3},{8,12},{9,13},{10,... | collective-permute-start | bytes 786440 | tf_op jit(solution)/shard_map/ppermute | solution.py:54
  117.2 6.4 %collective-permute-done.39.rest_6_ = bf16[512,256]{1,0:T(8,128)(2,1)S(1)} collective-permute-done((bf16[512,256]{1,0:T(8,128)(2,1)S(1)}, bf16[512,256]{1,0:T(8,128)(2,1)S(1)}, u32[]{:S(2)}, u32[]{:S(2)}) %collective-permute-start.39) | collective-permute-done | bytes 262176 | tf_op jit(solution)/shard_map/ppermute | solution.py:54
  124.8 2.6 %apply_part.2 = (f32[256,768]{1,0:T(8,128)S(1)}, bf16[256,768]{1,0:T(8,128)(2,1)S(1)}) custom-call(s32[5]{0:T(128)S(1)} %stack.23.where, bf16[512,256]{1,0:T(8,128)(2,1)S(1)} %collective-permute-done.33.rest_0_, bf16[512,256]{1,0:T(8,128)(2,1)S(1)} %collective-permute-done.34.rest_1_, bf16[512,256]{1,0:T(8,128)(2,1)S(1)} %collective-permute-done.35.rest_2_, ...), custom_call_target="tpu_custom_call" | custom-call | flops 1610612736 | bytes 6422528 | tf_op jit(solution)/shard_map/apply_part/pallas_call | solution.py:193
  127.5 2.7 %apply_part.3 = (f32[256,768]{1,0:T(8,128)S(1)}, bf16[256,768]{1,0:T(8,128)(2,1)S(1)}) custom-call(s32[5]{0:T(128)S(1)} %stack.23.where, bf16[512,256]{1,0:T(8,128)(2,1)S(1)} %collective-permute-done.33.rest_0_, bf16[512,256]{1,0:T(8,128)(2,1)S(1)} %collective-permute-done.34.rest_1_, bf16[512,256]{1,0:T(8,128)(2,1)S(1)} %collective-permute-done.35.rest_2_, ...), custom_call_target="tpu_custom_call" | custom-call | flops 1610612736 | bytes 6422528 | tf_op jit(solution)/shard_map/apply_part/pallas_call | solution.py:193
  (80 shorter events, 30.7 us)
Async XLA Ops:
  0.1 21.4 %collective-permute-start = (bf16[256,1536]{1,0:T(8,128)(2,1)}, bf16[256,1536]{1,0:T(8,128)(2,1)S(1)}, u32[]{:S(2)}, u32[]{:S(2)}) collective-permute-start(bf16[256,1536]{1,0:T(8,128)(2,1)} %rest_8_.1), channel_id=1, source_target_pairs={{0,8},{1,9},{2,10},{3,11},{4,12},{5,13},{6,14},{7,15},{8,0},{9,1},... | collective-permute-start | bytes 2359304 | tf_op jit(solution)/shard_map/ppermute | solution.py:54
  0.1 21.4 %collective-permute-start.1 = (bf16[256,1536]{1,0:T(8,128)(2,1)}, bf16[256,1536]{1,0:T(8,128)(2,1)S(1)}, u32[]{:S(2)}, u32[]{:S(2)}) collective-permute-start(bf16[256,1536]{1,0:T(8,128)(2,1)} %rest_8_.1), channel_id=1, source_target_pairs={{0,96},{1,97},{2,98},{3,99},{4,100},{5,101},{6,102},{7,103},{8,40}... | collective-permute-start | bytes 2359304 | tf_op jit(solution)/shard_map/ppermute | solution.py:54
  3.0 20.1 %collective-permute-start.3 = (bf16[256,1536]{1,0:T(8,128)(2,1)}, bf16[256,1536]{1,0:T(8,128)(2,1)S(1)}, u32[]{:S(2)}, u32[]{:S(2)}) collective-permute-start(bf16[256,1536]{1,0:T(8,128)(2,1)} %rest_8_.1), channel_id=1, source_target_pairs={{0,16},{1,17},{2,18},{3,19},{4,20},{5,21},{6,22},{7,23},{8,24},{9,... | collective-permute-start | bytes 2359304 | tf_op jit(solution)/shard_map/ppermute | solution.py:54
  7.4 9.9 %collective-permute-start.5 = (bf16[128,1536]{1,0:T(8,128)(2,1)S(1)}, bf16[128,1536]{1,0:T(8,128)(2,1)S(1)}, u32[]{:S(2)}, u32[]{:S(2)}) collective-permute-start(bf16[128,1536]{1,0:T(8,128)(2,1)S(1)} %get-tuple-element.53), channel_id=1, source_target_pairs={{0,32},{1,33},{2,34},{3,35},{4,36},{5,37},{6,38},{7,39},{8,104},{9... | collective-permute-start | bytes 1179656 | tf_op jit(solution)/shard_map/ppermute | solution.py:54
  7.5 14.0 %collective-permute-start.2 = (bf16[128,1536]{1,0:T(8,128)(2,1)S(1)}, bf16[128,1536]{1,0:T(8,128)(2,1)S(1)}, u32[]{:S(2)}, u32[]{:S(2)}) collective-permute-start(bf16[128,1536]{1,0:T(8,128)(2,1)S(1)} %get-tuple-element.54), channel_id=1, source_target_pairs={{0,32},{1,33},{2,34},{3,35},{4,36},{5,37},{6,38},{7,39},{8,104},{9... | collective-permute-start | bytes 1179656 | tf_op jit(solution)/shard_map/ppermute | solution.py:54
  17.3 9.0 %collective-permute-start.6 = (bf16[128,1536]{1,0:T(8,128)(2,1)S(1)}, bf16[128,1536]{1,0:T(8,128)(2,1)S(1)}, u32[]{:S(2)}, u32[]{:S(2)}) collective-permute-start(bf16[128,1536]{1,0:T(8,128)(2,1)S(1)} %collective-permute-done.5), channel_id=1, source_target_pairs={{0,32},{1,33},{2,34},{3,35},{4,36},{5,37},{6,38},{7,39},{8,104},{9... | collective-permute-start | bytes 1179656 | tf_op jit(solution)/shard_map/ppermute | solution.py:54
  21.5 9.0 %collective-permute-start.7 = (bf16[128,1536]{1,0:T(8,128)(2,1)S(1)}, bf16[128,1536]{1,0:T(8,128)(2,1)S(1)}, u32[]{:S(2)}, u32[]{:S(2)}) collective-permute-start(bf16[128,1536]{1,0:T(8,128)(2,1)S(1)} %collective-permute-done.2), channel_id=1, source_target_pairs={{0,32},{1,33},{2,34},{3,35},{4,36},{5,37},{6,38},{7,39},{8,104},{9... | collective-permute-start | bytes 1179656 | tf_op jit(solution)/shard_map/ppermute | solution.py:54
  33.5 9.4 %collective-permute-start.12 = (bf16[512,256]{1,0:T(8,128)(2,1)S(1)}, bf16[512,256]{1,0:T(8,128)(2,1)S(1)}, u32[]{:S(2)}, u32[]{:S(2)}) collective-permute-start(bf16[512,256]{1,0:T(8,128)(2,1)S(1)} %get-tuple-element.43), channel_id=1, source_target_pairs={{0,3},{1,0},{2,1},{3,2},{4,7},{5,4},{6,5},{7,6},{8,9},{9,10},{10,1... | collective-permute-start | bytes 786440 | tf_op jit(solution)/shard_map/ppermute | solution.py:54
  37.7 7.7 %collective-permute-start.8 = (bf16[512,256]{1,0:T(8,128)(2,1)S(1)}, bf16[512,256]{1,0:T(8,128)(2,1)S(1)}, u32[]{:S(2)}, u32[]{:S(2)}) collective-permute-start(bf16[512,256]{1,0:T(8,128)(2,1)S(1)} %get-tuple-element.38), channel_id=1, source_target_pairs={{0,3},{1,0},{2,1},{3,2},{4,7},{5,4},{6,5},{7,6},{8,9},{9,10},{10,1... | collective-permute-start | bytes 786440 | tf_op jit(solution)/shard_map/ppermute | solution.py:54
  38.1 21.5 %collective-permute-start.15 = (bf16[256,1536]{1,0:T(8,128)(2,1)S(1)}, bf16[256,1536]{1,0:T(8,128)(2,1)S(1)}, u32[]{:S(2)}, u32[]{:S(2)}) collective-permute-start(bf16[256,1536]{1,0:T(8,128)(2,1)S(1)} %collective-permute-done.3.across.rest_12_), channel_id=1, source_target_pairs={{0,32},{1,33},{2,34},{3,35},{4,36},{5,37},{6,38},{7,39},{8,104},{9... | collective-permute-start | bytes 2359304 | tf_op jit(solution)/shard_map/ppermute | solution.py:54
  38.1 21.5 %collective-permute-start.16 = (bf16[256,1536]{1,0:T(8,128)(2,1)S(1)}, bf16[256,1536]{1,0:T(8,128)(2,1)S(1)}, u32[]{:S(2)}, u32[]{:S(2)}) collective-permute-start(bf16[256,1536]{1,0:T(8,128)(2,1)S(1)} %collective-permute-done.3.across.rest_12_), channel_id=1, source_target_pairs={{0,96},{1,97},{2,98},{3,99},{4,100},{5,101},{6,102},{7,103},{8,40}... | collective-permute-start | bytes 2359304 | tf_op jit(solution)/shard_map/ppermute | solution.py:54
  43.0 8.5 %collective-permute-start.13 = (bf16[512,256]{1,0:T(8,128)(2,1)S(1)}, bf16[512,256]{1,0:T(8,128)(2,1)S(1)}, u32[]{:S(2)}, u32[]{:S(2)}) collective-permute-start(bf16[512,256]{1,0:T(8,128)(2,1)S(1)} %add_convert_fusion.3), channel_id=1, source_target_pairs={{0,3},{1,0},{2,1},{3,2},{4,7},{5,4},{6,5},{7,6},{8,9},{9,10},{10,1... | collective-permute-start | bytes 786440 | tf_op jit(solution)/shard_map/ppermute | solution.py:54
  45.5 9.6 %collective-permute-start.9 = (bf16[512,256]{1,0:T(8,128)(2,1)S(1)}, bf16[512,256]{1,0:T(8,128)(2,1)S(1)}, u32[]{:S(2)}, u32[]{:S(2)}) collective-permute-start(bf16[512,256]{1,0:T(8,128)(2,1)S(1)} %add_convert_fusion.5), channel_id=1, source_target_pairs={{0,3},{1,0},{2,1},{3,2},{4,7},{5,4},{6,5},{7,6},{8,9},{9,10},{10,1... | collective-permute-start | bytes 786440 | tf_op jit(solution)/shard_map/ppermute | solution.py:54
  48.3 7.7 %collective-permute-start.11 = (bf16[512,256]{1,0:T(8,128)(2,1)S(1)}, bf16[512,256]{1,0:T(8,128)(2,1)S(1)}, u32[]{:S(2)}, u32[]{:S(2)}) collective-permute-start(bf16[512,256]{1,0:T(8,128)(2,1)S(1)} %add_convert_fusion.4), channel_id=1, source_target_pairs={{0,1},{1,2},{2,3},{3,0},{4,5},{5,6},{6,7},{7,4},{8,11},{9,8},{10,9... | collective-permute-start | bytes 786440 | tf_op jit(solution)/shard_map/ppermute | solution.py:54
  59.8 10.6 %collective-permute-start.20 = (bf16[512,256]{1,0:T(8,128)(2,1)S(1)}, bf16[512,256]{1,0:T(8,128)(2,1)S(1)}, u32[]{:S(2)}, u32[]{:S(2)}) collective-permute-start(bf16[512,256]{1,0:T(8,128)(2,1)S(1)} %add_convert_fusion.1.rest_0_), channel_id=1, source_target_pairs={{0,16},{1,17},{2,18},{3,19},{4,20},{5,21},{6,22},{7,23},{8,24},{9,... | collective-permute-start | bytes 786440 | tf_op jit(solution)/shard_map/ppermute | solution.py:54
  63.0 9.2 %collective-permute-start.17 = (bf16[512,256]{1,0:T(8,128)(2,1)S(1)}, bf16[512,256]{1,0:T(8,128)(2,1)S(1)}, u32[]{:S(2)}, u32[]{:S(2)}) collective-permute-start(bf16[512,256]{1,0:T(8,128)(2,1)S(1)} %add_convert_fusion.1.rest_0_), channel_id=1, source_target_pairs={{0,1},{1,2},{2,3},{3,0},{4,5},{5,6},{6,7},{7,4},{8,11},{9,8},{10,9... | collective-permute-start | bytes 786440 | tf_op jit(solution)/shard_map/ppermute | solution.py:54
  64.6 9.0 %collective-permute-start.18 = (bf16[512,256]{1,0:T(8,128)(2,1)S(1)}, bf16[512,256]{1,0:T(8,128)(2,1)S(1)}, u32[]{:S(2)}, u32[]{:S(2)}) collective-permute-start(bf16[512,256]{1,0:T(8,128)(2,1)S(1)} %add_convert_fusion.1.rest_0_), channel_id=1, source_target_pairs={{0,3},{1,0},{2,1},{3,2},{4,7},{5,4},{6,5},{7,6},{8,9},{9,10},{10,1... | collective-permute-start | bytes 786440 | tf_op jit(solution)/shard_map/ppermute | solution.py:54
  66.2 9.6 %collective-permute-start.28 = (bf16[256,512]{1,0:T(8,128)(2,1)S(1)}, bf16[256,512]{1,0:T(8,128)(2,1)S(1)}, u32[]{:S(2)}, u32[]{:S(2)}) collective-permute-start(bf16[256,512]{1,0:T(8,128)(2,1)S(1)} %pad_maximum_fusion.rest_8_), channel_id=1, source_target_pairs={{0,4},{1,5},{2,6},{3,7},{4,0},{5,1},{6,2},{7,3},{8,12},{9,13},{10,... | collective-permute-start | bytes 786440 | tf_op jit(solution)/shard_map/ppermute | solution.py:54
  67.0 8.9 %collective-permute-start.25 = (bf16[256,512]{1,0:T(8,128)(2,1)S(1)}, bf16[256,512]{1,0:T(8,128)(2,1)S(1)}, u32[]{:S(2)}, u32[]{:S(2)}) collective-permute-start(bf16[256,512]{1,0:T(8,128)(2,1)S(1)} %pad_maximum_fusion.rest_8_), channel_id=1, source_target_pairs={{0,32},{1,33},{2,34},{3,35},{4,36},{5,37},{6,38},{7,39},{8,104},{9... | collective-permute-start | bytes 786440 | tf_op jit(solution)/shard_map/ppermute | solution.py:54
  73.6 8.9 %collective-permute-start.19 = (bf16[512,256]{1,0:T(8,128)(2,1)S(1)}, bf16[512,256]{1,0:T(8,128)(2,1)S(1)}, u32[]{:S(2)}, u32[]{:S(2)}) collective-permute-start(bf16[512,256]{1,0:T(8,128)(2,1)S(1)} %collective-permute-done.17.rest_1_), channel_id=1, source_target_pairs={{0,1},{1,2},{2,3},{3,0},{4,5},{5,6},{6,7},{7,4},{8,11},{9,8},{10,9... | collective-permute-start | bytes 786440 | tf_op jit(solution)/shard_map/ppermute | solution.py:54
  75.9 10.7 %collective-permute-start.22 = (bf16[512,256]{1,0:T(8,128)(2,1)S(1)}, bf16[512,256]{1,0:T(8,128)(2,1)S(1)}, u32[]{:S(2)}, u32[]{:S(2)}) collective-permute-start(bf16[512,256]{1,0:T(8,128)(2,1)S(1)} %collective-permute-done.18.rest_2_), channel_id=1, source_target_pairs={{0,16},{1,17},{2,18},{3,19},{4,20},{5,21},{6,22},{7,23},{8,24},{9,... | collective-permute-start | bytes 786440 | tf_op jit(solution)/shard_map/ppermute | solution.py:54
  77.7 8.8 %collective-permute-start.27 = (bf16[256,512]{1,0:T(8,128)(2,1)S(1)}, bf16[256,512]{1,0:T(8,128)(2,1)S(1)}, u32[]{:S(2)}, u32[]{:S(2)}) collective-permute-start(bf16[256,512]{1,0:T(8,128)(2,1)S(1)} %collective-permute-done.25.rest_9_), channel_id=1, source_target_pairs={{0,32},{1,33},{2,34},{3,35},{4,36},{5,37},{6,38},{7,39},{8,104},{9... | collective-permute-start | bytes 786440 | tf_op jit(solution)/shard_map/ppermute | solution.py:54
  79.7 10.4 %collective-permute-start.30 = (bf16[256,512]{1,0:T(8,128)(2,1)S(1)}, bf16[256,512]{1,0:T(8,128)(2,1)S(1)}, u32[]{:S(2)}, u32[]{:S(2)}) collective-permute-start(bf16[256,512]{1,0:T(8,128)(2,1)S(1)} %collective-permute-done.26.rest_10_), channel_id=1, source_target_pairs={{0,4},{1,5},{2,6},{3,7},{4,0},{5,1},{6,2},{7,3},{8,12},{9,13},{10,... | collective-permute-start | bytes 786440 | tf_op jit(solution)/shard_map/ppermute | solution.py:54
  82.6 7.6 %collective-permute-start.23 = (bf16[512,256]{1,0:T(8,128)(2,1)S(1)}, bf16[512,256]{1,0:T(8,128)(2,1)S(1)}, u32[]{:S(2)}, u32[]{:S(2)}) collective-permute-start(bf16[512,256]{1,0:T(8,128)(2,1)S(1)} %collective-permute-done.21.rest_5_), channel_id=1, source_target_pairs={{0,1},{1,2},{2,3},{3,0},{4,5},{5,6},{6,7},{7,4},{8,11},{9,8},{10,9... | collective-permute-start | bytes 786440 | tf_op jit(solution)/shard_map/ppermute | solution.py:54
  95.4 21.8 %collective-permute-start.41 = (bf16[256,1536]{1,0:T(8,128)(2,1)S(1)}, bf16[256,1536]{1,0:T(8,128)(2,1)S(1)}, u32[]{:S(2)}, u32[]{:S(2)}) collective-permute-start(bf16[256,1536]{1,0:T(8,128)(2,1)S(1)} %collective-permute-done.15.rest_13_), channel_id=1, source_target_pairs={{0,32},{1,33},{2,34},{3,35},{4,36},{5,37},{6,38},{7,39},{8,104},{9... | collective-permute-start | bytes 2359304 | tf_op jit(solution)/shard_map/ppermute | solution.py:54
  95.5 11.0 %collective-permute-start.37 = (bf16[512,256]{1,0:T(8,128)(2,1)S(1)}, bf16[512,256]{1,0:T(8,128)(2,1)S(1)}, u32[]{:S(2)}, u32[]{:S(2)}) collective-permute-start(bf16[512,256]{1,0:T(8,128)(2,1)S(1)} %add_convert_fusion), channel_id=1, source_target_pairs={{0,4},{1,5},{2,6},{3,7},{4,20},{5,21},{6,22},{7,23},{8,12},{9,13},... | collective-permute-start | bytes 786440 | tf_op jit(solution)/shard_map/ppermute | solution.py:54
  99.2 10.2 %collective-permute-start.34 = (bf16[512,256]{1,0:T(8,128)(2,1)S(1)}, bf16[512,256]{1,0:T(8,128)(2,1)S(1)}, u32[]{:S(2)}, u32[]{:S(2)}) collective-permute-start(bf16[512,256]{1,0:T(8,128)(2,1)S(1)} %collective-permute-done.33.rest_0_), channel_id=1, source_target_pairs={{0,1},{1,2},{2,3},{3,0},{4,5},{5,6},{6,7},{7,4},{8,11},{9,8},{10,9... | collective-permute-start | bytes 786440 | tf_op jit(solution)/shard_map/ppermute | solution.py:54
  100.4 9.0 %collective-permute-start.35 = (bf16[512,256]{1,0:T(8,128)(2,1)S(1)}, bf16[512,256]{1,0:T(8,128)(2,1)S(1)}, u32[]{:S(2)}, u32[]{:S(2)}) collective-permute-start(bf16[512,256]{1,0:T(8,128)(2,1)S(1)} %collective-permute-done.33.rest_0_), channel_id=1, source_target_pairs={{0,3},{1,0},{2,1},{3,2},{4,7},{5,4},{6,5},{7,6},{8,9},{9,10},{10,1... | collective-permute-start | bytes 786440 | tf_op jit(solution)/shard_map/ppermute | solution.py:54
  106.5 10.6 %collective-permute-start.38 = (bf16[512,256]{1,0:T(8,128)(2,1)S(1)}, bf16[512,256]{1,0:T(8,128)(2,1)S(1)}, u32[]{:S(2)}, u32[]{:S(2)}) collective-permute-start(bf16[512,256]{1,0:T(8,128)(2,1)S(1)} %collective-permute-done.37.rest_4_), channel_id=1, source_target_pairs={{0,1},{1,2},{2,3},{3,0},{4,5},{5,6},{6,7},{7,4},{8,11},{9,8},{10,9... | collective-permute-start | bytes 786440 | tf_op jit(solution)/shard_map/ppermute | solution.py:54
  109.4 7.8 %collective-permute-start.36 = (bf16[512,256]{1,0:T(8,128)(2,1)S(1)}, bf16[512,256]{1,0:T(8,128)(2,1)S(1)}, u32[]{:S(2)}, u32[]{:S(2)}) collective-permute-start(bf16[512,256]{1,0:T(8,128)(2,1)S(1)} %collective-permute-done.34.rest_1_), channel_id=1, source_target_pairs={{0,1},{1,2},{2,3},{3,0},{4,5},{5,6},{6,7},{7,4},{8,11},{9,8},{10,9... | collective-permute-start | bytes 786440 | tf_op jit(solution)/shard_map/ppermute | solution.py:54
  109.4 14.2 %collective-permute-start.39 = (bf16[512,256]{1,0:T(8,128)(2,1)S(1)}, bf16[512,256]{1,0:T(8,128)(2,1)S(1)}, u32[]{:S(2)}, u32[]{:S(2)}) collective-permute-start(bf16[512,256]{1,0:T(8,128)(2,1)S(1)} %collective-permute-done.35.rest_2_), channel_id=1, source_target_pairs={{0,4},{1,5},{2,6},{3,7},{4,0},{5,1},{6,2},{7,3},{8,12},{9,13},{10,... | collective-permute-start | bytes 786440 | tf_op jit(solution)/shard_map/ppermute | solution.py:54
  117.2 7.6 %collective-permute-start.40 = (bf16[512,256]{1,0:T(8,128)(2,1)S(1)}, bf16[512,256]{1,0:T(8,128)(2,1)S(1)}, u32[]{:S(2)}, u32[]{:S(2)}) collective-permute-start(bf16[512,256]{1,0:T(8,128)(2,1)S(1)} %collective-permute-done.38.rest_5_), channel_id=1, source_target_pairs={{0,1},{1,2},{2,3},{3,0},{4,5},{5,6},{6,7},{7,4},{8,11},{9,8},{10,9... | collective-permute-start | bytes 786440 | tf_op jit(solution)/shard_map/ppermute | solution.py:54
  (13 other events, 86.0 us)

commit v10 on v9

--- a/solution.py
+++ b/solution.py
@@ -96,21 +96,19 @@
         out[...] = tiles[row, col]
 
 
-def square_kernel(where, *rest):
-    left, right, (mine, theirs), (held,) = rest[:8], rest[8:16], rest[16:18], rest[18:]
+def square_kernel(others, where, *rest):
+    left, right, (out, held) = rest[:8], rest[8:16], rest[16:]
     x, yh, core, yl, z = (where[i] for i in range(5))
-    for dy in range(2):
-        for position in range(4):
-            held[dy, position] = right[dy * 4 + position][...]
-    total = jnp.zeros((TILE, TILE), jnp.float32)
-    for dy in range(2):
-        for position in range(4):
-            row = lax.rem(yh + dy + yl, 2)
-            col = place(z + ahead(position, core) - x, core)
-            total += nn(left[dy * 4 + position][...], held[row, col])
-    mine[...] = total[:, :BLOCK]
-    theirs[:BLOCK] = total[BLOCK:, BLOCK:].astype(theirs.dtype)
-    theirs[BLOCK:] = total[:BLOCK, BLOCK:].astype(theirs.dtype)
+    for index in range(8):
+        row = lax.rem(yh + index // 4 + yl, 2)
+        col = place(x + ahead(index % 4, core) - z, core)
+        depth = pl.ds(pl.multiple_of((row * 4 + col) * BLOCK, BLOCK), BLOCK)
+        held[depth] = right[index][:, others * BLOCK : (others + 1) * BLOCK]
+    total = nn(jnp.concatenate([ref[...] for ref in left], axis=1), held[...]).astype(out.dtype)
+    if others:
+        out[:BLOCK], out[BLOCK:] = total[BLOCK:], total[:BLOCK]
+    else:
+        out[...] = total
 
 
 def apply_kernel(begin, where, *rest):
@@ -173,19 +171,16 @@
     )(where, own, other, across, across_other, fore, back, far, near)
 
 
-def square_part(where, left, right):
-    return pl.pallas_call(
-        square_kernel,
+def square_part(others, where, left, right):
+    return pl.pallas_call(
+        functools.partial(square_kernel, others),
         in_specs=[smem()] + [whole() for _ in range(16)],
-        out_specs=[whole(), whole()],
-        out_shape=[
-            jax.ShapeDtypeStruct((TILE, BLOCK), jnp.float32),
-            jax.ShapeDtypeStruct((TILE, BLOCK), jnp.bfloat16),
-        ],
-        scratch_shapes=[pltpu.VMEM((2, 4, BLOCK, TILE), jnp.bfloat16)],
-        compiler_params=params(24),
-        cost_estimate=cost(2 * 8 * TILE * TILE * BLOCK, 16 * BLOCK * TILE * 2),
-        name="square_part",
+        out_specs=whole(),
+        out_shape=jax.ShapeDtypeStruct((TILE, BLOCK), jnp.bfloat16 if others else jnp.float32),
+        scratch_shapes=[pltpu.VMEM((8 * BLOCK, BLOCK), jnp.bfloat16)],
+        compiler_params=params(24),
+        cost_estimate=cost(2 * 8 * TILE * BLOCK * BLOCK, 13 * BLOCK * TILE * 2),
+        name="square_theirs" if others else "square_part",
     )(where, *left, *right)
 
 
@@ -256,8 +251,8 @@
     across_far = send(across_fore, "x_fore")
     gram = jnp.concatenate([gram_left[:BLOCK], send(gram_left[BLOCK:], "core")], axis=1)
     left, right = gather_even(gram_left, "z", "yh"), gather_even(gram, "x", "yl")
-    mine, theirs = square_part(where, left, right)
-    square = mine + send(theirs, "core").astype(jnp.float32)
+    theirs = send(square_part(1, where, left, right), "core")
+    square = square_part(0, where, left, right) + theirs.astype(jnp.float32)
     mixing = (cubic_coef * gram_left.astype(jnp.float32) + quintic_coef * square).astype(jnp.bfloat16)
 
     there = send(mixing, "turn_yl")

time: 135 us -> 134 us (level)
  waiting for transfers between devices: 61.6 us -> 60.2 us
    ppermute x44, waiting for transfers between devices: 61.6 us -> 60.2 us  [send(): return lax.ppermute(value, ('row', 'col'), pairs(MOVES[move]))]
  transfers between devices with their start and end apart: 44 -> 44, of which waited for: 25 -> 25; matrix products, arithmetic and copies ran while one was open for 1% -> 1% of each run, Pallas kernels for 3% -> 4%
where the time goes in v10:
time: 134 us; the launch traced here: 133 us
  waiting for transfers between devices  60.2 us (45%)
  starting transfers between devices  56.9 us (42%)
  Pallas kernels  12.4 us (9%)
  other arithmetic  1.68 us (1%)
  local copies, waits for them, and re-layouts  1.38 us (1%)
    ppermute x44, waiting for transfers between devices, send(): return lax.ppermute(value, ('row', 'col'), pairs(MOVES[move]))  60.2 us
    ppermute x44, starting transfers between devices, send(): return lax.ppermute(value, ('row', 'col'), pairs(MOVES[move]))  56.9 us
    pallas_call x2, Pallas kernels, apply_part(): pl.pallas_call(functools.partial(apply_kernel, begin), in_specs=[smem()]...  5.31 us
    pallas_call x1, Pallas kernels, gram_tiles(): pl.pallas_call(gram_kernel, in_specs=[smem()] + [whole() for _ in range(8...  2.97 us
    pallas_call x2, Pallas kernels, square_part(): pl.pallas_call(functools.partial(square_kernel, others), in_specs=[smem()...  2.69 us
  transfers between devices with their start and end apart: 44, of which 25 were waited for; matrix products, arithmetic and copies ran while one was open for 1% of the time, Pallas kernels for 4%

profile of v10, /device:TPU:0, one launch (start us, length us, event | category | flops | bytes accessed | tf_op | source)
XLA Modules:
  0.0 132.8 jit_solution(2394479448186218118)
XLA Ops:
  0.1 2.9 %collective-permute-start.1 = (bf16[256,1536]{1,0:T(8,128)(2,1)}, bf16[256,1536]{1,0:T(8,128)(2,1)S(1)}, u32[]{:S(2)}, u32[]{:S(2)}) collective-permute-start(bf16[256,1536]{1,0:T(8,128)(2,1)} %rest_8_.1), channel_id=1, source_target_pairs={{0,96},{1,97},{2,98},{3,99},{4,100},{5,101},{6,102},{7,103},{8,40}... | collective-permute-start | bytes 2359304 | tf_op jit(solution)/shard_map/ppermute | solution.py:54
  3.0 3.2 %collective-permute-start.3 = (bf16[256,1536]{1,0:T(8,128)(2,1)}, bf16[256,1536]{1,0:T(8,128)(2,1)S(1)}, u32[]{:S(2)}, u32[]{:S(2)}) collective-permute-start(bf16[256,1536]{1,0:T(8,128)(2,1)} %rest_8_.1), channel_id=1, source_target_pairs={{0,16},{1,17},{2,18},{3,19},{4,20},{5,21},{6,22},{7,23},{8,24},{9,... | collective-permute-start | bytes 2359304 | tf_op jit(solution)/shard_map/ppermute | solution.py:54
  8.2 9.0 %collective-permute-done.5 = bf16[128,1536]{1,0:T(8,128)(2,1)S(1)} collective-permute-done((bf16[128,1536]{1,0:T(8,128)(2,1)S(1)}, bf16[128,1536]{1,0:T(8,128)(2,1)S(1)}, u32[]{:S(2)}, u32[]{:S(2)}) %collective-permute-start.5) | collective-permute-done | bytes 393248 | tf_op jit(solution)/shard_map/ppermute | solution.py:54
  17.7 3.8 %collective-permute-done.2 = bf16[128,1536]{1,0:T(8,128)(2,1)S(1)} collective-permute-done((bf16[128,1536]{1,0:T(8,128)(2,1)S(1)}, bf16[128,1536]{1,0:T(8,128)(2,1)S(1)}, u32[]{:S(2)}, u32[]{:S(2)}) %collective-permute-start.2) | collective-permute-done | bytes 393248 | tf_op jit(solution)/shard_map/ppermute | solution.py:54
  26.3 4.2 %collective-permute-done.7 = bf16[128,1536]{1,0:T(8,128)(2,1)S(1)} collective-permute-done((bf16[128,1536]{1,0:T(8,128)(2,1)S(1)}, bf16[128,1536]{1,0:T(8,128)(2,1)S(1)}, u32[]{:S(2)}, u32[]{:S(2)}) %collective-permute-start.7) | collective-permute-done | bytes 393248 | tf_op jit(solution)/shard_map/ppermute | solution.py:54
  30.5 3.0 %gram_tiles.1 = (bf16[512,256]{1,0:T(8,128)(2,1)S(1)}, bf16[512,256]{1,0:T(8,128)(2,1)S(1)}, bf16[512,256]{1,0:T(8,128)(2,1)S(1)}, bf16[512,256]{1,0:T(8,128)(2,...) custom-call(s32[5]{0:T(128)S(1)} %stack.23.where, ...), custom_call_target="tpu_custom_call" | custom-call | flops 2013265920 | bytes 8388608 | tf_op jit(solution)/shard_map/gram_tiles/pallas_call | solution.py:162
  33.5 4.2 %collective-permute-start.12 = (bf16[512,256]{1,0:T(8,128)(2,1)S(1)}, bf16[512,256]{1,0:T(8,128)(2,1)S(1)}, u32[]{:S(2)}, u32[]{:S(2)}) collective-permute-start(bf16[512,256]{1,0:T(8,128)(2,1)S(1)} %get-tuple-element.41), channel_id=1, source_target_pairs={{0,3},{1,0},{2,1},{3,2},{4,7},{5,4},{6,5},{7,6},{8,9},{9,10},{10,1... | collective-permute-start | bytes 786440 | tf_op jit(solution)/shard_map/ppermute | solution.py:54
  38.1 3.2 %collective-permute-start.16 = (bf16[256,1536]{1,0:T(8,128)(2,1)S(1)}, bf16[256,1536]{1,0:T(8,128)(2,1)S(1)}, u32[]{:S(2)}, u32[]{:S(2)}) collective-permute-start(bf16[256,1536]{1,0:T(8,128)(2,1)S(1)} %collective-permute-done.3.across.rest_12_), channel_id=1, source_target_pairs={{0,96},{1,97},{2,98},{3,99},{4,100},{5,101},{6,102},{7,103},{8,40}... | collective-permute-start | bytes 2359304 | tf_op jit(solution)/shard_map/ppermute | solution.py:54
  43.0 2.4 %collective-permute-start.13 = (bf16[512,256]{1,0:T(8,128)(2,1)S(1)}, bf16[512,256]{1,0:T(8,128)(2,1)S(1)}, u32[]{:S(2)}, u32[]{:S(2)}) collective-permute-start(bf16[512,256]{1,0:T(8,128)(2,1)S(1)} %add_convert_fusion.3), channel_id=1, source_target_pairs={{0,3},{1,0},{2,1},{3,2},{4,7},{5,4},{6,5},{7,6},{8,9},{9,10},{10,1... | collective-permute-start | bytes 786440 | tf_op jit(solution)/shard_map/ppermute | solution.py:54
  45.5 2.7 %collective-permute-start.9 = (bf16[512,256]{1,0:T(8,128)(2,1)S(1)}, bf16[512,256]{1,0:T(8,128)(2,1)S(1)}, u32[]{:S(2)}, u32[]{:S(2)}) collective-permute-start(bf16[512,256]{1,0:T(8,128)(2,1)S(1)} %add_convert_fusion.5), channel_id=1, source_target_pairs={{0,3},{1,0},{2,1},{3,2},{4,7},{5,4},{6,5},{7,6},{8,9},{9,10},{10,1... | collective-permute-start | bytes 786440 | tf_op jit(solution)/shard_map/ppermute | solution.py:54
  49.4 2.0 %collective-permute-done.13 = bf16[512,256]{1,0:T(8,128)(2,1)S(1)} collective-permute-done((bf16[512,256]{1,0:T(8,128)(2,1)S(1)}, bf16[512,256]{1,0:T(8,128)(2,1)S(1)}, u32[]{:S(2)}, u32[]{:S(2)}) %collective-permute-start.13) | collective-permute-done | bytes 262176 | tf_op jit(solution)/shard_map/ppermute | solution.py:54
  51.5 1.7 %collective-permute-start.14 = (bf16[512,256]{1,0:T(8,128)(2,1)S(1)}, bf16[512,256]{1,0:T(8,128)(2,1)S(1)}, u32[]{:S(2)}, u32[]{:S(2)}) collective-permute-start(bf16[512,256]{1,0:T(8,128)(2,1)S(1)} %add_convert_fusion.2), channel_id=1, source_target_pairs={{0,4},{1,5},{2,6},{3,7},{4,0},{5,1},{6,2},{7,3},{8,12},{9,13},{10,... | collective-permute-start | bytes 786440 | tf_op jit(solution)/shard_map/ppermute | solution.py:54
  53.2 1.8 %collective-permute-done.9 = bf16[512,256]{1,0:T(8,128)(2,1)S(1)} collective-permute-done((bf16[512,256]{1,0:T(8,128)(2,1)S(1)}, bf16[512,256]{1,0:T(8,128)(2,1)S(1)}, u32[]{:S(2)}, u32[]{:S(2)}) %collective-permute-start.9) | collective-permute-done | bytes 262176 | tf_op jit(solution)/shard_map/ppermute | solution.py:54
  55.9 2.1 %collective-permute-done.14 = bf16[512,256]{1,0:T(8,128)(2,1)S(1)} collective-permute-done((bf16[512,256]{1,0:T(8,128)(2,1)S(1)}, bf16[512,256]{1,0:T(8,128)(2,1)S(1)}, u32[]{:S(2)}, u32[]{:S(2)}) %collective-permute-start.14) | collective-permute-done | bytes 262176 | tf_op jit(solution)/shard_map/ppermute | solution.py:54
  59.8 3.2 %collective-permute-start.20 = (bf16[512,256]{1,0:T(8,128)(2,1)S(1)}, bf16[512,256]{1,0:T(8,128)(2,1)S(1)}, u32[]{:S(2)}, u32[]{:S(2)}) collective-permute-start(bf16[512,256]{1,0:T(8,128)(2,1)S(1)} %add_convert_fusion.1.rest_0_), channel_id=1, source_target_pairs={{0,16},{1,17},{2,18},{3,19},{4,20},{5,21},{6,22},{7,23},{8,24},{9,... | collective-permute-start | bytes 786440 | tf_op jit(solution)/shard_map/ppermute | solution.py:54
  63.0 1.6 %collective-permute-start.17 = (bf16[512,256]{1,0:T(8,128)(2,1)S(1)}, bf16[512,256]{1,0:T(8,128)(2,1)S(1)}, u32[]{:S(2)}, u32[]{:S(2)}) collective-permute-start(bf16[512,256]{1,0:T(8,128)(2,1)S(1)} %add_convert_fusion.1.rest_0_), channel_id=1, source_target_pairs={{0,1},{1,2},{2,3},{3,0},{4,5},{5,6},{6,7},{7,4},{8,11},{9,8},{10,9... | collective-permute-start | bytes 786440 | tf_op jit(solution)/shard_map/ppermute | solution.py:54
  64.6 1.6 %collective-permute-start.18 = (bf16[512,256]{1,0:T(8,128)(2,1)S(1)}, bf16[512,256]{1,0:T(8,128)(2,1)S(1)}, u32[]{:S(2)}, u32[]{:S(2)}) collective-permute-start(bf16[512,256]{1,0:T(8,128)(2,1)S(1)} %add_convert_fusion.1.rest_0_), channel_id=1, source_target_pairs={{0,3},{1,0},{2,1},{3,2},{4,7},{5,4},{6,5},{7,6},{8,9},{9,10},{10,1... | collective-permute-start | bytes 786440 | tf_op jit(solution)/shard_map/ppermute | solution.py:54
  67.0 3.4 %collective-permute-done.20.rest_4_ = bf16[512,256]{1,0:T(8,128)(2,1)S(1)} collective-permute-done((bf16[512,256]{1,0:T(8,128)(2,1)S(1)}, bf16[512,256]{1,0:T(8,128)(2,1)S(1)}, u32[]{:S(2)}, u32[]{:S(2)}) %collective-permute-start.20) | collective-permute-done | bytes 262176 | tf_op jit(solution)/shard_map/ppermute | solution.py:54
  73.6 2.2 %collective-permute-done.28.rest_12_ = bf16[256,512]{1,0:T(8,128)(2,1)S(1)} collective-permute-done((bf16[256,512]{1,0:T(8,128)(2,1)S(1)}, bf16[256,512]{1,0:T(8,128)(2,1)S(1)}, u32[]{:S(2)}, u32[]{:S(2)}) %collective-permute-start.28) | collective-permute-done | bytes 262176 | tf_op jit(solution)/shard_map/ppermute | solution.py:54
  75.9 1.8 %collective-permute-start.22 = (bf16[512,256]{1,0:T(8,128)(2,1)S(1)}, bf16[512,256]{1,0:T(8,128)(2,1)S(1)}, u32[]{:S(2)}, u32[]{:S(2)}) collective-permute-start(bf16[512,256]{1,0:T(8,128)(2,1)S(1)} %collective-permute-done.18.rest_2_), channel_id=1, source_target_pairs={{0,16},{1,17},{2,18},{3,19},{4,20},{5,21},{6,22},{7,23},{8,24},{9,... | collective-permute-start | bytes 786440 | tf_op jit(solution)/shard_map/ppermute | solution.py:54
  77.7 2.0 %collective-permute-done.21.rest_5_ = bf16[512,256]{1,0:T(8,128)(2,1)S(1)} collective-permute-done((bf16[512,256]{1,0:T(8,128)(2,1)S(1)}, bf16[512,256]{1,0:T(8,128)(2,1)S(1)}, u32[]{:S(2)}, u32[]{:S(2)}) %collective-permute-start.21) | collective-permute-done | bytes 262176 | tf_op jit(solution)/shard_map/ppermute | solution.py:54
  80.4 2.1 %collective-permute-done.19.rest_3_ = bf16[512,256]{1,0:T(8,128)(2,1)S(1)} collective-permute-done((bf16[512,256]{1,0:T(8,128)(2,1)S(1)}, bf16[512,256]{1,0:T(8,128)(2,1)S(1)}, u32[]{:S(2)}, u32[]{:S(2)}) %collective-permute-start.19) | collective-permute-done | bytes 262176 | tf_op jit(solution)/shard_map/ppermute | solution.py:54
  83.5 3.1 %collective-permute-done.22.rest_6_ = bf16[512,256]{1,0:T(8,128)(2,1)S(1)} collective-permute-done((bf16[512,256]{1,0:T(8,128)(2,1)S(1)}, bf16[512,256]{1,0:T(8,128)(2,1)S(1)}, u32[]{:S(2)}, u32[]{:S(2)}) %collective-permute-start.22) | collective-permute-done | bytes 262176 | tf_op jit(solution)/shard_map/ppermute | solution.py:54
  86.6 3.6 %collective-permute-done.30.rest_14_ = bf16[256,512]{1,0:T(8,128)(2,1)S(1)} collective-permute-done((bf16[256,512]{1,0:T(8,128)(2,1)S(1)}, bf16[256,512]{1,0:T(8,128)(2,1)S(1)}, u32[]{:S(2)}, u32[]{:S(2)}) %collective-permute-start.30) | collective-permute-done | bytes 262176 | tf_op jit(solution)/shard_map/ppermute | solution.py:54
  94.9 3.7 %collective-permute-start.37 = (bf16[512,256]{1,0:T(8,128)(2,1)S(1)}, bf16[512,256]{1,0:T(8,128)(2,1)S(1)}, u32[]{:S(2)}, u32[]{:S(2)}) collective-permute-start(bf16[512,256]{1,0:T(8,128)(2,1)S(1)} %add_convert_fusion), channel_id=1, source_target_pairs={{0,4},{1,5},{2,6},{3,7},{4,20},{5,21},{6,22},{7,23},{8,12},{9,13},... | collective-permute-start | bytes 786440 | tf_op jit(solution)/shard_map/ppermute | solution.py:54
  99.8 2.0 %collective-permute-start.35 = (bf16[512,256]{1,0:T(8,128)(2,1)S(1)}, bf16[512,256]{1,0:T(8,128)(2,1)S(1)}, u32[]{:S(2)}, u32[]{:S(2)}) collective-permute-start(bf16[512,256]{1,0:T(8,128)(2,1)S(1)} %collective-permute-done.33.rest_0_), channel_id=1, source_target_pairs={{0,3},{1,0},{2,1},{3,2},{4,7},{5,4},{6,5},{7,6},{8,9},{9,10},{10,1... | collective-permute-start | bytes 786440 | tf_op jit(solution)/shard_map/ppermute | solution.py:54
  101.9 4.3 %collective-permute-done.37.rest_4_ = bf16[512,256]{1,0:T(8,128)(2,1)S(1)} collective-permute-done((bf16[512,256]{1,0:T(8,128)(2,1)S(1)}, bf16[512,256]{1,0:T(8,128)(2,1)S(1)}, u32[]{:S(2)}, u32[]{:S(2)}) %collective-permute-start.37) | collective-permute-done | bytes 262176 | tf_op jit(solution)/shard_map/ppermute | solution.py:54
  106.1 1.6 %collective-permute-start.38 = (bf16[512,256]{1,0:T(8,128)(2,1)S(1)}, bf16[512,256]{1,0:T(8,128)(2,1)S(1)}, u32[]{:S(2)}, u32[]{:S(2)}) collective-permute-start(bf16[512,256]{1,0:T(8,128)(2,1)S(1)} %collective-permute-done.37.rest_4_), channel_id=1, source_target_pairs={{0,1},{1,2},{2,3},{3,0},{4,5},{5,6},{6,7},{7,4},{8,11},{9,8},{10,9... | collective-permute-start | bytes 786440 | tf_op jit(solution)/shard_map/ppermute | solution.py:54
  108.8 8.0 %collective-permute-start.39 = (bf16[512,256]{1,0:T(8,128)(2,1)S(1)}, bf16[512,256]{1,0:T(8,128)(2,1)S(1)}, u32[]{:S(2)}, u32[]{:S(2)}) collective-permute-start(bf16[512,256]{1,0:T(8,128)(2,1)S(1)} %collective-permute-done.35.rest_2_), channel_id=1, source_target_pairs={{0,4},{1,5},{2,6},{3,7},{4,0},{5,1},{6,2},{7,3},{8,12},{9,13},{10,... | collective-permute-start | bytes 786440 | tf_op jit(solution)/shard_map/ppermute | solution.py:54
  116.8 6.5 %collective-permute-done.39.rest_6_ = bf16[512,256]{1,0:T(8,128)(2,1)S(1)} collective-permute-done((bf16[512,256]{1,0:T(8,128)(2,1)S(1)}, bf16[512,256]{1,0:T(8,128)(2,1)S(1)}, u32[]{:S(2)}, u32[]{:S(2)}) %collective-permute-start.39) | collective-permute-done | bytes 262176 | tf_op jit(solution)/shard_map/ppermute | solution.py:54
  124.4 2.6 %apply_part.2 = (f32[256,768]{1,0:T(8,128)S(1)}, bf16[256,768]{1,0:T(8,128)(2,1)S(1)}) custom-call(s32[5]{0:T(128)S(1)} %stack.23.where, bf16[512,256]{1,0:T(8,128)(2,1)S(1)} %collective-permute-done.33.rest_0_, bf16[512,256]{1,0:T(8,128)(2,1)S(1)} %collective-permute-done.34.rest_1_, bf16[512,256]{1,0:T(8,128)(2,1)S(1)} %collective-permute-done.35.rest_2_, ...), custom_call_target="tpu_custom_call" | custom-call | flops 1610612736 | bytes 6422528 | tf_op jit(solution)/shard_map/apply_part/pallas_call | solution.py:188
  127.1 2.7 %apply_part.3 = (f32[256,768]{1,0:T(8,128)S(1)}, bf16[256,768]{1,0:T(8,128)(2,1)S(1)}) custom-call(s32[5]{0:T(128)S(1)} %stack.23.where, bf16[512,256]{1,0:T(8,128)(2,1)S(1)} %collective-permute-done.33.rest_0_, bf16[512,256]{1,0:T(8,128)(2,1)S(1)} %collective-permute-done.34.rest_1_, bf16[512,256]{1,0:T(8,128)(2,1)S(1)} %collective-permute-done.35.rest_2_, ...), custom_call_target="tpu_custom_call" | custom-call | flops 1610612736 | bytes 6422528 | tf_op jit(solution)/shard_map/apply_part/pallas_call | solution.py:188
  (81 shorter events, 30.0 us)
Async XLA Ops:
  0.1 21.4 %collective-permute-start = (bf16[256,1536]{1,0:T(8,128)(2,1)}, bf16[256,1536]{1,0:T(8,128)(2,1)S(1)}, u32[]{:S(2)}, u32[]{:S(2)}) collective-permute-start(bf16[256,1536]{1,0:T(8,128)(2,1)} %rest_8_.1), channel_id=1, source_target_pairs={{0,8},{1,9},{2,10},{3,11},{4,12},{5,13},{6,14},{7,15},{8,0},{9,1},... | collective-permute-start | bytes 2359304 | tf_op jit(solution)/shard_map/ppermute | solution.py:54
  0.1 21.4 %collective-permute-start.1 = (bf16[256,1536]{1,0:T(8,128)(2,1)}, bf16[256,1536]{1,0:T(8,128)(2,1)S(1)}, u32[]{:S(2)}, u32[]{:S(2)}) collective-permute-start(bf16[256,1536]{1,0:T(8,128)(2,1)} %rest_8_.1), channel_id=1, source_target_pairs={{0,96},{1,97},{2,98},{3,99},{4,100},{5,101},{6,102},{7,103},{8,40}... | collective-permute-start | bytes 2359304 | tf_op jit(solution)/shard_map/ppermute | solution.py:54
  3.0 20.1 %collective-permute-start.3 = (bf16[256,1536]{1,0:T(8,128)(2,1)}, bf16[256,1536]{1,0:T(8,128)(2,1)S(1)}, u32[]{:S(2)}, u32[]{:S(2)}) collective-permute-start(bf16[256,1536]{1,0:T(8,128)(2,1)} %rest_8_.1), channel_id=1, source_target_pairs={{0,16},{1,17},{2,18},{3,19},{4,20},{5,21},{6,22},{7,23},{8,24},{9,... | collective-permute-start | bytes 2359304 | tf_op jit(solution)/shard_map/ppermute | solution.py:54
  7.4 9.9 %collective-permute-start.5 = (bf16[128,1536]{1,0:T(8,128)(2,1)S(1)}, bf16[128,1536]{1,0:T(8,128)(2,1)S(1)}, u32[]{:S(2)}, u32[]{:S(2)}) collective-permute-start(bf16[128,1536]{1,0:T(8,128)(2,1)S(1)} %get-tuple-element.49), channel_id=1, source_target_pairs={{0,32},{1,33},{2,34},{3,35},{4,36},{5,37},{6,38},{7,39},{8,104},{9... | collective-permute-start | bytes 1179656 | tf_op jit(solution)/shard_map/ppermute | solution.py:54
  7.5 14.0 %collective-permute-start.2 = (bf16[128,1536]{1,0:T(8,128)(2,1)S(1)}, bf16[128,1536]{1,0:T(8,128)(2,1)S(1)}, u32[]{:S(2)}, u32[]{:S(2)}) collective-permute-start(bf16[128,1536]{1,0:T(8,128)(2,1)S(1)} %get-tuple-element.50), channel_id=1, source_target_pairs={{0,32},{1,33},{2,34},{3,35},{4,36},{5,37},{6,38},{7,39},{8,104},{9... | collective-permute-start | bytes 1179656 | tf_op jit(solution)/shard_map/ppermute | solution.py:54
  17.3 9.0 %collective-permute-start.6 = (bf16[128,1536]{1,0:T(8,128)(2,1)S(1)}, bf16[128,1536]{1,0:T(8,128)(2,1)S(1)}, u32[]{:S(2)}, u32[]{:S(2)}) collective-permute-start(bf16[128,1536]{1,0:T(8,128)(2,1)S(1)} %collective-permute-done.5), channel_id=1, source_target_pairs={{0,32},{1,33},{2,34},{3,35},{4,36},{5,37},{6,38},{7,39},{8,104},{9... | collective-permute-start | bytes 1179656 | tf_op jit(solution)/shard_map/ppermute | solution.py:54
  21.5 9.0 %collective-permute-start.7 = (bf16[128,1536]{1,0:T(8,128)(2,1)S(1)}, bf16[128,1536]{1,0:T(8,128)(2,1)S(1)}, u32[]{:S(2)}, u32[]{:S(2)}) collective-permute-start(bf16[128,1536]{1,0:T(8,128)(2,1)S(1)} %collective-permute-done.2), channel_id=1, source_target_pairs={{0,32},{1,33},{2,34},{3,35},{4,36},{5,37},{6,38},{7,39},{8,104},{9... | collective-permute-start | bytes 1179656 | tf_op jit(solution)/shard_map/ppermute | solution.py:54
  33.5 9.4 %collective-permute-start.12 = (bf16[512,256]{1,0:T(8,128)(2,1)S(1)}, bf16[512,256]{1,0:T(8,128)(2,1)S(1)}, u32[]{:S(2)}, u32[]{:S(2)}) collective-permute-start(bf16[512,256]{1,0:T(8,128)(2,1)S(1)} %get-tuple-element.41), channel_id=1, source_target_pairs={{0,3},{1,0},{2,1},{3,2},{4,7},{5,4},{6,5},{7,6},{8,9},{9,10},{10,1... | collective-permute-start | bytes 786440 | tf_op jit(solution)/shard_map/ppermute | solution.py:54
  37.7 7.7 %collective-permute-start.8 = (bf16[512,256]{1,0:T(8,128)(2,1)S(1)}, bf16[512,256]{1,0:T(8,128)(2,1)S(1)}, u32[]{:S(2)}, u32[]{:S(2)}) collective-permute-start(bf16[512,256]{1,0:T(8,128)(2,1)S(1)} %get-tuple-element.36), channel_id=1, source_target_pairs={{0,3},{1,0},{2,1},{3,2},{4,7},{5,4},{6,5},{7,6},{8,9},{9,10},{10,1... | collective-permute-start | bytes 786440 | tf_op jit(solution)/shard_map/ppermute | solution.py:54
  38.1 21.5 %collective-permute-start.15 = (bf16[256,1536]{1,0:T(8,128)(2,1)S(1)}, bf16[256,1536]{1,0:T(8,128)(2,1)S(1)}, u32[]{:S(2)}, u32[]{:S(2)}) collective-permute-start(bf16[256,1536]{1,0:T(8,128)(2,1)S(1)} %collective-permute-done.3.across.rest_12_), channel_id=1, source_target_pairs={{0,32},{1,33},{2,34},{3,35},{4,36},{5,37},{6,38},{7,39},{8,104},{9... | collective-permute-start | bytes 2359304 | tf_op jit(solution)/shard_map/ppermute | solution.py:54
  38.1 21.5 %collective-permute-start.16 = (bf16[256,1536]{1,0:T(8,128)(2,1)S(1)}, bf16[256,1536]{1,0:T(8,128)(2,1)S(1)}, u32[]{:S(2)}, u32[]{:S(2)}) collective-permute-start(bf16[256,1536]{1,0:T(8,128)(2,1)S(1)} %collective-permute-done.3.across.rest_12_), channel_id=1, source_target_pairs={{0,96},{1,97},{2,98},{3,99},{4,100},{5,101},{6,102},{7,103},{8,40}... | collective-permute-start | bytes 2359304 | tf_op jit(solution)/shard_map/ppermute | solution.py:54
  43.0 8.5 %collective-permute-start.13 = (bf16[512,256]{1,0:T(8,128)(2,1)S(1)}, bf16[512,256]{1,0:T(8,128)(2,1)S(1)}, u32[]{:S(2)}, u32[]{:S(2)}) collective-permute-start(bf16[512,256]{1,0:T(8,128)(2,1)S(1)} %add_convert_fusion.3), channel_id=1, source_target_pairs={{0,3},{1,0},{2,1},{3,2},{4,7},{5,4},{6,5},{7,6},{8,9},{9,10},{10,1... | collective-permute-start | bytes 786440 | tf_op jit(solution)/shard_map/ppermute | solution.py:54
  45.5 9.6 %collective-permute-start.9 = (bf16[512,256]{1,0:T(8,128)(2,1)S(1)}, bf16[512,256]{1,0:T(8,128)(2,1)S(1)}, u32[]{:S(2)}, u32[]{:S(2)}) collective-permute-start(bf16[512,256]{1,0:T(8,128)(2,1)S(1)} %add_convert_fusion.5), channel_id=1, source_target_pairs={{0,3},{1,0},{2,1},{3,2},{4,7},{5,4},{6,5},{7,6},{8,9},{9,10},{10,1... | collective-permute-start | bytes 786440 | tf_op jit(solution)/shard_map/ppermute | solution.py:54
  48.3 7.7 %collective-permute-start.11 = (bf16[512,256]{1,0:T(8,128)(2,1)S(1)}, bf16[512,256]{1,0:T(8,128)(2,1)S(1)}, u32[]{:S(2)}, u32[]{:S(2)}) collective-permute-start(bf16[512,256]{1,0:T(8,128)(2,1)S(1)} %add_convert_fusion.4), channel_id=1, source_target_pairs={{0,1},{1,2},{2,3},{3,0},{4,5},{5,6},{6,7},{7,4},{8,11},{9,8},{10,9... | collective-permute-start | bytes 786440 | tf_op jit(solution)/shard_map/ppermute | solution.py:54
  59.8 10.6 %collective-permute-start.20 = (bf16[512,256]{1,0:T(8,128)(2,1)S(1)}, bf16[512,256]{1,0:T(8,128)(2,1)S(1)}, u32[]{:S(2)}, u32[]{:S(2)}) collective-permute-start(bf16[512,256]{1,0:T(8,128)(2,1)S(1)} %add_convert_fusion.1.rest_0_), channel_id=1, source_target_pairs={{0,16},{1,17},{2,18},{3,19},{4,20},{5,21},{6,22},{7,23},{8,24},{9,... | collective-permute-start | bytes 786440 | tf_op jit(solution)/shard_map/ppermute | solution.py:54
  63.0 9.2 %collective-permute-start.17 = (bf16[512,256]{1,0:T(8,128)(2,1)S(1)}, bf16[512,256]{1,0:T(8,128)(2,1)S(1)}, u32[]{:S(2)}, u32[]{:S(2)}) collective-permute-start(bf16[512,256]{1,0:T(8,128)(2,1)S(1)} %add_convert_fusion.1.rest_0_), channel_id=1, source_target_pairs={{0,1},{1,2},{2,3},{3,0},{4,5},{5,6},{6,7},{7,4},{8,11},{9,8},{10,9... | collective-permute-start | bytes 786440 | tf_op jit(solution)/shard_map/ppermute | solution.py:54
  64.6 9.0 %collective-permute-start.18 = (bf16[512,256]{1,0:T(8,128)(2,1)S(1)}, bf16[512,256]{1,0:T(8,128)(2,1)S(1)}, u32[]{:S(2)}, u32[]{:S(2)}) collective-permute-start(bf16[512,256]{1,0:T(8,128)(2,1)S(1)} %add_convert_fusion.1.rest_0_), channel_id=1, source_target_pairs={{0,3},{1,0},{2,1},{3,2},{4,7},{5,4},{6,5},{7,6},{8,9},{9,10},{10,1... | collective-permute-start | bytes 786440 | tf_op jit(solution)/shard_map/ppermute | solution.py:54
  66.2 9.6 %collective-permute-start.28 = (bf16[256,512]{1,0:T(8,128)(2,1)S(1)}, bf16[256,512]{1,0:T(8,128)(2,1)S(1)}, u32[]{:S(2)}, u32[]{:S(2)}) collective-permute-start(bf16[256,512]{1,0:T(8,128)(2,1)S(1)} %pad_maximum_fusion.rest_8_), channel_id=1, source_target_pairs={{0,4},{1,5},{2,6},{3,7},{4,0},{5,1},{6,2},{7,3},{8,12},{9,13},{10,... | collective-permute-start | bytes 786440 | tf_op jit(solution)/shard_map/ppermute | solution.py:54
  67.0 8.9 %collective-permute-start.25 = (bf16[256,512]{1,0:T(8,128)(2,1)S(1)}, bf16[256,512]{1,0:T(8,128)(2,1)S(1)}, u32[]{:S(2)}, u32[]{:S(2)}) collective-permute-start(bf16[256,512]{1,0:T(8,128)(2,1)S(1)} %pad_maximum_fusion.rest_8_), channel_id=1, source_target_pairs={{0,32},{1,33},{2,34},{3,35},{4,36},{5,37},{6,38},{7,39},{8,104},{9... | collective-permute-start | bytes 786440 | tf_op jit(solution)/shard_map/ppermute | solution.py:54
  73.6 8.9 %collective-permute-start.19 = (bf16[512,256]{1,0:T(8,128)(2,1)S(1)}, bf16[512,256]{1,0:T(8,128)(2,1)S(1)}, u32[]{:S(2)}, u32[]{:S(2)}) collective-permute-start(bf16[512,256]{1,0:T(8,128)(2,1)S(1)} %collective-permute-done.17.rest_1_), channel_id=1, source_target_pairs={{0,1},{1,2},{2,3},{3,0},{4,5},{5,6},{6,7},{7,4},{8,11},{9,8},{10,9... | collective-permute-start | bytes 786440 | tf_op jit(solution)/shard_map/ppermute | solution.py:54
  75.9 10.7 %collective-permute-start.22 = (bf16[512,256]{1,0:T(8,128)(2,1)S(1)}, bf16[512,256]{1,0:T(8,128)(2,1)S(1)}, u32[]{:S(2)}, u32[]{:S(2)}) collective-permute-start(bf16[512,256]{1,0:T(8,128)(2,1)S(1)} %collective-permute-done.18.rest_2_), channel_id=1, source_target_pairs={{0,16},{1,17},{2,18},{3,19},{4,20},{5,21},{6,22},{7,23},{8,24},{9,... | collective-permute-start | bytes 786440 | tf_op jit(solution)/shard_map/ppermute | solution.py:54
  77.7 8.8 %collective-permute-start.27 = (bf16[256,512]{1,0:T(8,128)(2,1)S(1)}, bf16[256,512]{1,0:T(8,128)(2,1)S(1)}, u32[]{:S(2)}, u32[]{:S(2)}) collective-permute-start(bf16[256,512]{1,0:T(8,128)(2,1)S(1)} %collective-permute-done.25.rest_9_), channel_id=1, source_target_pairs={{0,32},{1,33},{2,34},{3,35},{4,36},{5,37},{6,38},{7,39},{8,104},{9... | collective-permute-start | bytes 786440 | tf_op jit(solution)/shard_map/ppermute | solution.py:54
  79.7 10.4 %collective-permute-start.30 = (bf16[256,512]{1,0:T(8,128)(2,1)S(1)}, bf16[256,512]{1,0:T(8,128)(2,1)S(1)}, u32[]{:S(2)}, u32[]{:S(2)}) collective-permute-start(bf16[256,512]{1,0:T(8,128)(2,1)S(1)} %collective-permute-done.26.rest_10_), channel_id=1, source_target_pairs={{0,4},{1,5},{2,6},{3,7},{4,0},{5,1},{6,2},{7,3},{8,12},{9,13},{10,... | collective-permute-start | bytes 786440 | tf_op jit(solution)/shard_map/ppermute | solution.py:54
  82.6 7.6 %collective-permute-start.23 = (bf16[512,256]{1,0:T(8,128)(2,1)S(1)}, bf16[512,256]{1,0:T(8,128)(2,1)S(1)}, u32[]{:S(2)}, u32[]{:S(2)}) collective-permute-start(bf16[512,256]{1,0:T(8,128)(2,1)S(1)} %collective-permute-done.21.rest_5_), channel_id=1, source_target_pairs={{0,1},{1,2},{2,3},{3,0},{4,5},{5,6},{6,7},{7,4},{8,11},{9,8},{10,9... | collective-permute-start | bytes 786440 | tf_op jit(solution)/shard_map/ppermute | solution.py:54
  94.8 22.0 %collective-permute-start.41 = (bf16[256,1536]{1,0:T(8,128)(2,1)S(1)}, bf16[256,1536]{1,0:T(8,128)(2,1)S(1)}, u32[]{:S(2)}, u32[]{:S(2)}) collective-permute-start(bf16[256,1536]{1,0:T(8,128)(2,1)S(1)} %collective-permute-done.15.rest_13_), channel_id=1, source_target_pairs={{0,32},{1,33},{2,34},{3,35},{4,36},{5,37},{6,38},{7,39},{8,104},{9... | collective-permute-start | bytes 2359304 | tf_op jit(solution)/shard_map/ppermute | solution.py:54
  94.9 11.2 %collective-permute-start.37 = (bf16[512,256]{1,0:T(8,128)(2,1)S(1)}, bf16[512,256]{1,0:T(8,128)(2,1)S(1)}, u32[]{:S(2)}, u32[]{:S(2)}) collective-permute-start(bf16[512,256]{1,0:T(8,128)(2,1)S(1)} %add_convert_fusion), channel_id=1, source_target_pairs={{0,4},{1,5},{2,6},{3,7},{4,20},{5,21},{6,22},{7,23},{8,12},{9,13},... | collective-permute-start | bytes 786440 | tf_op jit(solution)/shard_map/ppermute | solution.py:54
  98.6 10.1 %collective-permute-start.34 = (bf16[512,256]{1,0:T(8,128)(2,1)S(1)}, bf16[512,256]{1,0:T(8,128)(2,1)S(1)}, u32[]{:S(2)}, u32[]{:S(2)}) collective-permute-start(bf16[512,256]{1,0:T(8,128)(2,1)S(1)} %collective-permute-done.33.rest_0_), channel_id=1, source_target_pairs={{0,1},{1,2},{2,3},{3,0},{4,5},{5,6},{6,7},{7,4},{8,11},{9,8},{10,9... | collective-permute-start | bytes 786440 | tf_op jit(solution)/shard_map/ppermute | solution.py:54
  99.8 8.9 %collective-permute-start.35 = (bf16[512,256]{1,0:T(8,128)(2,1)S(1)}, bf16[512,256]{1,0:T(8,128)(2,1)S(1)}, u32[]{:S(2)}, u32[]{:S(2)}) collective-permute-start(bf16[512,256]{1,0:T(8,128)(2,1)S(1)} %collective-permute-done.33.rest_0_), channel_id=1, source_target_pairs={{0,3},{1,0},{2,1},{3,2},{4,7},{5,4},{6,5},{7,6},{8,9},{9,10},{10,1... | collective-permute-start | bytes 786440 | tf_op jit(solution)/shard_map/ppermute | solution.py:54
  106.1 10.7 %collective-permute-start.38 = (bf16[512,256]{1,0:T(8,128)(2,1)S(1)}, bf16[512,256]{1,0:T(8,128)(2,1)S(1)}, u32[]{:S(2)}, u32[]{:S(2)}) collective-permute-start(bf16[512,256]{1,0:T(8,128)(2,1)S(1)} %collective-permute-done.37.rest_4_), channel_id=1, source_target_pairs={{0,1},{1,2},{2,3},{3,0},{4,5},{5,6},{6,7},{7,4},{8,11},{9,8},{10,9... | collective-permute-start | bytes 786440 | tf_op jit(solution)/shard_map/ppermute | solution.py:54
  108.7 8.1 %collective-permute-start.36 = (bf16[512,256]{1,0:T(8,128)(2,1)S(1)}, bf16[512,256]{1,0:T(8,128)(2,1)S(1)}, u32[]{:S(2)}, u32[]{:S(2)}) collective-permute-start(bf16[512,256]{1,0:T(8,128)(2,1)S(1)} %collective-permute-done.34.rest_1_), channel_id=1, source_target_pairs={{0,1},{1,2},{2,3},{3,0},{4,5},{5,6},{6,7},{7,4},{8,11},{9,8},{10,9... | collective-permute-start | bytes 786440 | tf_op jit(solution)/shard_map/ppermute | solution.py:54
  108.8 14.6 %collective-permute-start.39 = (bf16[512,256]{1,0:T(8,128)(2,1)S(1)}, bf16[512,256]{1,0:T(8,128)(2,1)S(1)}, u32[]{:S(2)}, u32[]{:S(2)}) collective-permute-start(bf16[512,256]{1,0:T(8,128)(2,1)S(1)} %collective-permute-done.35.rest_2_), channel_id=1, source_target_pairs={{0,4},{1,5},{2,6},{3,7},{4,0},{5,1},{6,2},{7,3},{8,12},{9,13},{10,... | collective-permute-start | bytes 786440 | tf_op jit(solution)/shard_map/ppermute | solution.py:54
  116.8 7.6 %collective-permute-start.40 = (bf16[512,256]{1,0:T(8,128)(2,1)S(1)}, bf16[512,256]{1,0:T(8,128)(2,1)S(1)}, u32[]{:S(2)}, u32[]{:S(2)}) collective-permute-start(bf16[512,256]{1,0:T(8,128)(2,1)S(1)} %collective-permute-done.38.rest_5_), channel_id=1, source_target_pairs={{0,1},{1,2},{2,3},{3,0},{4,5},{5,6},{6,7},{7,4},{8,11},{9,8},{10,9... | collective-permute-start | bytes 786440 | tf_op jit(solution)/shard_map/ppermute | solution.py:54
  (13 other events, 86.0 us)

commit v11 on v10

--- a/solution.py
+++ b/solution.py
@@ -72,24 +72,21 @@
     return lax.dot_general(left, right, (((1,), (0,)), ((), ())), preferred_element_type=jnp.float32)
 
 
-def gram_near_kernel(own, other, fore, back, out):
-    for r, rows in enumerate((own, other)):
+def gram_near_kernel(first, second, own, fore, back, out):
+    for r, rows in enumerate((first, second)):
         for q, cols in enumerate((own, fore, back)):
             part = nt(rows[...], cols[...])
             out[q, r * BLOCK : (r + 1) * BLOCK] = part.astype(out.dtype)
 
 
-def gram_kernel(where, own, other, across, across_other, fore, back, far, near, *rest):
+def gram_kernel(where, own, other, across, across_other, far, near, near_across, *rest):
     outs, tiles = rest[:8], rest[8]
     x, yh, core, yl, z = (where[i] for i in range(5))
     tiles[0, :3] = near[...]
-    for r, rows in enumerate((own, other)):
+    tiles[1, :3] = near_across[...]
+    for r, rows in enumerate((own, other, across, across_other)):
         part = nt(rows[...], far[...])
-        tiles[0, 3, r * BLOCK : (r + 1) * BLOCK] = part.astype(tiles.dtype)
-    for r, rows in enumerate((across, across_other)):
-        for q, cols in enumerate((own, fore, back, far)):
-            part = nt(rows[...], cols[...])
-            tiles[1, q, r * BLOCK : (r + 1) * BLOCK] = part.astype(tiles.dtype)
+        tiles[r // 2, 3, (r % 2) * BLOCK : (r % 2 + 1) * BLOCK] = part.astype(tiles.dtype)
     for index, out in enumerate(outs):
         row = lax.rem(yl + index // 4 + yh, 2)
         col = place(z + ahead(index % 4, core) - x, core)
@@ -144,31 +141,31 @@
     return pl.CostEstimate(flops=flops, bytes_accessed=moved, transcendentals=0)
 
 
-def gram_near(own, other, fore, back):
+def gram_near(first, second, own, fore, back):
     depth = own.shape[1]
     return pl.pallas_call(
         gram_near_kernel,
-        in_specs=[whole() for _ in range(4)],
+        in_specs=[whole() for _ in range(5)],
         out_specs=whole(),
         out_shape=jax.ShapeDtypeStruct((3, TILE, BLOCK), jnp.bfloat16),
         compiler_params=params(24),
         cost_estimate=cost(2 * 3 * BLOCK * TILE * depth, 4 * BLOCK * depth * 2 + 3 * BLOCK * TILE * 2),
         name="gram_near",
-    )(own, other, fore, back)
-
-
-def gram_tiles(where, own, other, across, across_other, fore, back, far, near):
+    )(first, second, own, fore, back)
+
+
+def gram_tiles(where, own, other, across, across_other, far, near, near_across):
     depth = own.shape[1]
     return pl.pallas_call(
         gram_kernel,
-        in_specs=[smem()] + [whole() for _ in range(8)],
+        in_specs=[smem()] + [whole() for _ in range(7)],
         out_specs=[whole() for _ in range(8)],
         out_shape=[jax.ShapeDtypeStruct((TILE, BLOCK), jnp.bfloat16) for _ in range(8)],
         scratch_shapes=[pltpu.VMEM((2, 4, TILE, BLOCK), jnp.bfloat16)],
         compiler_params=params(24),
-        cost_estimate=cost(2 * 5 * BLOCK * TILE * depth, 7 * BLOCK * depth * 2 + 11 * BLOCK * TILE * 2),
+        cost_estimate=cost(2 * 2 * BLOCK * TILE * depth, 5 * BLOCK * depth * 2 + 14 * BLOCK * TILE * 2),
         name="gram_tiles",
-    )(where, own, other, across, across_other, fore, back, far, near)
+    )(where, own, other, across, across_other, far, near, near_across)
 
 
 def square_part(others, where, left, right):
@@ -240,11 +237,12 @@
     top = send(iterate[:half], "x_fore")
     far = [send(top, "x_fore"), send(low, "x_fore")]
     fore = jnp.concatenate([top, low], axis=0)
-    near = gram_near(iterate, other, fore, back)
-    far[0], near = lax.optimization_barrier((far[0], near))
+    near = gram_near(iterate, other, iterate, fore, back)
+    rows = (iterate, other, across, send(across, "core"))
+    near_across = gram_near(rows[2], rows[3], iterate, fore, back)
+    far[0], near, near_across = lax.optimization_barrier((far[0], near, near_across))
     far = jnp.concatenate(far, axis=0)
-    rows = (iterate, other, across, send(across, "core"))
-    gram_left = sum_over_col(gram_tiles(where, *rows, fore, back, far, near))
+    gram_left = sum_over_col(gram_tiles(where, *rows, far, near, near_across))
 
     across_fore, across_back = send(across, "x_fore"), send(across, "x_back")
     gram_left, across_fore, across_back = lax.optimization_barrier((gram_left, across_fore, across_back))

time: 134 us -> 141 us (1.052)
  waiting for transfers between devices: 60.2 us -> 64.8 us
  starting transfers between devices: 56.9 us -> 58.7 us
    ppermute x44, waiting for transfers between devices: 60.2 us -> 64.8 us  [send(): return lax.ppermute(value, ('row', 'col'), pairs(MOVES[move]))]
    ppermute x44, starting transfers between devices: 56.9 us -> 58.7 us  [send(): return lax.ppermute(value, ('row', 'col'), pairs(MOVES[move]))]
    pallas_call x2 -> x3, Pallas kernels: 4.4 us -> 4.69 us  [the longest x2 2.89 us: gram_near(): pl.pallas_call(gram_near_kernel, in_specs=[whole() for _ in range(5)], ou...]
  transfers between devices with their start and end apart: 44 -> 44, of which waited for: 25 -> 24; matrix products, arithmetic and copies ran while one was open for 1% -> 1% of each run, Pallas kernels for 4% -> 5%
where the time goes in v11:
time: 141 us; the launch traced here: 139 us
  waiting for transfers between devices  64.8 us (46%)
  starting transfers between devices  58.7 us (42%)
  Pallas kernels  12.7 us (9%)
  other arithmetic  1.71 us (1%)
    ppermute x44, waiting for transfers between devices, send(): return lax.ppermute(value, ('row', 'col'), pairs(MOVES[move]))  64.8 us
    ppermute x44, starting transfers between devices, send(): return lax.ppermute(value, ('row', 'col'), pairs(MOVES[move]))  58.7 us
    pallas_call x2, Pallas kernels, apply_part(): pl.pallas_call(functools.partial(apply_kernel, begin), in_specs=[smem()]...  5.31 us
    pallas_call x2, Pallas kernels, gram_near(): pl.pallas_call(gram_near_kernel, in_specs=[whole() for _ in range(5)], ou...  2.89 us
  transfers between devices with their start and end apart: 44, of which 24 were waited for; matrix products, arithmetic and copies ran while one was open for 1% of the time, Pallas kernels for 5%

profile of v11, /device:TPU:0, one launch (start us, length us, event | category | flops | bytes accessed | tf_op | source)
XLA Modules:
  0.0 139.5 jit_solution(16430186516006785098)
XLA Ops:
  0.1 3.3 %collective-permute-start.3 = (bf16[256,1536]{1,0:T(8,128)(2,1)}, bf16[256,1536]{1,0:T(8,128)(2,1)S(1)}, u32[]{:S(2)}, u32[]{:S(2)}) collective-permute-start(bf16[256,1536]{1,0:T(8,128)(2,1)} %rest_8_.1), channel_id=1, source_target_pairs={{0,16},{1,17},{2,18},{3,19},{4,20},{5,21},{6,22},{7,23},{8,24},{9,... | collective-permute-start | bytes 2359304 | tf_op jit(solution)/shard_map/ppermute | solution.py:54
  3.4 2.8 %collective-permute-start.1 = (bf16[256,1536]{1,0:T(8,128)(2,1)}, bf16[256,1536]{1,0:T(8,128)(2,1)S(1)}, u32[]{:S(2)}, u32[]{:S(2)}) collective-permute-start(bf16[256,1536]{1,0:T(8,128)(2,1)} %rest_8_.1), channel_id=1, source_target_pairs={{0,96},{1,97},{2,98},{3,99},{4,100},{5,101},{6,102},{7,103},{8,40}... | collective-permute-start | bytes 2359304 | tf_op jit(solution)/shard_map/ppermute | solution.py:54
  7.4 13.7 %collective-permute-done.3.first.across.rest_12_ = bf16[256,1536]{1,0:T(8,128)(2,1)S(1)} collective-permute-done((bf16[256,1536]{1,0:T(8,128)(2,1)}, bf16[256,1536]{1,0:T(8,128)(2,1)S(1)}, u32[]{:S(2)}, u32[]{:S(2)}) %collective-permute-start.3) | collective-permute-done | bytes 786464 | tf_op jit(solution)/shard_map/ppermute | solution.py:54
  24.2 5.9 %collective-permute-done.2 = bf16[128,1536]{1,0:T(8,128)(2,1)S(1)} collective-permute-done((bf16[128,1536]{1,0:T(8,128)(2,1)S(1)}, bf16[128,1536]{1,0:T(8,128)(2,1)S(1)}, u32[]{:S(2)}, u32[]{:S(2)}) %collective-permute-start.2) | collective-permute-done | bytes 393248 | tf_op jit(solution)/shard_map/ppermute | solution.py:54
  34.4 4.8 %collective-permute-done.7 = bf16[128,1536]{1,0:T(8,128)(2,1)S(1)} collective-permute-done((bf16[128,1536]{1,0:T(8,128)(2,1)S(1)}, bf16[128,1536]{1,0:T(8,128)(2,1)S(1)}, u32[]{:S(2)}, u32[]{:S(2)}) %collective-permute-start.7) | collective-permute-done | bytes 393248 | tf_op jit(solution)/shard_map/ppermute | solution.py:54
  39.1 1.8 %gram_tiles.1 = (bf16[512,256]{1,0:T(8,128)(2,1)S(1)}, bf16[512,256]{1,0:T(8,128)(2,1)S(1)}, bf16[512,256]{1,0:T(8,128)(2,1)S(1)}, bf16[512,256]{1,0:T(8,128)(2,...) custom-call(s32[5]{0:T(128)S(1)} %stack.23.where, ...), custom_call_target="tpu_custom_call" | custom-call | flops 805306368 | bytes 7602176 | tf_op jit(solution)/shard_map/gram_tiles/pallas_call | solution.py:159
  41.0 4.2 %collective-permute-start.12 = (bf16[512,256]{1,0:T(8,128)(2,1)S(1)}, bf16[512,256]{1,0:T(8,128)(2,1)S(1)}, u32[]{:S(2)}, u32[]{:S(2)}) collective-permute-start(bf16[512,256]{1,0:T(8,128)(2,1)S(1)} %get-tuple-element.43), channel_id=1, source_target_pairs={{0,3},{1,0},{2,1},{3,2},{4,7},{5,4},{6,5},{7,6},{8,9},{9,10},{10,1... | collective-permute-start | bytes 786440 | tf_op jit(solution)/shard_map/ppermute | solution.py:54
  45.5 3.2 %collective-permute-start.16 = (bf16[256,1536]{1,0:T(8,128)(2,1)S(1)}, bf16[256,1536]{1,0:T(8,128)(2,1)S(1)}, u32[]{:S(2)}, u32[]{:S(2)}) collective-permute-start(bf16[256,1536]{1,0:T(8,128)(2,1)S(1)} %collective-permute-done.3.first.across.rest_12_), channel_id=1, source_target_pairs={{0,96},{1,97},{2,98},{3,99},{4,100},{5,101},{6,102},{7,103},{8,40}... | collective-permute-start | bytes 2359304 | tf_op jit(solution)/shard_map/ppermute | solution.py:54
  48.7 1.6 %collective-permute-start.10 = (bf16[512,256]{1,0:T(8,128)(2,1)S(1)}, bf16[512,256]{1,0:T(8,128)(2,1)S(1)}, u32[]{:S(2)}, u32[]{:S(2)}) collective-permute-start(bf16[512,256]{1,0:T(8,128)(2,1)S(1)} %get-tuple-element.40), channel_id=1, source_target_pairs={{0,4},{1,5},{2,6},{3,7},{4,0},{5,1},{6,2},{7,3},{8,12},{9,13},{10,... | collective-permute-start | bytes 786440 | tf_op jit(solution)/shard_map/ppermute | solution.py:54
  50.4 2.4 %collective-permute-start.13 = (bf16[512,256]{1,0:T(8,128)(2,1)S(1)}, bf16[512,256]{1,0:T(8,128)(2,1)S(1)}, u32[]{:S(2)}, u32[]{:S(2)}) collective-permute-start(bf16[512,256]{1,0:T(8,128)(2,1)S(1)} %add_convert_fusion.3), channel_id=1, source_target_pairs={{0,3},{1,0},{2,1},{3,2},{4,7},{5,4},{6,5},{7,6},{8,9},{9,10},{10,1... | collective-permute-start | bytes 786440 | tf_op jit(solution)/shard_map/ppermute | solution.py:54
  52.9 2.7 %collective-permute-start.9 = (bf16[512,256]{1,0:T(8,128)(2,1)S(1)}, bf16[512,256]{1,0:T(8,128)(2,1)S(1)}, u32[]{:S(2)}, u32[]{:S(2)}) collective-permute-start(bf16[512,256]{1,0:T(8,128)(2,1)S(1)} %add_convert_fusion.5), channel_id=1, source_target_pairs={{0,3},{1,0},{2,1},{3,2},{4,7},{5,4},{6,5},{7,6},{8,9},{9,10},{10,1... | collective-permute-start | bytes 786440 | tf_op jit(solution)/shard_map/ppermute | solution.py:54
  56.9 2.6 %collective-permute-done.13 = bf16[512,256]{1,0:T(8,128)(2,1)S(1)} collective-permute-done((bf16[512,256]{1,0:T(8,128)(2,1)S(1)}, bf16[512,256]{1,0:T(8,128)(2,1)S(1)}, u32[]{:S(2)}, u32[]{:S(2)}) %collective-permute-start.13) | collective-permute-done | bytes 262176 | tf_op jit(solution)/shard_map/ppermute | solution.py:54
  60.2 2.1 %collective-permute-done.9 = bf16[512,256]{1,0:T(8,128)(2,1)S(1)} collective-permute-done((bf16[512,256]{1,0:T(8,128)(2,1)S(1)}, bf16[512,256]{1,0:T(8,128)(2,1)S(1)}, u32[]{:S(2)}, u32[]{:S(2)}) %collective-permute-start.9) | collective-permute-done | bytes 262176 | tf_op jit(solution)/shard_map/ppermute | solution.py:54
  63.4 2.6 %collective-permute-done.14 = bf16[512,256]{1,0:T(8,128)(2,1)S(1)} collective-permute-done((bf16[512,256]{1,0:T(8,128)(2,1)S(1)}, bf16[512,256]{1,0:T(8,128)(2,1)S(1)}, u32[]{:S(2)}, u32[]{:S(2)}) %collective-permute-start.14) | collective-permute-done | bytes 262176 | tf_op jit(solution)/shard_map/ppermute | solution.py:54
  66.4 3.3 %collective-permute-start.20 = (bf16[512,256]{1,0:T(8,128)(2,1)S(1)}, bf16[512,256]{1,0:T(8,128)(2,1)S(1)}, u32[]{:S(2)}, u32[]{:S(2)}) collective-permute-start(bf16[512,256]{1,0:T(8,128)(2,1)S(1)} %add_convert_fusion.1.rest_0_), channel_id=1, source_target_pairs={{0,16},{1,17},{2,18},{3,19},{4,20},{5,21},{6,22},{7,23},{8,24},{9,... | collective-permute-start | bytes 786440 | tf_op jit(solution)/shard_map/ppermute | solution.py:54
  69.7 1.6 %collective-permute-start.17 = (bf16[512,256]{1,0:T(8,128)(2,1)S(1)}, bf16[512,256]{1,0:T(8,128)(2,1)S(1)}, u32[]{:S(2)}, u32[]{:S(2)}) collective-permute-start(bf16[512,256]{1,0:T(8,128)(2,1)S(1)} %add_convert_fusion.1.rest_0_), channel_id=1, source_target_pairs={{0,1},{1,2},{2,3},{3,0},{4,5},{5,6},{6,7},{7,4},{8,11},{9,8},{10,9... | collective-permute-start | bytes 786440 | tf_op jit(solution)/shard_map/ppermute | solution.py:54
  71.3 1.6 %collective-permute-start.18 = (bf16[512,256]{1,0:T(8,128)(2,1)S(1)}, bf16[512,256]{1,0:T(8,128)(2,1)S(1)}, u32[]{:S(2)}, u32[]{:S(2)}) collective-permute-start(bf16[512,256]{1,0:T(8,128)(2,1)S(1)} %add_convert_fusion.1.rest_0_), channel_id=1, source_target_pairs={{0,3},{1,0},{2,1},{3,2},{4,7},{5,4},{6,5},{7,6},{8,9},{9,10},{10,1... | collective-permute-start | bytes 786440 | tf_op jit(solution)/shard_map/ppermute | solution.py:54
  73.7 3.4 %collective-permute-done.20.rest_4_ = bf16[512,256]{1,0:T(8,128)(2,1)S(1)} collective-permute-done((bf16[512,256]{1,0:T(8,128)(2,1)S(1)}, bf16[512,256]{1,0:T(8,128)(2,1)S(1)}, u32[]{:S(2)}, u32[]{:S(2)}) %collective-permute-start.20) | collective-permute-done | bytes 262176 | tf_op jit(solution)/shard_map/ppermute | solution.py:54
  78.5 1.8 %collective-permute-start.21 = (bf16[512,256]{1,0:T(8,128)(2,1)S(1)}, bf16[512,256]{1,0:T(8,128)(2,1)S(1)}, u32[]{:S(2)}, u32[]{:S(2)}) collective-permute-start(bf16[512,256]{1,0:T(8,128)(2,1)S(1)} %collective-permute-done.20.rest_4_), channel_id=1, source_target_pairs={{0,1},{1,2},{2,3},{3,0},{4,5},{5,6},{6,7},{7,4},{8,11},{9,8},{10,9... | collective-permute-start | bytes 786440 | tf_op jit(solution)/shard_map/ppermute | solution.py:54
  80.3 2.2 %collective-permute-done.28.rest_12_ = bf16[256,512]{1,0:T(8,128)(2,1)S(1)} collective-permute-done((bf16[256,512]{1,0:T(8,128)(2,1)S(1)}, bf16[256,512]{1,0:T(8,128)(2,1)S(1)}, u32[]{:S(2)}, u32[]{:S(2)}) %collective-permute-start.28) | collective-permute-done | bytes 262176 | tf_op jit(solution)/shard_map/ppermute | solution.py:54
  82.6 1.8 %collective-permute-start.22 = (bf16[512,256]{1,0:T(8,128)(2,1)S(1)}, bf16[512,256]{1,0:T(8,128)(2,1)S(1)}, u32[]{:S(2)}, u32[]{:S(2)}) collective-permute-start(bf16[512,256]{1,0:T(8,128)(2,1)S(1)} %collective-permute-done.18.rest_2_), channel_id=1, source_target_pairs={{0,16},{1,17},{2,18},{3,19},{4,20},{5,21},{6,22},{7,23},{8,24},{9,... | collective-permute-start | bytes 786440 | tf_op jit(solution)/shard_map/ppermute | solution.py:54
  86.7 2.1 %collective-permute-done.19.rest_3_ = bf16[512,256]{1,0:T(8,128)(2,1)S(1)} collective-permute-done((bf16[512,256]{1,0:T(8,128)(2,1)S(1)}, bf16[512,256]{1,0:T(8,128)(2,1)S(1)}, u32[]{:S(2)}, u32[]{:S(2)}) %collective-permute-start.19) | collective-permute-done | bytes 262176 | tf_op jit(solution)/shard_map/ppermute | solution.py:54
  90.2 3.1 %collective-permute-done.22.rest_6_ = bf16[512,256]{1,0:T(8,128)(2,1)S(1)} collective-permute-done((bf16[512,256]{1,0:T(8,128)(2,1)S(1)}, bf16[512,256]{1,0:T(8,128)(2,1)S(1)}, u32[]{:S(2)}, u32[]{:S(2)}) %collective-permute-start.22) | collective-permute-done | bytes 262176 | tf_op jit(solution)/shard_map/ppermute | solution.py:54
  93.3 3.7 %collective-permute-done.30.rest_14_ = bf16[256,512]{1,0:T(8,128)(2,1)S(1)} collective-permute-done((bf16[256,512]{1,0:T(8,128)(2,1)S(1)}, bf16[256,512]{1,0:T(8,128)(2,1)S(1)}, u32[]{:S(2)}, u32[]{:S(2)}) %collective-permute-start.30) | collective-permute-done | bytes 262176 | tf_op jit(solution)/shard_map/ppermute | solution.py:54
  101.6 4.7 %collective-permute-start.37 = (bf16[512,256]{1,0:T(8,128)(2,1)S(1)}, bf16[512,256]{1,0:T(8,128)(2,1)S(1)}, u32[]{:S(2)}, u32[]{:S(2)}) collective-permute-start(bf16[512,256]{1,0:T(8,128)(2,1)S(1)} %add_convert_fusion), channel_id=1, source_target_pairs={{0,4},{1,5},{2,6},{3,7},{4,20},{5,21},{6,22},{7,23},{8,12},{9,13},... | collective-permute-start | bytes 786440 | tf_op jit(solution)/shard_map/ppermute | solution.py:54
  106.6 2.9 %collective-permute-start.35 = (bf16[512,256]{1,0:T(8,128)(2,1)S(1)}, bf16[512,256]{1,0:T(8,128)(2,1)S(1)}, u32[]{:S(2)}, u32[]{:S(2)}) collective-permute-start(bf16[512,256]{1,0:T(8,128)(2,1)S(1)} %collective-permute-done.33.rest_0_), channel_id=1, source_target_pairs={{0,3},{1,0},{2,1},{3,2},{4,7},{5,4},{6,5},{7,6},{8,9},{9,10},{10,1... | collective-permute-start | bytes 786440 | tf_op jit(solution)/shard_map/ppermute | solution.py:54
  109.5 3.3 %collective-permute-done.37.rest_4_ = bf16[512,256]{1,0:T(8,128)(2,1)S(1)} collective-permute-done((bf16[512,256]{1,0:T(8,128)(2,1)S(1)}, bf16[512,256]{1,0:T(8,128)(2,1)S(1)}, u32[]{:S(2)}, u32[]{:S(2)}) %collective-permute-start.37) | collective-permute-done | bytes 262176 | tf_op jit(solution)/shard_map/ppermute | solution.py:54
  112.8 1.6 %collective-permute-start.38 = (bf16[512,256]{1,0:T(8,128)(2,1)S(1)}, bf16[512,256]{1,0:T(8,128)(2,1)S(1)}, u32[]{:S(2)}, u32[]{:S(2)}) collective-permute-start(bf16[512,256]{1,0:T(8,128)(2,1)S(1)} %collective-permute-done.37.rest_4_), channel_id=1, source_target_pairs={{0,1},{1,2},{2,3},{3,0},{4,5},{5,6},{6,7},{7,4},{8,11},{9,8},{10,9... | collective-permute-start | bytes 786440 | tf_op jit(solution)/shard_map/ppermute | solution.py:54
  115.4 8.1 %collective-permute-start.39 = (bf16[512,256]{1,0:T(8,128)(2,1)S(1)}, bf16[512,256]{1,0:T(8,128)(2,1)S(1)}, u32[]{:S(2)}, u32[]{:S(2)}) collective-permute-start(bf16[512,256]{1,0:T(8,128)(2,1)S(1)} %collective-permute-done.35.rest_2_), channel_id=1, source_target_pairs={{0,4},{1,5},{2,6},{3,7},{4,0},{5,1},{6,2},{7,3},{8,12},{9,13},{10,... | collective-permute-start | bytes 786440 | tf_op jit(solution)/shard_map/ppermute | solution.py:54
  123.9 6.6 %collective-permute-done.39.rest_6_ = bf16[512,256]{1,0:T(8,128)(2,1)S(1)} collective-permute-done((bf16[512,256]{1,0:T(8,128)(2,1)S(1)}, bf16[512,256]{1,0:T(8,128)(2,1)S(1)}, u32[]{:S(2)}, u32[]{:S(2)}) %collective-permute-start.39) | collective-permute-done | bytes 262176 | tf_op jit(solution)/shard_map/ppermute | solution.py:54
  131.1 2.6 %apply_part.2 = (f32[256,768]{1,0:T(8,128)S(1)}, bf16[256,768]{1,0:T(8,128)(2,1)S(1)}) custom-call(s32[5]{0:T(128)S(1)} %stack.23.where, bf16[512,256]{1,0:T(8,128)(2,1)S(1)} %collective-permute-done.33.rest_0_, bf16[512,256]{1,0:T(8,128)(2,1)S(1)} %collective-permute-done.34.rest_1_, bf16[512,256]{1,0:T(8,128)(2,1)S(1)} %collective-permute-done.35.rest_2_, ...), custom_call_target="tpu_custom_call" | custom-call | flops 1610612736 | bytes 6422528 | tf_op jit(solution)/shard_map/apply_part/pallas_call | solution.py:185
  133.8 2.7 %apply_part.3 = (f32[256,768]{1,0:T(8,128)S(1)}, bf16[256,768]{1,0:T(8,128)(2,1)S(1)}) custom-call(s32[5]{0:T(128)S(1)} %stack.23.where, bf16[512,256]{1,0:T(8,128)(2,1)S(1)} %collective-permute-done.33.rest_0_, bf16[512,256]{1,0:T(8,128)(2,1)S(1)} %collective-permute-done.34.rest_1_, bf16[512,256]{1,0:T(8,128)(2,1)S(1)} %collective-permute-done.35.rest_2_, ...), custom_call_target="tpu_custom_call" | custom-call | flops 1610612736 | bytes 6422528 | tf_op jit(solution)/shard_map/apply_part/pallas_call | solution.py:185
  (82 shorter events, 28.3 us)
Async XLA Ops:
  0.1 21.0 %collective-permute-start.3 = (bf16[256,1536]{1,0:T(8,128)(2,1)}, bf16[256,1536]{1,0:T(8,128)(2,1)S(1)}, u32[]{:S(2)}, u32[]{:S(2)}) collective-permute-start(bf16[256,1536]{1,0:T(8,128)(2,1)} %rest_8_.1), channel_id=1, source_target_pairs={{0,16},{1,17},{2,18},{3,19},{4,20},{5,21},{6,22},{7,23},{8,24},{9,... | collective-permute-start | bytes 2359304 | tf_op jit(solution)/shard_map/ppermute | solution.py:54
  3.4 26.8 %collective-permute-start = (bf16[256,1536]{1,0:T(8,128)(2,1)}, bf16[256,1536]{1,0:T(8,128)(2,1)S(1)}, u32[]{:S(2)}, u32[]{:S(2)}) collective-permute-start(bf16[256,1536]{1,0:T(8,128)(2,1)} %rest_8_.1), channel_id=1, source_target_pairs={{0,8},{1,9},{2,10},{3,11},{4,12},{5,13},{6,14},{7,15},{8,0},{9,1},... | collective-permute-start | bytes 2359304 | tf_op jit(solution)/shard_map/ppermute | solution.py:54
  3.4 26.8 %collective-permute-start.1 = (bf16[256,1536]{1,0:T(8,128)(2,1)}, bf16[256,1536]{1,0:T(8,128)(2,1)S(1)}, u32[]{:S(2)}, u32[]{:S(2)}) collective-permute-start(bf16[256,1536]{1,0:T(8,128)(2,1)} %rest_8_.1), channel_id=1, source_target_pairs={{0,96},{1,97},{2,98},{3,99},{4,100},{5,101},{6,102},{7,103},{8,40}... | collective-permute-start | bytes 2359304 | tf_op jit(solution)/shard_map/ppermute | solution.py:54
  7.3 15.4 %collective-permute-start.5 = (bf16[128,1536]{1,0:T(8,128)(2,1)S(1)}, bf16[128,1536]{1,0:T(8,128)(2,1)S(1)}, u32[]{:S(2)}, u32[]{:S(2)}) collective-permute-start(bf16[128,1536]{1,0:T(8,128)(2,1)S(1)} %get-tuple-element.51), channel_id=1, source_target_pairs={{0,32},{1,33},{2,34},{3,35},{4,36},{5,37},{6,38},{7,39},{8,104},{9... | collective-permute-start | bytes 1179656 | tf_op jit(solution)/shard_map/ppermute | solution.py:54
  21.1 10.8 %collective-permute-start.4 = (bf16[256,1536]{1,0:T(8,128)(2,1)S(1)}, bf16[256,1536]{1,0:T(8,128)(2,1)S(1)}, u32[]{:S(2)}, u32[]{:S(2)}) collective-permute-start(bf16[256,1536]{1,0:T(8,128)(2,1)S(1)} %collective-permute-done.3.first.across.rest_12_), channel_id=1, source_target_pairs={{0,8},{1,9},{2,10},{3,11},{4,12},{5,13},{6,14},{7,15},{8,0},{9,1},... | collective-permute-start | bytes 2359304 | tf_op jit(solution)/shard_map/ppermute | solution.py:54
  21.1 9.0 %collective-permute-start.2 = (bf16[128,1536]{1,0:T(8,128)(2,1)S(1)}, bf16[128,1536]{1,0:T(8,128)(2,1)S(1)}, u32[]{:S(2)}, u32[]{:S(2)}) collective-permute-start(bf16[128,1536]{1,0:T(8,128)(2,1)S(1)} %get-tuple-element.52), channel_id=1, source_target_pairs={{0,32},{1,33},{2,34},{3,35},{4,36},{5,37},{6,38},{7,39},{8,104},{9... | collective-permute-start | bytes 1179656 | tf_op jit(solution)/shard_map/ppermute | solution.py:54
  22.7 11.7 %collective-permute-start.6 = (bf16[128,1536]{1,0:T(8,128)(2,1)S(1)}, bf16[128,1536]{1,0:T(8,128)(2,1)S(1)}, u32[]{:S(2)}, u32[]{:S(2)}) collective-permute-start(bf16[128,1536]{1,0:T(8,128)(2,1)S(1)} %collective-permute-done.5), channel_id=1, source_target_pairs={{0,32},{1,33},{2,34},{3,35},{4,36},{5,37},{6,38},{7,39},{8,104},{9... | collective-permute-start | bytes 1179656 | tf_op jit(solution)/shard_map/ppermute | solution.py:54
  30.1 9.0 %collective-permute-start.7 = (bf16[128,1536]{1,0:T(8,128)(2,1)S(1)}, bf16[128,1536]{1,0:T(8,128)(2,1)S(1)}, u32[]{:S(2)}, u32[]{:S(2)}) collective-permute-start(bf16[128,1536]{1,0:T(8,128)(2,1)S(1)} %collective-permute-done.2), channel_id=1, source_target_pairs={{0,32},{1,33},{2,34},{3,35},{4,36},{5,37},{6,38},{7,39},{8,104},{9... | collective-permute-start | bytes 1179656 | tf_op jit(solution)/shard_map/ppermute | solution.py:54
  41.0 9.4 %collective-permute-start.12 = (bf16[512,256]{1,0:T(8,128)(2,1)S(1)}, bf16[512,256]{1,0:T(8,128)(2,1)S(1)}, u32[]{:S(2)}, u32[]{:S(2)}) collective-permute-start(bf16[512,256]{1,0:T(8,128)(2,1)S(1)} %get-tuple-element.43), channel_id=1, source_target_pairs={{0,3},{1,0},{2,1},{3,2},{4,7},{5,4},{6,5},{7,6},{8,9},{9,10},{10,1... | collective-permute-start | bytes 786440 | tf_op jit(solution)/shard_map/ppermute | solution.py:54
  45.1 7.7 %collective-permute-start.8 = (bf16[512,256]{1,0:T(8,128)(2,1)S(1)}, bf16[512,256]{1,0:T(8,128)(2,1)S(1)}, u32[]{:S(2)}, u32[]{:S(2)}) collective-permute-start(bf16[512,256]{1,0:T(8,128)(2,1)S(1)} %get-tuple-element.38), channel_id=1, source_target_pairs={{0,3},{1,0},{2,1},{3,2},{4,7},{5,4},{6,5},{7,6},{8,9},{9,10},{10,1... | collective-permute-start | bytes 786440 | tf_op jit(solution)/shard_map/ppermute | solution.py:54
  45.5 20.8 %collective-permute-start.15 = (bf16[256,1536]{1,0:T(8,128)(2,1)S(1)}, bf16[256,1536]{1,0:T(8,128)(2,1)S(1)}, u32[]{:S(2)}, u32[]{:S(2)}) collective-permute-start(bf16[256,1536]{1,0:T(8,128)(2,1)S(1)} %collective-permute-done.3.first.across.rest_12_), channel_id=1, source_target_pairs={{0,32},{1,33},{2,34},{3,35},{4,36},{5,37},{6,38},{7,39},{8,104},{9... | collective-permute-start | bytes 2359304 | tf_op jit(solution)/shard_map/ppermute | solution.py:54
  45.5 20.8 %collective-permute-start.16 = (bf16[256,1536]{1,0:T(8,128)(2,1)S(1)}, bf16[256,1536]{1,0:T(8,128)(2,1)S(1)}, u32[]{:S(2)}, u32[]{:S(2)}) collective-permute-start(bf16[256,1536]{1,0:T(8,128)(2,1)S(1)} %collective-permute-done.3.first.across.rest_12_), channel_id=1, source_target_pairs={{0,96},{1,97},{2,98},{3,99},{4,100},{5,101},{6,102},{7,103},{8,40}... | collective-permute-start | bytes 2359304 | tf_op jit(solution)/shard_map/ppermute | solution.py:54
  50.4 9.1 %collective-permute-start.13 = (bf16[512,256]{1,0:T(8,128)(2,1)S(1)}, bf16[512,256]{1,0:T(8,128)(2,1)S(1)}, u32[]{:S(2)}, u32[]{:S(2)}) collective-permute-start(bf16[512,256]{1,0:T(8,128)(2,1)S(1)} %add_convert_fusion.3), channel_id=1, source_target_pairs={{0,3},{1,0},{2,1},{3,2},{4,7},{5,4},{6,5},{7,6},{8,9},{9,10},{10,1... | collective-permute-start | bytes 786440 | tf_op jit(solution)/shard_map/ppermute | solution.py:54
  52.9 9.4 %collective-permute-start.9 = (bf16[512,256]{1,0:T(8,128)(2,1)S(1)}, bf16[512,256]{1,0:T(8,128)(2,1)S(1)}, u32[]{:S(2)}, u32[]{:S(2)}) collective-permute-start(bf16[512,256]{1,0:T(8,128)(2,1)S(1)} %add_convert_fusion.5), channel_id=1, source_target_pairs={{0,3},{1,0},{2,1},{3,2},{4,7},{5,4},{6,5},{7,6},{8,9},{9,10},{10,1... | collective-permute-start | bytes 786440 | tf_op jit(solution)/shard_map/ppermute | solution.py:54
  55.7 7.7 %collective-permute-start.11 = (bf16[512,256]{1,0:T(8,128)(2,1)S(1)}, bf16[512,256]{1,0:T(8,128)(2,1)S(1)}, u32[]{:S(2)}, u32[]{:S(2)}) collective-permute-start(bf16[512,256]{1,0:T(8,128)(2,1)S(1)} %add_convert_fusion.4), channel_id=1, source_target_pairs={{0,1},{1,2},{2,3},{3,0},{4,5},{5,6},{6,7},{7,4},{8,11},{9,8},{10,9... | collective-permute-start | bytes 786440 | tf_op jit(solution)/shard_map/ppermute | solution.py:54
  66.4 10.7 %collective-permute-start.20 = (bf16[512,256]{1,0:T(8,128)(2,1)S(1)}, bf16[512,256]{1,0:T(8,128)(2,1)S(1)}, u32[]{:S(2)}, u32[]{:S(2)}) collective-permute-start(bf16[512,256]{1,0:T(8,128)(2,1)S(1)} %add_convert_fusion.1.rest_0_), channel_id=1, source_target_pairs={{0,16},{1,17},{2,18},{3,19},{4,20},{5,21},{6,22},{7,23},{8,24},{9,... | collective-permute-start | bytes 786440 | tf_op jit(solution)/shard_map/ppermute | solution.py:54
  69.7 8.8 %collective-permute-start.17 = (bf16[512,256]{1,0:T(8,128)(2,1)S(1)}, bf16[512,256]{1,0:T(8,128)(2,1)S(1)}, u32[]{:S(2)}, u32[]{:S(2)}) collective-permute-start(bf16[512,256]{1,0:T(8,128)(2,1)S(1)} %add_convert_fusion.1.rest_0_), channel_id=1, source_target_pairs={{0,1},{1,2},{2,3},{3,0},{4,5},{5,6},{6,7},{7,4},{8,11},{9,8},{10,9... | collective-permute-start | bytes 786440 | tf_op jit(solution)/shard_map/ppermute | solution.py:54
  71.3 9.0 %collective-permute-start.18 = (bf16[512,256]{1,0:T(8,128)(2,1)S(1)}, bf16[512,256]{1,0:T(8,128)(2,1)S(1)}, u32[]{:S(2)}, u32[]{:S(2)}) collective-permute-start(bf16[512,256]{1,0:T(8,128)(2,1)S(1)} %add_convert_fusion.1.rest_0_), channel_id=1, source_target_pairs={{0,3},{1,0},{2,1},{3,2},{4,7},{5,4},{6,5},{7,6},{8,9},{9,10},{10,1... | collective-permute-start | bytes 786440 | tf_op jit(solution)/shard_map/ppermute | solution.py:54
  72.9 9.6 %collective-permute-start.28 = (bf16[256,512]{1,0:T(8,128)(2,1)S(1)}, bf16[256,512]{1,0:T(8,128)(2,1)S(1)}, u32[]{:S(2)}, u32[]{:S(2)}) collective-permute-start(bf16[256,512]{1,0:T(8,128)(2,1)S(1)} %pad_maximum_fusion.rest_8_), channel_id=1, source_target_pairs={{0,4},{1,5},{2,6},{3,7},{4,0},{5,1},{6,2},{7,3},{8,12},{9,13},{10,... | collective-permute-start | bytes 786440 | tf_op jit(solution)/shard_map/ppermute | solution.py:54
  73.7 8.9 %collective-permute-start.25 = (bf16[256,512]{1,0:T(8,128)(2,1)S(1)}, bf16[256,512]{1,0:T(8,128)(2,1)S(1)}, u32[]{:S(2)}, u32[]{:S(2)}) collective-permute-start(bf16[256,512]{1,0:T(8,128)(2,1)S(1)} %pad_maximum_fusion.rest_8_), channel_id=1, source_target_pairs={{0,32},{1,33},{2,34},{3,35},{4,36},{5,37},{6,38},{7,39},{8,104},{9... | collective-permute-start | bytes 786440 | tf_op jit(solution)/shard_map/ppermute | solution.py:54
  80.3 8.6 %collective-permute-start.19 = (bf16[512,256]{1,0:T(8,128)(2,1)S(1)}, bf16[512,256]{1,0:T(8,128)(2,1)S(1)}, u32[]{:S(2)}, u32[]{:S(2)}) collective-permute-start(bf16[512,256]{1,0:T(8,128)(2,1)S(1)} %collective-permute-done.17.rest_1_), channel_id=1, source_target_pairs={{0,1},{1,2},{2,3},{3,0},{4,5},{5,6},{6,7},{7,4},{8,11},{9,8},{10,9... | collective-permute-start | bytes 786440 | tf_op jit(solution)/shard_map/ppermute | solution.py:54
  82.6 10.7 %collective-permute-start.22 = (bf16[512,256]{1,0:T(8,128)(2,1)S(1)}, bf16[512,256]{1,0:T(8,128)(2,1)S(1)}, u32[]{:S(2)}, u32[]{:S(2)}) collective-permute-start(bf16[512,256]{1,0:T(8,128)(2,1)S(1)} %collective-permute-done.18.rest_2_), channel_id=1, source_target_pairs={{0,16},{1,17},{2,18},{3,19},{4,20},{5,21},{6,22},{7,23},{8,24},{9,... | collective-permute-start | bytes 786440 | tf_op jit(solution)/shard_map/ppermute | solution.py:54
  84.4 8.9 %collective-permute-start.27 = (bf16[256,512]{1,0:T(8,128)(2,1)S(1)}, bf16[256,512]{1,0:T(8,128)(2,1)S(1)}, u32[]{:S(2)}, u32[]{:S(2)}) collective-permute-start(bf16[256,512]{1,0:T(8,128)(2,1)S(1)} %collective-permute-done.25.rest_9_), channel_id=1, source_target_pairs={{0,32},{1,33},{2,34},{3,35},{4,36},{5,37},{6,38},{7,39},{8,104},{9... | collective-permute-start | bytes 786440 | tf_op jit(solution)/shard_map/ppermute | solution.py:54
  86.1 11.0 %collective-permute-start.30 = (bf16[256,512]{1,0:T(8,128)(2,1)S(1)}, bf16[256,512]{1,0:T(8,128)(2,1)S(1)}, u32[]{:S(2)}, u32[]{:S(2)}) collective-permute-start(bf16[256,512]{1,0:T(8,128)(2,1)S(1)} %collective-permute-done.26.rest_10_), channel_id=1, source_target_pairs={{0,4},{1,5},{2,6},{3,7},{4,0},{5,1},{6,2},{7,3},{8,12},{9,13},{10,... | collective-permute-start | bytes 786440 | tf_op jit(solution)/shard_map/ppermute | solution.py:54
  88.9 8.2 %collective-permute-start.23 = (bf16[512,256]{1,0:T(8,128)(2,1)S(1)}, bf16[512,256]{1,0:T(8,128)(2,1)S(1)}, u32[]{:S(2)}, u32[]{:S(2)}) collective-permute-start(bf16[512,256]{1,0:T(8,128)(2,1)S(1)} %collective-permute-done.21.rest_5_), channel_id=1, source_target_pairs={{0,1},{1,2},{2,3},{3,0},{4,5},{5,6},{6,7},{7,4},{8,11},{9,8},{10,9... | collective-permute-start | bytes 786440 | tf_op jit(solution)/shard_map/ppermute | solution.py:54
  101.5 22.4 %collective-permute-start.41 = (bf16[256,1536]{1,0:T(8,128)(2,1)S(1)}, bf16[256,1536]{1,0:T(8,128)(2,1)S(1)}, u32[]{:S(2)}, u32[]{:S(2)}) collective-permute-start(bf16[256,1536]{1,0:T(8,128)(2,1)S(1)} %collective-permute-done.15.rest_13_), channel_id=1, source_target_pairs={{0,32},{1,33},{2,34},{3,35},{4,36},{5,37},{6,38},{7,39},{8,104},{9... | collective-permute-start | bytes 2359304 | tf_op jit(solution)/shard_map/ppermute | solution.py:54
  101.6 11.2 %collective-permute-start.37 = (bf16[512,256]{1,0:T(8,128)(2,1)S(1)}, bf16[512,256]{1,0:T(8,128)(2,1)S(1)}, u32[]{:S(2)}, u32[]{:S(2)}) collective-permute-start(bf16[512,256]{1,0:T(8,128)(2,1)S(1)} %add_convert_fusion), channel_id=1, source_target_pairs={{0,4},{1,5},{2,6},{3,7},{4,20},{5,21},{6,22},{7,23},{8,12},{9,13},... | collective-permute-start | bytes 786440 | tf_op jit(solution)/shard_map/ppermute | solution.py:54
  106.3 9.1 %collective-permute-start.34 = (bf16[512,256]{1,0:T(8,128)(2,1)S(1)}, bf16[512,256]{1,0:T(8,128)(2,1)S(1)}, u32[]{:S(2)}, u32[]{:S(2)}) collective-permute-start(bf16[512,256]{1,0:T(8,128)(2,1)S(1)} %collective-permute-done.33.rest_0_), channel_id=1, source_target_pairs={{0,1},{1,2},{2,3},{3,0},{4,5},{5,6},{6,7},{7,4},{8,11},{9,8},{10,9... | collective-permute-start | bytes 786440 | tf_op jit(solution)/shard_map/ppermute | solution.py:54
  106.6 8.8 %collective-permute-start.35 = (bf16[512,256]{1,0:T(8,128)(2,1)S(1)}, bf16[512,256]{1,0:T(8,128)(2,1)S(1)}, u32[]{:S(2)}, u32[]{:S(2)}) collective-permute-start(bf16[512,256]{1,0:T(8,128)(2,1)S(1)} %collective-permute-done.33.rest_0_), channel_id=1, source_target_pairs={{0,3},{1,0},{2,1},{3,2},{4,7},{5,4},{6,5},{7,6},{8,9},{9,10},{10,1... | collective-permute-start | bytes 786440 | tf_op jit(solution)/shard_map/ppermute | solution.py:54
  112.8 10.7 %collective-permute-start.38 = (bf16[512,256]{1,0:T(8,128)(2,1)S(1)}, bf16[512,256]{1,0:T(8,128)(2,1)S(1)}, u32[]{:S(2)}, u32[]{:S(2)}) collective-permute-start(bf16[512,256]{1,0:T(8,128)(2,1)S(1)} %collective-permute-done.37.rest_4_), channel_id=1, source_target_pairs={{0,1},{1,2},{2,3},{3,0},{4,5},{5,6},{6,7},{7,4},{8,11},{9,8},{10,9... | collective-permute-start | bytes 786440 | tf_op jit(solution)/shard_map/ppermute | solution.py:54
  115.4 8.4 %collective-permute-start.36 = (bf16[512,256]{1,0:T(8,128)(2,1)S(1)}, bf16[512,256]{1,0:T(8,128)(2,1)S(1)}, u32[]{:S(2)}, u32[]{:S(2)}) collective-permute-start(bf16[512,256]{1,0:T(8,128)(2,1)S(1)} %collective-permute-done.34.rest_1_), channel_id=1, source_target_pairs={{0,1},{1,2},{2,3},{3,0},{4,5},{5,6},{6,7},{7,4},{8,11},{9,8},{10,9... | collective-permute-start | bytes 786440 | tf_op jit(solution)/shard_map/ppermute | solution.py:54
  115.4 15.0 %collective-permute-start.39 = (bf16[512,256]{1,0:T(8,128)(2,1)S(1)}, bf16[512,256]{1,0:T(8,128)(2,1)S(1)}, u32[]{:S(2)}, u32[]{:S(2)}) collective-permute-start(bf16[512,256]{1,0:T(8,128)(2,1)S(1)} %collective-permute-done.35.rest_2_), channel_id=1, source_target_pairs={{0,4},{1,5},{2,6},{3,7},{4,0},{5,1},{6,2},{7,3},{8,12},{9,13},{10,... | collective-permute-start | bytes 786440 | tf_op jit(solution)/shard_map/ppermute | solution.py:54
  (13 other events, 79.3 us)
